TPU v7x, 32 devices: a whole 2x2x4 slice. The times are simulated.
32 devices in a mesh: dp: 2 (over core), ctx: 16 (over z, y, x).
Axes of the slice: x: 2, y: 2, z: 4, core: 2. Of those that a mesh axis runs over, the one named last changes fastest.
Arguments:
- latent_in: bfloat16 [4096, 1024], P(('dp', 'ctx')), may hold values from -6 to 6
- gain_attn: float32 [1024], replicated, may hold values from 0.4 to 1.6
- w_query: bfloat16 [1024, 1024], replicated, may hold values from -0.1875 to 0.1875
- w_key: bfloat16 [1024, 1024], replicated, may hold values from -0.1875 to 0.1875
- w_value: bfloat16 [1024, 1024], replicated, may hold values from -0.1875 to 0.1875
- w_out: bfloat16 [1024, 1024], replicated, may hold values from -0.75 to 0.75
- gain_ffn: float32 [1024], replicated, may hold values from 0.4 to 1.6
- w_gate: bfloat16 [1024, 2816], replicated, may hold values from -0.1875 to 0.1875
- w_up: bfloat16 [1024, 2816], replicated, may hold values from -0.1875 to 0.1875
- w_down: bfloat16 [2816, 1024], replicated, may hold values from -0.109375 to 0.109375
- cotangent: bfloat16 [4096, 1024], P(('dp', 'ctx')), may hold values from -6 to 6
- seq_lengths: int32 [2, 4], P('dp'), may hold values from 1 to 1024, as said below
- span_order: int32 [2, 16], P('dp'), may hold values from 0 to 15, as said below
Outputs:
- latents: bfloat16 [4096, 1024], P(('dp', 'ctx'))
- latent_grad: bfloat16 [4096, 1024], P(('dp', 'ctx'))
- gain_attn_grad: float32 [1024], P(('dp', 'ctx'))
- query_grad: float32 [1024, 1024], P(('dp', 'ctx'))
- key_grad: float32 [1024, 1024], P(('dp', 'ctx'))
- value_grad: float32 [1024, 1024], P(('dp', 'ctx'))
- out_grad: float32 [1024, 1024], P(('dp', 'ctx'))
- gain_ffn_grad: float32 [1024], P(('dp', 'ctx'))
- gate_grad: float32 [1024, 2816], P(('dp', 'ctx'))
- up_grad: float32 [1024, 2816], P(('dp', 'ctx'))
- down_grad: float32 [2816, 1024], P(('dp', 'ctx'))
Inputs may be any that keep to these rules, and one draw needn't show every extreme that they name: `seq_lengths`: in each row the 4 lengths sum to at most 2048; exactly one of them is 1024; positions at or after the sum are padding. `span_order`: each row is a permutation of the 16 blocks of 128 positions of a group.
All inputs are finite; a program needn't handle non-finite values.
Results may differ from a plain program's by a relative error of at most 0.023.
Values may be sent and summed in bfloat16 or wider, within the bound.
No kernel may reach another device: no remote copies, remote signals or barrier semaphores. Data moves between devices by JAX's collectives and lax.ppermute only.
A program may use at most 256 MiB of HBM per device.

v0:
```python
import jax
import jax.numpy as jnp
from jax import lax
from jax.sharding import PartitionSpec as P

HEADS = 16
HEAD_DIM = 64


EPS = 1e-06
NEG_FILL = -1e30


def layout(lengths, span_of, rows_dev):
    group_rows = span_of.shape[0] * rows_dev
    row_ids = jnp.arange(group_rows, dtype=jnp.int32)
    position = span_of[row_ids // rows_dev] * rows_dev + row_ids % rows_dev
    seq_ends = jnp.cumsum(lengths)
    seq_id = jnp.sum((position[:, None] >= seq_ends[None, :]).astype(jnp.int32), axis=1)
    return (position, seq_id)


def norm_back(grad_normed, unit_rows, inv_rows, gain_vec):
    scaled = grad_normed * gain_vec
    return inv_rows * (scaled - unit_rows * jnp.mean(scaled * unit_rows, axis=-1, keepdims=True))


def sum_bucket(parts):
    return lax.psum_scatter(parts, ("dp", "ctx"), scatter_dimension=0, tiled=True)


def score_grads(
    query_b, grad_b, top_b, mass_b, delta_b, key_block, value_block, key_mask, score_scale
):
    scores = (
        jnp.einsum("qhd,khd->hqk", query_b, key_block, preferred_element_type=jnp.float32)
        * score_scale
    )
    scores = jnp.where(key_mask[None], scores, NEG_FILL)
    prob = jnp.where(key_mask[None], jnp.exp(scores - top_b[..., None]) / mass_b[..., None], 0.0)
    grad_prob = jnp.einsum("qhd,khd->hqk", grad_b, value_block, preferred_element_type=jnp.float32)
    grad_score = (prob * (grad_prob - delta_b[..., None])).astype(jnp.bfloat16)
    return (prob, grad_score)


def per_device(
    latent_in,
    gain_attn,
    w_query,
    w_key,
    w_value,
    w_out,
    gain_ffn,
    w_gate,
    w_up,
    w_down,
    cotangent,
    seq_lengths,
    span_order,
):
    rows_dev, width = latent_in.shape
    score_scale = HEAD_DIM ** (-0.5)
    position, seq_id = layout(seq_lengths[0], span_order[0], rows_dev)
    group_rows = position.shape[0]
    key_rows = 2 * rows_dev
    count_blk = group_rows // key_rows
    offset = lax.axis_index("ctx") * rows_dev
    query_pos = lax.dynamic_slice_in_dim(position, offset, rows_dev)
    query_seq = lax.dynamic_slice_in_dim(seq_id, offset, rows_dev)
    key_pos = position.reshape(count_blk, key_rows)
    key_seq = seq_id.reshape(count_blk, key_rows)
    latent_f = latent_in.astype(jnp.float32)
    inv_one = lax.rsqrt(jnp.mean(latent_f * latent_f, axis=-1, keepdims=True) + EPS)
    unit_one = latent_f * inv_one
    normed_one = (unit_one * gain_attn).astype(jnp.bfloat16)
    query_proj = jnp.dot(normed_one, w_query, preferred_element_type=jnp.float32).astype(
        jnp.bfloat16
    )
    key_proj = jnp.dot(normed_one, w_key, preferred_element_type=jnp.float32).astype(jnp.bfloat16)
    value_proj = jnp.dot(normed_one, w_value, preferred_element_type=jnp.float32).astype(
        jnp.bfloat16
    )
    keys_all, values_all = (
        lax.all_gather(key_proj, "ctx", axis=0, tiled=True),
        lax.all_gather(value_proj, "ctx", axis=0, tiled=True),
    )
    query_heads = query_proj.reshape(rows_dev, HEADS, HEAD_DIM)

    def split_blocks(keys_whole, values_whole):
        return (
            keys_whole.reshape(count_blk, key_rows, HEADS, HEAD_DIM),
            values_whole.reshape(count_blk, key_rows, HEADS, HEAD_DIM),
            key_pos,
            key_seq,
        )

    def block_mask(pos_blk, seq_blk):
        return (query_seq[:, None] == seq_blk[None, :]) & (pos_blk[None, :] <= query_pos[:, None])

    def forward_block(state_now, pieces):
        key_block, value_block, pos_blk, seq_blk = pieces
        key_mask = block_mask(pos_blk, seq_blk)
        row_top, row_mass, accum = state_now
        scores = (
            jnp.einsum("qhd,khd->hqk", query_heads, key_block, preferred_element_type=jnp.float32)
            * score_scale
        )
        scores = jnp.where(key_mask[None], scores, NEG_FILL)
        new_top = jnp.maximum(row_top, jnp.max(scores, axis=-1))
        shrink = jnp.exp(row_top - new_top)
        weight = jnp.where(key_mask[None], jnp.exp(scores - new_top[..., None]), 0.0)
        row_mass = row_mass * shrink + jnp.sum(weight, axis=-1)
        accum = accum * shrink.T[..., None] + jnp.einsum(
            "hqk,khd->qhd",
            weight.astype(jnp.bfloat16),
            value_block,
            preferred_element_type=jnp.float32,
        )
        state_now = (new_top, row_mass, accum)
        return (state_now, None)

    start_state = (
        jnp.full((HEADS, rows_dev), NEG_FILL, jnp.float32),
        jnp.zeros((HEADS, rows_dev), jnp.float32),
        jnp.zeros((rows_dev, HEADS, HEAD_DIM), jnp.float32),
    )
    (row_top, row_mass, accum), _ = lax.scan(
        forward_block, start_state, split_blocks(keys_all, values_all)
    )
    attn = accum / row_mass.T[..., None]
    attn_low = attn.reshape(rows_dev, width).astype(jnp.bfloat16)
    resid = latent_f + jnp.dot(attn_low, w_out, preferred_element_type=jnp.float32)
    inv_two = lax.rsqrt(jnp.mean(resid * resid, axis=-1, keepdims=True) + EPS)
    unit_two = resid * inv_two
    normed_two = (unit_two * gain_ffn).astype(jnp.bfloat16)
    gate_pre = jnp.dot(normed_two, w_gate, preferred_element_type=jnp.float32)
    up_pre = jnp.dot(normed_two, w_up, preferred_element_type=jnp.float32)
    gate_sig = jax.nn.sigmoid(gate_pre)
    swish = gate_pre * gate_sig
    hidden = (swish * up_pre).astype(jnp.bfloat16)
    latents = (resid + jnp.dot(hidden, w_down, preferred_element_type=jnp.float32)).astype(
        jnp.bfloat16
    )
    grad_top = cotangent.astype(jnp.float32)
    down_grad = jnp.einsum("tf,td->fd", hidden, cotangent, preferred_element_type=jnp.float32)
    (down_sum,) = sum_bucket((down_grad,))
    grad_hidden = jnp.einsum("td,fd->tf", cotangent, w_down, preferred_element_type=jnp.float32)
    grad_gate = (grad_hidden * up_pre * gate_sig * (1.0 + gate_pre * (1.0 - gate_sig))).astype(
        jnp.bfloat16
    )
    grad_up = (grad_hidden * swish).astype(jnp.bfloat16)
    grad_norm_two = jnp.einsum(
        "tf,df->td", grad_gate, w_gate, preferred_element_type=jnp.float32
    ) + jnp.einsum("tf,df->td", grad_up, w_up, preferred_element_type=jnp.float32)
    gain_ffn_grad = jnp.sum(grad_norm_two * unit_two, axis=0)
    gate_grad = jnp.einsum("td,tf->df", normed_two, grad_gate, preferred_element_type=jnp.float32)
    gate_sum, gain_ffn_sum = sum_bucket((gate_grad, gain_ffn_grad))
    up_grad = jnp.einsum("td,tf->df", normed_two, grad_up, preferred_element_type=jnp.float32)
    (up_sum,) = sum_bucket((up_grad,))
    grad_resid = grad_top + norm_back(grad_norm_two, unit_two, inv_two, gain_ffn)
    grad_mixed = grad_resid.astype(jnp.bfloat16)
    out_grad = jnp.einsum("td,te->de", attn_low, grad_mixed, preferred_element_type=jnp.float32)
    (out_sum,) = sum_bucket((out_grad,))
    grad_attn = jnp.einsum(
        "te,de->td", grad_mixed, w_out, preferred_element_type=jnp.float32
    ).astype(jnp.bfloat16)
    grad_heads = grad_attn.reshape(rows_dev, HEADS, HEAD_DIM)
    row_delta = jnp.sum(grad_heads.astype(jnp.float32) * attn, axis=-1).T
    keys_back, values_back = (
        lax.all_gather(key_proj, "ctx", axis=0, tiled=True),
        lax.all_gather(value_proj, "ctx", axis=0, tiled=True),
    )
    zeros_local = jnp.zeros((rows_dev, HEADS, HEAD_DIM), jnp.float32)

    def backward_block(grad_query, pieces):
        key_block, value_block, pos_blk, seq_blk = pieces
        key_mask = block_mask(pos_blk, seq_blk)
        grad_in = grad_query
        prob, grad_score = score_grads(
            query_heads,
            grad_heads,
            row_top,
            row_mass,
            row_delta,
            key_block,
            value_block,
            key_mask,
            score_scale,
        )
        grad_in = (
            grad_in
            + jnp.einsum("hqk,khd->qhd", grad_score, key_block, preferred_element_type=jnp.float32)
            * score_scale
        )
        grad_keys = (
            jnp.einsum("hqk,qhd->khd", grad_score, query_heads, preferred_element_type=jnp.float32)
            * score_scale
        )
        grad_values = jnp.einsum(
            "hqk,qhd->khd",
            prob.astype(jnp.bfloat16),
            grad_heads,
            preferred_element_type=jnp.float32,
        )
        return (grad_in, (grad_keys, grad_values))

    grad_query_heads, (key_parts, value_parts) = lax.scan(
        backward_block, zeros_local, split_blocks(keys_back, values_back)
    )
    key_sum, value_sum = (
        lax.psum_scatter(
            key_parts.reshape(group_rows, width).astype(jnp.bfloat16),
            "ctx",
            scatter_dimension=0,
            tiled=True,
        ).astype(jnp.float32),
        lax.psum_scatter(
            value_parts.reshape(group_rows, width).astype(jnp.bfloat16),
            "ctx",
            scatter_dimension=0,
            tiled=True,
        ).astype(jnp.float32),
    )
    grad_query = grad_query_heads.reshape(rows_dev, width).astype(jnp.bfloat16)
    grad_key = key_sum.astype(jnp.bfloat16)
    grad_value = value_sum.astype(jnp.bfloat16)
    query_grad = jnp.einsum("td,te->de", normed_one, grad_query, preferred_element_type=jnp.float32)
    key_grad = jnp.einsum("td,te->de", normed_one, grad_key, preferred_element_type=jnp.float32)
    value_grad = jnp.einsum("td,te->de", normed_one, grad_value, preferred_element_type=jnp.float32)
    grad_norm_one = (
        jnp.einsum("te,de->td", grad_query, w_query, preferred_element_type=jnp.float32)
        + jnp.einsum("te,de->td", grad_key, w_key, preferred_element_type=jnp.float32)
        + jnp.einsum("te,de->td", grad_value, w_value, preferred_element_type=jnp.float32)
    )
    gain_attn_grad = jnp.sum(grad_norm_one * unit_one, axis=0)
    latent_grad = (grad_resid + norm_back(grad_norm_one, unit_one, inv_one, gain_attn)).astype(
        jnp.bfloat16
    )
    gain_attn_sum, query_sum, key_grad_sum, value_grad_sum = sum_bucket(
        (gain_attn_grad, query_grad, key_grad, value_grad)
    )
    return (
        latents,
        latent_grad,
        gain_attn_sum,
        query_sum,
        key_grad_sum,
        value_grad_sum,
        out_sum,
        gain_ffn_sum,
        gate_sum,
        up_sum,
        down_sum,
    )


def solution(mesh):
    in_specs = (
        P(("dp", "ctx"), None),
        P(),
        P(),
        P(),
        P(),
        P(),
        P(),
        P(),
        P(),
        P(),
        P(("dp", "ctx"), None),
        P("dp", None),
        P("dp", None),
    )
    out_specs = (
        P(("dp", "ctx"), None),
        P(("dp", "ctx"), None),
        P(("dp", "ctx")),
        P(("dp", "ctx"), None),
        P(("dp", "ctx"), None),
        P(("dp", "ctx"), None),
        P(("dp", "ctx"), None),
        P(("dp", "ctx")),
        P(("dp", "ctx"), None),
        P(("dp", "ctx"), None),
        P(("dp", "ctx"), None),
    )
    return jax.shard_map(
        per_device, mesh=mesh, in_specs=in_specs, out_specs=out_specs, check_vma=False
    )
```

profile of v0, /device:TPU:10, one launch (start us, length us, event | category | flops | bytes accessed | tf_op | source)
XLA Modules:
  0.0 1879.9 jit_solution(2951099671496005023)
XLA Ops:
  8.5 2.9 convolution_convert_fusion.3
  14.1 4.6 compare_select_fusion.1
  18.7 5.6 fusion.59
  24.6 2.1 convolution_convert_fusion.2
  26.9 61.7 %all-gather.3.cloned.1.call-done = bf16[2048,1024]{1,0:T(8,128)(2,1)} async-done(((bf16[128,1024]{1,0:T(8,128)(2,1)}), bf16[2048,1024]{1,0:T(8,128)(2,1)}) %all-gather.3.cloned.1.call-update) | async-done | bytes 4194320 | tf_op jit(solution)/shard_map/all_gather | solution.py:84
  88.6 11.6 reshape.391
  100.2 10.3 copy.71
  110.5 56.2 %all-gather.5.cloned.1.call-done = bf16[2048,1024]{1,0:T(8,128)(2,1)} async-done(((bf16[128,1024]{1,0:T(8,128)(2,1)}), bf16[2048,1024]{1,0:T(8,128)(2,1)}) %all-gather.5.cloned.1.call-update) | async-done | bytes 4194320 | tf_op jit(solution)/shard_map/all_gather | solution.py:85
  166.7 11.6 reshape.392
  178.2 10.3 copy.72
  188.6 39.7 %while.30 = (s32[]{:T(128)}, f32[16,128]{1,0:T(8,128)S(1)}, f32[16,128]{1,0:T(8,128)S(1)}, f32[128,16,64]{0,2,1:T(8,128)}, s32[128]{0:T(128)S(1)}, /*index=5*/s3...) while((s32[]{:T(128)}, f32[16,128]{1,0:T(8,128)S(1)}, ...), condition=%wide.region_6.7_spmd.clone, body=%wide.region_3.6_spmd.clone.sunk | while | flops 141537280 | bytes 13114581 | solution.py:127
  229.5 2.3 multiply_reduce_fusion.3
  232.0 4.5 fusion.76
  237.5 3.2 multiply_convert_fusion
  240.8 2.0 fusion.77
  242.8 2.1 multiply_reduce_fusion
  249.7 60.7 %while.31 = (s32[]{:T(128)}, f32[128,16,64]{0,2,1:T(8,128)S(1)}, bf16[8,256,16,64]{1,3,2,0:T(8,128)(2,1)}, bf16[8,256,16,64]{1,3,2,0:T(8,128)(2,1)}, bf16[8,256,...) while((s32[]{:T(128)}, f32[128,16,64]{0,2,1:T(8,128)S(1)}, ...), condition=%wide.region_11.12_spmd.clone, body=%wide.region_10.11_spmd.clone.sunk | while | flops 341016576 | bytes 15301831 | solution.py:207
  249.9 1.8 fusion.164
  257.4 1.8 fusion.164
  265.0 1.8 fusion.164
  272.7 1.8 fusion.164
  280.3 1.8 fusion.164
  287.8 1.8 fusion.164
  295.4 1.8 fusion.164
  303.0 1.8 fusion.164
  310.4 10.9 copy.91
  321.3 11.9 reshape.389
  333.3 11.1 copy.90
  344.4 11.9 reshape.387
  357.4 3.6 fusion.56
  361.8 2.9 fusion.69
  364.8 61.9 %reduce-scatter.30.cloned.1.call-done = bf16[128,1024]{1,0:T(8,128)(2,1)} async-done(((bf16[2048,1024]{1,0:T(8,128)(2,1)}), bf16[128,1024]{1,0:T(8,128)(2,1)}) %reduce-scatter.30.cloned.1.call-update) | async-done | bytes 262160
  426.7 3.8 fusion.65
  430.6 93.0 %reduce-scatter.28.cloned.1.call-done = bf16[128,1024]{1,0:T(8,128)(2,1)} async-done(((bf16[2048,1024]{1,0:T(8,128)(2,1)}), bf16[128,1024]{1,0:T(8,128)(2,1)}) %reduce-scatter.28.cloned.1.call-update) | async-done | bytes 262160
  523.6 3.7 fusion.67
  528.3 7.2 fusion.80
  535.5 7.0 fusion.79
  543.5 7.0 fusion.81
  551.4 2.5 fusion.78
  554.0 4.5 fusion.42
  560.4 41.5 %all-reduce.2 = (f32[1024]{0:T(1024)S(1)}, f32[1024]{0:T(1024)S(1)}) all-reduce(f32[1024]{0:T(1024)S(1)} %get-tuple-element.345, f32[1024]{0:T(1024)S(1)} %get-tuple-element.343), channel_id=4, replica_groups=mesh['dp'=2,'ctx'=16] {'dp','ctx'}, use_global_device_ids=true, to_apply=%region_16.17.clone | all-reduce | flops 2048 | bytes 16384
  604.0 62.4 %reduce-scatter.20.cloned.1.call-done = f32[32,1024]{1,0:T(8,128)} async-done(((f32[1024,1024]{1,0:T(8,128)}), f32[32,1024]{1,0:T(8,128)}) %reduce-scatter.20.cloned.1.call-update) | async-done | bytes 131088 | tf_op jit(solution)/shard_map/reduce_scatter | solution.py:29
  666.4 146.7 %reduce-scatter.14.cloned.1.call-done = f32[32,1024]{1,0:T(8,128)} async-done(((f32[1024,1024]{1,0:T(8,128)}), f32[32,1024]{1,0:T(8,128)}) %reduce-scatter.14.cloned.1.call-update) | async-done | bytes 131088 | tf_op jit(solution)/shard_map/reduce_scatter | solution.py:29
  813.1 147.2 %reduce-scatter.18.cloned.1.call-done = f32[32,1024]{1,0:T(8,128)} async-done(((f32[1024,1024]{1,0:T(8,128)}), f32[32,1024]{1,0:T(8,128)}) %reduce-scatter.18.cloned.1.call-update) | async-done | bytes 131088 | tf_op jit(solution)/shard_map/reduce_scatter | solution.py:29
  960.3 147.1 %reduce-scatter.16.cloned.1.call-done = f32[32,1024]{1,0:T(8,128)} async-done(((f32[1024,1024]{1,0:T(8,128)}), f32[32,1024]{1,0:T(8,128)}) %reduce-scatter.16.cloned.1.call-update) | async-done | bytes 131088 | tf_op jit(solution)/shard_map/reduce_scatter | solution.py:29
  1107.3 259.2 %reduce-scatter.24.cloned.1.call-done = f32[32,2816]{1,0:T(8,128)} async-done(((f32[1024,2816]{1,0:T(8,128)}), f32[32,2816]{1,0:T(8,128)}) %reduce-scatter.24.cloned.1.call-update) | async-done | bytes 360464 | tf_op jit(solution)/shard_map/reduce_scatter | solution.py:29
  1366.6 253.3 %reduce-scatter.22.cloned.1.call-done = f32[32,2816]{1,0:T(8,128)} async-done(((f32[1024,2816]{1,0:T(8,128)}), f32[32,2816]{1,0:T(8,128)}) %reduce-scatter.22.cloned.1.call-update) | async-done | bytes 360464 | tf_op jit(solution)/shard_map/reduce_scatter | solution.py:29
  1619.9 253.5 %reduce-scatter.26.cloned.1.call-done = f32[88,1024]{1,0:T(8,128)} async-done(((f32[2816,1024]{1,0:T(8,128)}), f32[88,1024]{1,0:T(8,128)}) %reduce-scatter.26.cloned.1.call-update) | async-done | bytes 360464 | tf_op jit(solution)/shard_map/reduce_scatter | solution.py:29
  (274 shorter events, 105.2 us)
Async XLA Ops:
  7.2 4.3 copy-start
  7.2 4.3 copy-start.1
  7.2 4.3 copy-start.23
  7.2 81.4 %all-gather.3.cloned.1.call-start = ((), (), s32[]{:S(2)}) async-start(), calls=%async_computation.9 | async-start | bytes 4456448 | tf_op jit(solution)/shard_map/all_gather | solution.py:84
  11.4 1.4 copy-start.26
  11.4 2.0 copy-start.24
  11.4 155.2 %all-gather.5.cloned.1.call-start = ((), (), s32[]{:S(2)}) async-start(), calls=%async_computation.10 | async-start | bytes 4456448 | tf_op jit(solution)/shard_map/all_gather | solution.py:85
  12.7 414.0 %reduce-scatter.30.cloned.1.call-start = ((), (), s32[]{:S(2)}) async-start(), calls=%async_computation.19 | async-start | bytes 4456448
  188.7 2.2 copy-start.17
  193.7 2.2 copy-start.17
  198.7 2.2 copy-start.17
  203.6 2.2 copy-start.17
  208.6 2.2 copy-start.17
  213.6 2.2 copy-start.17
  218.5 2.2 copy-start.17
  223.5 2.2 copy-start.17
  228.3 3.5 copy-start.25
  229.4 2.4 copy-start.14
  229.4 7.0 slice-start
  229.5 8.0 slice-start.4
  231.8 13.1 copy-start.2
  231.9 4.5 copy-start.4
  231.9 4.6 slice-start.1
  231.9 5.5 slice-start.5
  236.5 1.0 copy-start.19
  236.5 6.2 slice-start.2
  237.5 5.2 slice-start.3
  240.7 2.0 copy-start.12
  240.7 2.0 copy-start.13
  242.8 3.1 copy-start.6
  333.2 190.4 %reduce-scatter.28.cloned.1.call-start = ((), (), s32[]{:S(2)}) async-start(), calls=%async_computation.18 | async-start | bytes 4456448
  356.3 1.0 copy-start.9
  356.4 310.0 %reduce-scatter.20.cloned.1.call-start = ((), (), s32[]{:S(2)}) async-start(), calls=%async_computation.14 | async-start | bytes 4325376 | tf_op jit(solution)/shard_map/reduce_scatter | solution.py:29
  361.0 452.1 %reduce-scatter.14.cloned.1.call-start = ((), (), s32[]{:S(2)}) async-start(), calls=%async_computation.11 | async-start | bytes 4325376 | tf_op jit(solution)/shard_map/reduce_scatter | solution.py:29
  364.8 595.5 %reduce-scatter.18.cloned.1.call-start = ((), (), s32[]{:S(2)}) async-start(), calls=%async_computation.13 | async-start | bytes 4325376 | tf_op jit(solution)/shard_map/reduce_scatter | solution.py:29
  430.5 676.8 %reduce-scatter.16.cloned.1.call-start = ((), (), s32[]{:S(2)}) async-start(), calls=%async_computation.12 | async-start | bytes 4325376 | tf_op jit(solution)/shard_map/reduce_scatter | solution.py:29
  527.3 0.9 copy-start.5
  527.4 839.2 %reduce-scatter.24.cloned.1.call-start = ((), (), s32[]{:S(2)}) async-start(), calls=%async_computation.16 | async-start | bytes 11894784 | tf_op jit(solution)/shard_map/reduce_scatter | solution.py:29
  535.5 1084.4 %reduce-scatter.22.cloned.1.call-start = ((), (), s32[]{:S(2)}) async-start(), calls=%async_computation.15 | async-start | bytes 11894784 | tf_op jit(solution)/shard_map/reduce_scatter | solution.py:29
  542.5 1.0 copy-start.20
  542.6 1330.8 %reduce-scatter.26.cloned.1.call-start = ((), (), s32[]{:S(2)}) async-start(), calls=%async_computation.17 | async-start | bytes 11894784 | tf_op jit(solution)/shard_map/reduce_scatter | solution.py:29
  550.5 1.0 copy-start.16
  550.5 3.4 copy-start.3
  551.4 2.5 copy-start.11
  554.0 4.5 copy-start.7
  554.0 4.5 copy-start.22
  558.5 1.0 copy-start.21
  559.4 43.7 %copy-start.10 = (f32[128,1024]{1,0:T(8,128)S(1)}, f32[128,1024]{1,0:T(8,128)}, u32[]{:S(2)}) copy-start(f32[128,1024]{1,0:T(8,128)} %copy-done.8) | copy-start | bytes 1572868
  (10 other events, 7.9 us)
Sparse Core Ops, SparseCore 0:
  11.6 76.9 all-gather.2
  91.9 74.6 all-gather.4
  333.4 93.3 reduce-scatter.29
  428.9 94.7 reduce-scatter.27
  526.3 140.0 reduce-scatter.19
  669.1 143.9 reduce-scatter.13
  816.0 144.2 reduce-scatter.17
  963.1 144.1 reduce-scatter.15
  1110.2 256.3 reduce-scatter.23
  1369.3 250.5 reduce-scatter.21
  1622.8 250.5 reduce-scatter.25
where the time goes:
time: 1880 us
  waiting for transfers between devices  1540 us (82%)
  matrix products  154 us (8%)
  local copies, waits for them, and re-layouts  104 us (6%)
  blocking collectives  41.5 us (2%)
  other arithmetic  22 us (1%)
    reduce_scatter x7, waiting for transfers between devices, sum_bucket(): lax.psum_scatter(parts, ('dp', 'ctx'), scatter_dimension=0, tiled=True)  1270 us
    unnamed x13, waiting for transfers between devices  155 us
    unnamed x70, local copies, waits for them, and re-layouts  72.8 us
    all_gather x1, waiting for transfers between devices, per_device(): lax.all_gather(key_proj, 'ctx', axis=0, tiled=True)  61.7 us
    all_gather x1, waiting for transfers between devices, per_device(): lax.all_gather(value_proj, 'ctx', axis=0, tiled=True)  56.2 us
    unnamed x1, blocking collectives  41.5 us
  transfers between devices with their start and end apart: 11, of which 11 were waited for; matrix products, arithmetic and copies ran while one was open for 6% of the time, Pallas kernels for 0%

commit v1 on v0

v1 whole, which is shorter than its diff:
```python
import functools

import jax
import jax.numpy as jnp
from jax import lax
from jax.experimental import pallas as pl
from jax.experimental.pallas import tpu as pltpu
from jax.sharding import PartitionSpec as P

HEADS = 16
HEAD_DIM = 64
EPS = 1e-06
NEG_FILL = -1e30
LOG2E = 1.4426950408889634
SCALE = HEAD_DIM**-0.5

BF16 = jnp.bfloat16
F32 = jnp.float32


def dot(a, b, dims):
    return lax.dot_general(a, b, (dims, ((), ())), preferred_element_type=F32)


def query_starts(ends_ref, pos):
    start = jnp.zeros_like(pos)
    for n in range(ends_ref.shape[0]):
        start = jnp.where(pos >= ends_ref[n], ends_ref[n], start)
    return start


def block_mask(ends_ref, i, j, blk):
    pos = lax.broadcasted_iota(jnp.int32, (1, blk), 1) + i * blk
    start = query_starts(ends_ref, pos) - j * blk
    key = lax.broadcasted_iota(jnp.int32, (blk, blk), 0)
    return (key <= pos - j * blk) & (key >= start)


def attn_fwd_kernel(rep, slot_ref, low_ref, ends_ref, part_ref, qkv_ref, out_ref, full_ref, top_ref, inv_ref, key_ref):
    slots, _, rows = qkv_ref.shape
    blk = 2 * rows
    count = slots // 2
    hd = HEAD_DIM

    def flip(s, c):
        key_ref[s] = qkv_ref[s, hd : 2 * hd, :].T
        return c

    lax.fori_loop(0, slots, flip, 0)
    if rep > 1:
        out_ref[...] = jnp.zeros_like(out_ref)
        full_ref[...] = jnp.zeros_like(full_ref)

    def query_block(i, c):
        s0, s1 = slot_ref[2 * i], slot_ref[2 * i + 1]
        q = jnp.concatenate([qkv_ref[s0, :hd, :], qkv_ref[s1, :hd, :]], axis=1)

        def key_block(j, state):
            top, mass, acc = state
            k0, k1 = slot_ref[2 * j], slot_ref[2 * j + 1]
            k = jnp.concatenate([key_ref[k0], key_ref[k1]], axis=0)
            v = jnp.concatenate([qkv_ref[k0, 2 * hd :, :], qkv_ref[k1, 2 * hd :, :]], axis=1)
            s = dot(k, q, ((1,), (0,))) * (SCALE * LOG2E)
            s = jnp.where(block_mask(ends_ref, i, j, blk), s, NEG_FILL)
            new_top = jnp.maximum(top, jnp.max(s, axis=0, keepdims=True))
            shrink = jnp.exp2(top - new_top)
            w = jnp.exp2(s - new_top)
            mass = mass * shrink + jnp.sum(w, axis=0, keepdims=True)
            acc = acc * shrink + dot(v, w.astype(BF16), ((1,), (0,)))
            return new_top, mass, acc

        init = (
            jnp.full((1, blk), NEG_FILL, F32),
            jnp.zeros((1, blk), F32),
            jnp.zeros((hd, blk), F32),
        )
        top, mass, acc = lax.fori_loop(low_ref[i], i + 1, key_block, init)
        inv = 1.0 / mass
        acc = acc * inv
        full_ref[s0] = acc[:, :rows]
        full_ref[s1] = acc[:, rows:]
        low = acc.astype(BF16)
        out_ref[s0] = low[:, :rows]
        out_ref[s1] = low[:, rows:]
        top_ref[i] = top
        inv_ref[i] = inv
        return c

    lax.fori_loop(0, count // rep, lambda n, c: query_block(n * rep + part_ref[0], c), 0)


def attn_bwd_kernel(
    rep, slot_ref, low_ref, ends_ref, part_ref, qkv_ref, da_ref, full_ref, top_ref, inv_ref,
    out_ref, key_ref, value_ref, dk_ref, dv_ref,
):
    slots, _, rows = qkv_ref.shape
    blk = 2 * rows
    count = slots // 2
    hd = HEAD_DIM

    def flip(s, c):
        key_ref[s] = qkv_ref[s, hd : 2 * hd, :].T
        value_ref[s] = qkv_ref[s, 2 * hd :, :].T
        return c

    lax.fori_loop(0, slots, flip, 0)
    dk_ref[...] = jnp.zeros_like(dk_ref)
    dv_ref[...] = jnp.zeros_like(dv_ref)
    if rep > 1:
        out_ref[...] = jnp.zeros_like(out_ref)

    def pair(ref, a, b, lo, hi):
        return jnp.concatenate([ref[a, lo:hi, :], ref[b, lo:hi, :]], axis=1)

    def query_block(i, c):
        s0, s1 = slot_ref[2 * i], slot_ref[2 * i + 1]
        q = pair(qkv_ref, s0, s1, 0, hd)
        da = pair(da_ref, s0, s1, 0, hd)
        full = pair(full_ref, s0, s1, 0, hd)
        delta = jnp.sum(da.astype(F32) * full, axis=0, keepdims=True)
        top, inv = top_ref[i], inv_ref[i]

        def key_block(j, dq):
            k0, k1 = slot_ref[2 * j], slot_ref[2 * j + 1]
            k = jnp.concatenate([key_ref[k0], key_ref[k1]], axis=0)
            v = jnp.concatenate([value_ref[k0], value_ref[k1]], axis=0)
            s = dot(k, q, ((1,), (0,))) * (SCALE * LOG2E)
            s = jnp.where(block_mask(ends_ref, i, j, blk), s, NEG_FILL)
            p = jnp.exp2(s - top) * inv
            dp = dot(v, da, ((1,), (0,)))
            ds = (p * (dp - delta)).astype(BF16)
            dk_ref[j] += dot(q, ds, ((1,), (1,)))
            dv_ref[j] += dot(da, p.astype(BF16), ((1,), (1,)))
            return dq + dot(pair(qkv_ref, k0, k1, hd, 2 * hd), ds, ((1,), (0,)))

        dq = lax.fori_loop(low_ref[i], i + 1, key_block, jnp.zeros((hd, blk), F32))
        dq = (dq * SCALE).astype(BF16)
        out_ref[s0, :hd, :] = dq[:, :rows]
        out_ref[s1, :hd, :] = dq[:, rows:]
        return c

    lax.fori_loop(0, count // rep, lambda n, c: query_block(n * rep + part_ref[0], c), 0)

    def finish(j, c):
        k0, k1 = slot_ref[2 * j], slot_ref[2 * j + 1]
        dk = (dk_ref[j] * SCALE).astype(BF16)
        dv = dv_ref[j].astype(BF16)
        out_ref[k0, hd : 2 * hd, :] = dk[:, :rows]
        out_ref[k1, hd : 2 * hd, :] = dk[:, rows:]
        out_ref[k0, 2 * hd :, :] = dv[:, :rows]
        out_ref[k1, 2 * hd :, :] = dv[:, rows:]
        return c

    lax.fori_loop(0, count, finish, 0)


SMEM = pl.BlockSpec(memory_space=pltpu.SMEM)
VMEM = pl.BlockSpec(memory_space=pltpu.VMEM)


def attn_fwd(rep, scalars, qkv):
    slots, _, rows = qkv.shape
    stat = jax.ShapeDtypeStruct((slots // 2, 1, 2 * rows), F32)
    return pl.pallas_call(
        functools.partial(attn_fwd_kernel, rep),
        in_specs=[SMEM] * 4 + [VMEM],
        out_specs=[VMEM] * 4,
        out_shape=[
            jax.ShapeDtypeStruct((slots, HEAD_DIM, rows), BF16),
            jax.ShapeDtypeStruct((slots, HEAD_DIM, rows), F32),
            stat,
            stat,
        ],
        scratch_shapes=[pltpu.VMEM((slots, rows, HEAD_DIM), BF16)],
        cost_estimate=pl.CostEstimate(flops=10**9, bytes_accessed=3 * 10**6, transcendentals=2 * 10**6),
        compiler_params=pltpu.CompilerParams(vmem_limit_bytes=32 * 2**20),
        name="attn_fwd",
    )(*scalars, qkv)


def attn_bwd(rep, scalars, qkv, da, full, top, inv):
    slots, _, rows = qkv.shape
    return pl.pallas_call(
        functools.partial(attn_bwd_kernel, rep),
        in_specs=[SMEM] * 4 + [VMEM] * 5,
        out_specs=VMEM,
        out_shape=jax.ShapeDtypeStruct((slots, 3 * HEAD_DIM, rows), BF16),
        scratch_shapes=[
            pltpu.VMEM((slots, rows, HEAD_DIM), BF16),
            pltpu.VMEM((slots, rows, HEAD_DIM), BF16),
            pltpu.VMEM((slots // 2, HEAD_DIM, 2 * rows), F32),
            pltpu.VMEM((slots // 2, HEAD_DIM, 2 * rows), F32),
        ],
        cost_estimate=pl.CostEstimate(flops=2 * 10**9, bytes_accessed=4 * 10**6, transcendentals=2 * 10**6),
        compiler_params=pltpu.CompilerParams(vmem_limit_bytes=32 * 2**20),
        name="attn_bwd",
    )(*scalars, qkv, da, full, top, inv)


def norm_back(grad_normed, unit_rows, inv_rows, gain_vec):
    scaled = grad_normed * gain_vec
    return inv_rows * (scaled - unit_rows * jnp.mean(scaled * unit_rows, axis=-1, keepdims=True))


class Moves:
    def __init__(self, n_dp, n_ctx):
        self.n_dp, self.n_ctx = n_dp, n_ctx
        self.grid = n_dp == 2 and n_ctx == 16

    def swap(self, v):
        return lax.ppermute(v, "dp", [(0, 1), (1, 0)])

    def rows_gather(self, v):
        if self.grid:
            return jnp.concatenate([v, self.swap(v)], axis=0)
        return lax.all_gather(v, "dp", axis=0, tiled=True)

    def rows_sum(self, v):
        if self.grid:
            rows = v.shape[0] // 2
            return v[:rows] + self.swap(v[rows:].astype(BF16)).astype(F32)
        return lax.psum_scatter(v, "dp", scatter_dimension=0, tiled=True)

    def columns_gather(self, v):
        if self.grid:
            rows = v.shape[0] // 2
            other = self.swap(v)
            other = jnp.concatenate([other[rows:], other[:rows]], axis=0)
            first = lax.axis_index("dp") == 0
            return jnp.concatenate([jnp.where(first, v, other), jnp.where(first, other, v)], axis=1)
        return lax.all_gather(v, "dp", axis=1, tiled=True)

    def to_ctx(self, v):
        return lax.all_to_all(v, "ctx", 0, 0, tiled=True)

    def sum_product(self, left, right, first):
        if not self.grid:
            part = dot(left, right, ((1,), (0,))).astype(BF16)
            return lax.psum_scatter(part, "ctx", scatter_dimension=0, tiled=True).astype(F32)
        chunk, depth, wide = left.shape[0] // 16, left.shape[1], right.shape[1]
        c = lax.axis_index("ctx")
        z, y, x = c // 4, (c // 2) % 2, c % 2
        left = left.reshape(4, 2, 2, chunk, depth)
        axis = {"x": 2, "y": 1}[first]
        here = {"x": x, "y": y}
        step = {"x": 1, "y": 2}
        second = {"x": "y", "y": "x"}[first]

        def product(at):
            rows = lax.dynamic_index_in_dim(left, at, axis, keepdims=False)
            out = dot(rows.reshape(8 * chunk, depth), right, ((1,), (0,)))
            return out.astype(BF16).reshape(4, 2, chunk, wide)

        def across(v, name):
            return lax.ppermute(v, "ctx", [(i, i ^ step[name]) for i in range(16)])

        got = across(product(1 - here[first]), first)
        kept = product(here[first])

        def half(at):
            a = lax.dynamic_index_in_dim(got, at, 1, keepdims=False)
            b = lax.dynamic_index_in_dim(kept, at, 1, keepdims=False)
            return a.astype(F32) + b.astype(F32)

        got_two = across(half(1 - here[second]).astype(BF16), second)
        own = half(here[second]) + got_two.astype(F32)
        up = jnp.zeros((chunk, wide), F32)
        down = jnp.zeros((chunk, wide), F32)

        def level(at):
            return lax.dynamic_index_in_dim(own, jnp.clip(at, 0, 3), 0, keepdims=False)

        for n in range(1, 4):
            send_up = (level(z + 4 - n) + up).astype(BF16)
            send_down = (level(z - 4 + n) + down).astype(BF16)
            up = lax.ppermute(send_up, "ctx", [(i, i + 4) for i in range(12)]).astype(F32)
            down = lax.ppermute(send_down, "ctx", [(i + 4, i) for i in range(12)]).astype(F32)
        return level(z) + up + down


def per_device(
    moves,
    latent_in,
    gain_attn,
    w_query,
    w_key,
    w_value,
    w_out,
    gain_ffn,
    w_gate,
    w_up,
    w_down,
    cotangent,
    seq_lengths,
    span_order,
):
    n_dp, n_ctx = moves.n_dp, moves.n_ctx
    rows, width = latent_in.shape
    ff = w_gate.shape[1]
    dp, ctx = lax.axis_index("dp"), lax.axis_index("ctx")
    rep = n_ctx // HEADS

    ends = jnp.cumsum(seq_lengths[0]).astype(jnp.int32)
    slot_of = jnp.zeros((n_ctx,), jnp.int32).at[span_order[0]].set(jnp.arange(n_ctx, dtype=jnp.int32))
    starts = jnp.arange(n_ctx // 2, dtype=jnp.int32) * (2 * rows)
    low = jnp.max(jnp.where(starts[:, None] >= ends[None, :], ends[None, :], 0), axis=1) // (2 * rows)
    scalars = (slot_of, low, ends, (ctx % rep).reshape(1).astype(jnp.int32))

    share = ff // n_dp
    gate_w = lax.dynamic_slice_in_dim(w_gate, dp * share, share, 1)
    up_w = lax.dynamic_slice_in_dim(w_up, dp * share, share, 1)
    down_w = lax.dynamic_slice_in_dim(w_down, dp * share, share, 0)

    latent_f = latent_in.astype(F32)
    inv_one = lax.rsqrt(jnp.mean(latent_f * latent_f, axis=-1, keepdims=True) + EPS)
    unit_one = latent_f * inv_one
    normed_one = (unit_one * gain_attn).astype(BF16)

    def project(w):
        return dot(w, normed_one, ((0,), (1,))).astype(BF16).reshape(HEADS, HEAD_DIM, rows)

    qkv = jnp.concatenate([project(w_query), project(w_key), project(w_value)], axis=1)
    qkv = moves.to_ctx(jnp.repeat(qkv, rep, axis=0) if rep > 1 else qkv)
    normed_all = lax.all_gather(normed_one, "ctx", axis=0, tiled=True)

    out, full, top, inv = attn_fwd(rep, scalars, qkv)

    def from_heads(v):
        v = moves.to_ctx(v)
        if rep > 1:
            v = jnp.sum(v.astype(F32).reshape((HEADS, rep) + v.shape[1:]), axis=1).astype(BF16)
        return v

    attn_t = from_heads(out).reshape(width, rows)
    resid = latent_f + dot(attn_t, w_out, ((0,), (0,)))
    inv_two = lax.rsqrt(jnp.mean(resid * resid, axis=-1, keepdims=True) + EPS)
    unit_two = resid * inv_two
    normed_two = (unit_two * gain_ffn).astype(BF16)

    top_all = moves.rows_gather(cotangent)
    grad_hidden = dot(top_all, down_w, ((1,), (1,)))
    normed_two_all = moves.rows_gather(normed_two)
    gate_pre = dot(normed_two_all, gate_w, ((1,), (0,)))
    up_pre = dot(normed_two_all, up_w, ((1,), (0,)))
    gate_sig = jax.nn.sigmoid(gate_pre)
    swish = gate_pre * gate_sig
    hidden = (swish * up_pre).astype(BF16)
    latents = (resid + moves.rows_sum(dot(hidden, down_w, ((1,), (0,))))).astype(BF16)
    grad_gate = (grad_hidden * up_pre * gate_sig * (1.0 + gate_pre * (1.0 - gate_sig))).astype(BF16)
    grad_up = (grad_hidden * swish).astype(BF16)
    grad_norm_two = moves.rows_sum(
        dot(grad_gate, gate_w, ((1,), (1,))) + dot(grad_up, up_w, ((1,), (1,)))
    )
    grad_resid = cotangent.astype(F32) + norm_back(grad_norm_two, unit_two, inv_two, gain_ffn)
    grad_mixed = grad_resid.astype(BF16)

    grad_attn = dot(w_out, grad_mixed, ((1,), (1,))).astype(BF16).reshape(HEADS, HEAD_DIM, rows)
    grad_attn = moves.to_ctx(jnp.repeat(grad_attn, rep, axis=0) if rep > 1 else grad_attn)
    grad_qkv = attn_bwd(rep, scalars, qkv, grad_attn, full, top, inv)

    strip = width // n_dp
    down_sum = moves.sum_product(hidden.T, top_all, "x")
    normed_rows = lax.dynamic_slice_in_dim(normed_two_all, dp * strip, strip, 1).T
    gate_sum = moves.sum_product(normed_rows, moves.columns_gather(grad_gate), "y")
    up_sum = moves.sum_product(normed_rows, moves.columns_gather(grad_up), "x")
    attn_rows = moves.rows_gather(attn_t.T)
    attn_rows = lax.dynamic_slice_in_dim(attn_rows, dp * strip, strip, 1).T
    out_sum = moves.sum_product(attn_rows, moves.rows_gather(grad_mixed), "y")

    lanes = jnp.transpose(grad_qkv, (0, 2, 1)).reshape(n_ctx * rows, 3 * HEAD_DIM)
    head_grad = dot(normed_all, lanes, ((0,), (0,)))
    head_grad = head_grad.reshape(n_dp, strip, 3 * HEAD_DIM)
    if moves.grid:
        mine = lax.dynamic_index_in_dim(head_grad, dp, 0, keepdims=False)
        theirs = lax.dynamic_index_in_dim(head_grad, 1 - dp, 0, keepdims=False)
        head_grad = mine + moves.swap(theirs.astype(BF16)).astype(F32)
    else:
        head_grad = lax.psum_scatter(head_grad, "dp", scatter_dimension=0, tiled=False)
    own = strip // n_ctx
    head_grad = moves.to_ctx(head_grad.astype(BF16).reshape(n_ctx, own, 3 * HEAD_DIM)).astype(F32)
    head_grad = jnp.sum(head_grad.reshape(HEADS, rep, own, 3, HEAD_DIM), axis=1)
    head_grad = jnp.transpose(head_grad, (2, 1, 0, 3)).reshape(3, own, width)
    query_sum, key_sum, value_sum = head_grad[0], head_grad[1], head_grad[2]

    first_row = (dp * n_ctx + ctx) * own

    def own_rows(w):
        return lax.dynamic_slice_in_dim(w, first_row, own, 0).astype(F32)

    def own_gain(v):
        return lax.dynamic_slice_in_dim(v, first_row, own, 0)

    gain_ffn_sum = jnp.sum(own_rows(w_gate) * gate_sum + own_rows(w_up) * up_sum, axis=1) / own_gain(gain_ffn)
    gain_attn_sum = jnp.sum(
        own_rows(w_query) * query_sum + own_rows(w_key) * key_sum + own_rows(w_value) * value_sum, axis=1
    ) / own_gain(gain_attn)

    back = from_heads(grad_qkv).reshape(HEADS, 3, HEAD_DIM, rows)
    grad_norm_one = sum(
        dot(back[:, n].reshape(width, rows), w, ((0,), (1,)))
        for n, w in enumerate((w_query, w_key, w_value))
    )
    latent_grad = (grad_resid + norm_back(grad_norm_one, unit_one, inv_one, gain_attn)).astype(BF16)
    return (
        latents,
        latent_grad,
        gain_attn_sum,
        query_sum,
        key_sum,
        value_sum,
        out_sum,
        gain_ffn_sum,
        gate_sum,
        up_sum,
        down_sum,
    )


def solution(mesh):
    moves = Moves(mesh.shape["dp"], mesh.shape["ctx"])
    rows, whole, share = P(("dp", "ctx"), None), P(), P("dp", None)
    flat = P(("dp", "ctx"))
    return jax.shard_map(
        functools.partial(per_device, moves),
        mesh=mesh,
        in_specs=(rows,) + (whole,) * 9 + (rows, share, share),
        out_specs=(rows, rows, flat, rows, rows, rows, rows, flat, rows, rows, rows),
        check_vma=False,
    )
```

time: 1880 us -> 355 us (0.19)
  waiting for transfers between devices: 1540 us -> 82 us
  matrix products: 154 us -> 42.8 us
  starting transfers between devices: 0.72 us -> 111 us
  local copies, waits for them, and re-layouts: 104 us -> 37.3 us
  blocking collectives: 41.5 us -> 0 us
  Pallas kernels: 0 us -> 22.4 us
    reduce_scatter x7 -> x0, waiting for transfers between devices: 1270 us -> none  [sum_bucket(): lax.psum_scatter(parts, ('dp', 'ctx'), scatter_dimension=0, tiled=True)]
    unnamed x13 -> x1, waiting for transfers between devices: 155 us -> 0.02 us
    all_gather x2 -> x1, waiting for transfers between devices: 118 us -> 0.02 us  [per_device(): normed_all = lax.all_gather(normed_one, 'ctx', axis=0, tiled=True)]
    dot_general x77 -> x23, matrix products: 154 us -> 42.8 us  [dot(): return lax.dot_general(a, b, (dims, ((), ())), preferred_element_type=F32)]
    ppermute x0 -> x41, starting transfers between devices: none -> 78.6 us  [the longest x12 36.8 us: sum_product(): lax.ppermute(send_up, 'ctx', [(i, i + 4) for i in range(12)]).astype(F32)]
    unnamed x70 -> x85, local copies, waits for them, and re-layouts: 72.8 us -> 4.42 us
    ppermute x0 -> x41, waiting for transfers between devices: none -> 51.7 us  [the longest x8 29.7 us: across(): return lax.ppermute(v, 'ctx', [(i, i ^ step[name]) for i in range(16)])]
    unnamed x1 -> x0, blocking collectives: 41.5 us -> none
  transfers between devices with their start and end apart: 11 -> 47, of which waited for: 11 -> 13; matrix products, arithmetic and copies ran while one was open for 6% -> 29% of each run, Pallas kernels for 0% -> 3%
where the time goes in v1:
time: 355 us; the launch traced here: 348 us
  starting transfers between devices  111 us (31%)
  waiting for transfers between devices  82 us (23%)
  matrix products  42.8 us (12%)
  other arithmetic  37.7 us (11%)
  local copies, waits for them, and re-layouts  37.3 us (11%)
  Pallas kernels  22.4 us (6%)
  between operations  15.3 us (4%)
    dot_general x23, matrix products, dot(): return lax.dot_general(a, b, (dims, ((), ())), preferred_element_type=F32)  42.8 us
    ppermute x12, starting transfers between devices, sum_product(): lax.ppermute(send_up, 'ctx', [(i, i + 4) for i in range(12)]).astype(F32)  36.8 us
    all_to_all x5, starting transfers between devices, to_ctx(): return lax.all_to_all(v, 'ctx', 0, 0, tiled=True)  32 us
    ppermute x12, starting transfers between devices, sum_product(): lax.ppermute(send_down, 'ctx', [(i + 4, i) for i in range(12)]).astype(F32)  30.8 us
    all_to_all x5, waiting for transfers between devices, to_ctx(): return lax.all_to_all(v, 'ctx', 0, 0, tiled=True)  30.2 us
    ppermute x8, waiting for transfers between devices, across(): return lax.ppermute(v, 'ctx', [(i, i ^ step[name]) for i in range(16)])  29.7 us
    ppermute x12, waiting for transfers between devices, sum_product(): lax.ppermute(send_up, 'ctx', [(i, i + 4) for i in range(12)]).astype(F32)  13.1 us
    pallas_call x1, Pallas kernels, attn_bwd(): pl.pallas_call(functools.partial(attn_bwd_kernel, rep), in_specs=[SMEM] *...  11.7 us
  transfers between devices with their start and end apart: 47, of which 13 were waited for; matrix products, arithmetic and copies ran while one was open for 29% of the time, Pallas kernels for 3%

profile of v1, /device:TPU:10, one launch (start us, length us, event | category | flops | bytes accessed | tf_op | source)
XLA Modules:
  0.0 348.4 jit_solution(1353677138048604600)
XLA Ops:
  17.3 7.2 %all-to-all-start = ((bf16[16,192,128]{2,1,0:T(8,128)(2,1)}), bf16[16,192,128]{2,1,0:T(8,128)(2,1)S(1)}, u32[]{:S(2)}, u32[]{:S(2)}) async-start(bf16[16,192,128]{2,1,0:T(8,128)(2,1)} %pad_maximum_fusion.6), calls=%async_computation | async-start | bytes 1572864 | tf_op jit(solution)/shard_map/all_to_all | solution.py:234
  25.5 18.1 %all-to-all-done.qkv_ref = bf16[16,192,128]{2,1,0:T(8,128)(2,1)S(1)} async-done(((bf16[16,192,128]{2,1,0:T(8,128)(2,1)}), bf16[16,192,128]{2,1,0:T(8,128)(2,1)S(1)}, u32[]{:S(2)}, u32[]{:S(2)}) %all-to-all-start) | async-done | bytes 786464 | tf_op jit(solution)/shard_map/all_to_all | solution.py:234
  43.6 10.8 %attn_fwd.1 = (bf16[16,64,128]{2,1,0:T(8,128)(2,1)}, f32[16,64,128]{2,1,0:T(8,128)S(1)}, f32[8,1,256]{2,1,0:T(1,128)S(1)}, f32[8,1,256]{2,1,0:T(1,128)S(1)}) custom-call(s32[16]{0:T(128)S(1)} %scatter_custom_fusion.slot_ref, s32[8]{0:T(128)S(1)} %and_select_fusion.low_ref, s32[4]{0:T(128)S(1)} %bitcast.246, s32[1]{0:T(128)} %constant.263.clone.1.part_ref, ...), custom_call_target="tpu_custom_call" | custom-call | flops 1000000000 | bytes 3000000 | tf_op jit(solution)/shard_map/attn_fwd/pallas_call | solution.py:164
  54.4 5.6 %all-to-all-start.1 = ((bf16[16,64,128]{2,1,0:T(8,128)(2,1)}), bf16[16,64,128]{2,1,0:T(8,128)(2,1)}, u32[]{:S(2)}, u32[]{:S(2)}) async-start(bf16[16,64,128]{2,1,0:T(8,128)(2,1)} %get-tuple-element.15), calls=%async_computation.1 | async-start | bytes 524288 | tf_op jit(solution)/shard_map/all_to_all | solution.py:234
  60.3 6.6 %all-to-all-done.1 = bf16[16,64,128]{2,1,0:T(8,128)(2,1)} async-done(((bf16[16,64,128]{2,1,0:T(8,128)(2,1)}), bf16[16,64,128]{2,1,0:T(8,128)(2,1)}, u32[]{:S(2)}, u32[]{:S(2)}) %all-to-all-start.1) | async-done | bytes 262176 | tf_op jit(solution)/shard_map/all_to_all | solution.py:234
  72.9 3.1 fusion.10
  76.0 4.0 %fusion.12 = (bf16[1408,256]{0,1:T(8,128)(2,1)}, f32[256,1408]{1,0:T(8,128)S(1)}) fusion(f32[256,1408]{1,0:T(8,128)S(1)} %fusion.10, bf16[1024,2816]{1,0:T(8,128)(2,1)} %param.21, s32[]{:T(128)S(6)} %select_n.174, bf16[128,1024]{1,0:T(8,128)(2,1)} %collective-permute-done, bf16[128,1024]{1,0:T(8,128)(2,1)} %multiply_convert_fusion.4), kind=kOutput, calls=%fused_computation.23 | convolution fusion | flops 741408768 | bytes 7012356 | tf_op jit(solution)/shard_map/dot_general | solution.py:22
  81.1 2.5 multiply_convert_fusion.1
  96.2 2.4 copy.131
  108.6 2.3 fusion.96
  110.9 2.5 fusion.24
  115.2 5.5 %all-to-all-start.2 = ((bf16[16,64,128]{2,1,0:T(8,128)(2,1)}), bf16[16,64,128]{2,1,0:T(8,128)(2,1)S(1)}, u32[]{:S(2)}, u32[]{:S(2)}) async-start(bf16[16,64,128]{2,1,0:T(8,128)(2,1)} %bitcast.12), calls=%async_computation.2 | async-start | bytes 524288 | tf_op jit(solution)/shard_map/all_to_all | solution.py:234
  132.5 16.9 %collective-permute-done.7 = bf16[4,2,32,1024]{3,2,0,1:T(8,128)(2,1)S(1)} collective-permute-done((bf16[4,2,32,1024]{3,2,0,1:T(8,128)(2,1)S(1)}, bf16[4,2,32,1024]{3,2,0,1:T(8,128)(2,1)S(1)}, u32[]{:S(2)}, u32[]{:S(2)}) %collective-permute-start.7) | collective-permute-done | bytes 524320 | tf_op jit(solution)/shard_map/ppermute | solution.py:255
  151.8 7.9 %collective-permute-done.8 = bf16[4,32,1024]{2,1,0:T(8,128)(2,1)S(1)} collective-permute-done((bf16[4,32,1024]{2,1,0:T(8,128)(2,1)S(1)}, bf16[4,32,1024]{2,1,0:T(8,128)(2,1)S(1)}, u32[]{:S(2)}, u32[]{:S(2)}) %collective-permute-start.8) | collective-permute-done | bytes 262176 | tf_op jit(solution)/shard_map/ppermute | solution.py:255
  159.8 3.1 collective-permute-start.9
  166.2 2.6 collective-permute-start.12
  168.9 3.2 collective-permute-start.10
  177.7 11.7 %attn_bwd.1 = bf16[16,192,128]{2,1,0:T(8,128)(2,1)} custom-call(s32[16]{0:T(128)S(1)} %scatter_custom_fusion.slot_ref, s32[8]{0:T(128)S(1)} %and_select_fusion.low_ref, s32[4]{0:T(128)S(1)} %bitcast.247, s32[1]{0:T(128)} %constant.263.clone.1.part_ref, bf16[16,192,128]{2,1,0:T(8,128)(2,1)S(1)} %all-to-all-done.qkv_ref, ...), custom_call_target="tpu_custom_call" | custom-call | flops 2000000000 | bytes 4000000 | tf_op jit(solution)/shard_map/attn_bwd/pallas_call | solution.py:183
  189.3 7.3 %all-to-all-start.3 = ((bf16[16,192,128]{2,1,0:T(8,128)(2,1)}), bf16[16,192,128]{2,1,0:T(8,128)(2,1)}, u32[]{:S(2)}, u32[]{:S(2)}) async-start(bf16[16,192,128]{2,1,0:T(8,128)(2,1)} %attn_bwd.1), calls=%async_computation.3 | async-start | bytes 1572864 | tf_op jit(solution)/shard_map/all_to_all | solution.py:234
  199.6 3.5 %collective-permute-start.11 = (bf16[32,1024]{1,0:T(8,128)(2,1)}, bf16[32,1024]{1,0:T(8,128)(2,1)S(1)}, u32[]{:S(2)}, u32[]{:S(2)}) collective-permute-start(bf16[32,1024]{1,0:T(8,128)(2,1)} %get-tuple-element.54), channel_id=1, source_target_pairs={{0,4},{1,5},{2,6},{3,7},{4,8},{5,9},{6,10},{7,11},{8,12},{9,13},{1... | collective-permute-start | bytes 196616 | tf_op jit(solution)/shard_map/ppermute | solution.py:276
  203.2 2.5 collective-permute-start.14
  208.5 4.5 %collective-permute-done.11 = bf16[32,1024]{1,0:T(8,128)(2,1)S(1)} collective-permute-done((bf16[32,1024]{1,0:T(8,128)(2,1)}, bf16[32,1024]{1,0:T(8,128)(2,1)S(1)}, u32[]{:S(2)}, u32[]{:S(2)}) %collective-permute-start.11) | collective-permute-done | bytes 65568 | tf_op jit(solution)/shard_map/ppermute | solution.py:276
  218.3 2.2 fusion.29
  222.1 4.9 %collective-permute-done.34 = bf16[4,88,1024]{2,1,0:T(8,128)(2,1)S(1)} collective-permute-done((bf16[4,88,1024]{2,1,0:T(8,128)(2,1)S(1)}, bf16[4,88,1024]{2,1,0:T(8,128)(2,1)S(1)}, u32[]{:S(2)}, u32[]{:S(2)}) %collective-permute-start.34) | collective-permute-done | bytes 720928 | tf_op jit(solution)/shard_map/ppermute | solution.py:255
  229.2 3.7 %collective-permute-start.35 = (bf16[88,1024]{1,0:T(8,128)(2,1)}, bf16[88,1024]{1,0:T(8,128)(2,1)}, u32[]{:S(2)}, u32[]{:S(2)}) collective-permute-start(bf16[88,1024]{1,0:T(8,128)(2,1)} %get-tuple-element.28), channel_id=1, source_target_pairs={{0,4},{1,5},{2,6},{3,7},{4,8},{5,9},{6,10},{7,11},{8,12},{9,13},{1... | collective-permute-start | bytes 540680 | tf_op jit(solution)/shard_map/ppermute | solution.py:276
  232.9 2.8 collective-permute-start.38
  236.9 2.6 fusion.101
  241.3 3.0 collective-permute-start.36
  245.4 3.4 collective-permute-done.36
  251.7 3.9 %collective-permute-start.37 = (bf16[88,1024]{1,0:T(8,128)(2,1)S(1)}, bf16[88,1024]{1,0:T(8,128)(2,1)S(1)}, u32[]{:S(2)}, u32[]{:S(2)}) collective-permute-start(bf16[88,1024]{1,0:T(8,128)(2,1)S(1)} %get-tuple-element.26), channel_id=1, source_target_pairs={{0,4},{1,5},{2,6},{3,7},{4,8},{5,9},{6,10},{7,11},{8,12},{9,13},{1... | collective-permute-start | bytes 540680 | tf_op jit(solution)/shard_map/ppermute | solution.py:276
  255.6 2.8 collective-permute-done.39
  258.5 2.3 collective-permute-start.40
  261.8 4.2 %collective-permute-done.40 = bf16[88,1024]{1,0:T(8,128)(2,1)S(1)} collective-permute-done((bf16[88,1024]{1,0:T(8,128)(2,1)S(1)}, bf16[88,1024]{1,0:T(8,128)(2,1)S(1)}, u32[]{:S(2)}, u32[]{:S(2)}) %collective-permute-start.40) | collective-permute-done | bytes 180256 | tf_op jit(solution)/shard_map/ppermute | solution.py:277
  268.5 2.4 collective-permute-start.18
  271.0 3.4 collective-permute-start.21
  276.1 2.4 collective-permute-start.27
  278.5 3.4 collective-permute-start.30
  282.0 2.4 collective-permute-start.19
  286.4 3.9 %collective-permute-done.19 = bf16[32,2816]{1,0:T(8,128)(2,1)S(1)} collective-permute-done((bf16[32,2816]{1,0:T(8,128)(2,1)S(1)}, bf16[32,2816]{1,0:T(8,128)(2,1)S(1)}, u32[]{:S(2)}, u32[]{:S(2)}) %collective-permute-start.19) | collective-permute-done | bytes 180256 | tf_op jit(solution)/shard_map/ppermute | solution.py:276
  292.9 3.9 %collective-permute-start.20 = (bf16[32,2816]{1,0:T(8,128)(2,1)}, bf16[32,2816]{1,0:T(8,128)(2,1)}, u32[]{:S(2)}, u32[]{:S(2)}) collective-permute-start(bf16[32,2816]{1,0:T(8,128)(2,1)} %get-tuple-element.36), channel_id=1, source_target_pairs={{0,4},{1,5},{2,6},{3,7},{4,8},{5,9},{6,10},{7,11},{8,12},{9,13},{1... | collective-permute-start | bytes 540680 | tf_op jit(solution)/shard_map/ppermute | solution.py:276
  297.7 2.6 collective-permute-start.31
  300.3 3.3 collective-permute-start.29
  304.3 3.5 %collective-permute-start.23 = (bf16[32,2816]{1,0:T(8,128)(2,1)}, bf16[32,2816]{1,0:T(8,128)(2,1)}, u32[]{:S(2)}, u32[]{:S(2)}) collective-permute-start(bf16[32,2816]{1,0:T(8,128)(2,1)} %fusion.53), channel_id=1, source_target_pairs={{4,0},{5,1},{6,2},{7,3},{8,4},{9,5},{10,6},{11,7},{12,8},{13,9},{1... | collective-permute-start | bytes 540680 | tf_op jit(solution)/shard_map/ppermute | solution.py:277
  307.8 6.5 %copy.135 = bf16[1024,2048]{1,0:T(8,128)(2,1)} copy(bf16[1024,2048]{0,1:T(8,128)(2,1)} %bitcast.253) | data formatting | bytes 8388608 | tf_op jit(solution)/shard_map/dot_general | solution.py:22
  314.3 3.9 %fusion.102 = f32[2,512,192]{1,2,0:T(8,128)S(1)} fusion(bf16[2,512,2048]{2,1,0:T(8,128)(2,1)} %bitcast.254, bf16[2048,192,1]{0,1,2:T(8,128)(2,1)} %reshape.283), kind=kOutput, calls=%fused_computation.208 | convolution fusion | flops 805306368 | bytes 5767168 | tf_op jit(solution)/shard_map/dot_general | solution.py:22
  322.8 6.5 %all-to-all-start.4 = ((bf16[16,32,192]{2,1,0:T(8,128)(2,1)}), bf16[16,32,192]{2,1,0:T(8,128)(2,1)S(1)}, u32[]{:S(2)}, u32[]{:S(2)}) async-start(bf16[16,32,192]{2,1,0:T(8,128)(2,1)} %bitcast.22), calls=%async_computation.4 | async-start | bytes 524288 | tf_op jit(solution)/shard_map/all_to_all | solution.py:234
  329.3 2.4 add_reduce_fusion
  332.4 5.5 %all-to-all-done.4 = bf16[16,32,192]{2,1,0:T(8,128)(2,1)S(1)} async-done(((bf16[16,32,192]{2,1,0:T(8,128)(2,1)}), bf16[16,32,192]{2,1,0:T(8,128)(2,1)S(1)}, u32[]{:S(2)}, u32[]{:S(2)}) %all-to-all-start.4) | async-done | bytes 196640 | tf_op jit(solution)/shard_map/all_to_all | solution.py:234
  (245 shorter events, 107.5 us)
Async XLA Ops:
  7.2 59.8 %copy-start = (bf16[1024,1024]{1,0:T(8,128)(2,1)S(1)}, bf16[1024,1024]{1,0:T(8,128)(2,1)}, u32[]{:S(2)}) copy-start(bf16[1024,1024]{1,0:T(8,128)(2,1)} %param.18) | copy-start | bytes 6291460
  17.3 26.3 %all-to-all-start = ((bf16[16,192,128]{2,1,0:T(8,128)(2,1)}), bf16[16,192,128]{2,1,0:T(8,128)(2,1)S(1)}, u32[]{:S(2)}, u32[]{:S(2)}) async-start(bf16[16,192,128]{2,1,0:T(8,128)(2,1)} %pad_maximum_fusion.6), calls=%async_computation | async-start | bytes 1572864 | tf_op jit(solution)/shard_map/all_to_all | solution.py:234
  54.4 12.5 %all-to-all-start.1 = ((bf16[16,64,128]{2,1,0:T(8,128)(2,1)}), bf16[16,64,128]{2,1,0:T(8,128)(2,1)}, u32[]{:S(2)}, u32[]{:S(2)}) async-start(bf16[16,64,128]{2,1,0:T(8,128)(2,1)} %get-tuple-element.15), calls=%async_computation.1 | async-start | bytes 524288 | tf_op jit(solution)/shard_map/all_to_all | solution.py:234
  60.0 247.8 %all-gather.2.cloned.1.call-start = ((), (), s32[]{:S(2)}) async-start(), calls=%async_computation.5 | async-start | bytes 4456448 | tf_op jit(solution)/shard_map/all_gather | solution.py:324
  60.2 11.1 %collective-permute-start.2 = (bf16[128,1024]{1,0:T(8,128)(2,1)}, bf16[128,1024]{1,0:T(8,128)(2,1)}, u32[]{:S(2)}, u32[]{:S(2)}) collective-permute-start(bf16[128,1024]{1,0:T(8,128)(2,1)} %param.23), channel_id=1, source_target_pairs={{0,16},{16,0},{1,17},{17,1},{2,18},{18,2},{3,19},{19,3},{4,20},{20... | collective-permute-start | bytes 786440 | tf_op jit(solution)/shard_map/ppermute | solution.py:211
  70.2 2.7 collective-permute-start
  72.3 30.2 %collective-permute-start.5 = (bf16[128,1024]{0,1:T(8,128)(2,1)}, bf16[128,1024]{0,1:T(8,128)(2,1)}, u32[]{:S(2)}, u32[]{:S(2)}) collective-permute-start(bf16[128,1024]{0,1:T(8,128)(2,1)} %bitcast.24), channel_id=1, source_target_pairs={{0,16},{16,0},{1,17},{17,1},{2,18},{18,2},{3,19},{19,3},{4,20},{20... | collective-permute-start | bytes 786440 | tf_op jit(solution)/shard_map/ppermute | solution.py:211
  87.1 42.8 %collective-permute-start.24 = (bf16[256,1408]{1,0:T(8,128)(2,1)}, bf16[256,1408]{1,0:T(8,128)(2,1)}, u32[]{:S(2)}, u32[]{:S(2)}) collective-permute-start(bf16[256,1408]{1,0:T(8,128)(2,1)} %get-tuple-element.25), channel_id=1, source_target_pairs={{0,16},{16,0},{1,17},{17,1},{2,18},{18,2},{3,19},{19,3},{4,20},{20... | collective-permute-start | bytes 2162696 | tf_op jit(solution)/shard_map/ppermute | solution.py:211
  87.2 37.8 %collective-permute-start.15 = (bf16[256,1408]{1,0:T(8,128)(2,1)}, bf16[256,1408]{1,0:T(8,128)(2,1)}, u32[]{:S(2)}, u32[]{:S(2)}) collective-permute-start(bf16[256,1408]{1,0:T(8,128)(2,1)} %get-tuple-element.24), channel_id=1, source_target_pairs={{0,16},{16,0},{1,17},{17,1},{2,18},{18,2},{3,19},{19,3},{4,20},{20... | collective-permute-start | bytes 2162696 | tf_op jit(solution)/shard_map/ppermute | solution.py:211
  91.5 15.9 %collective-permute-start.3 = (bf16[128,1024]{1,0:T(8,128)(2,1)}, bf16[128,1024]{1,0:T(8,128)(2,1)}, u32[]{:S(2)}, u32[]{:S(2)}) collective-permute-start(bf16[128,1024]{1,0:T(8,128)(2,1)} %slice.89), channel_id=1, source_target_pairs={{0,16},{16,0},{1,17},{17,1},{2,18},{18,2},{3,19},{19,3},{4,20},{20... | collective-permute-start | bytes 786440 | tf_op jit(solution)/shard_map/ppermute | solution.py:211
  92.3 16.3 %collective-permute-start.1 = (bf16[128,1024]{1,0:T(8,128)(2,1)}, bf16[128,1024]{1,0:T(8,128)(2,1)}, u32[]{:S(2)}, u32[]{:S(2)}) collective-permute-start(bf16[128,1024]{1,0:T(8,128)(2,1)} %slice.90), channel_id=1, source_target_pairs={{0,16},{16,0},{1,17},{17,1},{2,18},{18,2},{3,19},{19,3},{4,20},{20... | collective-permute-start | bytes 786440 | tf_op jit(solution)/shard_map/ppermute | solution.py:211
  102.5 103.2 %collective-permute-start.33 = (bf16[4,2,88,1024]{3,2,0,1:T(8,128)(2,1)}, bf16[4,2,88,1024]{3,2,0,1:T(8,128)(2,1)}, u32[]{:S(2)}, u32[]{:S(2)}) collective-permute-start(bf16[4,2,88,1024]{3,2,0,1:T(8,128)(2,1)} %copy.132), channel_id=1, source_target_pairs={{0,1},{1,0},{2,3},{3,2},{4,5},{5,4},{6,7},{7,6},{8,9},{9,8},{10,11... | collective-permute-start | bytes 4325384 | tf_op jit(solution)/shard_map/ppermute | solution.py:255
  110.9 9.8 %collective-permute-start.6 = (bf16[128,1024]{1,0:T(8,128)(2,1)}, bf16[128,1024]{1,0:T(8,128)(2,1)}, u32[]{:S(2)}, u32[]{:S(2)}) collective-permute-start(bf16[128,1024]{1,0:T(8,128)(2,1)} %get-tuple-element.22), channel_id=1, source_target_pairs={{0,16},{16,0},{1,17},{17,1},{2,18},{18,2},{3,19},{19,3},{4,20},{20... | collective-permute-start | bytes 786440 | tf_op jit(solution)/shard_map/ppermute | solution.py:211
  115.2 62.5 %all-to-all-start.2 = ((bf16[16,64,128]{2,1,0:T(8,128)(2,1)}), bf16[16,64,128]{2,1,0:T(8,128)(2,1)S(1)}, u32[]{:S(2)}, u32[]{:S(2)}) async-start(bf16[16,64,128]{2,1,0:T(8,128)(2,1)} %bitcast.12), calls=%async_computation.2 | async-start | bytes 524288 | tf_op jit(solution)/shard_map/all_to_all | solution.py:234
  122.1 27.2 %collective-permute-start.7 = (bf16[4,2,32,1024]{3,2,0,1:T(8,128)(2,1)S(1)}, bf16[4,2,32,1024]{3,2,0,1:T(8,128)(2,1)S(1)}, u32[]{:S(2)}, u32[]{:S(2)}) collective-permute-start(bf16[4,2,32,1024]{3,2,0,1:T(8,128)(2,1)S(1)} %copy.121), channel_id=1, source_target_pairs={{0,2},{1,3},{2,0},{3,1},{4,6},{5,7},{6,4},{7,5},{8,10},{9,11},{10,... | collective-permute-start | bytes 1572872 | tf_op jit(solution)/shard_map/ppermute | solution.py:255
  129.3 86.3 %collective-permute-start.16 = (bf16[4,2,32,2816]{3,2,0,1:T(8,128)(2,1)}, bf16[4,2,32,2816]{3,2,0,1:T(8,128)(2,1)}, u32[]{:S(2)}, u32[]{:S(2)}) collective-permute-start(bf16[4,2,32,2816]{3,2,0,1:T(8,128)(2,1)} %copy.125), channel_id=1, source_target_pairs={{0,2},{1,3},{2,0},{3,1},{4,6},{5,7},{6,4},{7,5},{8,10},{9,11},{10,... | collective-permute-start | bytes 4325384 | tf_op jit(solution)/shard_map/ppermute | solution.py:255
  149.4 10.2 %collective-permute-start.8 = (bf16[4,32,1024]{2,1,0:T(8,128)(2,1)S(1)}, bf16[4,32,1024]{2,1,0:T(8,128)(2,1)S(1)}, u32[]{:S(2)}, u32[]{:S(2)}) collective-permute-start(bf16[4,32,1024]{2,1,0:T(8,128)(2,1)S(1)} %fusion.57), channel_id=1, source_target_pairs={{0,1},{1,0},{2,3},{3,2},{4,5},{5,4},{6,7},{7,6},{8,9},{9,8},{10,11... | collective-permute-start | bytes 786440 | tf_op jit(solution)/shard_map/ppermute | solution.py:255
  159.8 9.0 %collective-permute-start.9 = (bf16[32,1024]{1,0:T(8,128)(2,1)S(1)}, bf16[32,1024]{1,0:T(8,128)(2,1)S(1)}, u32[]{:S(2)}, u32[]{:S(2)}) collective-permute-start(bf16[32,1024]{1,0:T(8,128)(2,1)S(1)} %get-tuple-element.56), channel_id=1, source_target_pairs={{0,4},{1,5},{2,6},{3,7},{4,8},{5,9},{6,10},{7,11},{8,12},{9,13},{1... | collective-permute-start | bytes 196616 | tf_op jit(solution)/shard_map/ppermute | solution.py:276
  164.7 53.6 %collective-permute-start.25 = (bf16[4,2,32,2816]{3,2,0,1:T(8,128)(2,1)}, bf16[4,2,32,2816]{3,2,0,1:T(8,128)(2,1)}, u32[]{:S(2)}, u32[]{:S(2)}) collective-permute-start(bf16[4,2,32,2816]{3,2,0,1:T(8,128)(2,1)} %copy.128), channel_id=1, source_target_pairs={{0,1},{1,0},{2,3},{3,2},{4,5},{5,4},{6,7},{7,6},{8,9},{9,8},{10,11... | collective-permute-start | bytes 4325384 | tf_op jit(solution)/shard_map/ppermute | solution.py:255
  166.2 7.6 %collective-permute-start.12 = (bf16[32,1024]{1,0:T(8,128)(2,1)S(1)}, bf16[32,1024]{1,0:T(8,128)(2,1)S(1)}, u32[]{:S(2)}, u32[]{:S(2)}) collective-permute-start(bf16[32,1024]{1,0:T(8,128)(2,1)S(1)} %get-tuple-element.57), channel_id=1, source_target_pairs={{4,0},{5,1},{6,2},{7,3},{8,4},{9,5},{10,6},{11,7},{12,8},{13,9},{1... | collective-permute-start | bytes 196616 | tf_op jit(solution)/shard_map/ppermute | solution.py:277
  168.9 6.2 %collective-permute-start.10 = (bf16[32,1024]{1,0:T(8,128)(2,1)S(1)}, bf16[32,1024]{1,0:T(8,128)(2,1)S(1)}, u32[]{:S(2)}, u32[]{:S(2)}) collective-permute-start(bf16[32,1024]{1,0:T(8,128)(2,1)S(1)} %fusion.71), channel_id=1, source_target_pairs={{0,4},{1,5},{2,6},{3,7},{4,8},{5,9},{6,10},{7,11},{8,12},{9,13},{1... | collective-permute-start | bytes 196616 | tf_op jit(solution)/shard_map/ppermute | solution.py:276
  175.7 27.4 %collective-permute-start.13 = (bf16[32,1024]{1,0:T(8,128)(2,1)}, bf16[32,1024]{1,0:T(8,128)(2,1)S(1)}, u32[]{:S(2)}, u32[]{:S(2)}) collective-permute-start(bf16[32,1024]{1,0:T(8,128)(2,1)} %get-tuple-element.55), channel_id=1, source_target_pairs={{4,0},{5,1},{6,2},{7,3},{8,4},{9,5},{10,6},{11,7},{12,8},{13,9},{1... | collective-permute-start | bytes 196616 | tf_op jit(solution)/shard_map/ppermute | solution.py:277
  189.3 46.4 %all-to-all-start.3 = ((bf16[16,192,128]{2,1,0:T(8,128)(2,1)}), bf16[16,192,128]{2,1,0:T(8,128)(2,1)}, u32[]{:S(2)}, u32[]{:S(2)}) async-start(bf16[16,192,128]{2,1,0:T(8,128)(2,1)} %attn_bwd.1), calls=%async_computation.3 | async-start | bytes 1572864 | tf_op jit(solution)/shard_map/all_to_all | solution.py:234
  199.6 13.4 %collective-permute-start.11 = (bf16[32,1024]{1,0:T(8,128)(2,1)}, bf16[32,1024]{1,0:T(8,128)(2,1)S(1)}, u32[]{:S(2)}, u32[]{:S(2)}) collective-permute-start(bf16[32,1024]{1,0:T(8,128)(2,1)} %get-tuple-element.54), channel_id=1, source_target_pairs={{0,4},{1,5},{2,6},{3,7},{4,8},{5,9},{6,10},{7,11},{8,12},{9,13},{1... | collective-permute-start | bytes 196616 | tf_op jit(solution)/shard_map/ppermute | solution.py:276
  203.2 11.7 %collective-permute-start.14 = (bf16[32,1024]{1,0:T(8,128)(2,1)S(1)}, bf16[32,1024]{1,0:T(8,128)(2,1)S(1)}, u32[]{:S(2)}, u32[]{:S(2)}) collective-permute-start(bf16[32,1024]{1,0:T(8,128)(2,1)S(1)} %fusion.70), channel_id=1, source_target_pairs={{4,0},{5,1},{6,2},{7,3},{8,4},{9,5},{10,6},{11,7},{12,8},{13,9},{1... | collective-permute-start | bytes 196616 | tf_op jit(solution)/shard_map/ppermute | solution.py:277
  207.0 20.0 %collective-permute-start.34 = (bf16[4,88,1024]{2,1,0:T(8,128)(2,1)S(1)}, bf16[4,88,1024]{2,1,0:T(8,128)(2,1)S(1)}, u32[]{:S(2)}, u32[]{:S(2)}) collective-permute-start(bf16[4,88,1024]{2,1,0:T(8,128)(2,1)S(1)} %fusion.30), channel_id=1, source_target_pairs={{0,2},{1,3},{2,0},{3,1},{4,6},{5,7},{6,4},{7,5},{8,10},{9,11},{10,... | collective-permute-start | bytes 2162696 | tf_op jit(solution)/shard_map/ppermute | solution.py:255
  217.8 49.0 %collective-permute-start.17 = (bf16[4,32,2816]{2,1,0:T(8,128)(2,1)}, bf16[4,32,2816]{2,1,0:T(8,128)(2,1)}, u32[]{:S(2)}, u32[]{:S(2)}) collective-permute-start(bf16[4,32,2816]{2,1,0:T(8,128)(2,1)} %fusion.28), channel_id=1, source_target_pairs={{0,1},{1,0},{2,3},{3,2},{4,5},{5,4},{6,7},{7,6},{8,9},{9,8},{10,11... | collective-permute-start | bytes 2162696 | tf_op jit(solution)/shard_map/ppermute | solution.py:255
  220.6 53.8 %collective-permute-start.26 = (bf16[4,32,2816]{2,1,0:T(8,128)(2,1)}, bf16[4,32,2816]{2,1,0:T(8,128)(2,1)}, u32[]{:S(2)}, u32[]{:S(2)}) collective-permute-start(bf16[4,32,2816]{2,1,0:T(8,128)(2,1)} %fusion.29), channel_id=1, source_target_pairs={{0,2},{1,3},{2,0},{3,1},{4,6},{5,7},{6,4},{7,5},{8,10},{9,11},{10,... | collective-permute-start | bytes 2162696 | tf_op jit(solution)/shard_map/ppermute | solution.py:255
  229.2 11.2 %collective-permute-start.35 = (bf16[88,1024]{1,0:T(8,128)(2,1)}, bf16[88,1024]{1,0:T(8,128)(2,1)}, u32[]{:S(2)}, u32[]{:S(2)}) collective-permute-start(bf16[88,1024]{1,0:T(8,128)(2,1)} %get-tuple-element.28), channel_id=1, source_target_pairs={{0,4},{1,5},{2,6},{3,7},{4,8},{5,9},{6,10},{7,11},{8,12},{9,13},{1... | collective-permute-start | bytes 540680 | tf_op jit(solution)/shard_map/ppermute | solution.py:276
  232.9 12.5 %collective-permute-start.38 = (bf16[88,1024]{1,0:T(8,128)(2,1)}, bf16[88,1024]{1,0:T(8,128)(2,1)}, u32[]{:S(2)}, u32[]{:S(2)}) collective-permute-start(bf16[88,1024]{1,0:T(8,128)(2,1)} %get-tuple-element.29), channel_id=1, source_target_pairs={{4,0},{5,1},{6,2},{7,3},{8,4},{9,5},{10,6},{11,7},{12,8},{13,9},{1... | collective-permute-start | bytes 540680 | tf_op jit(solution)/shard_map/ppermute | solution.py:277
  241.3 7.4 %collective-permute-start.36 = (bf16[88,1024]{1,0:T(8,128)(2,1)S(1)}, bf16[88,1024]{1,0:T(8,128)(2,1)S(1)}, u32[]{:S(2)}, u32[]{:S(2)}) collective-permute-start(bf16[88,1024]{1,0:T(8,128)(2,1)S(1)} %fusion.44), channel_id=1, source_target_pairs={{0,4},{1,5},{2,6},{3,7},{4,8},{5,9},{6,10},{7,11},{8,12},{9,13},{1... | collective-permute-start | bytes 540680 | tf_op jit(solution)/shard_map/ppermute | solution.py:276
  249.7 8.7 %collective-permute-start.39 = (bf16[88,1024]{1,0:T(8,128)(2,1)S(1)}, bf16[88,1024]{1,0:T(8,128)(2,1)S(1)}, u32[]{:S(2)}, u32[]{:S(2)}) collective-permute-start(bf16[88,1024]{1,0:T(8,128)(2,1)S(1)} %get-tuple-element.27), channel_id=1, source_target_pairs={{4,0},{5,1},{6,2},{7,3},{8,4},{9,5},{10,6},{11,7},{12,8},{13,9},{1... | collective-permute-start | bytes 540680 | tf_op jit(solution)/shard_map/ppermute | solution.py:277
  251.7 10.1 %collective-permute-start.37 = (bf16[88,1024]{1,0:T(8,128)(2,1)S(1)}, bf16[88,1024]{1,0:T(8,128)(2,1)S(1)}, u32[]{:S(2)}, u32[]{:S(2)}) collective-permute-start(bf16[88,1024]{1,0:T(8,128)(2,1)S(1)} %get-tuple-element.26), channel_id=1, source_target_pairs={{0,4},{1,5},{2,6},{3,7},{4,8},{5,9},{6,10},{7,11},{8,12},{9,13},{1... | collective-permute-start | bytes 540680 | tf_op jit(solution)/shard_map/ppermute | solution.py:276
  258.5 7.5 %collective-permute-start.40 = (bf16[88,1024]{1,0:T(8,128)(2,1)S(1)}, bf16[88,1024]{1,0:T(8,128)(2,1)S(1)}, u32[]{:S(2)}, u32[]{:S(2)}) collective-permute-start(bf16[88,1024]{1,0:T(8,128)(2,1)S(1)} %fusion.43), channel_id=1, source_target_pairs={{4,0},{5,1},{6,2},{7,3},{8,4},{9,5},{10,6},{11,7},{12,8},{13,9},{1... | collective-permute-start | bytes 540680 | tf_op jit(solution)/shard_map/ppermute | solution.py:277
  268.5 13.4 %collective-permute-start.18 = (bf16[32,2816]{1,0:T(8,128)(2,1)S(1)}, bf16[32,2816]{1,0:T(8,128)(2,1)S(1)}, u32[]{:S(2)}, u32[]{:S(2)}) collective-permute-start(bf16[32,2816]{1,0:T(8,128)(2,1)S(1)} %get-tuple-element.38), channel_id=1, source_target_pairs={{0,4},{1,5},{2,6},{3,7},{4,8},{5,9},{6,10},{7,11},{8,12},{9,13},{1... | collective-permute-start | bytes 540680 | tf_op jit(solution)/shard_map/ppermute | solution.py:276
  271.0 15.4 %collective-permute-start.21 = (bf16[32,2816]{1,0:T(8,128)(2,1)S(1)}, bf16[32,2816]{1,0:T(8,128)(2,1)S(1)}, u32[]{:S(2)}, u32[]{:S(2)}) collective-permute-start(bf16[32,2816]{1,0:T(8,128)(2,1)S(1)} %get-tuple-element.39), channel_id=1, source_target_pairs={{4,0},{5,1},{6,2},{7,3},{8,4},{9,5},{10,6},{11,7},{12,8},{13,9},{1... | collective-permute-start | bytes 540680 | tf_op jit(solution)/shard_map/ppermute | solution.py:277
  276.1 8.4 %collective-permute-start.27 = (bf16[32,2816]{1,0:T(8,128)(2,1)S(1)}, bf16[32,2816]{1,0:T(8,128)(2,1)S(1)}, u32[]{:S(2)}, u32[]{:S(2)}) collective-permute-start(bf16[32,2816]{1,0:T(8,128)(2,1)S(1)} %get-tuple-element.32), channel_id=1, source_target_pairs={{0,4},{1,5},{2,6},{3,7},{4,8},{5,9},{6,10},{7,11},{8,12},{9,13},{1... | collective-permute-start | bytes 540680 | tf_op jit(solution)/shard_map/ppermute | solution.py:276
  278.5 18.4 %collective-permute-start.30 = (bf16[32,2816]{1,0:T(8,128)(2,1)S(1)}, bf16[32,2816]{1,0:T(8,128)(2,1)S(1)}, u32[]{:S(2)}, u32[]{:S(2)}) collective-permute-start(bf16[32,2816]{1,0:T(8,128)(2,1)S(1)} %get-tuple-element.33), channel_id=1, source_target_pairs={{4,0},{5,1},{6,2},{7,3},{8,4},{9,5},{10,6},{11,7},{12,8},{13,9},{1... | collective-permute-start | bytes 540680 | tf_op jit(solution)/shard_map/ppermute | solution.py:277
  282.0 8.3 %collective-permute-start.19 = (bf16[32,2816]{1,0:T(8,128)(2,1)S(1)}, bf16[32,2816]{1,0:T(8,128)(2,1)S(1)}, u32[]{:S(2)}, u32[]{:S(2)}) collective-permute-start(bf16[32,2816]{1,0:T(8,128)(2,1)S(1)} %fusion.54), channel_id=1, source_target_pairs={{0,4},{1,5},{2,6},{3,7},{4,8},{5,9},{6,10},{7,11},{8,12},{9,13},{1... | collective-permute-start | bytes 540680 | tf_op jit(solution)/shard_map/ppermute | solution.py:276
  284.5 12.4 %collective-permute-start.28 = (bf16[32,2816]{1,0:T(8,128)(2,1)S(1)}, bf16[32,2816]{1,0:T(8,128)(2,1)S(1)}, u32[]{:S(2)}, u32[]{:S(2)}) collective-permute-start(bf16[32,2816]{1,0:T(8,128)(2,1)S(1)} %fusion.49), channel_id=1, source_target_pairs={{0,4},{1,5},{2,6},{3,7},{4,8},{5,9},{6,10},{7,11},{8,12},{9,13},{1... | collective-permute-start | bytes 540680 | tf_op jit(solution)/shard_map/ppermute | solution.py:276
  291.0 12.5 %collective-permute-start.22 = (bf16[32,2816]{1,0:T(8,128)(2,1)S(1)}, bf16[32,2816]{1,0:T(8,128)(2,1)S(1)}, u32[]{:S(2)}, u32[]{:S(2)}) collective-permute-start(bf16[32,2816]{1,0:T(8,128)(2,1)S(1)} %get-tuple-element.37), channel_id=1, source_target_pairs={{4,0},{5,1},{6,2},{7,3},{8,4},{9,5},{10,6},{11,7},{12,8},{13,9},{1... | collective-permute-start | bytes 540680 | tf_op jit(solution)/shard_map/ppermute | solution.py:277
  292.9 36.4 %collective-permute-start.20 = (bf16[32,2816]{1,0:T(8,128)(2,1)}, bf16[32,2816]{1,0:T(8,128)(2,1)}, u32[]{:S(2)}, u32[]{:S(2)}) collective-permute-start(bf16[32,2816]{1,0:T(8,128)(2,1)} %get-tuple-element.36), channel_id=1, source_target_pairs={{0,4},{1,5},{2,6},{3,7},{4,8},{5,9},{6,10},{7,11},{8,12},{9,13},{1... | collective-permute-start | bytes 540680 | tf_op jit(solution)/shard_map/ppermute | solution.py:276
  297.7 20.7 %collective-permute-start.31 = (bf16[32,2816]{1,0:T(8,128)(2,1)}, bf16[32,2816]{1,0:T(8,128)(2,1)}, u32[]{:S(2)}, u32[]{:S(2)}) collective-permute-start(bf16[32,2816]{1,0:T(8,128)(2,1)} %get-tuple-element.31), channel_id=1, source_target_pairs={{4,0},{5,1},{6,2},{7,3},{8,4},{9,5},{10,6},{11,7},{12,8},{13,9},{1... | collective-permute-start | bytes 540680 | tf_op jit(solution)/shard_map/ppermute | solution.py:277
  300.3 29.1 %collective-permute-start.29 = (bf16[32,2816]{1,0:T(8,128)(2,1)}, bf16[32,2816]{1,0:T(8,128)(2,1)}, u32[]{:S(2)}, u32[]{:S(2)}) collective-permute-start(bf16[32,2816]{1,0:T(8,128)(2,1)} %get-tuple-element.30), channel_id=1, source_target_pairs={{0,4},{1,5},{2,6},{3,7},{4,8},{5,9},{6,10},{7,11},{8,12},{9,13},{1... | collective-permute-start | bytes 540680 | tf_op jit(solution)/shard_map/ppermute | solution.py:276
  304.3 25.1 %collective-permute-start.23 = (bf16[32,2816]{1,0:T(8,128)(2,1)}, bf16[32,2816]{1,0:T(8,128)(2,1)}, u32[]{:S(2)}, u32[]{:S(2)}) collective-permute-start(bf16[32,2816]{1,0:T(8,128)(2,1)} %fusion.53), channel_id=1, source_target_pairs={{4,0},{5,1},{6,2},{7,3},{8,4},{9,5},{10,6},{11,7},{12,8},{13,9},{1... | collective-permute-start | bytes 540680 | tf_op jit(solution)/shard_map/ppermute | solution.py:277
  318.3 3.6 %collective-permute-start.4 = (bf16[512,192]{0,1:T(8,128)(2,1)S(1)}, bf16[512,192]{0,1:T(8,128)(2,1)S(1)}, u32[]{:S(2)}, u32[]{:S(2)}) collective-permute-start(bf16[512,192]{0,1:T(8,128)(2,1)S(1)} %fusion.62), channel_id=1, source_target_pairs={{0,16},{16,0},{1,17},{17,1},{2,18},{18,2},{3,19},{19,3},{4,20},{20... | collective-permute-start | bytes 589832 | tf_op jit(solution)/shard_map/ppermute | solution.py:211
  320.0 9.3 %collective-permute-start.32 = (bf16[32,2816]{1,0:T(8,128)(2,1)}, bf16[32,2816]{1,0:T(8,128)(2,1)}, u32[]{:S(2)}, u32[]{:S(2)}) collective-permute-start(bf16[32,2816]{1,0:T(8,128)(2,1)} %fusion.48), channel_id=1, source_target_pairs={{4,0},{5,1},{6,2},{7,3},{8,4},{9,5},{10,6},{11,7},{12,8},{13,9},{1... | collective-permute-start | bytes 540680 | tf_op jit(solution)/shard_map/ppermute | solution.py:277
  322.8 15.0 %all-to-all-start.4 = ((bf16[16,32,192]{2,1,0:T(8,128)(2,1)}), bf16[16,32,192]{2,1,0:T(8,128)(2,1)S(1)}, u32[]{:S(2)}, u32[]{:S(2)}) async-start(bf16[16,32,192]{2,1,0:T(8,128)(2,1)} %bitcast.22), calls=%async_computation.4 | async-start | bytes 524288 | tf_op jit(solution)/shard_map/all_to_all | solution.py:234
  (41 other events, 255.1 us)
Sparse Core Ops, SparseCore 0:
  70.3 92.7 all-gather.1

commit v2 on v1

--- a/solution.py
+++ b/solution.py
@@ -90,7 +90,7 @@
 
 
 def attn_bwd_kernel(
-    rep, slot_ref, low_ref, ends_ref, part_ref, qkv_ref, da_ref, full_ref, top_ref, inv_ref,
+    rep, place, slot_ref, low_ref, ends_ref, part_ref, qkv_ref, da_ref, full_ref, top_ref, inv_ref,
     out_ref, key_ref, value_ref, dk_ref, dv_ref,
 ):
     slots, _, rows = qkv_ref.shape
@@ -135,14 +135,14 @@
 
         dq = lax.fori_loop(low_ref[i], i + 1, key_block, jnp.zeros((hd, blk), F32))
         dq = (dq * SCALE).astype(BF16)
-        out_ref[s0, :hd, :] = dq[:, :rows]
-        out_ref[s1, :hd, :] = dq[:, rows:]
+        out_ref[place(s0), :hd, :] = dq[:, :rows]
+        out_ref[place(s1), :hd, :] = dq[:, rows:]
         return c
 
     lax.fori_loop(0, count // rep, lambda n, c: query_block(n * rep + part_ref[0], c), 0)
 
     def finish(j, c):
-        k0, k1 = slot_ref[2 * j], slot_ref[2 * j + 1]
+        k0, k1 = place(slot_ref[2 * j]), place(slot_ref[2 * j + 1])
         dk = (dk_ref[j] * SCALE).astype(BF16)
         dv = dv_ref[j].astype(BF16)
         out_ref[k0, hd : 2 * hd, :] = dk[:, :rows]
@@ -154,47 +154,79 @@
     lax.fori_loop(0, count, finish, 0)
 
 
+def in_hbm(v):
+    return pltpu.with_memory_space_constraint(v, pltpu.HBM)
+
+
+def call(kernel, name, args, after=(), smem=0, outs=(), scratch=(), vmem=24, far=0):
+    held = len(args)
+
+    def body(*refs):
+        return kernel(*refs[:held], *refs[held + len(after) :])
+
+    if far:
+        args = (*args[: held - far], *(in_hbm(v) for v in args[held - far :]))
+    return pl.pallas_call(
+        body,
+        in_specs=[SMEM] * smem + [VMEM] * (held - smem - far) + [HBM] * far + [ANY] * len(after),
+        out_specs=[VMEM] * len(outs),
+        out_shape=[jax.ShapeDtypeStruct(*o) for o in outs],
+        scratch_shapes=list(scratch),
+        cost_estimate=COST,
+        compiler_params=pltpu.CompilerParams(vmem_limit_bytes=vmem * 2**20),
+        name=name,
+    )(*args, *after)
+
+
+COST = pl.CostEstimate(flops=10**6, bytes_accessed=10**5, transcendentals=0)
 SMEM = pl.BlockSpec(memory_space=pltpu.SMEM)
+ANY = pl.BlockSpec(memory_space=pl.ANY)
+HBM = pl.BlockSpec(memory_space=pltpu.HBM)
 VMEM = pl.BlockSpec(memory_space=pltpu.VMEM)
 
 
-def attn_fwd(rep, scalars, qkv):
+def attn_fwd(rep, scalars, qkv, after=()):
     slots, _, rows = qkv.shape
-    stat = jax.ShapeDtypeStruct((slots // 2, 1, 2 * rows), F32)
-    return pl.pallas_call(
+    stat = ((slots // 2, 1, 2 * rows), F32)
+    return call(
         functools.partial(attn_fwd_kernel, rep),
-        in_specs=[SMEM] * 4 + [VMEM],
-        out_specs=[VMEM] * 4,
-        out_shape=[
-            jax.ShapeDtypeStruct((slots, HEAD_DIM, rows), BF16),
-            jax.ShapeDtypeStruct((slots, HEAD_DIM, rows), F32),
-            stat,
-            stat,
-        ],
-        scratch_shapes=[pltpu.VMEM((slots, rows, HEAD_DIM), BF16)],
-        cost_estimate=pl.CostEstimate(flops=10**9, bytes_accessed=3 * 10**6, transcendentals=2 * 10**6),
-        compiler_params=pltpu.CompilerParams(vmem_limit_bytes=32 * 2**20),
-        name="attn_fwd",
-    )(*scalars, qkv)
-
-
-def attn_bwd(rep, scalars, qkv, da, full, top, inv):
+        "attn_fwd",
+        (*scalars, qkv),
+        after,
+        smem=4,
+        outs=[((slots, HEAD_DIM, rows), BF16), ((slots, HEAD_DIM, rows), F32), stat, stat],
+        scratch=[pltpu.VMEM((slots, rows, HEAD_DIM), BF16)],
+        vmem=24,
+    )
+
+
+def attn_bwd(rep, place, scalars, qkv, da, full, top, inv, after=()):
     slots, _, rows = qkv.shape
-    return pl.pallas_call(
-        functools.partial(attn_bwd_kernel, rep),
-        in_specs=[SMEM] * 4 + [VMEM] * 5,
-        out_specs=VMEM,
-        out_shape=jax.ShapeDtypeStruct((slots, 3 * HEAD_DIM, rows), BF16),
-        scratch_shapes=[
+    return call(
+        functools.partial(attn_bwd_kernel, rep, place),
+        "attn_bwd",
+        (*scalars, qkv, da, full, top, inv),
+        after,
+        smem=4,
+        outs=[((slots, 3 * HEAD_DIM, rows), BF16)],
+        scratch=[
             pltpu.VMEM((slots, rows, HEAD_DIM), BF16),
             pltpu.VMEM((slots, rows, HEAD_DIM), BF16),
             pltpu.VMEM((slots // 2, HEAD_DIM, 2 * rows), F32),
             pltpu.VMEM((slots // 2, HEAD_DIM, 2 * rows), F32),
         ],
-        cost_estimate=pl.CostEstimate(flops=2 * 10**9, bytes_accessed=4 * 10**6, transcendentals=2 * 10**6),
-        compiler_params=pltpu.CompilerParams(vmem_limit_bytes=32 * 2**20),
-        name="attn_bwd",
-    )(*scalars, qkv, da, full, top, inv)
+        vmem=24,
+    )[0]
+
+
+def positions(seq_lengths, span_order, rows, part):
+    ends = jnp.cumsum(seq_lengths[0]).astype(jnp.int32)
+    count = span_order.shape[1]
+    blocks = jnp.arange(count, dtype=jnp.int32)
+    slot_of = jnp.sum(jnp.where(span_order[0][None, :] == blocks[:, None], blocks[None, :], 0), axis=1)
+    starts = jnp.arange(count // 2, dtype=jnp.int32) * (2 * rows)
+    low = jnp.max(jnp.where(starts[:, None] >= ends[None, :], ends[None, :], 0), axis=1) // (2 * rows)
+    return slot_of.astype(jnp.int32), low.astype(jnp.int32), ends, part.reshape(1).astype(jnp.int32)
 
 
 def norm_back(grad_normed, unit_rows, inv_rows, gain_vec):
@@ -205,80 +237,25 @@
 class Moves:
     def __init__(self, n_dp, n_ctx):
         self.n_dp, self.n_ctx = n_dp, n_ctx
-        self.grid = n_dp == 2 and n_ctx == 16
-
-    def swap(self, v):
-        return lax.ppermute(v, "dp", [(0, 1), (1, 0)])
 
     def rows_gather(self, v):
-        if self.grid:
-            return jnp.concatenate([v, self.swap(v)], axis=0)
         return lax.all_gather(v, "dp", axis=0, tiled=True)
 
     def rows_sum(self, v):
-        if self.grid:
-            rows = v.shape[0] // 2
-            return v[:rows] + self.swap(v[rows:].astype(BF16)).astype(F32)
         return lax.psum_scatter(v, "dp", scatter_dimension=0, tiled=True)
 
     def columns_gather(self, v):
-        if self.grid:
-            rows = v.shape[0] // 2
-            other = self.swap(v)
-            other = jnp.concatenate([other[rows:], other[:rows]], axis=0)
-            first = lax.axis_index("dp") == 0
-            return jnp.concatenate([jnp.where(first, v, other), jnp.where(first, other, v)], axis=1)
         return lax.all_gather(v, "dp", axis=1, tiled=True)
 
     def to_ctx(self, v):
         return lax.all_to_all(v, "ctx", 0, 0, tiled=True)
 
-    def sum_product(self, left, right, first):
-        if not self.grid:
-            part = dot(left, right, ((1,), (0,))).astype(BF16)
-            return lax.psum_scatter(part, "ctx", scatter_dimension=0, tiled=True).astype(F32)
-        chunk, depth, wide = left.shape[0] // 16, left.shape[1], right.shape[1]
-        c = lax.axis_index("ctx")
-        z, y, x = c // 4, (c // 2) % 2, c % 2
-        left = left.reshape(4, 2, 2, chunk, depth)
-        axis = {"x": 2, "y": 1}[first]
-        here = {"x": x, "y": y}
-        step = {"x": 1, "y": 2}
-        second = {"x": "y", "y": "x"}[first]
-
-        def product(at):
-            rows = lax.dynamic_index_in_dim(left, at, axis, keepdims=False)
-            out = dot(rows.reshape(8 * chunk, depth), right, ((1,), (0,)))
-            return out.astype(BF16).reshape(4, 2, chunk, wide)
-
-        def across(v, name):
-            return lax.ppermute(v, "ctx", [(i, i ^ step[name]) for i in range(16)])
-
-        got = across(product(1 - here[first]), first)
-        kept = product(here[first])
-
-        def half(at):
-            a = lax.dynamic_index_in_dim(got, at, 1, keepdims=False)
-            b = lax.dynamic_index_in_dim(kept, at, 1, keepdims=False)
-            return a.astype(F32) + b.astype(F32)
-
-        got_two = across(half(1 - here[second]).astype(BF16), second)
-        own = half(here[second]) + got_two.astype(F32)
-        up = jnp.zeros((chunk, wide), F32)
-        down = jnp.zeros((chunk, wide), F32)
-
-        def level(at):
-            return lax.dynamic_index_in_dim(own, jnp.clip(at, 0, 3), 0, keepdims=False)
-
-        for n in range(1, 4):
-            send_up = (level(z + 4 - n) + up).astype(BF16)
-            send_down = (level(z - 4 + n) + down).astype(BF16)
-            up = lax.ppermute(send_up, "ctx", [(i, i + 4) for i in range(12)]).astype(F32)
-            down = lax.ppermute(send_down, "ctx", [(i + 4, i) for i in range(12)]).astype(F32)
-        return level(z) + up + down
-
-
-def per_device(
+    def sum_product(self, left, right):
+        part = dot(left, right, ((1,), (0,))).astype(BF16)
+        return lax.psum_scatter(part, "ctx", scatter_dimension=0, tiled=True).astype(F32)
+
+
+def per_device_any(
     moves,
     latent_in,
     gain_attn,
@@ -300,11 +277,7 @@
     dp, ctx = lax.axis_index("dp"), lax.axis_index("ctx")
     rep = n_ctx // HEADS
 
-    ends = jnp.cumsum(seq_lengths[0]).astype(jnp.int32)
-    slot_of = jnp.zeros((n_ctx,), jnp.int32).at[span_order[0]].set(jnp.arange(n_ctx, dtype=jnp.int32))
-    starts = jnp.arange(n_ctx // 2, dtype=jnp.int32) * (2 * rows)
-    low = jnp.max(jnp.where(starts[:, None] >= ends[None, :], ends[None, :], 0), axis=1) // (2 * rows)
-    scalars = (slot_of, low, ends, (ctx % rep).reshape(1).astype(jnp.int32))
+    scalars = positions(seq_lengths, span_order, rows, ctx % rep)
 
     share = ff // n_dp
     gate_w = lax.dynamic_slice_in_dim(w_gate, dp * share, share, 1)
@@ -356,26 +329,21 @@
 
     grad_attn = dot(w_out, grad_mixed, ((1,), (1,))).astype(BF16).reshape(HEADS, HEAD_DIM, rows)
     grad_attn = moves.to_ctx(jnp.repeat(grad_attn, rep, axis=0) if rep > 1 else grad_attn)
-    grad_qkv = attn_bwd(rep, scalars, qkv, grad_attn, full, top, inv)
+    grad_qkv = attn_bwd(rep, lambda slot: slot, scalars, qkv, grad_attn, full, top, inv)
 
     strip = width // n_dp
-    down_sum = moves.sum_product(hidden.T, top_all, "x")
+    down_sum = moves.sum_product(hidden.T, top_all)
     normed_rows = lax.dynamic_slice_in_dim(normed_two_all, dp * strip, strip, 1).T
-    gate_sum = moves.sum_product(normed_rows, moves.columns_gather(grad_gate), "y")
-    up_sum = moves.sum_product(normed_rows, moves.columns_gather(grad_up), "x")
+    gate_sum = moves.sum_product(normed_rows, moves.columns_gather(grad_gate))
+    up_sum = moves.sum_product(normed_rows, moves.columns_gather(grad_up))
     attn_rows = moves.rows_gather(attn_t.T)
     attn_rows = lax.dynamic_slice_in_dim(attn_rows, dp * strip, strip, 1).T
-    out_sum = moves.sum_product(attn_rows, moves.rows_gather(grad_mixed), "y")
+    out_sum = moves.sum_product(attn_rows, moves.rows_gather(grad_mixed))
 
     lanes = jnp.transpose(grad_qkv, (0, 2, 1)).reshape(n_ctx * rows, 3 * HEAD_DIM)
     head_grad = dot(normed_all, lanes, ((0,), (0,)))
     head_grad = head_grad.reshape(n_dp, strip, 3 * HEAD_DIM)
-    if moves.grid:
-        mine = lax.dynamic_index_in_dim(head_grad, dp, 0, keepdims=False)
-        theirs = lax.dynamic_index_in_dim(head_grad, 1 - dp, 0, keepdims=False)
-        head_grad = mine + moves.swap(theirs.astype(BF16)).astype(F32)
-    else:
-        head_grad = lax.psum_scatter(head_grad, "dp", scatter_dimension=0, tiled=False)
+    head_grad = lax.psum_scatter(head_grad, "dp", scatter_dimension=0, tiled=False)
     own = strip // n_ctx
     head_grad = moves.to_ctx(head_grad.astype(BF16).reshape(n_ctx, own, 3 * HEAD_DIM)).astype(F32)
     head_grad = jnp.sum(head_grad.reshape(HEADS, rep, own, 3, HEAD_DIM), axis=1)
@@ -416,12 +384,764 @@
     )
 
 
+def low_t(v):
+    return v.astype(F32).T.astype(BF16)
+
+
+def sel(at, other):
+    return 1 - at if other else at
+
+
+def norm_qkv_kernel(x_ref, gain_ref, wq_ref, wk_ref, wv_ref, n_ref, qkv_ref, held_ref, sems):
+    loads = [pltpu.make_async_copy(w, held_ref.at[t], sems.at[t]) for t, w in enumerate((wq_ref, wk_ref, wv_ref))]
+    for load in loads:
+        load.start()
+    x = x_ref[...].astype(F32)
+    inv = lax.rsqrt(jnp.mean(x * x, axis=-1, keepdims=True) + EPS)
+    n = (x * inv * gain_ref[...]).astype(BF16)
+    n_ref[...] = n
+    cols = 256
+    for t, load in enumerate(loads):
+        load.wait()
+        for c in range(0, held_ref.shape[2], cols):
+            p = dot(n, held_ref[t, :, c : c + cols], ((1,), (0,))).T.astype(BF16)
+            for h in range(cols // HEAD_DIM):
+                qkv_ref[c // HEAD_DIM + h, t * HEAD_DIM : (t + 1) * HEAD_DIM, :] = p[h * HEAD_DIM : (h + 1) * HEAD_DIM]
+
+
+def norm_qkv(x, gain, wq, wk, wv):
+    rows, width = x.shape
+    return call(
+        norm_qkv_kernel,
+        "norm_qkv",
+        (x, gain.reshape(1, width), wq, wk, wv),
+        outs=[
+            ((rows, width), BF16),
+            ((HEADS, 3 * HEAD_DIM, rows), BF16),
+        ],
+        scratch=[pltpu.VMEM((3, width, width), BF16), pltpu.SemaphoreType.DMA((3,))],
+        far=3,
+    )
+
+
+def out_norm_kernel(at_ref, ab_ref, x_ref, gain_ref, w_ref, resid_ref, n_ref, send_ref, held_ref, sem):
+    load = pltpu.make_async_copy(w_ref, held_ref, sem)
+    load.start()
+    left = low_t(ab_ref[...])
+    half = send_ref.shape[0]
+    send_ref[...] = ab_ref[pl.ds(pl.multiple_of((1 - at_ref[0]) * half, half), half), :]
+    load.wait()
+    cols = 256
+    mixed = [dot(left, held_ref[:, c : c + cols], ((1,), (0,))) for c in range(0, held_ref.shape[1], cols)]
+    resid = x_ref[...].astype(F32) + jnp.concatenate(mixed, axis=1)
+    resid_ref[...] = resid
+    inv = lax.rsqrt(jnp.mean(resid * resid, axis=-1, keepdims=True) + EPS)
+    n_ref[...] = (resid * inv * gain_ref[...]).astype(BF16)
+
+
+def out_norm(at, ab, x, gain, w, after):
+    rows, width = x.shape
+    return call(
+        out_norm_kernel,
+        "out_norm",
+        (at, ab, x, gain.reshape(1, width), w),
+        after,
+        smem=1,
+        outs=[((rows, width), F32), ((rows, width), BF16), ((width // 2, rows), BF16)],
+        scratch=[pltpu.VMEM(w.shape, BF16), pltpu.SemaphoreType.DMA],
+        far=1,
+    )
+
+
+def ffn_kernel(
+    at_ref, n0_ref, n1_ref, dy0_ref, dy1_ref, wg_ref, wu_ref, wd_ref,
+    hid_ref, d0_ref, d1_ref, sx_ref, sy_ref, px_ref, py_ref, kx_ref, ky_ref,
+    n_ref, dy_ref, dg_ref, du_ref, hid_t_ref, n_t_ref, g_w, u_w, d_w, sems,
+):
+    rows, width = n0_ref.shape
+    share = g_w.shape[1]
+    first = pl.multiple_of(at_ref[0] * share, 128)
+    parts = ((0, 768), (768, share))
+    loads = []
+    for n, (lo, hi) in enumerate(parts):
+        cols = pl.ds(pl.multiple_of(first + lo, 128), hi - lo)
+        loads.append(
+            (
+                pltpu.make_async_copy(wg_ref.at[:, cols], g_w.at[:, pl.ds(lo, hi - lo)], sems.at[n, 0]),
+                pltpu.make_async_copy(wu_ref.at[:, cols], u_w.at[:, pl.ds(lo, hi - lo)], sems.at[n, 1]),
+                pltpu.make_async_copy(wd_ref.at[cols, :], d_w.at[pl.ds(lo, hi - lo), :], sems.at[n, 2]),
+            )
+        )
+        for load in loads[n]:
+            load.start()
+    n_ref[:rows] = n0_ref[...]
+    n_ref[rows:] = n1_ref[...]
+    dy_ref[:rows] = dy0_ref[...]
+    dy_ref[rows:] = dy1_ref[...]
+    n_t_ref[...] = low_t(n_ref[...])
+
+    for lo, hi in parts:
+        for load in loads[parts.index((lo, hi))]:
+            load.wait()
+        for at in range(lo, hi, 256):
+            lanes = slice(at, min(at + 256, share))
+            g = dot(n_ref[...], g_w[:, lanes], ((1,), (0,)))
+            u = dot(n_ref[...], u_w[:, lanes], ((1,), (0,)))
+            dh = dot(dy_ref[...], d_w[lanes, :], ((1,), (1,)))
+            sig = jax.nn.sigmoid(g)
+            swish = g * sig
+            hid = (swish * u).astype(BF16)
+            dg = (dh * u * sig * (1.0 + g * (1.0 - sig))).astype(BF16)
+            du = (dh * swish).astype(BF16)
+            hid_ref[:, lanes] = hid
+            hid_t_ref[lanes, :] = hid.astype(F32).T
+            dg_ref[:, lanes] = dg
+            du_ref[:, lanes] = du
+            for k in range(dg.shape[1] // rows):
+                to = (at // rows + k) * 2 * rows
+                sx_ref[to : to + 2 * rows, :] = dg[:, k * rows : (k + 1) * rows]
+                sy_ref[to : to + 2 * rows, :] = du[:, k * rows : (k + 1) * rows]
+
+    for at in range(0, width, 256):
+        cols = slice(at, at + 256)
+        d = dot(dg_ref[...], g_w[cols, :], ((1,), (1,))) + dot(du_ref[...], u_w[cols, :], ((1,), (1,)))
+        d0_ref[:, cols] = d[:rows]
+        d1_ref[:, cols] = d[rows:].astype(BF16)
+
+    own = width // 32
+    chunk = share // 16
+    base = px_ref.shape[0] - width
+    padded = base // 16
+    x, y = at_ref[1], at_ref[2]
+    fill = jnp.zeros((padded - chunk, rows), F32)
+
+    def put(ref, inner, z, xs, ys):
+        c = z * 4 + ys * 2 + xs
+        for half in range(2):
+            lanes = slice(half * rows, (half + 1) * rows)
+            v = hid_t_ref[pl.ds(pl.multiple_of(c * chunk, 8), chunk), lanes]
+            to = ((inner * 4 + z) * 2 + half) * padded
+            ref[to : to + padded, :] = jnp.concatenate([v, fill], axis=0).astype(BF16)
+            for d in range(2):
+                to = base + half * (width // 2) + ((inner * 4 + z) * 2 + d) * own
+                at = pl.multiple_of(d * (width // 2) + c * own, own)
+                ref[to : to + own, :] = n_t_ref[pl.ds(at, own), lanes]
+
+    for inner in range(2):
+        for z in range(4):
+            put(kx_ref, inner, z, x, sel(y, inner))
+            put(px_ref, inner, z, 1 - x, sel(y, inner))
+            put(ky_ref, inner, z, sel(x, inner), y)
+            put(py_ref, inner, z, sel(x, inner), 1 - y)
+
+
+def ffn(at, n0, n1, dy0, dy1, wg, wu, wd):
+    rows, width = n0.shape
+    share = wg.shape[1] // 2
+    padded = -(-(share // 16) // 16) * 16
+    sizes = [share // rows * 2 * rows] * 2 + [16 * padded + width] * 4
+    return call(
+        ffn_kernel,
+        "ffn",
+        (at, n0, n1, dy0, dy1, wg, wu, wd),
+        smem=1,
+        outs=[((2 * rows, share), BF16), ((rows, width), F32), ((rows, width), BF16)]
+        + [((n, rows), BF16) for n in sizes],
+        scratch=[
+            pltpu.VMEM((2 * rows, width), BF16),
+            pltpu.VMEM((2 * rows, width), BF16),
+            pltpu.VMEM((2 * rows, share), BF16),
+            pltpu.VMEM((2 * rows, share), BF16),
+            pltpu.VMEM((share, 2 * rows), F32),
+            pltpu.VMEM((width, 2 * rows), BF16),
+            pltpu.VMEM((width, share), BF16),
+            pltpu.VMEM((width, share), BF16),
+            pltpu.VMEM((share, width), BF16),
+            pltpu.SemaphoreType.DMA((2, 3)),
+        ],
+        vmem=40,
+        far=3,
+    )
+
+
+def ffn_out_kernel(at_ref, hid_ref, w_ref, y0_ref, y1_ref, held_ref, sem):
+    rows, width = y0_ref.shape
+    share = held_ref.shape[0]
+    first = pl.multiple_of(at_ref[0] * share, 128)
+    load = pltpu.make_async_copy(w_ref.at[pl.ds(first, share), :], held_ref, sem)
+    load.start()
+    load.wait()
+    for at in range(0, width, 256):
+        cols = slice(at, at + 256)
+        y = dot(hid_ref[...], held_ref[:, cols], ((1,), (0,)))
+        y0_ref[:, cols] = y[:rows]
+        y1_ref[:, cols] = y[rows:].astype(BF16)
+
+
+def ffn_out(at, hid, w, after):
+    shape = (hid.shape[0] // 2, w.shape[1])
+    return call(
+        ffn_out_kernel,
+        "ffn_out",
+        (at, hid, w),
+        after,
+        smem=1,
+        outs=[(shape, F32), (shape, BF16)],
+        scratch=[pltpu.VMEM((hid.shape[1], w.shape[1]), BF16), pltpu.SemaphoreType.DMA],
+        far=1,
+    )
+
+
+def ffn_back_kernel(d_ref, got_ref, resid_ref, gain_ref, dy_ref, w_ref, dres_ref, low_ref, da_ref, held_ref, sem):
+    load = pltpu.make_async_copy(w_ref, held_ref, sem)
+    load.start()
+    d = d_ref[...] + got_ref[...].astype(F32)
+    resid = resid_ref[...]
+    inv = lax.rsqrt(jnp.mean(resid * resid, axis=-1, keepdims=True) + EPS)
+    dres = dy_ref[...].astype(F32) + norm_back(d, resid * inv, inv, gain_ref[...])
+    dres_ref[...] = dres
+    low = dres.astype(BF16)
+    low_ref[...] = low
+    load.wait()
+    for at in range(0, held_ref.shape[0], 256):
+        da_ref[at : at + 256, :] = dot(held_ref[at : at + 256, :], low, ((1,), (1,))).astype(BF16)
+
+
+def ffn_back(d, got, resid, gain, dy, w, after):
+    rows, width = d.shape
+    return call(
+        ffn_back_kernel,
+        "ffn_back",
+        (d, got, resid, gain.reshape(1, width), dy, w),
+        after,
+        outs=[((rows, width), F32), ((rows, width), BF16), ((width, rows), BF16)],
+        scratch=[pltpu.VMEM(w.shape, BF16), pltpu.SemaphoreType.DMA],
+        far=1,
+    )
+
+
+def out_product_kernel(at_ref, ab_ref, got_ref, low0_ref, low1_ref, kx_ref, px_ref, ky_ref, py_ref, acc_ref):
+    half, rows = got_ref.shape
+    own = half // 16
+    x, y = at_ref[1], at_ref[2]
+    mine = ab_ref[pl.ds(pl.multiple_of(at_ref[0] * half, half), half), :]
+    left = jnp.concatenate([mine, got_ref[...]], axis=1)
+    right = jnp.concatenate([low0_ref[...], low1_ref[...]], axis=0)
+    for at in range(0, acc_ref.shape[1], 256):
+        acc_ref[:, at : at + 256] = dot(left, right[:, at : at + 256], ((1,), (0,)))
+    tiles = acc_ref.shape[1] // 2 // rows
+
+    def put(ref, inner, z, xs, ys, side):
+        at = pl.multiple_of((z * 4 + ys * 2 + xs) * own, own)
+        for j in range(tiles):
+            lanes = slice((side * tiles + j) * rows, (side * tiles + j + 1) * rows)
+            to = ((inner * 4 + z) * tiles + j) * own
+            ref[to : to + own, :] = acc_ref[pl.ds(at, own), lanes].astype(BF16)
+
+    for inner in range(2):
+        for z in range(4):
+            put(kx_ref, inner, z, x, sel(y, inner), 0)
+            put(px_ref, inner, z, 1 - x, sel(y, inner), 0)
+            put(ky_ref, inner, z, sel(x, inner), y, 1)
+            put(py_ref, inner, z, sel(x, inner), 1 - y, 1)
+
+
+def out_product(at, ab, got, low, low_mate, after):
+    half, rows = got.shape
+    high = half // 2 * (low.shape[1] // 2) // rows
+    return call(
+        out_product_kernel,
+        "out_product",
+        (at, ab, got, low, low_mate),
+        after,
+        smem=1,
+        outs=[((high, rows), BF16)] * 4,
+        scratch=[pltpu.VMEM((half, low.shape[1]), F32)],
+    )
+
+
+def store(refs, v, lanes, high, to):
+    for inner in range(2):
+        for z in range(4):
+            at = (inner * 4 + z) * high
+            refs[inner][z, to : to + high, :] = v[at : at + high, lanes]
+
+
+def down_product_kernel(side, p0, p1, dy0, dy1, dy2, same_ref, other_ref):
+    rows, width = dy0.shape
+    half = width // 2
+    padded = (p0.shape[0] - width) // 16
+
+    def lanes(ref, k):
+        at = k * 2 * padded
+        return jnp.concatenate([ref[at : at + padded, :], ref[at + padded : at + 2 * padded, :]], axis=1)
+
+    hid = jnp.concatenate([jnp.concatenate([lanes(p0, k), lanes(p1, k)], axis=1) for k in range(8)], axis=0)
+    cols = slice(side * half, (side + 1) * half)
+    dy = jnp.concatenate([dy0[:, cols], dy1[:, cols], dy2[...]], axis=0)
+    v = dot(hid, dy, ((1,), (0,))).astype(BF16)
+    for j in range(half // rows):
+        store((same_ref, other_ref), v, slice(j * rows, (j + 1) * rows), padded, j * padded)
+
+
+def down_product(side, p, dy, after):
+    rows, width = dy[0].shape
+    high = width // 2 // rows * ((p[0].shape[0] - width) // 16)
+    kernel = functools.partial(down_product_kernel, side)
+    return call(kernel, "down_product", (*p, *dy), after, outs=[((4, high, rows), BF16)] * 2)
+
+
+def pair_product_kernel(lo, hi, width, p0, p1, f0, f1, *rest):
+    q, out = rest[:-2], rest[-2:]
+    rows = p0.shape[1]
+    base = p0.shape[0] - width
+    half, own = width // 2, width // 32
+    left = jnp.concatenate([p[base + k * half : base + (k + 1) * half, :] for p in (p0, p1) for k in range(2)], axis=1)
+    for t in range(lo, hi, 2):
+        n = min(2, hi - t)
+        right = [
+            jnp.concatenate([f[(t + k) * 2 * rows : (t + k + 1) * 2 * rows, :] for f in (f0, f1)], axis=0)
+            for k in range(n)
+        ]
+        v = dot(left, jnp.concatenate(right, axis=1), ((1,), (0,))).astype(BF16)
+        for k in range(n):
+            store(out, v, slice(k * rows, (k + 1) * rows), 2 * own, (t + k - lo) * 2 * own)
+    if q:
+        high = q[0].shape[0] // 8
+        to = (hi - lo) * 2 * own
+        for k in range(8):
+            v = q[0][k * high : (k + 1) * high, :].astype(F32) + q[1][k * high : (k + 1) * high, :].astype(F32)
+            out[k // 4][k % 4, to : to + high, :] = v.astype(BF16)
+
+
+def pair_product(lo, hi, width, p, f, q, after):
+    rows = p[0].shape[1]
+    high = (hi - lo) * 2 * (width // 32) + (q[0].shape[0] // 8 if q else 0)
+    kernel = functools.partial(pair_product_kernel, lo, hi, width)
+    return call(kernel, "pair_product", (*p, *f, *q), after, outs=[((4, high, rows), BF16)] * 2)
+
+
+def combine_kernel(at_ref, a_ref, got_a_ref, b_ref, got_b_ref, *outs):
+    high = a_ref.shape[1]
+    for k, out_ref in enumerate(outs):
+        z = jnp.bitwise_xor(at_ref[3], k)
+        out_ref[:high, :] = (a_ref[z].astype(F32) + got_a_ref[z].astype(F32)).astype(BF16)
+        out_ref[high:, :] = (b_ref[z].astype(F32) + got_b_ref[z].astype(F32)).astype(BF16)
+
+
+def combine(at, a, got_a, b, got_b, after):
+    _, high, rows = a.shape
+    outs = [((2 * high, rows), BF16)] * 4
+    return call(combine_kernel, "combine", (at, a, got_a, b, got_b), after, smem=1, outs=outs)
+
+
+def add_lines(refs, sum_ref):
+    total = refs[0][...].astype(F32)
+    for ref in refs[1:]:
+        total += ref[...].astype(F32)
+    sum_ref[...] = total
+
+
+def unpack_down_kernel(i0, i1, i2, i3, down_ref, sum_ref):
+    add_lines((i0, i1, i2, i3), sum_ref)
+    rows, (chunk, width) = i0.shape[1], down_ref.shape
+    count = width // rows
+    padded = i0.shape[0] // count
+    for j in range(count):
+        down_ref[:, j * rows : (j + 1) * rows] = sum_ref[j * padded : j * padded + chunk, :]
+
+
+def unpack_down(v, chunk, width, after):
+    scratch = [pltpu.VMEM(v[0].shape, F32)]
+    return call(unpack_down_kernel, "unpack_down", v, after, outs=[((chunk, width), F32)], scratch=scratch)[0]
+
+
+def unpack_kernel(at_ref, i0, i1, i2, i3, mine_ref, theirs_ref, *rest):
+    out_ref, sum_ref = rest[:-1], rest[-1]
+    add_lines((i0, i1, i2, i3), sum_ref)
+    _, own, wide = mine_ref.shape
+    high, rows = i0.shape[0] // 2, i0.shape[1]
+    dp = at_ref[0]
+    for part in range(2):
+        for t in range(wide // rows):
+            at = part * high + t * 2 * own
+            lanes = slice(t * rows, (t + 1) * rows)
+            mine_ref[part, :, lanes] = sum_ref[pl.ds(pl.multiple_of(at + dp * own, own), own), :]
+            theirs = sum_ref[pl.ds(pl.multiple_of(at + (1 - dp) * own, own), own), :]
+            theirs_ref[part, :, lanes] = theirs.astype(BF16)
+        if out_ref:
+            count = (high - wide // rows * 2 * own) // own
+            for j in range(count):
+                at = part * high + wide // rows * 2 * own + j * own
+                out_ref[0][:, (part * count + j) * rows : (part * count + j + 1) * rows] = sum_ref[at : at + own, :]
+
+
+def unpack(at, v, own, wide, width, after):
+    outs = [((2, own, wide), F32), ((2, own, wide), BF16)] + ([((own, width), F32)] if width else [])
+    scratch = [pltpu.VMEM(v[0].shape, F32)]
+    return call(unpack_kernel, "unpack", (at, *v), after, smem=1, outs=outs, scratch=scratch)
+
+
+def finish_kernel(at_ref, m0, m1, o0, o1, wg_ref, wu_ref, gate_ref, up_ref, dots_ref):
+    dp = at_ref[0]
+    share = gate_ref.shape[1] // 2
+    early = m0.shape[2]
+    for part, ref in enumerate((gate_ref, up_ref)):
+
+        def put(at, a, b):
+            ref[:, at : at + early] = a[part].astype(F32)
+            ref[:, at + early : at + share] = b[part].astype(F32)
+
+        @pl.when(dp == 0)
+        def _():
+            put(0, m0, m1)
+            put(share, o0, o1)
+
+        @pl.when(dp == 1)
+        def _():
+            put(0, o0, o1)
+            put(share, m0, m1)
+
+    total = gate_ref[...] * wg_ref[...].astype(F32) + up_ref[...] * wu_ref[...].astype(F32)
+    dots_ref[...] = jnp.sum(total, axis=1, keepdims=True)
+
+
+def finish(at, place, mine, theirs, wg, wu):
+    own, ff = mine[0].shape[1], wg.shape[1]
+
+    def whole(*shape):
+        return pl.BlockSpec(shape, lambda g, at: (0,) * len(shape))
+
+    weight = pl.BlockSpec((own, ff), lambda g, at: (at[1], 0))
+    where = jnp.stack([at[0], place]).astype(jnp.int32)
+    return pl.pallas_call(
+        finish_kernel,
+        grid_spec=pltpu.PrefetchScalarGridSpec(
+            num_scalar_prefetch=1,
+            grid=(1,),
+            in_specs=[whole(*v.shape) for v in (*mine, *theirs)] + [weight, weight],
+            out_specs=[whole(own, ff), whole(own, ff), whole(own, 1)],
+        ),
+        out_shape=[jax.ShapeDtypeStruct((own, ff), F32)] * 2 + [jax.ShapeDtypeStruct((own, 1), F32)],
+        cost_estimate=COST,
+        name="finish",
+    )(where, *mine, *theirs, in_hbm(wg), in_hbm(wu))
+
+
+def turn_kernel(in_ref, out_ref):
+    for h in range(4):
+        for z in range(4):
+            out_ref[z, h] = in_ref[h, z]
+
+
+def turn(v, after):
+    return call(turn_kernel, "turn", (v,), after, outs=[(v.shape, BF16)])[0]
+
+
+def head_product_kernel(at_ref, n0, n1, n2, n3, in_ref, mine_ref, theirs_ref, acc_ref):
+    half = mine_ref.shape[0]
+    left = jnp.concatenate(
+        [
+            jnp.concatenate([in_ref[h, jnp.bitwise_xor(at_ref[3], k)] for k in range(4)], axis=1)
+            for h in range(4)
+        ],
+        axis=0,
+    )
+    right = jnp.concatenate([r[...] for r in (n0, n1, n2, n3)], axis=0)
+    for at in range(0, acc_ref.shape[0], 256):
+        acc_ref[at : at + 256, :] = dot(left, right[:, at : at + 256], ((1,), (0,))).T
+    dp = at_ref[0]
+    mine_ref[...] = acc_ref[pl.ds(pl.multiple_of(dp * half, half), half), :]
+    theirs_ref[...] = acc_ref[pl.ds(pl.multiple_of((1 - dp) * half, half), half), :].astype(BF16)
+
+
+def head_product(at, n, v, after):
+    width, wide = n[0].shape[1], 4 * v.shape[2]
+    return call(
+        head_product_kernel,
+        "head_product",
+        (at, *n, v),
+        after,
+        smem=1,
+        outs=[((width // 2, wide), F32), ((width // 2, wide), BF16)],
+        scratch=[pltpu.VMEM((width, wide), F32)],
+    )
+
+
+def head_split_kernel(at_ref, mine_ref, got_ref, kx_ref, px_ref, ky_ref, py_ref, acc_ref):
+    half, wide = mine_ref.shape
+    own = half // 16
+    x, y = at_ref[1], at_ref[2]
+    acc_ref[...] = mine_ref[...] + got_ref[...].astype(F32)
+
+    def put(ref, inner, z, xs, ys, lanes):
+        to = (inner * 4 + z) * own
+        at = pl.multiple_of((z * 4 + ys * 2 + xs) * own, own)
+        ref[to : to + own, :] = acc_ref[pl.ds(at, own), lanes].astype(BF16)
+
+    for inner in range(2):
+        for z in range(4):
+            low, high = slice(0, wide // 2), slice(wide // 2, wide)
+            put(kx_ref, inner, z, x, sel(y, inner), low)
+            put(px_ref, inner, z, 1 - x, sel(y, inner), low)
+            put(ky_ref, inner, z, sel(x, inner), y, high)
+            put(py_ref, inner, z, sel(x, inner), 1 - y, high)
+
+
+def head_split(at, mine, got, after):
+    half, wide = mine.shape
+    outs = [((half // 2, wide // 2), BF16)] * 4
+    scratch = [pltpu.VMEM((half, wide), F32)]
+    return call(head_split_kernel, "head_split", (at, mine, got), after, smem=1, outs=outs, scratch=scratch)
+
+
+def head_mid_kernel(kx, gx, ky, gy, same_a, other_a, same_b, other_b):
+    half = kx.shape[0] // 2
+    for k, g, same, other in ((kx, gx, same_a, other_a), (ky, gy, same_b, other_b)):
+        v = (k[...].astype(F32) + g[...].astype(F32)).astype(BF16)
+        same[...] = v[:half]
+        other[...] = v[half:]
+
+
+def head_mid(kx, gx, ky, gy, after):
+    outs = [((kx.shape[0] // 2, kx.shape[1]), BF16)] * 4
+    return call(head_mid_kernel, "head_mid", (kx, gx, ky, gy), after, outs=outs)
+
+
+def head_end_kernel(a, ga, b, gb, out_ref):
+    own = a.shape[0] // 4
+    v = jnp.concatenate(
+        [(r[...].astype(F32) + g[...].astype(F32)).astype(BF16) for r, g in ((a, ga), (b, gb))], axis=1
+    )
+    for z in range(4):
+        out_ref[z] = v[z * own : (z + 1) * own]
+
+
+def head_end(a, ga, b, gb, after):
+    outs = [((4, a.shape[0] // 4, 2 * a.shape[1]), BF16)]
+    return call(head_end_kernel, "head_end", (a, ga, b, gb), after, outs=outs)[0]
+
+
+def latent_back_kernel(
+    back_ref, dres_ref, x_ref, gain_ref, wq_ref, wk_ref, wv_ref, out_ref, left_ref, d_ref, held_ref, sems
+):
+    loads = [pltpu.make_async_copy(w, held_ref.at[t], sems.at[t]) for t, w in enumerate((wq_ref, wk_ref, wv_ref))]
+    for load in loads:
+        load.start()
+    for h in range(HEADS):
+        for t in range(3):
+            left_ref[t, h * HEAD_DIM : (h + 1) * HEAD_DIM, :] = back_ref[h, t * HEAD_DIM : (t + 1) * HEAD_DIM, :]
+    for load in loads:
+        load.wait()
+    for at in range(0, d_ref.shape[1], 256):
+        v = dot(held_ref[0, at : at + 256, :], left_ref[0], ((1,), (0,)))
+        v += dot(held_ref[1, at : at + 256, :], left_ref[1], ((1,), (0,)))
+        v += dot(held_ref[2, at : at + 256, :], left_ref[2], ((1,), (0,)))
+        d_ref[:, at : at + 256] = v.T
+    x = x_ref[...].astype(F32)
+    inv = lax.rsqrt(jnp.mean(x * x, axis=-1, keepdims=True) + EPS)
+    out_ref[...] = (dres_ref[...] + norm_back(d_ref[...], x * inv, inv, gain_ref[...])).astype(BF16)
+
+
+def latent_back(back, dres, x, gain, wq, wk, wv, after):
+    rows, width = x.shape
+    return call(
+        latent_back_kernel,
+        "latent_back",
+        (back, dres, x, gain.reshape(1, width), wq, wk, wv),
+        after,
+        outs=[((rows, width), BF16)],
+        scratch=[
+            pltpu.VMEM((3, width, rows), BF16),
+            pltpu.VMEM((rows, width), F32),
+            pltpu.VMEM((3, width, width), BF16),
+            pltpu.SemaphoreType.DMA((3,)),
+        ],
+        far=3,
+    )[0]
+
+
+def head_rows_kernel(at_ref, in_ref, wq_ref, wk_ref, wv_ref, q_ref, k_ref, v_ref, dots_ref):
+    total = None
+    for t, (w_ref, o_ref) in enumerate(((wq_ref, q_ref), (wk_ref, k_ref), (wv_ref, v_ref))):
+        for h in range(0, HEADS, 2):
+            lanes = [((h + n) % 4 * 3 + t) * HEAD_DIM for n in range(2)]
+            pair = [in_ref[h // 4][:, at : at + HEAD_DIM] for at in lanes]
+            o_ref[:, h * HEAD_DIM : (h + 2) * HEAD_DIM] = jnp.concatenate(pair, axis=1).astype(F32)
+        v = jnp.sum(o_ref[...] * w_ref[...].astype(F32), axis=1, keepdims=True)
+        total = v if total is None else total + v
+    dots_ref[...] = total
+
+
+def head_rows(place, v, wq, wk, wv):
+    own, width = v.shape[1], wq.shape[1]
+    weight = pl.BlockSpec((own, width), lambda g, at: (at[0], 0))
+    out = pl.BlockSpec((own, width), lambda g, at: (0, 0))
+    return pl.pallas_call(
+        head_rows_kernel,
+        grid_spec=pltpu.PrefetchScalarGridSpec(
+            num_scalar_prefetch=1,
+            grid=(1,),
+            in_specs=[pl.BlockSpec(v.shape, lambda g, at: (0, 0, 0)), weight, weight, weight],
+            out_specs=[out, out, out, pl.BlockSpec((own, 1), lambda g, at: (0, 0))],
+        ),
+        out_shape=[jax.ShapeDtypeStruct((own, width), F32)] * 3 + [jax.ShapeDtypeStruct((own, 1), F32)],
+        cost_estimate=COST,
+        name="head_rows",
+    )(place, v, in_hbm(wq), in_hbm(wk), in_hbm(wv))
+
+
+X_PAIRS = [(i, i ^ 1) for i in range(16)]
+Y_PAIRS = [(i, i ^ 2) for i in range(16)]
+
+
+def swap(v):
+    return lax.ppermute(v, "dp", [(0, 1), (1, 0)])
+
+
+def over_x(v):
+    return lax.ppermute(v, "ctx", X_PAIRS)
+
+
+def over_y(v):
+    return lax.ppermute(v, "ctx", Y_PAIRS)
+
+
+def over_z(v, k):
+    return lax.ppermute(v, "ctx", [(i, i ^ (4 * k)) for i in range(16)])
+
+
+Z_LINES = [[i + 4 * z for z in range(4)] for i in range(4)]
+PLANES = [[i + 4 * z for i in range(4)] for z in range(4)]
+
+
+def in_group(v, groups):
+    return lax.all_to_all(v, "ctx", 0, 0, tiled=True, axis_index_groups=groups)
+
+
+def sum_z(v):
+    return (v[0], *(over_z(v[k], k) for k in range(1, 4)))
+
+
+def to_ctx(v):
+    return lax.all_to_all(v, "ctx", 0, 0, tiled=True)
+
+
+def per_device_grid(
+    latent_in,
+    gain_attn,
+    w_query,
+    w_key,
+    w_value,
+    w_out,
+    gain_ffn,
+    w_gate,
+    w_up,
+    w_down,
+    cotangent,
+    seq_lengths,
+    span_order,
+):
+    rows, width = latent_in.shape
+    ff = w_gate.shape[1]
+    half, own = width // 2, width // 32
+    dp, ctx = lax.axis_index("dp"), lax.axis_index("ctx")
+    at = jnp.stack([dp, ctx % 2, (ctx // 2) % 2, ctx // 4]).astype(jnp.int32)
+    scalars = positions(seq_lengths, span_order, rows, ctx * 0)
+
+    dy_mate = swap(cotangent)
+    dy_x = over_x(jnp.concatenate([cotangent[:, :half], dy_mate[:, :half]], axis=0))
+    dy_y = over_y(jnp.concatenate([cotangent[:, half:], dy_mate[:, half:]], axis=0))
+
+    normed, qkv = norm_qkv(latent_in, gain_attn, w_query, w_key, w_value)
+    qkv = to_ctx(qkv)
+
+    out, full, top, inv = attn_fwd(1, scalars, qkv, (dy_x, dy_y))
+    attn_t = to_ctx(out).reshape(width, rows)
+    line = (normed, *(over_z(normed, k) for k in range(1, 4)))
+    resid, normed_two, attn_send = out_norm(at, attn_t, latent_in, gain_ffn, w_out, ())
+    normed_mate = swap(normed_two)
+    attn_mate = swap(attn_send)
+
+    hid, d_own, d_mate, send_x, send_y, left_sx, left_sy, left_x, left_y = ffn(
+        at, normed_two, normed_mate, cotangent, dy_mate, w_gate, w_up, w_down
+    )
+    d_got = swap(d_mate)
+    left_gx, left_gy = over_x(left_sx), over_y(left_sy)
+    f_x, f_y = over_x(send_x), over_y(send_y)
+    dres, dres_low, grad_attn = ffn_back(d_own, d_got, resid, gain_ffn, cotangent, w_out, line[1:])
+    grad_attn = to_ctx(grad_attn.reshape(HEADS, HEAD_DIM, rows))
+    y_own, y_mate = ffn_out(at, hid, w_down, (dres_low,))
+    latents = (resid + y_own + swap(y_mate).astype(F32)).astype(BF16)
+    out_x, out_sx, out_y, out_sy = out_product(at, attn_t, attn_mate, dres_low, swap(dres_low), (y_own,))
+    out_gx, out_gy = over_x(out_sx), over_y(out_sy)
+
+    same_a, other_a = down_product(0, (left_x, left_gx), (cotangent, dy_mate, dy_x), (out_x,))
+    same_b, other_b = down_product(1, (left_y, left_gy), (cotangent, dy_mate, dy_y), (same_a,))
+    sent_a, sent_b = over_y(other_a), over_x(other_b)
+
+    grad_qkv = attn_bwd(
+        1, lambda slot: (slot & 3) * 4 + (slot >> 2), scalars, qkv, grad_attn, full, top, inv, (same_b,)
+    )
+    four = in_group(grad_qkv, PLANES).reshape(4, 4, 3 * HEAD_DIM, rows)
+
+    tiles = send_x.shape[0] // (2 * rows)
+    split = (tiles + 1) // 2
+    early_a, other_a = pair_product(0, split, width, (left_x, left_gx), (send_x, f_x), (), (grad_qkv,))
+    early_b, other_b = pair_product(0, split, width, (left_y, left_gy), (send_y, f_y), (), (early_a,))
+    early_sa, early_sb = over_y(other_a), over_x(other_b)
+    down = combine(at, same_a, sent_a, same_b, sent_b, (early_b,))
+
+    back = in_group(turn(four, (down[0],)), Z_LINES).reshape(16, 3 * HEAD_DIM, rows)
+    late_a, other_a = pair_product(split, tiles, width, (left_x, left_gx), (send_x, f_x), (out_x, out_gx), (four,))
+    late_b, other_b = pair_product(split, tiles, width, (left_y, left_gy), (send_y, f_y), (out_y, out_gy), (late_a,))
+    late_sa, late_sb = over_y(other_a), over_x(other_b)
+    head_mine, head_theirs = head_product(at, line, four, (late_b,))
+    head_x, head_sx, head_y, head_sy = head_split(at, head_mine, swap(head_theirs), (late_b,))
+    early = combine(at, early_a, early_sa, early_b, early_sb, (head_x,))
+    head_a, other_a, head_b, other_b = head_mid(head_x, over_x(head_sx), head_y, over_y(head_sy), (early[0],))
+    late = combine(at, late_a, late_sa, late_b, late_sb, (head_a,))
+    heads = head_end(head_a, over_y(other_a), head_b, over_x(other_b), (late[0],))
+    latent_grad = latent_back(back, dres, latent_in, gain_attn, w_query, w_key, w_value, (heads,))
+    heads = in_group(heads, Z_LINES)
+    place = dp * 16 + ctx
+    down_sum = unpack_down(sum_z(down), ff // 32, width, (latent_grad,))
+    wide = split * rows
+    mine0, theirs0 = unpack(at, sum_z(early), own, wide, 0, (down_sum,))
+    query_sum, key_sum, value_sum, dots = head_rows(place.reshape(1).astype(jnp.int32), heads, w_query, w_key, w_value)
+    mine1, theirs1, out_sum = unpack(at, sum_z(late), own, ff // 2 - wide, width, (mine0, dots))
+    gate_sum, up_sum, ffn_dots = finish(at, place, (mine0, mine1), (swap(theirs0), swap(theirs1)), w_gate, w_up)
+
+    def own_gain(v):
+        return lax.dynamic_slice_in_dim(v, place * own, own, 0)
+
+    gain_attn_sum = dots[:, 0] / own_gain(gain_attn)
+    gain_ffn_sum = ffn_dots[:, 0] / own_gain(gain_ffn)
+    return (
+        latents,
+        latent_grad,
+        gain_attn_sum,
+        query_sum,
+        key_sum,
+        value_sum,
+        out_sum,
+        gain_ffn_sum,
+        gate_sum,
+        up_sum,
+        down_sum,
+    )
+
+
 def solution(mesh):
-    moves = Moves(mesh.shape["dp"], mesh.shape["ctx"])
+    n_dp, n_ctx = mesh.shape["dp"], mesh.shape["ctx"]
+    if n_dp == 2 and n_ctx == 16:
+        body = per_device_grid
+    else:
+        body = functools.partial(per_device_any, Moves(n_dp, n_ctx))
     rows, whole, share = P(("dp", "ctx"), None), P(), P("dp", None)
     flat = P(("dp", "ctx"))
     return jax.shard_map(
-        functools.partial(per_device, moves),
+        body,
         mesh=mesh,
         in_specs=(rows,) + (whole,) * 9 + (rows, share, share),
         out_specs=(rows, rows, flat, rows, rows, rows, rows, flat, rows, rows, rows),

time: 355 us -> 279 us (0.79)
  Pallas kernels: 22.4 us -> 77.2 us
  matrix products: 42.8 us -> 0 us
  starting transfers between devices: 111 us -> 70.5 us
  other arithmetic: 37.7 us -> 5.67 us
  between operations: 15.3 us -> 1.5 us
    pallas_call x2 -> x28, Pallas kernels: 22.4 us -> 77.2 us  [the longest x26 72.6 us: call(): pl.pallas_call(body, in_specs=[SMEM] * smem + [VMEM] * (held - smem - far...]
    ppermute x32 -> x30, starting transfers between devices: 76.8 us -> 33.7 us  [the longest x12 15.7 us: over_z(): return lax.ppermute(v, 'ctx', [(i, i ^ 4 * k) for i in range(16)])]
    dot_general x23 -> x0, matrix products: 42.8 us -> none  [dot(): return lax.dot_general(a, b, (dims, ((), ())), preferred_element_type=F32)]
    unnamed x85 -> x194, local copies, waits for them, and re-layouts: 4.42 us -> 37.8 us
    all_to_all x5 -> x3, waiting for transfers between devices: 30.2 us -> 12 us  [to_ctx(): return lax.all_to_all(v, 'ctx', 0, 0, tiled=True)]
    convert_element_type x21 -> x1, other arithmetic: 17.6 us -> 1.75 us  [per_device_grid(): latents = (resid + y_own + swap(y_mate).astype(F32)).astype(BF16)]
    all_to_all x0 -> x3, starting transfers between devices: none -> 15.3 us  [in_group(): return lax.all_to_all(v, 'ctx', 0, 0, tiled=True, axis_index_groups=groups)]
    ppermute x32 -> x30, waiting for transfers between devices: 51.7 us -> 66.8 us  [the longest x9 35.9 us: over_x(): return lax.ppermute(v, 'ctx', X_PAIRS)]
  transfers between devices with their start and end apart: 47 -> 45, of which waited for: 13 -> 18; matrix products, arithmetic and copies ran while one was open for 29% -> 2% of each run, Pallas kernels for 3% -> 21%
where the time goes in v2:
time: 279 us; the launch traced here: 275 us
  waiting for transfers between devices  82.1 us (29%)
  Pallas kernels  77.2 us (28%)
  starting transfers between devices  70.5 us (25%)
  local copies, waits for them, and re-layouts  37.8 us (14%)
  other arithmetic  5.67 us (2%)
    pallas_call x26, Pallas kernels, call(): pl.pallas_call(body, in_specs=[SMEM] * smem + [VMEM] * (held - smem - far...  72.6 us
    unnamed x194, local copies, waits for them, and re-layouts  37.8 us
    ppermute x9, waiting for transfers between devices, over_x(): return lax.ppermute(v, 'ctx', X_PAIRS)  35.9 us
    ppermute x12, waiting for transfers between devices, over_z(): return lax.ppermute(v, 'ctx', [(i, i ^ 4 * k) for i in range(16)])  27.8 us
    all_to_all x3, starting transfers between devices, to_ctx(): return lax.all_to_all(v, 'ctx', 0, 0, tiled=True)  20.7 us
    ppermute x12, starting transfers between devices, over_z(): return lax.ppermute(v, 'ctx', [(i, i ^ 4 * k) for i in range(16)])  15.7 us
    all_to_all x3, starting transfers between devices, in_group(): return lax.all_to_all(v, 'ctx', 0, 0, tiled=True, axis_index_groups=groups)  15.3 us
    all_to_all x3, waiting for transfers between devices, to_ctx(): return lax.all_to_all(v, 'ctx', 0, 0, tiled=True)  12 us
  transfers between devices with their start and end apart: 45, of which 18 were waited for; matrix products, arithmetic and copies ran while one was open for 2% of the time, Pallas kernels for 21%

profile of v2, /device:TPU:10, one launch (start us, length us, event | category | flops | bytes accessed | tf_op | source)
XLA Modules:
  0.0 274.8 jit_solution(13490472050490442803)
XLA Ops:
  2.3 4.3 %norm_qkv.1 = (bf16[128,1024]{1,0:T(8,128)(2,1)}, bf16[16,192,128]{2,1,0:T(8,128)(2,1)}) custom-call(bf16[128,1024]{1,0:T(8,128)(2,1)S(1)} %copy-done.8, f32[1,1024]{1,0:T(1,128)S(1)} %bitcast.22, bf16[1024,1024]{1,0:T(8,128)(2,1)} %wq_ref.1, bf16[1024,1024]{1,0:T(8,128)(2,1)} %wk_ref.1, bf16[1024,1024]{1,0:T(8,128)(2,1)} %wv_ref.1), custom_call_target="tpu_custom_call" | custom-call | flops 1000000 | bytes 100000 | tf_op jit(solution)/shard_map/norm_qkv/pallas_call | solution.py:169
  6.7 7.2 %all-to-all-start = ((bf16[16,192,128]{2,1,0:T(8,128)(2,1)}), bf16[16,192,128]{2,1,0:T(8,128)(2,1)S(1)}, u32[]{:S(2)}, u32[]{:S(2)}) async-start(bf16[16,192,128]{2,1,0:T(8,128)(2,1)} %get-tuple-element.84), calls=%async_computation | async-start | bytes 1572864 | tf_op jit(solution)/shard_map/all_to_all | solution.py:1027
  16.2 1.5 collective-permute-start.2
  17.9 9.9 %collective-permute-done.1.refs_5_.refs_4_ = bf16[256,512]{1,0:T(8,128)(2,1)S(1)} collective-permute-done((bf16[256,512]{1,0:T(8,128)(2,1)S(1)}, bf16[256,512]{1,0:T(8,128)(2,1)S(1)}, u32[]{:S(2)}, u32[]{:S(2)}) %collective-permute-start.1) | collective-permute-done | bytes 262176 | tf_op jit(solution)/shard_map/ppermute | solution.py:1003
  29.1 3.9 %all-to-all-done.refs_4_ = bf16[16,192,128]{2,1,0:T(8,128)(2,1)S(1)} async-done(((bf16[16,192,128]{2,1,0:T(8,128)(2,1)}), bf16[16,192,128]{2,1,0:T(8,128)(2,1)S(1)}, u32[]{:S(2)}, u32[]{:S(2)}) %all-to-all-start) | async-done | bytes 786464 | tf_op jit(solution)/shard_map/all_to_all | solution.py:1027
  32.9 9.6 %attn_fwd.1 = (bf16[16,64,128]{2,1,0:T(8,128)(2,1)}, f32[16,64,128]{2,1,0:T(8,128)S(1)}, f32[8,1,256]{2,1,0:T(1,128)S(1)}, f32[8,1,256]{2,1,0:T(1,128)S(1)}) custom-call(s32[16]{0:T(128)S(1)} %select_reduce_fusion.refs_0_, s32[8]{0:T(128)S(1)} %and_select_fusion.refs_1_, s32[4]{0:T(128)S(1)} %bitcast.25, s32[1]{0:T(128)} %constant.72.clone.1.refs_3_, ...), custom_call_target="tpu_custom_call" | custom-call | flops 1000000 | bytes 100000 | tf_op jit(solution)/shard_map/attn_fwd/pallas_call | solution.py:169
  43.9 5.6 %all-to-all-start.1 = ((bf16[16,64,128]{2,1,0:T(8,128)(2,1)}), bf16[16,64,128]{2,1,0:T(8,128)(2,1)S(1)}, u32[]{:S(2)}, u32[]{:S(2)}) async-start(bf16[16,64,128]{2,1,0:T(8,128)(2,1)} %get-tuple-element.85), calls=%async_computation.1 | async-start | bytes 524288 | tf_op jit(solution)/shard_map/all_to_all | solution.py:1027
  49.6 8.1 %all-to-all-done.1 = bf16[16,64,128]{2,1,0:T(8,128)(2,1)S(1)} async-done(((bf16[16,64,128]{2,1,0:T(8,128)(2,1)}), bf16[16,64,128]{2,1,0:T(8,128)(2,1)S(1)}, u32[]{:S(2)}, u32[]{:S(2)}) %all-to-all-start.1) | async-done | bytes 262176 | tf_op jit(solution)/shard_map/all_to_all | solution.py:1027
  57.7 2.7 out_norm.1
  61.9 2.8 %collective-permute-start.6 = (bf16[128,1024]{1,0:T(8,128)(2,1)}, bf16[128,1024]{1,0:T(8,128)(2,1)S(1)}, u32[]{:S(2)}, u32[]{:S(2)}) collective-permute-start(bf16[128,1024]{1,0:T(8,128)(2,1)} %get-tuple-element.91.refs_1_), channel_id=1, source_target_pairs={{0,8},{1,9},{2,10},{3,11},{4,12},{5,13},{6,14},{7,15},{8,0},{9,1},... | collective-permute-start | bytes 786440 | tf_op jit(solution)/shard_map/ppermute | solution.py:1011
  64.6 8.8 %ffn.1 = (bf16[256,1408]{1,0:T(8,128)(2,1)S(1)}, f32[128,1024]{1,0:T(8,128)S(1)}, bf16[128,1024]{1,0:T(8,128)(2,1)S(1)}, bf16[2816,128]{1,0:T(8,128)(2,1)S(1)}, ...) custom-call(s32[4]{0:T(128)S(1)} %pad_add_fusion.refs_0_, ...), custom_call_target="tpu_custom_call" | custom-call | flops 1000000 | bytes 100000 | tf_op jit(solution)/shard_map/ffn/pallas_call | solution.py:169
  73.6 1.5 collective-permute-start.10
  75.1 6.6 %collective-permute-done.7.refs_8_.refs_4_ = bf16[128,1024]{1,0:T(8,128)(2,1)S(1)} collective-permute-done((bf16[128,1024]{1,0:T(8,128)(2,1)}, bf16[128,1024]{1,0:T(8,128)(2,1)S(1)}, u32[]{:S(2)}, u32[]{:S(2)}) %collective-permute-start.7) | collective-permute-done | bytes 262176 | tf_op jit(solution)/shard_map/ppermute | solution.py:1011
  82.4 2.9 %collective-permute-done.6.refs_7_.refs_3_ = bf16[128,1024]{1,0:T(8,128)(2,1)S(1)} collective-permute-done((bf16[128,1024]{1,0:T(8,128)(2,1)}, bf16[128,1024]{1,0:T(8,128)(2,1)S(1)}, u32[]{:S(2)}, u32[]{:S(2)}) %collective-permute-start.6) | collective-permute-done | bytes 262176 | tf_op jit(solution)/shard_map/ppermute | solution.py:1011
  85.3 2.5 ffn_back.1
  90.1 7.9 %all-to-all-start.2 = ((bf16[16,64,128]{2,1,0:T(8,128)(2,1)}), bf16[16,64,128]{2,1,0:T(8,128)(2,1)}, u32[]{:S(2)}, u32[]{:S(2)}) async-start(bf16[16,64,128]{2,1,0:T(8,128)(2,1)} %bitcast.19), calls=%async_computation.2 | async-start | bytes 524288 | tf_op jit(solution)/shard_map/all_to_all | solution.py:1027
  100.6 1.5 collective-permute-start.15
  104.1 4.0 %ffn_out.1 = (f32[128,1024]{1,0:T(8,128)S(1)}, bf16[128,1024]{1,0:T(8,128)(2,1)}) custom-call(s32[4]{0:T(128)S(1)} %pad_add_fusion.refs_0_, bf16[256,1408]{1,0:T(8,128)(2,1)S(1)} %copy-done.48, bf16[2816,1024]{1,0:T(8,128)(2,1)} %refs_2_.8, bf16[128,1024]{1,0:T(8,128)(2,1)S(1)} %copy-done.40), custom_call_target="tpu_custom_call" | custom-call | flops 1000000 | bytes 100000 | tf_op jit(solution)/shard_map/ffn_out/pallas_call | solution.py:169
  111.4 1.7 down_product.3
  119.9 10.8 %attn_bwd.1.refs_4_ = bf16[16,192,128]{2,1,0:T(8,128)(2,1)} custom-call(s32[16]{0:T(128)S(1)} %copy-done.76, s32[8]{0:T(128)S(1)} %copy-done.78, s32[4]{0:T(128)S(1)} %bitcast.26, s32[1]{0:T(128)} %constant.72.clone.1.refs_3_, bf16[16,192,128]{2,1,0:T(8,128)(2,1)S(1)} %all-to-all-done.refs_4_, bf16[16,64,128]{2,1,0:T(8,128)(2,1)} %all-to-all-done.2.refs_5_, ...), custom_call_target="tpu_custom_call" | custom-call | flops 1000000 | bytes 100000 | tf_op jit(solution)/shard_map/attn_bwd/pallas_call | solution.py:169
  130.8 4.9 %all-to-all-start.3 = ((bf16[16,192,128]{2,1,0:T(8,128)(2,1)}), bf16[16,192,128]{2,1,0:T(8,128)(2,1)S(1)}, u32[]{:S(2)}, u32[]{:S(2)}) async-start(bf16[16,192,128]{2,1,0:T(8,128)(2,1)} %attn_bwd.1.refs_4_), calls=%async_computation.3 | async-start | bytes 1572864 | tf_op jit(solution)/shard_map/all_to_all | solution.py:1019
  136.0 1.7 collective-permute-start.13
  137.7 1.5 collective-permute-start.18
  140.9 1.7 pair_product.4
  143.3 2.0 pair_product.5
  146.2 8.1 %collective-permute-done.14.refs_4_ = bf16[4,384,128]{2,1,0:T(8,128)(2,1)S(1)} collective-permute-done((bf16[4,384,128]{2,1,0:T(8,128)(2,1)}, bf16[4,384,128]{2,1,0:T(8,128)(2,1)S(1)}, u32[]{:S(2)}, u32[]{:S(2)}) %collective-permute-start.14) | collective-permute-done | bytes 393248 | tf_op jit(solution)/shard_map/ppermute | solution.py:1003
  160.5 5.1 %all-to-all-start.4 = ((bf16[4,4,192,128]{3,2,1,0:T(8,128)(2,1)}), bf16[4,4,192,128]{3,2,1,0:T(8,128)(2,1)}, u32[]{:S(2)}, u32[]{:S(2)}) async-start(bf16[4,4,192,128]{3,2,1,0:T(8,128)(2,1)} %copy-done.1), calls=%async_computation.4 | async-start | bytes 1572864 | tf_op jit(solution)/shard_map/all_to_all | solution.py:1019
  166.8 1.8 pair_product.6
  168.7 2.2 pair_product.7
  170.9 2.5 head_product.1
  174.2 1.5 collective-permute-start.22
  179.1 6.4 %collective-permute-done.23.refs_4_ = bf16[4,384,128]{2,1,0:T(8,128)(2,1)S(1)} collective-permute-done((bf16[4,384,128]{2,1,0:T(8,128)(2,1)S(1)}, bf16[4,384,128]{2,1,0:T(8,128)(2,1)S(1)}, u32[]{:S(2)}, u32[]{:S(2)}) %collective-permute-start.23) | collective-permute-done | bytes 393248 | tf_op jit(solution)/shard_map/ppermute | solution.py:1003
  187.5 11.6 %collective-permute-done.20.refs_1_ = bf16[256,384]{1,0:T(8,128)(2,1)S(1)} collective-permute-done((bf16[256,384]{1,0:T(8,128)(2,1)S(1)}, bf16[256,384]{1,0:T(8,128)(2,1)S(1)}, u32[]{:S(2)}, u32[]{:S(2)}) %collective-permute-start.20) | collective-permute-done | bytes 196640 | tf_op jit(solution)/shard_map/ppermute | solution.py:1003
  200.1 1.5 collective-permute-start.24
  203.7 2.9 %collective-permute-start.35 = (bf16[768,128]{1,0:T(8,128)(2,1)}, bf16[768,128]{1,0:T(8,128)(2,1)}, u32[]{:S(2)}, u32[]{:S(2)}) collective-permute-start(bf16[768,128]{1,0:T(8,128)(2,1)} %get-tuple-element.147), channel_id=1, source_target_pairs={{0,8},{1,9},{2,10},{3,11},{4,12},{5,13},{6,14},{7,15},{8,0},{9,1},... | collective-permute-start | bytes 589832 | tf_op jit(solution)/shard_map/ppermute | solution.py:1011
  218.2 5.2 %all-to-all-start.5 = ((bf16[4,32,768]{2,1,0:T(8,128)(2,1)}), bf16[4,32,768]{2,1,0:T(8,128)(2,1)}, u32[]{:S(2)}, u32[]{:S(2)}) async-start(bf16[4,32,768]{2,1,0:T(8,128)(2,1)} %head_end.1.refs_7_), calls=%async_computation.5 | async-start | bytes 393216 | tf_op jit(solution)/shard_map/all_to_all | solution.py:1019
  223.9 2.4 collective-permute-start.32
  226.3 2.0 collective-permute-start.28
  228.3 6.0 %collective-permute-done.36.refs_3_ = bf16[768,128]{1,0:T(8,128)(2,1)} collective-permute-done((bf16[768,128]{1,0:T(8,128)(2,1)}, bf16[768,128]{1,0:T(8,128)(2,1)}, u32[]{:S(2)}, u32[]{:S(2)}) %collective-permute-start.36) | collective-permute-done | bytes 196640 | tf_op jit(solution)/shard_map/ppermute | solution.py:1011
  234.3 3.0 %collective-permute-start.30 = (bf16[896,128]{1,0:T(8,128)(2,1)}, bf16[896,128]{1,0:T(8,128)(2,1)S(1)}, u32[]{:S(2)}, u32[]{:S(2)}) collective-permute-start(bf16[896,128]{1,0:T(8,128)(2,1)} %copy-done.87), channel_id=1, source_target_pairs={{0,12},{1,13},{2,14},{3,15},{4,8},{5,9},{6,10},{7,11},{8,4},{9,5},... | collective-permute-start | bytes 688136 | tf_op jit(solution)/shard_map/ppermute | solution.py:1011
  237.3 1.7 add_convert_fusion
  239.1 6.8 %latent_back.1.refs_4_ = bf16[128,1024]{1,0:T(8,128)(2,1)} custom-call(bf16[16,192,128]{2,1,0:T(8,128)(2,1)} %bitcast.12.refs_0_, f32[128,1024]{1,0:T(8,128)S(1)} %copy-done.52, bf16[128,1024]{1,0:T(8,128)(2,1)S(1)} %copy-done.10, f32[1,1024]{1,0:T(1,128)S(1)} %bitcast.23, bf16[1024,1024]{1,0:T(8,128)(2,1)} %wq_ref.1, bf16[1024,1024]{1,0:T(8,128)(2,1)} %wk_ref.1, ...), custom_call_target="tpu_custom_call" | custom-call | flops 1000000 | bytes 100000 | tf_op jit(solution)/shard_map/latent_back/pallas_call | solution.py:169
  246.8 1.8 unpack_down.1.refs_5_
  248.6 3.0 %collective-permute-done.32.refs_3_ = bf16[768,128]{1,0:T(8,128)(2,1)S(1)} collective-permute-done((bf16[768,128]{1,0:T(8,128)(2,1)}, bf16[768,128]{1,0:T(8,128)(2,1)S(1)}, u32[]{:S(2)}, u32[]{:S(2)}) %collective-permute-start.32) | collective-permute-done | bytes 196640 | tf_op jit(solution)/shard_map/ppermute | solution.py:1011
  251.6 5.4 %collective-permute-done.33.refs_4_ = bf16[768,128]{1,0:T(8,128)(2,1)S(1)} collective-permute-done((bf16[768,128]{1,0:T(8,128)(2,1)}, bf16[768,128]{1,0:T(8,128)(2,1)S(1)}, u32[]{:S(2)}, u32[]{:S(2)}) %collective-permute-start.33) | collective-permute-done | bytes 196640 | tf_op jit(solution)/shard_map/ppermute | solution.py:1011
  259.2 1.8 head_rows.1
  261.9 4.0 %collective-permute-done.30.refs_4_ = bf16[896,128]{1,0:T(8,128)(2,1)S(1)} collective-permute-done((bf16[896,128]{1,0:T(8,128)(2,1)}, bf16[896,128]{1,0:T(8,128)(2,1)S(1)}, u32[]{:S(2)}, u32[]{:S(2)}) %collective-permute-start.30) | collective-permute-done | bytes 229408 | tf_op jit(solution)/shard_map/ppermute | solution.py:1011
  270.5 2.8 %finish.1 = (f32[32,2816]{1,0:T(8,128)}, f32[32,2816]{1,0:T(8,128)}, f32[32,1]{1,0:T(8,128)}) custom-call(s32[2]{0:T(128)} %pad_add_fusion.1.at_ref, f32[2,32,768]{2,1,0:T(8,128)} %copy-done.46, f32[2,32,640]{2,1,0:T(8,128)} %copy-done.60, bf16[2,32,768]{2,1,0:T(8,128)(2,1)} %copy-done.93, bf16[2,32,640]{2,1,0:T(8,128)(2,1)} %copy-done.94, ...), custom_call_target="tpu_custom_call" | custom-call | flops 1000000 | bytes 100000 | tf_op jit(solution)/shard_map/finish/pallas_call | solution.py:817
  (280 shorter events, 68.3 us)
Async XLA Ops:
  6.7 26.3 %all-to-all-start = ((bf16[16,192,128]{2,1,0:T(8,128)(2,1)}), bf16[16,192,128]{2,1,0:T(8,128)(2,1)S(1)}, u32[]{:S(2)}, u32[]{:S(2)}) async-start(bf16[16,192,128]{2,1,0:T(8,128)(2,1)} %get-tuple-element.84), calls=%async_computation | async-start | bytes 1572864 | tf_op jit(solution)/shard_map/all_to_all | solution.py:1027
  13.9 1.6 collective-permute-start
  14.2 46.3 %copy-start.73 = (s32[4,1]{0,1:T(1,128)}, s32[4,1]{0,1:T(1,128)S(1)}, u32[]{:S(2)}) copy-start(s32[4,1]{0,1:T(1,128)S(1)} %reduce-window.8) | copy-start | bytes 52
  15.5 12.2 %collective-permute-start.1 = (bf16[256,512]{1,0:T(8,128)(2,1)S(1)}, bf16[256,512]{1,0:T(8,128)(2,1)S(1)}, u32[]{:S(2)}, u32[]{:S(2)}) collective-permute-start(bf16[256,512]{1,0:T(8,128)(2,1)S(1)} %pad_maximum_fusion), channel_id=1, source_target_pairs={{0,1},{1,0},{2,3},{3,2},{4,5},{5,4},{6,7},{7,6},{8,9},{9,8},{10,11... | collective-permute-start | bytes 786440 | tf_op jit(solution)/shard_map/ppermute | solution.py:1003
  16.2 12.9 %collective-permute-start.2 = (bf16[256,512]{1,0:T(8,128)(2,1)S(1)}, bf16[256,512]{1,0:T(8,128)(2,1)S(1)}, u32[]{:S(2)}, u32[]{:S(2)}) collective-permute-start(bf16[256,512]{1,0:T(8,128)(2,1)S(1)} %pad_maximum_fusion.1), channel_id=1, source_target_pairs={{0,2},{1,3},{2,0},{3,1},{4,6},{5,7},{6,4},{7,5},{8,10},{9,11},{10,... | collective-permute-start | bytes 786440 | tf_op jit(solution)/shard_map/ppermute | solution.py:1007
  43.9 13.8 %all-to-all-start.1 = ((bf16[16,64,128]{2,1,0:T(8,128)(2,1)}), bf16[16,64,128]{2,1,0:T(8,128)(2,1)S(1)}, u32[]{:S(2)}, u32[]{:S(2)}) async-start(bf16[16,64,128]{2,1,0:T(8,128)(2,1)} %get-tuple-element.85), calls=%async_computation.1 | async-start | bytes 524288 | tf_op jit(solution)/shard_map/all_to_all | solution.py:1027
  61.1 3.5 %collective-permute-start.3 = (bf16[128,1024]{1,0:T(8,128)(2,1)S(1)}, bf16[128,1024]{1,0:T(8,128)(2,1)S(1)}, u32[]{:S(2)}, u32[]{:S(2)}) collective-permute-start(bf16[128,1024]{1,0:T(8,128)(2,1)S(1)} %get-tuple-element.87.refs_1_), channel_id=1, source_target_pairs={{0,16},{16,0},{1,17},{17,1},{2,18},{18,2},{3,19},{19,3},{4,20},{20... | collective-permute-start | bytes 786440 | tf_op jit(solution)/shard_map/ppermute | solution.py:999
  61.1 20.5 %collective-permute-start.7 = (bf16[128,1024]{1,0:T(8,128)(2,1)}, bf16[128,1024]{1,0:T(8,128)(2,1)S(1)}, u32[]{:S(2)}, u32[]{:S(2)}) collective-permute-start(bf16[128,1024]{1,0:T(8,128)(2,1)} %get-tuple-element.91.refs_1_), channel_id=1, source_target_pairs={{0,12},{1,13},{2,14},{3,15},{4,8},{5,9},{6,10},{7,11},{8,4},{9,5},... | collective-permute-start | bytes 786440 | tf_op jit(solution)/shard_map/ppermute | solution.py:1011
  61.9 23.4 %collective-permute-start.6 = (bf16[128,1024]{1,0:T(8,128)(2,1)}, bf16[128,1024]{1,0:T(8,128)(2,1)S(1)}, u32[]{:S(2)}, u32[]{:S(2)}) collective-permute-start(bf16[128,1024]{1,0:T(8,128)(2,1)} %get-tuple-element.91.refs_1_), channel_id=1, source_target_pairs={{0,8},{1,9},{2,10},{3,11},{4,12},{5,13},{6,14},{7,15},{8,0},{9,1},... | collective-permute-start | bytes 786440 | tf_op jit(solution)/shard_map/ppermute | solution.py:1011
  64.6 20.6 %collective-permute-start.5 = (bf16[128,1024]{1,0:T(8,128)(2,1)}, bf16[128,1024]{1,0:T(8,128)(2,1)S(1)}, u32[]{:S(2)}, u32[]{:S(2)}) collective-permute-start(bf16[128,1024]{1,0:T(8,128)(2,1)} %get-tuple-element.91.refs_1_), channel_id=1, source_target_pairs={{0,4},{1,5},{2,6},{3,7},{4,0},{5,1},{6,2},{7,3},{8,12},{9,13},{10,... | collective-permute-start | bytes 786440 | tf_op jit(solution)/shard_map/ppermute | solution.py:1011
  73.5 11.8 %collective-permute-start.4 = (bf16[128,1024]{1,0:T(8,128)(2,1)S(1)}, bf16[128,1024]{1,0:T(8,128)(2,1)S(1)}, u32[]{:S(2)}, u32[]{:S(2)}) collective-permute-start(bf16[128,1024]{1,0:T(8,128)(2,1)S(1)} %get-tuple-element.90), channel_id=1, source_target_pairs={{0,16},{16,0},{1,17},{17,1},{2,18},{18,2},{3,19},{19,3},{4,20},{20... | collective-permute-start | bytes 786440 | tf_op jit(solution)/shard_map/ppermute | solution.py:999
  73.6 36.4 %collective-permute-start.10 = (bf16[2560,128]{1,0:T(8,128)(2,1)}, bf16[2560,128]{1,0:T(8,128)(2,1)S(1)}, u32[]{:S(2)}, u32[]{:S(2)}) collective-permute-start(bf16[2560,128]{1,0:T(8,128)(2,1)} %get-tuple-element.102), channel_id=1, source_target_pairs={{0,1},{1,0},{2,3},{3,2},{4,5},{5,4},{6,7},{7,6},{8,9},{9,8},{10,11... | collective-permute-start | bytes 1966088 | tf_op jit(solution)/shard_map/ppermute | solution.py:1003
  81.7 29.7 %collective-permute-start.9 = (bf16[2560,128]{1,0:T(8,128)(2,1)}, bf16[2560,128]{1,0:T(8,128)(2,1)}, u32[]{:S(2)}, u32[]{:S(2)}) collective-permute-start(bf16[2560,128]{1,0:T(8,128)(2,1)} %get-tuple-element.100), channel_id=1, source_target_pairs={{0,2},{1,3},{2,0},{3,1},{4,6},{5,7},{6,4},{7,5},{8,10},{9,11},{10,... | collective-permute-start | bytes 1966088 | tf_op jit(solution)/shard_map/ppermute | solution.py:1007
  90.1 25.2 %all-to-all-start.2 = ((bf16[16,64,128]{2,1,0:T(8,128)(2,1)}), bf16[16,64,128]{2,1,0:T(8,128)(2,1)}, u32[]{:S(2)}, u32[]{:S(2)}) async-start(bf16[16,64,128]{2,1,0:T(8,128)(2,1)} %bitcast.19), calls=%async_computation.2 | async-start | bytes 524288 | tf_op jit(solution)/shard_map/all_to_all | solution.py:1027
  98.1 41.1 %collective-permute-start.16 = (bf16[2816,128]{1,0:T(8,128)(2,1)}, bf16[2816,128]{1,0:T(8,128)(2,1)}, u32[]{:S(2)}, u32[]{:S(2)}) collective-permute-start(bf16[2816,128]{1,0:T(8,128)(2,1)} %copy-done.5), channel_id=1, source_target_pairs={{0,1},{1,0},{2,3},{3,2},{4,5},{5,4},{6,7},{7,6},{8,9},{9,8},{10,11... | collective-permute-start | bytes 2162696 | tf_op jit(solution)/shard_map/ppermute | solution.py:1003
  98.6 9.6 %collective-permute-start.12 = (bf16[128,1024]{1,0:T(8,128)(2,1)}, bf16[128,1024]{1,0:T(8,128)(2,1)S(1)}, u32[]{:S(2)}, u32[]{:S(2)}) collective-permute-start(bf16[128,1024]{1,0:T(8,128)(2,1)} %copy-done.39), channel_id=1, source_target_pairs={{0,16},{16,0},{1,17},{17,1},{2,18},{18,2},{3,19},{19,3},{4,20},{20... | collective-permute-start | bytes 786440 | tf_op jit(solution)/shard_map/ppermute | solution.py:999
  98.6 1.9 collective-permute-start.11
  100.6 42.7 %collective-permute-start.15 = (bf16[2816,128]{1,0:T(8,128)(2,1)}, bf16[2816,128]{1,0:T(8,128)(2,1)}, u32[]{:S(2)}, u32[]{:S(2)}) collective-permute-start(bf16[2816,128]{1,0:T(8,128)(2,1)} %copy-done.2), channel_id=1, source_target_pairs={{0,2},{1,3},{2,0},{3,1},{4,6},{5,7},{6,4},{7,5},{8,10},{9,11},{10,... | collective-permute-start | bytes 2162696 | tf_op jit(solution)/shard_map/ppermute | solution.py:1007
  130.8 27.8 %all-to-all-start.3 = ((bf16[16,192,128]{2,1,0:T(8,128)(2,1)}), bf16[16,192,128]{2,1,0:T(8,128)(2,1)S(1)}, u32[]{:S(2)}, u32[]{:S(2)}) async-start(bf16[16,192,128]{2,1,0:T(8,128)(2,1)} %attn_bwd.1.refs_4_), calls=%async_computation.3 | async-start | bytes 1572864 | tf_op jit(solution)/shard_map/all_to_all | solution.py:1019
  135.7 18.5 %collective-permute-start.14 = (bf16[4,384,128]{2,1,0:T(8,128)(2,1)}, bf16[4,384,128]{2,1,0:T(8,128)(2,1)S(1)}, u32[]{:S(2)}, u32[]{:S(2)}) collective-permute-start(bf16[4,384,128]{2,1,0:T(8,128)(2,1)} %copy-done.84), channel_id=1, source_target_pairs={{0,1},{1,0},{2,3},{3,2},{4,5},{5,4},{6,7},{7,6},{8,9},{9,8},{10,11... | collective-permute-start | bytes 1179656 | tf_op jit(solution)/shard_map/ppermute | solution.py:1003
  136.0 19.6 %collective-permute-start.13 = (bf16[4,384,128]{2,1,0:T(8,128)(2,1)}, bf16[4,384,128]{2,1,0:T(8,128)(2,1)S(1)}, u32[]{:S(2)}, u32[]{:S(2)}) collective-permute-start(bf16[4,384,128]{2,1,0:T(8,128)(2,1)} %copy-done.83), channel_id=1, source_target_pairs={{0,2},{1,3},{2,0},{3,1},{4,6},{5,7},{6,4},{7,5},{8,10},{9,11},{10,... | collective-permute-start | bytes 1179656 | tf_op jit(solution)/shard_map/ppermute | solution.py:1007
  137.7 27.9 %collective-permute-start.18 = (bf16[1024,128]{1,0:T(8,128)(2,1)}, bf16[1024,128]{1,0:T(8,128)(2,1)}, u32[]{:S(2)}, u32[]{:S(2)}) collective-permute-start(bf16[1024,128]{1,0:T(8,128)(2,1)} %copy-done.86), channel_id=1, source_target_pairs={{0,1},{1,0},{2,3},{3,2},{4,5},{5,4},{6,7},{7,6},{8,9},{9,8},{10,11... | collective-permute-start | bytes 786440 | tf_op jit(solution)/shard_map/ppermute | solution.py:1003
  139.2 29.5 %collective-permute-start.17 = (bf16[1024,128]{1,0:T(8,128)(2,1)}, bf16[1024,128]{1,0:T(8,128)(2,1)}, u32[]{:S(2)}, u32[]{:S(2)}) collective-permute-start(bf16[1024,128]{1,0:T(8,128)(2,1)} %copy-done.85), channel_id=1, source_target_pairs={{0,2},{1,3},{2,0},{3,1},{4,6},{5,7},{6,4},{7,5},{8,10},{9,11},{10,... | collective-permute-start | bytes 786440 | tf_op jit(solution)/shard_map/ppermute | solution.py:1007
  160.5 57.7 %all-to-all-start.4 = ((bf16[4,4,192,128]{3,2,1,0:T(8,128)(2,1)}), bf16[4,4,192,128]{3,2,1,0:T(8,128)(2,1)}, u32[]{:S(2)}, u32[]{:S(2)}) async-start(bf16[4,4,192,128]{3,2,1,0:T(8,128)(2,1)} %copy-done.1), calls=%async_computation.4 | async-start | bytes 1572864 | tf_op jit(solution)/shard_map/all_to_all | solution.py:1019
  173.4 4.2 %collective-permute-start.19 = (bf16[512,768]{1,0:T(8,128)(2,1)S(1)}, bf16[512,768]{1,0:T(8,128)(2,1)S(1)}, u32[]{:S(2)}, u32[]{:S(2)}) collective-permute-start(bf16[512,768]{1,0:T(8,128)(2,1)S(1)} %get-tuple-element.121), channel_id=1, source_target_pairs={{0,16},{16,0},{1,17},{17,1},{2,18},{18,2},{3,19},{19,3},{4,20},{20... | collective-permute-start | bytes 2359304 | tf_op jit(solution)/shard_map/ppermute | solution.py:999
  173.5 12.0 %collective-permute-start.23 = (bf16[4,384,128]{2,1,0:T(8,128)(2,1)S(1)}, bf16[4,384,128]{2,1,0:T(8,128)(2,1)S(1)}, u32[]{:S(2)}, u32[]{:S(2)}) collective-permute-start(bf16[4,384,128]{2,1,0:T(8,128)(2,1)S(1)} %copy-done.82), channel_id=1, source_target_pairs={{0,1},{1,0},{2,3},{3,2},{4,5},{5,4},{6,7},{7,6},{8,9},{9,8},{10,11... | collective-permute-start | bytes 1179656 | tf_op jit(solution)/shard_map/ppermute | solution.py:1003
  174.2 12.0 %collective-permute-start.22 = (bf16[4,384,128]{2,1,0:T(8,128)(2,1)S(1)}, bf16[4,384,128]{2,1,0:T(8,128)(2,1)S(1)}, u32[]{:S(2)}, u32[]{:S(2)}) collective-permute-start(bf16[4,384,128]{2,1,0:T(8,128)(2,1)S(1)} %copy-done.80), channel_id=1, source_target_pairs={{0,2},{1,3},{2,0},{3,1},{4,6},{5,7},{6,4},{7,5},{8,10},{9,11},{10,... | collective-permute-start | bytes 1179656 | tf_op jit(solution)/shard_map/ppermute | solution.py:1007
  175.6 26.5 %collective-permute-start.27 = (bf16[4,448,128]{2,1,0:T(8,128)(2,1)S(1)}, bf16[4,448,128]{2,1,0:T(8,128)(2,1)S(1)}, u32[]{:S(2)}, u32[]{:S(2)}) collective-permute-start(bf16[4,448,128]{2,1,0:T(8,128)(2,1)S(1)} %get-tuple-element.134), channel_id=1, source_target_pairs={{0,1},{1,0},{2,3},{3,2},{4,5},{5,4},{6,7},{7,6},{8,9},{9,8},{10,11... | collective-permute-start | bytes 1376264 | tf_op jit(solution)/shard_map/ppermute | solution.py:1003
  176.2 26.8 %collective-permute-start.26 = (bf16[4,448,128]{2,1,0:T(8,128)(2,1)S(1)}, bf16[4,448,128]{2,1,0:T(8,128)(2,1)S(1)}, u32[]{:S(2)}, u32[]{:S(2)}) collective-permute-start(bf16[4,448,128]{2,1,0:T(8,128)(2,1)S(1)} %get-tuple-element.133), channel_id=1, source_target_pairs={{0,2},{1,3},{2,0},{3,1},{4,6},{5,7},{6,4},{7,5},{8,10},{9,11},{10,... | collective-permute-start | bytes 1376264 | tf_op jit(solution)/shard_map/ppermute | solution.py:1007
  178.4 20.6 %collective-permute-start.20 = (bf16[256,384]{1,0:T(8,128)(2,1)S(1)}, bf16[256,384]{1,0:T(8,128)(2,1)S(1)}, u32[]{:S(2)}, u32[]{:S(2)}) collective-permute-start(bf16[256,384]{1,0:T(8,128)(2,1)S(1)} %get-tuple-element.123), channel_id=1, source_target_pairs={{0,1},{1,0},{2,3},{3,2},{4,5},{5,4},{6,7},{7,6},{8,9},{9,8},{10,11... | collective-permute-start | bytes 589832 | tf_op jit(solution)/shard_map/ppermute | solution.py:1003
  185.5 13.9 %collective-permute-start.21 = (bf16[256,384]{1,0:T(8,128)(2,1)S(1)}, bf16[256,384]{1,0:T(8,128)(2,1)S(1)}, u32[]{:S(2)}, u32[]{:S(2)}) collective-permute-start(bf16[256,384]{1,0:T(8,128)(2,1)S(1)} %get-tuple-element.125), channel_id=1, source_target_pairs={{0,2},{1,3},{2,0},{3,1},{4,6},{5,7},{6,4},{7,5},{8,10},{9,11},{10,... | collective-permute-start | bytes 589832 | tf_op jit(solution)/shard_map/ppermute | solution.py:1007
  187.5 49.8 %copy-start.12 = (f32[128,1024]{1,0:T(8,128)S(1)}, f32[128,1024]{1,0:T(8,128)}, u32[]{:S(2)}) copy-start(f32[128,1024]{1,0:T(8,128)} %copy-done.11) | copy-start | bytes 1572868
  187.5 49.8 %copy-start.14 = (f32[128,1024]{1,0:T(8,128)S(1)}, f32[128,1024]{1,0:T(8,128)}, u32[]{:S(2)}) copy-start(f32[128,1024]{1,0:T(8,128)} %copy-done.13) | copy-start | bytes 1572868
  200.1 6.5 %collective-permute-start.24 = (bf16[128,384]{1,0:T(8,128)(2,1)S(1)}, bf16[128,384]{1,0:T(8,128)(2,1)S(1)}, u32[]{:S(2)}, u32[]{:S(2)}) collective-permute-start(bf16[128,384]{1,0:T(8,128)(2,1)S(1)} %get-tuple-element.130), channel_id=1, source_target_pairs={{0,2},{1,3},{2,0},{3,1},{4,6},{5,7},{6,4},{7,5},{8,10},{9,11},{10,... | collective-permute-start | bytes 294920 | tf_op jit(solution)/shard_map/ppermute | solution.py:1007
  201.6 6.3 %collective-permute-start.25 = (bf16[128,384]{1,0:T(8,128)(2,1)S(1)}, bf16[128,384]{1,0:T(8,128)(2,1)S(1)}, u32[]{:S(2)}, u32[]{:S(2)}) collective-permute-start(bf16[128,384]{1,0:T(8,128)(2,1)S(1)} %get-tuple-element.132), channel_id=1, source_target_pairs={{0,1},{1,0},{2,3},{3,2},{4,5},{5,4},{6,7},{7,6},{8,9},{9,8},{10,11... | collective-permute-start | bytes 294920 | tf_op jit(solution)/shard_map/ppermute | solution.py:1003
  202.2 21.8 %collective-permute-start.8 = (bf16[128,1024]{1,0:T(8,128)(2,1)}, bf16[128,1024]{1,0:T(8,128)(2,1)}, u32[]{:S(2)}, u32[]{:S(2)}) collective-permute-start(bf16[128,1024]{1,0:T(8,128)(2,1)} %get-tuple-element.94), channel_id=1, source_target_pairs={{0,16},{16,0},{1,17},{17,1},{2,18},{18,2},{3,19},{19,3},{4,20},{20... | collective-permute-start | bytes 786440 | tf_op jit(solution)/shard_map/ppermute | solution.py:999
  203.0 23.3 %collective-permute-start.34 = (bf16[768,128]{1,0:T(8,128)(2,1)}, bf16[768,128]{1,0:T(8,128)(2,1)S(1)}, u32[]{:S(2)}, u32[]{:S(2)}) collective-permute-start(bf16[768,128]{1,0:T(8,128)(2,1)} %get-tuple-element.146), channel_id=1, source_target_pairs={{0,4},{1,5},{2,6},{3,7},{4,0},{5,1},{6,2},{7,3},{8,12},{9,13},{10,... | collective-permute-start | bytes 589832 | tf_op jit(solution)/shard_map/ppermute | solution.py:1011
  203.7 22.6 %collective-permute-start.35 = (bf16[768,128]{1,0:T(8,128)(2,1)}, bf16[768,128]{1,0:T(8,128)(2,1)}, u32[]{:S(2)}, u32[]{:S(2)}) collective-permute-start(bf16[768,128]{1,0:T(8,128)(2,1)} %get-tuple-element.147), channel_id=1, source_target_pairs={{0,8},{1,9},{2,10},{3,11},{4,12},{5,13},{6,14},{7,15},{8,0},{9,1},... | collective-permute-start | bytes 589832 | tf_op jit(solution)/shard_map/ppermute | solution.py:1011
  207.3 27.0 %collective-permute-start.36 = (bf16[768,128]{1,0:T(8,128)(2,1)}, bf16[768,128]{1,0:T(8,128)(2,1)}, u32[]{:S(2)}, u32[]{:S(2)}) collective-permute-start(bf16[768,128]{1,0:T(8,128)(2,1)} %get-tuple-element.148), channel_id=1, source_target_pairs={{0,12},{1,13},{2,14},{3,15},{4,8},{5,9},{6,10},{7,11},{8,4},{9,5},... | collective-permute-start | bytes 589832 | tf_op jit(solution)/shard_map/ppermute | solution.py:1011
  208.5 25.8 %collective-permute-start.31 = (bf16[768,128]{1,0:T(8,128)(2,1)}, bf16[768,128]{1,0:T(8,128)(2,1)}, u32[]{:S(2)}, u32[]{:S(2)}) collective-permute-start(bf16[768,128]{1,0:T(8,128)(2,1)} %get-tuple-element.143), channel_id=1, source_target_pairs={{0,4},{1,5},{2,6},{3,7},{4,0},{5,1},{6,2},{7,3},{8,12},{9,13},{10,... | collective-permute-start | bytes 589832 | tf_op jit(solution)/shard_map/ppermute | solution.py:1011
  218.2 41.0 %all-to-all-start.5 = ((bf16[4,32,768]{2,1,0:T(8,128)(2,1)}), bf16[4,32,768]{2,1,0:T(8,128)(2,1)}, u32[]{:S(2)}, u32[]{:S(2)}) async-start(bf16[4,32,768]{2,1,0:T(8,128)(2,1)} %head_end.1.refs_7_), calls=%async_computation.5 | async-start | bytes 393216 | tf_op jit(solution)/shard_map/all_to_all | solution.py:1019
  223.9 27.7 %collective-permute-start.32 = (bf16[768,128]{1,0:T(8,128)(2,1)}, bf16[768,128]{1,0:T(8,128)(2,1)S(1)}, u32[]{:S(2)}, u32[]{:S(2)}) collective-permute-start(bf16[768,128]{1,0:T(8,128)(2,1)} %copy-done.91), channel_id=1, source_target_pairs={{0,8},{1,9},{2,10},{3,11},{4,12},{5,13},{6,14},{7,15},{8,0},{9,1},... | collective-permute-start | bytes 589832 | tf_op jit(solution)/shard_map/ppermute | solution.py:1011
  226.3 30.7 %collective-permute-start.33 = (bf16[768,128]{1,0:T(8,128)(2,1)}, bf16[768,128]{1,0:T(8,128)(2,1)S(1)}, u32[]{:S(2)}, u32[]{:S(2)}) collective-permute-start(bf16[768,128]{1,0:T(8,128)(2,1)} %copy-done.90), channel_id=1, source_target_pairs={{0,12},{1,13},{2,14},{3,15},{4,8},{5,9},{6,10},{7,11},{8,4},{9,5},... | collective-permute-start | bytes 589832 | tf_op jit(solution)/shard_map/ppermute | solution.py:1011
  226.3 35.5 %collective-permute-start.28 = (bf16[896,128]{1,0:T(8,128)(2,1)}, bf16[896,128]{1,0:T(8,128)(2,1)S(1)}, u32[]{:S(2)}, u32[]{:S(2)}) collective-permute-start(bf16[896,128]{1,0:T(8,128)(2,1)} %copy-done.89), channel_id=1, source_target_pairs={{0,4},{1,5},{2,6},{3,7},{4,0},{5,1},{6,2},{7,3},{8,12},{9,13},{10,... | collective-permute-start | bytes 688136 | tf_op jit(solution)/shard_map/ppermute | solution.py:1011
  234.3 27.5 %collective-permute-start.29 = (bf16[896,128]{1,0:T(8,128)(2,1)}, bf16[896,128]{1,0:T(8,128)(2,1)S(1)}, u32[]{:S(2)}, u32[]{:S(2)}) collective-permute-start(bf16[896,128]{1,0:T(8,128)(2,1)} %copy-done.88), channel_id=1, source_target_pairs={{0,8},{1,9},{2,10},{3,11},{4,12},{5,13},{6,14},{7,15},{8,0},{9,1},... | collective-permute-start | bytes 688136 | tf_op jit(solution)/shard_map/ppermute | solution.py:1011
  234.3 31.6 %collective-permute-start.30 = (bf16[896,128]{1,0:T(8,128)(2,1)}, bf16[896,128]{1,0:T(8,128)(2,1)S(1)}, u32[]{:S(2)}, u32[]{:S(2)}) collective-permute-start(bf16[896,128]{1,0:T(8,128)(2,1)} %copy-done.87), channel_id=1, source_target_pairs={{0,12},{1,13},{2,14},{3,15},{4,8},{5,9},{6,10},{7,11},{8,4},{9,5},... | collective-permute-start | bytes 688136 | tf_op jit(solution)/shard_map/ppermute | solution.py:1011
  259.1 10.1 %collective-permute-start.37 = (bf16[2,32,768]{2,1,0:T(8,128)(2,1)S(1)}, bf16[2,32,768]{2,1,0:T(8,128)(2,1)S(1)}, u32[]{:S(2)}, u32[]{:S(2)}) collective-permute-start(bf16[2,32,768]{2,1,0:T(8,128)(2,1)S(1)} %get-tuple-element.152), channel_id=1, source_target_pairs={{0,16},{16,0},{1,17},{17,1},{2,18},{18,2},{3,19},{19,3},{4,20},{20... | collective-permute-start | bytes 294920 | tf_op jit(solution)/shard_map/ppermute | solution.py:999
  268.6 1.3 collective-permute-start.38
  (94 other events, 684.7 us)

commit v3 on v2

--- a/solution.py
+++ b/solution.py
@@ -176,6 +176,18 @@
         compiler_params=pltpu.CompilerParams(vmem_limit_bytes=vmem * 2**20),
         name=name,
     )(*args, *after)
+
+
+def order(v, after):
+    return pl.pallas_call(
+        lambda *refs: None,
+        in_specs=[ANY] * (1 + len(after)),
+        out_specs=ANY,
+        out_shape=jax.ShapeDtypeStruct(v.shape, v.dtype),
+        input_output_aliases={0: 0},
+        cost_estimate=COST,
+        name="order",
+    )(v, *after)
 
 
 COST = pl.CostEstimate(flops=10**6, bytes_accessed=10**5, transcendentals=0)
@@ -439,13 +451,12 @@
     n_ref[...] = (resid * inv * gain_ref[...]).astype(BF16)
 
 
-def out_norm(at, ab, x, gain, w, after):
+def out_norm(at, ab, x, gain, w):
     rows, width = x.shape
     return call(
         out_norm_kernel,
         "out_norm",
         (at, ab, x, gain.reshape(1, width), w),
-        after,
         smem=1,
         outs=[((rows, width), F32), ((rows, width), BF16), ((width // 2, rows), BF16)],
         scratch=[pltpu.VMEM(w.shape, BF16), pltpu.SemaphoreType.DMA],
@@ -455,11 +466,12 @@
 
 def ffn_kernel(
     at_ref, n0_ref, n1_ref, dy0_ref, dy1_ref, wg_ref, wu_ref, wd_ref,
-    hid_ref, d0_ref, d1_ref, sx_ref, sy_ref, px_ref, py_ref, kx_ref, ky_ref,
+    hid_ref, d0_ref, d1_ref, px_ref, py_ref, tx_ref, ty_ref, kx_ref, ky_ref,
     n_ref, dy_ref, dg_ref, du_ref, hid_t_ref, n_t_ref, g_w, u_w, d_w, sems,
 ):
     rows, width = n0_ref.shape
     share = g_w.shape[1]
+    high = kx_ref.shape[0]
     first = pl.multiple_of(at_ref[0] * share, 128)
     parts = ((0, 768), (768, share))
     loads = []
@@ -498,9 +510,12 @@
             dg_ref[:, lanes] = dg
             du_ref[:, lanes] = du
             for k in range(dg.shape[1] // rows):
-                to = (at // rows + k) * 2 * rows
-                sx_ref[to : to + 2 * rows, :] = dg[:, k * rows : (k + 1) * rows]
-                sy_ref[to : to + 2 * rows, :] = du[:, k * rows : (k + 1) * rows]
+                to = high + (at // rows + k) * 2 * rows
+                x_ref, y_ref = px_ref, py_ref
+                if to >= px_ref.shape[0]:
+                    to, x_ref, y_ref = to - px_ref.shape[0], tx_ref, ty_ref
+                x_ref[to : to + 2 * rows, :] = dg[:, k * rows : (k + 1) * rows]
+                y_ref[to : to + 2 * rows, :] = du[:, k * rows : (k + 1) * rows]
 
     for at in range(0, width, 256):
         cols = slice(at, at + 256)
@@ -510,7 +525,7 @@
 
     own = width // 32
     chunk = share // 16
-    base = px_ref.shape[0] - width
+    base = high - width
     padded = base // 16
     x, y = at_ref[1], at_ref[2]
     fill = jnp.zeros((padded - chunk, rows), F32)
@@ -535,15 +550,18 @@
             put(py_ref, inner, z, sel(x, inner), 1 - y)
 
 
-def ffn(at, n0, n1, dy0, dy1, wg, wu, wd):
+def ffn(at, n0, n1, dy0, dy1, wg, wu, wd, after):
     rows, width = n0.shape
     share = wg.shape[1] // 2
     padded = -(-(share // 16) // 16) * 16
-    sizes = [share // rows * 2 * rows] * 2 + [16 * padded + width] * 4
+    high = 16 * padded + width
+    early = EARLY * 2 * rows
+    sizes = [high + early] * 2 + [2 * share - early] * 2 + [high] * 2
     return call(
         ffn_kernel,
         "ffn",
         (at, n0, n1, dy0, dy1, wg, wu, wd),
+        after,
         smem=1,
         outs=[((2 * rows, share), BF16), ((rows, width), F32), ((rows, width), BF16)]
         + [((n, rows), BF16) for n in sizes],
@@ -620,6 +638,9 @@
     )
 
 
+EARLY = 4
+
+
 def out_product_kernel(at_ref, ab_ref, got_ref, low0_ref, low1_ref, kx_ref, px_ref, ky_ref, py_ref, acc_ref):
     half, rows = got_ref.shape
     own = half // 16
@@ -667,72 +688,96 @@
             refs[inner][z, to : to + high, :] = v[at : at + high, lanes]
 
 
-def down_product_kernel(side, p0, p1, dy0, dy1, dy2, same_ref, other_ref):
-    rows, width = dy0.shape
-    half = width // 2
-    padded = (p0.shape[0] - width) // 16
+def pair_tiles(out, left, f0, f1, start, count, base, own):
+    rows = f0.shape[1]
+    for t in range(0, count, 2):
+        n = min(2, count - t)
+        at = [start + (t + k) * 2 * rows for k in range(n)]
+        right = [jnp.concatenate([f[a : a + 2 * rows, :] for f in (f0, f1)], axis=0) for a in at]
+        v = dot(left, jnp.concatenate(right, axis=1), ((1,), (0,))).astype(BF16)
+        for k in range(n):
+            store(out, v, slice(k * rows, (k + 1) * rows), 2 * own, base + (t + k) * 2 * own)
+
+
+def left_rows(k0, p1, width):
+    high, half = k0.shape[0], width // 2
+    at = high - width
+    return jnp.concatenate([r[at + k * half : at + (k + 1) * half, :] for r in (k0, p1) for k in range(2)], axis=1)
+
+
+def first_product_kernel(side, k0, p0, p1, dy0, dy1, dy2, same_ref, other_ref):
+    out = (same_ref, other_ref)
+    high, rows = k0.shape
+    width = dy0.shape[1]
+    half, own = width // 2, width // 32
+    padded = (high - width) // 16
 
     def lanes(ref, k):
         at = k * 2 * padded
         return jnp.concatenate([ref[at : at + padded, :], ref[at + padded : at + 2 * padded, :]], axis=1)
 
-    hid = jnp.concatenate([jnp.concatenate([lanes(p0, k), lanes(p1, k)], axis=1) for k in range(8)], axis=0)
+    hid = jnp.concatenate([jnp.concatenate([lanes(k0, k), lanes(p1, k)], axis=1) for k in range(8)], axis=0)
     cols = slice(side * half, (side + 1) * half)
     dy = jnp.concatenate([dy0[:, cols], dy1[:, cols], dy2[...]], axis=0)
     v = dot(hid, dy, ((1,), (0,))).astype(BF16)
     for j in range(half // rows):
-        store((same_ref, other_ref), v, slice(j * rows, (j + 1) * rows), padded, j * padded)
-
-
-def down_product(side, p, dy, after):
-    rows, width = dy[0].shape
-    high = width // 2 // rows * ((p[0].shape[0] - width) // 16)
-    kernel = functools.partial(down_product_kernel, side)
-    return call(kernel, "down_product", (*p, *dy), after, outs=[((4, high, rows), BF16)] * 2)
-
-
-def pair_product_kernel(lo, hi, width, p0, p1, f0, f1, *rest):
-    q, out = rest[:-2], rest[-2:]
-    rows = p0.shape[1]
-    base = p0.shape[0] - width
-    half, own = width // 2, width // 32
-    left = jnp.concatenate([p[base + k * half : base + (k + 1) * half, :] for p in (p0, p1) for k in range(2)], axis=1)
-    for t in range(lo, hi, 2):
-        n = min(2, hi - t)
-        right = [
-            jnp.concatenate([f[(t + k) * 2 * rows : (t + k + 1) * 2 * rows, :] for f in (f0, f1)], axis=0)
-            for k in range(n)
-        ]
-        v = dot(left, jnp.concatenate(right, axis=1), ((1,), (0,))).astype(BF16)
-        for k in range(n):
-            store(out, v, slice(k * rows, (k + 1) * rows), 2 * own, (t + k - lo) * 2 * own)
-    if q:
-        high = q[0].shape[0] // 8
-        to = (hi - lo) * 2 * own
-        for k in range(8):
-            v = q[0][k * high : (k + 1) * high, :].astype(F32) + q[1][k * high : (k + 1) * high, :].astype(F32)
-            out[k // 4][k % 4, to : to + high, :] = v.astype(BF16)
-
-
-def pair_product(lo, hi, width, p, f, q, after):
-    rows = p[0].shape[1]
-    high = (hi - lo) * 2 * (width // 32) + (q[0].shape[0] // 8 if q else 0)
-    kernel = functools.partial(pair_product_kernel, lo, hi, width)
-    return call(kernel, "pair_product", (*p, *f, *q), after, outs=[((4, high, rows), BF16)] * 2)
-
-
-def combine_kernel(at_ref, a_ref, got_a_ref, b_ref, got_b_ref, *outs):
-    high = a_ref.shape[1]
-    for k, out_ref in enumerate(outs):
+        store(out, v, slice(j * rows, (j + 1) * rows), padded, j * padded)
+    count = (p0.shape[0] - high) // (2 * rows)
+    pair_tiles(out, left_rows(k0, p1, width), p0, p1, high, count, half // rows * padded, own)
+
+
+def first_product(side, kept, sent, got, dy, after):
+    (high, rows), width = kept.shape, dy[0].shape[1]
+    tall = width // 2 // rows * (high - width) // 16 + (sent.shape[0] - high) // (2 * rows) * (width // 16)
+    kernel = functools.partial(first_product_kernel, side)
+    outs = [((4, tall, rows), BF16)] * 2
+    return call(kernel, "first_product", (kept, sent, got, *dy), after, outs=outs)
+
+
+def second_product_kernel(width, k0, p1, f0, f1, q0, q1, same_ref, other_ref):
+    out = (same_ref, other_ref)
+    count, own = f0.shape[0] // (2 * f0.shape[1]), width // 32
+    pair_tiles(out, left_rows(k0, p1, width), f0, f1, 0, count, 0, own)
+    base, tall = count * 2 * own, q0.shape[0] // 8
+    for k in range(8):
+        v = q0[k * tall : (k + 1) * tall, :].astype(F32) + q1[k * tall : (k + 1) * tall, :].astype(F32)
+        out[k // 4][k % 4, base : base + tall, :] = v.astype(BF16)
+
+
+def second_product(width, kept, got, tiles, q, after):
+    rows = kept.shape[1]
+    tall = tiles[0].shape[0] // (2 * rows) * (width // 16) + q[0].shape[0] // 8
+    kernel = functools.partial(second_product_kernel, width)
+    outs = [((4, tall, rows), BF16)] * 2
+    return call(kernel, "second_product", (kept, got, *tiles, *q), after, outs=outs)
+
+
+def combine_kernel(at_ref, *refs):
+    parts, (own_ref, far_ref, send_ref) = refs[:-3], refs[-3:]
+    high = own_ref.shape[0]
+    for k, out_ref, start in ((0, own_ref, 0), (3, far_ref, 0), (1, send_ref, 0), (2, send_ref, high)):
         z = jnp.bitwise_xor(at_ref[3], k)
-        out_ref[:high, :] = (a_ref[z].astype(F32) + got_a_ref[z].astype(F32)).astype(BF16)
-        out_ref[high:, :] = (b_ref[z].astype(F32) + got_b_ref[z].astype(F32)).astype(BF16)
-
-
-def combine(at, a, got_a, b, got_b, after):
-    _, high, rows = a.shape
-    outs = [((2 * high, rows), BF16)] * 4
-    return call(combine_kernel, "combine", (at, a, got_a, b, got_b), after, smem=1, outs=outs)
+        to = start
+        for n in range(0, len(parts), 2):
+            rows = parts[n].shape[1]
+            out_ref[to : to + rows, :] = (parts[n][z].astype(F32) + parts[n + 1][z].astype(F32)).astype(BF16)
+            to += rows
+
+
+def combine(at, parts, after):
+    high, rows = sum(v.shape[1] for v in parts[::2]), parts[0].shape[2]
+    outs = [((high, rows), BF16), ((high, rows), BF16), ((2 * high, rows), BF16)]
+    return call(combine_kernel, "combine", (at, *parts), after, smem=1, outs=outs)
+
+
+def cross_kernel(own_ref, far_ref, got_ref, sum_ref, send_ref):
+    high = own_ref.shape[0]
+    sum_ref[...] = (own_ref[...].astype(F32) + got_ref[:high, :].astype(F32)).astype(BF16)
+    send_ref[...] = (far_ref[...].astype(F32) + got_ref[high:, :].astype(F32)).astype(BF16)
+
+
+def cross(own, far, got, after):
+    return call(cross_kernel, "cross", (own, far, got), after, outs=[(own.shape, BF16)] * 2)
 
 
 def add_lines(refs, sum_ref):
@@ -742,90 +787,79 @@
     sum_ref[...] = total
 
 
-def unpack_down_kernel(i0, i1, i2, i3, down_ref, sum_ref):
-    add_lines((i0, i1, i2, i3), sum_ref)
-    rows, (chunk, width) = i0.shape[1], down_ref.shape
-    count = width // rows
-    padded = i0.shape[0] // count
-    for j in range(count):
-        down_ref[:, j * rows : (j + 1) * rows] = sum_ref[j * padded : j * padded + chunk, :]
-
-
-def unpack_down(v, chunk, width, after):
-    scratch = [pltpu.VMEM(v[0].shape, F32)]
-    return call(unpack_down_kernel, "unpack_down", v, after, outs=[((chunk, width), F32)], scratch=scratch)[0]
-
-
-def unpack_kernel(at_ref, i0, i1, i2, i3, mine_ref, theirs_ref, *rest):
-    out_ref, sum_ref = rest[:-1], rest[-1]
-    add_lines((i0, i1, i2, i3), sum_ref)
+def unpack_kernel(at_ref, a0, a1, b0, b1, down_ref, mine_ref, theirs_ref, out_ref, a_ref, b_ref):
+    add_lines((a0, a1), a_ref)
+    add_lines((b0, b1), b_ref)
+    rows = a0.shape[1]
     _, own, wide = mine_ref.shape
-    high, rows = i0.shape[0] // 2, i0.shape[1]
+    chunk, width = down_ref.shape
+    padded = -(-chunk // 16) * 16
+    count = width // 2 // rows
     dp = at_ref[0]
     for part in range(2):
+        base = part * (a0.shape[0] // 2)
+        for j in range(count):
+            lanes = slice((part * count + j) * rows, (part * count + j + 1) * rows)
+            down_ref[:, lanes] = a_ref[base + j * padded : base + j * padded + chunk, :]
         for t in range(wide // rows):
-            at = part * high + t * 2 * own
+            ref, at = a_ref, base + count * padded + t * 2 * own
+            if t >= EARLY:
+                ref, at = b_ref, part * (b0.shape[0] // 2) + (t - EARLY) * 2 * own
             lanes = slice(t * rows, (t + 1) * rows)
-            mine_ref[part, :, lanes] = sum_ref[pl.ds(pl.multiple_of(at + dp * own, own), own), :]
-            theirs = sum_ref[pl.ds(pl.multiple_of(at + (1 - dp) * own, own), own), :]
-            theirs_ref[part, :, lanes] = theirs.astype(BF16)
-        if out_ref:
-            count = (high - wide // rows * 2 * own) // own
-            for j in range(count):
-                at = part * high + wide // rows * 2 * own + j * own
-                out_ref[0][:, (part * count + j) * rows : (part * count + j + 1) * rows] = sum_ref[at : at + own, :]
-
-
-def unpack(at, v, own, wide, width, after):
-    outs = [((2, own, wide), F32), ((2, own, wide), BF16)] + ([((own, width), F32)] if width else [])
-    scratch = [pltpu.VMEM(v[0].shape, F32)]
+            mine_ref[part, :, lanes] = ref[pl.ds(pl.multiple_of(at + dp * own, own), own), :]
+            theirs_ref[part, :, lanes] = ref[pl.ds(pl.multiple_of(at + (1 - dp) * own, own), own), :].astype(BF16)
+        base = part * (b0.shape[0] // 2) + (wide // rows - EARLY) * 2 * own
+        for j in range(count):
+            lanes = slice((part * count + j) * rows, (part * count + j + 1) * rows)
+            out_ref[:, lanes] = b_ref[base + j * own : base + (j + 1) * own, :]
+
+
+def unpack(at, v, own, wide, chunk, width, after):
+    outs = [((chunk, width), F32), ((2, own, wide), F32), ((2, own, wide), BF16), ((own, width), F32)]
+    scratch = [pltpu.VMEM(v[0].shape, F32), pltpu.VMEM(v[2].shape, F32)]
     return call(unpack_kernel, "unpack", (at, *v), after, smem=1, outs=outs, scratch=scratch)
 
 
-def finish_kernel(at_ref, m0, m1, o0, o1, wg_ref, wu_ref, gate_ref, up_ref, dots_ref):
-    dp = at_ref[0]
+def finish_kernel(at_ref, mine, theirs, gain_ref, wg_ref, wu_ref, gate_ref, up_ref, dots_ref):
+    dp = at_ref[1]
     share = gate_ref.shape[1] // 2
-    early = m0.shape[2]
     for part, ref in enumerate((gate_ref, up_ref)):
-
-        def put(at, a, b):
-            ref[:, at : at + early] = a[part].astype(F32)
-            ref[:, at + early : at + share] = b[part].astype(F32)
 
         @pl.when(dp == 0)
         def _():
-            put(0, m0, m1)
-            put(share, o0, o1)
+            ref[:, :share] = mine[part]
+            ref[:, share:] = theirs[part].astype(F32)
 
         @pl.when(dp == 1)
         def _():
-            put(0, o0, o1)
-            put(share, m0, m1)
+            ref[:, :share] = theirs[part].astype(F32)
+            ref[:, share:] = mine[part]
 
     total = gate_ref[...] * wg_ref[...].astype(F32) + up_ref[...] * wu_ref[...].astype(F32)
-    dots_ref[...] = jnp.sum(total, axis=1, keepdims=True)
-
-
-def finish(at, place, mine, theirs, wg, wu):
-    own, ff = mine[0].shape[1], wg.shape[1]
+    dots_ref[...] = by_gain(jnp.sum(total, axis=1, keepdims=True), gain_ref, at_ref[0])
+
+
+def finish(where, mine, theirs, gain, wg, wu):
+    own, ff = mine.shape[1], wg.shape[1]
+    count = wg.shape[0] // own
 
     def whole(*shape):
         return pl.BlockSpec(shape, lambda g, at: (0,) * len(shape))
 
-    weight = pl.BlockSpec((own, ff), lambda g, at: (at[1], 0))
-    where = jnp.stack([at[0], place]).astype(jnp.int32)
-    return pl.pallas_call(
+    weight = pl.BlockSpec((own, ff), lambda g, at: (at[0], 0))
+    gate, up, dots = pl.pallas_call(
         finish_kernel,
         grid_spec=pltpu.PrefetchScalarGridSpec(
             num_scalar_prefetch=1,
             grid=(1,),
-            in_specs=[whole(*v.shape) for v in (*mine, *theirs)] + [weight, weight],
-            out_specs=[whole(own, ff), whole(own, ff), whole(own, 1)],
+            in_specs=[whole(*mine.shape), whole(*theirs.shape), whole(count, own), weight, weight],
+            out_specs=[whole(own, ff), whole(own, ff), whole(1, own)],
         ),
-        out_shape=[jax.ShapeDtypeStruct((own, ff), F32)] * 2 + [jax.ShapeDtypeStruct((own, 1), F32)],
+        out_shape=[jax.ShapeDtypeStruct((own, ff), F32)] * 2 + [jax.ShapeDtypeStruct((1, own), F32)],
         cost_estimate=COST,
         name="finish",
-    )(where, *mine, *theirs, in_hbm(wg), in_hbm(wu))
+    )(where, mine, theirs, gain.reshape(count, own), in_hbm(wg), in_hbm(wu))
+    return gate, up, dots.reshape(own)
 
 
 def turn_kernel(in_ref, out_ref):
@@ -838,16 +872,17 @@
     return call(turn_kernel, "turn", (v,), after, outs=[(v.shape, BF16)])[0]
 
 
-def head_product_kernel(at_ref, n0, n1, n2, n3, in_ref, mine_ref, theirs_ref, acc_ref):
+def head_product_kernel(at_ref, n0, n1, in_ref, mine_ref, theirs_ref, acc_ref):
     half = mine_ref.shape[0]
+    x, y = at_ref[1], at_ref[2]
     left = jnp.concatenate(
         [
-            jnp.concatenate([in_ref[h, jnp.bitwise_xor(at_ref[3], k)] for k in range(4)], axis=1)
+            jnp.concatenate([in_ref[h, sel(y, oy) * 2 + sel(x, ox)] for oy in range(2) for ox in range(2)], axis=1)
             for h in range(4)
         ],
         axis=0,
     )
-    right = jnp.concatenate([r[...] for r in (n0, n1, n2, n3)], axis=0)
+    right = jnp.concatenate([n0[...], n1[...]], axis=0)
     for at in range(0, acc_ref.shape[0], 256):
         acc_ref[at : at + 256, :] = dot(left, right[:, at : at + 256], ((1,), (0,))).T
     dp = at_ref[0]
@@ -868,58 +903,29 @@
     )
 
 
-def head_split_kernel(at_ref, mine_ref, got_ref, kx_ref, px_ref, ky_ref, py_ref, acc_ref):
-    half, wide = mine_ref.shape
-    own = half // 16
-    x, y = at_ref[1], at_ref[2]
-    acc_ref[...] = mine_ref[...] + got_ref[...].astype(F32)
-
-    def put(ref, inner, z, xs, ys, lanes):
-        to = (inner * 4 + z) * own
-        at = pl.multiple_of((z * 4 + ys * 2 + xs) * own, own)
-        ref[to : to + own, :] = acc_ref[pl.ds(at, own), lanes].astype(BF16)
-
-    for inner in range(2):
-        for z in range(4):
-            low, high = slice(0, wide // 2), slice(wide // 2, wide)
-            put(kx_ref, inner, z, x, sel(y, inner), low)
-            put(px_ref, inner, z, 1 - x, sel(y, inner), low)
-            put(ky_ref, inner, z, sel(x, inner), y, high)
-            put(py_ref, inner, z, sel(x, inner), 1 - y, high)
+def head_split_kernel(at_ref, mine_ref, got_ref, own_ref, far_ref, send_ref):
+    high = own_ref.shape[0]
+    for k, ref, to in ((0, own_ref, 0), (3, far_ref, 0), (1, send_ref, 0), (2, send_ref, high)):
+        rows = pl.ds(pl.multiple_of(jnp.bitwise_xor(at_ref[3], k) * high, high), high)
+        ref[to : to + high, :] = (mine_ref[rows, :] + got_ref[rows, :].astype(F32)).astype(BF16)
 
 
 def head_split(at, mine, got, after):
     half, wide = mine.shape
-    outs = [((half // 2, wide // 2), BF16)] * 4
-    scratch = [pltpu.VMEM((half, wide), F32)]
-    return call(head_split_kernel, "head_split", (at, mine, got), after, smem=1, outs=outs, scratch=scratch)
-
-
-def head_mid_kernel(kx, gx, ky, gy, same_a, other_a, same_b, other_b):
-    half = kx.shape[0] // 2
-    for k, g, same, other in ((kx, gx, same_a, other_a), (ky, gy, same_b, other_b)):
-        v = (k[...].astype(F32) + g[...].astype(F32)).astype(BF16)
-        same[...] = v[:half]
-        other[...] = v[half:]
-
-
-def head_mid(kx, gx, ky, gy, after):
-    outs = [((kx.shape[0] // 2, kx.shape[1]), BF16)] * 4
-    return call(head_mid_kernel, "head_mid", (kx, gx, ky, gy), after, outs=outs)
-
-
-def head_end_kernel(a, ga, b, gb, out_ref):
+    outs = [((half // 4, wide), BF16), ((half // 4, wide), BF16), ((half // 2, wide), BF16)]
+    return call(head_split_kernel, "head_split", (at, mine, got), after, smem=1, outs=outs)
+
+
+def head_end_kernel(a, ga, out_ref):
     own = a.shape[0] // 4
-    v = jnp.concatenate(
-        [(r[...].astype(F32) + g[...].astype(F32)).astype(BF16) for r, g in ((a, ga), (b, gb))], axis=1
-    )
-    for z in range(4):
-        out_ref[z] = v[z * own : (z + 1) * own]
-
-
-def head_end(a, ga, b, gb, after):
-    outs = [((4, a.shape[0] // 4, 2 * a.shape[1]), BF16)]
-    return call(head_end_kernel, "head_end", (a, ga, b, gb), after, outs=outs)[0]
+    v = (a[...].astype(F32) + ga[...].astype(F32)).astype(BF16)
+    for p in range(4):
+        out_ref[p] = v[p * own : (p + 1) * own]
+
+
+def head_end(a, ga, after):
+    outs = [((4, a.shape[0] // 4, a.shape[1]), BF16)]
+    return call(head_end_kernel, "head_end", (a, ga), after, outs=outs)[0]
 
 
 def latent_back_kernel(
@@ -930,7 +936,7 @@
         load.start()
     for h in range(HEADS):
         for t in range(3):
-            left_ref[t, h * HEAD_DIM : (h + 1) * HEAD_DIM, :] = back_ref[h, t * HEAD_DIM : (t + 1) * HEAD_DIM, :]
+            left_ref[t, h * HEAD_DIM : (h + 1) * HEAD_DIM, :] = back_ref[h % 4 * 4 + h // 4, t * HEAD_DIM : (t + 1) * HEAD_DIM, :]
     for load in loads:
         load.wait()
     for at in range(0, d_ref.shape[1], 256):
@@ -961,34 +967,42 @@
     )[0]
 
 
-def head_rows_kernel(at_ref, in_ref, wq_ref, wk_ref, wv_ref, q_ref, k_ref, v_ref, dots_ref):
+def by_gain(sums, gain_ref, place):
+    return jnp.broadcast_to(sums, (sums.shape[0], 128)).T[:1] / gain_ref[pl.ds(place, 1), :]
+
+
+def head_rows_kernel(at_ref, in_ref, gain_ref, wq_ref, wk_ref, wv_ref, q_ref, k_ref, v_ref, dots_ref):
     total = None
     for t, (w_ref, o_ref) in enumerate(((wq_ref, q_ref), (wk_ref, k_ref), (wv_ref, v_ref))):
         for h in range(0, HEADS, 2):
-            lanes = [((h + n) % 4 * 3 + t) * HEAD_DIM for n in range(2)]
-            pair = [in_ref[h // 4][:, at : at + HEAD_DIM] for at in lanes]
+            at = (h // 4 * 3 + t) * HEAD_DIM
+            pair = [in_ref[h % 4 + n][:, at : at + HEAD_DIM] for n in range(2)]
             o_ref[:, h * HEAD_DIM : (h + 2) * HEAD_DIM] = jnp.concatenate(pair, axis=1).astype(F32)
         v = jnp.sum(o_ref[...] * w_ref[...].astype(F32), axis=1, keepdims=True)
         total = v if total is None else total + v
-    dots_ref[...] = total
-
-
-def head_rows(place, v, wq, wk, wv):
+    dots_ref[...] = by_gain(total, gain_ref, at_ref[0])
+
+
+def head_rows(where, v, gain, wq, wk, wv):
     own, width = v.shape[1], wq.shape[1]
     weight = pl.BlockSpec((own, width), lambda g, at: (at[0], 0))
-    out = pl.BlockSpec((own, width), lambda g, at: (0, 0))
-    return pl.pallas_call(
+
+    def whole(*shape):
+        return pl.BlockSpec(shape, lambda g, at: (0,) * len(shape))
+
+    out = pl.pallas_call(
         head_rows_kernel,
         grid_spec=pltpu.PrefetchScalarGridSpec(
             num_scalar_prefetch=1,
             grid=(1,),
-            in_specs=[pl.BlockSpec(v.shape, lambda g, at: (0, 0, 0)), weight, weight, weight],
-            out_specs=[out, out, out, pl.BlockSpec((own, 1), lambda g, at: (0, 0))],
+            in_specs=[whole(*v.shape), whole(width // own, own), weight, weight, weight],
+            out_specs=[whole(own, width)] * 3 + [whole(1, own)],
         ),
-        out_shape=[jax.ShapeDtypeStruct((own, width), F32)] * 3 + [jax.ShapeDtypeStruct((own, 1), F32)],
+        out_shape=[jax.ShapeDtypeStruct((own, width), F32)] * 3 + [jax.ShapeDtypeStruct((1, own), F32)],
         cost_estimate=COST,
         name="head_rows",
-    )(place, v, in_hbm(wq), in_hbm(wk), in_hbm(wv))
+    )(where, v, gain.reshape(width // own, own), in_hbm(wq), in_hbm(wk), in_hbm(wv))
+    return *out[:3], out[3].reshape(own)
 
 
 X_PAIRS = [(i, i ^ 1) for i in range(16)]
@@ -1017,10 +1031,6 @@
 
 def in_group(v, groups):
     return lax.all_to_all(v, "ctx", 0, 0, tiled=True, axis_index_groups=groups)
-
-
-def sum_z(v):
-    return (v[0], *(over_z(v[k], k) for k in range(1, 4)))
 
 
 def to_ctx(v):
@@ -1056,67 +1066,57 @@
     normed, qkv = norm_qkv(latent_in, gain_attn, w_query, w_key, w_value)
     qkv = to_ctx(qkv)
 
+    line = jnp.concatenate([normed, over_x(normed)], axis=0)
+    line = (line, over_y(line))
     out, full, top, inv = attn_fwd(1, scalars, qkv, (dy_x, dy_y))
     attn_t = to_ctx(out).reshape(width, rows)
-    line = (normed, *(over_z(normed, k) for k in range(1, 4)))
-    resid, normed_two, attn_send = out_norm(at, attn_t, latent_in, gain_ffn, w_out, ())
+    resid, normed_two, attn_send = out_norm(at, attn_t, latent_in, gain_ffn, w_out)
     normed_mate = swap(normed_two)
     attn_mate = swap(attn_send)
 
-    hid, d_own, d_mate, send_x, send_y, left_sx, left_sy, left_x, left_y = ffn(
-        at, normed_two, normed_mate, cotangent, dy_mate, w_gate, w_up, w_down
+    hid, d_own, d_mate, send_x, send_y, tiles_x, tiles_y, kept_x, kept_y = ffn(
+        at, normed_two, normed_mate, cotangent, dy_mate, w_gate, w_up, w_down, (line[1],)
     )
     d_got = swap(d_mate)
-    left_gx, left_gy = over_x(left_sx), over_y(left_sy)
-    f_x, f_y = over_x(send_x), over_y(send_y)
-    dres, dres_low, grad_attn = ffn_back(d_own, d_got, resid, gain_ffn, cotangent, w_out, line[1:])
+    got_x, got_y = over_x(send_x), over_y(send_y)
+    tiles_x, tiles_y = (tiles_x, over_x(tiles_x)), (tiles_y, over_y(tiles_y))
+    dres, dres_low, grad_attn = ffn_back(d_own, d_got, resid, gain_ffn, cotangent, w_out, ())
     grad_attn = to_ctx(grad_attn.reshape(HEADS, HEAD_DIM, rows))
-    y_own, y_mate = ffn_out(at, hid, w_down, (dres_low,))
+    out_x, out_sx, out_y, out_sy = out_product(at, attn_t, attn_mate, dres_low, swap(dres_low), ())
+    out_x, out_y = (out_x, over_x(out_sx)), (out_y, over_y(out_sy))
+
+    dy_a, dy_b = (cotangent, dy_mate, dy_x), (cotangent, dy_mate, dy_y)
+    one_a, other_a = first_product(0, kept_x, send_x, got_x, dy_a, (out_x[0],))
+    one_b, other_b = first_product(1, kept_y, send_y, got_y, dy_b, (one_a,))
+    one = (one_a, over_y(other_a), one_b, over_x(other_b))
+    grad_qkv = attn_bwd(1, lambda slot: slot, scalars, qkv, grad_attn, full, top, inv, (one_b,))
+    four = in_group(grad_qkv, Z_LINES).reshape(4, 4, 3 * HEAD_DIM, rows)
+    two_a, other_a = second_product(width, kept_x, got_x, tiles_x, out_x, (grad_qkv,))
+    two_b, other_b = second_product(width, kept_y, got_y, tiles_y, out_y, (two_a,))
+    two = (two_a, over_y(other_a), two_b, over_x(other_b))
+    one_own, one_far, one_send = combine(at, one, (two_b,))
+    one_got = over_z(one_send, 1)
+    y_own, y_mate = ffn_out(at, hid, w_down, (one_own,))
     latents = (resid + y_own + swap(y_mate).astype(F32)).astype(BF16)
-    out_x, out_sx, out_y, out_sy = out_product(at, attn_t, attn_mate, dres_low, swap(dres_low), (y_own,))
-    out_gx, out_gy = over_x(out_sx), over_y(out_sy)
-
-    same_a, other_a = down_product(0, (left_x, left_gx), (cotangent, dy_mate, dy_x), (out_x,))
-    same_b, other_b = down_product(1, (left_y, left_gy), (cotangent, dy_mate, dy_y), (same_a,))
-    sent_a, sent_b = over_y(other_a), over_x(other_b)
-
-    grad_qkv = attn_bwd(
-        1, lambda slot: (slot & 3) * 4 + (slot >> 2), scalars, qkv, grad_attn, full, top, inv, (same_b,)
-    )
-    four = in_group(grad_qkv, PLANES).reshape(4, 4, 3 * HEAD_DIM, rows)
-
-    tiles = send_x.shape[0] // (2 * rows)
-    split = (tiles + 1) // 2
-    early_a, other_a = pair_product(0, split, width, (left_x, left_gx), (send_x, f_x), (), (grad_qkv,))
-    early_b, other_b = pair_product(0, split, width, (left_y, left_gy), (send_y, f_y), (), (early_a,))
-    early_sa, early_sb = over_y(other_a), over_x(other_b)
-    down = combine(at, same_a, sent_a, same_b, sent_b, (early_b,))
-
-    back = in_group(turn(four, (down[0],)), Z_LINES).reshape(16, 3 * HEAD_DIM, rows)
-    late_a, other_a = pair_product(split, tiles, width, (left_x, left_gx), (send_x, f_x), (out_x, out_gx), (four,))
-    late_b, other_b = pair_product(split, tiles, width, (left_y, left_gy), (send_y, f_y), (out_y, out_gy), (late_a,))
-    late_sa, late_sb = over_y(other_a), over_x(other_b)
-    head_mine, head_theirs = head_product(at, line, four, (late_b,))
-    head_x, head_sx, head_y, head_sy = head_split(at, head_mine, swap(head_theirs), (late_b,))
-    early = combine(at, early_a, early_sa, early_b, early_sb, (head_x,))
-    head_a, other_a, head_b, other_b = head_mid(head_x, over_x(head_sx), head_y, over_y(head_sy), (early[0],))
-    late = combine(at, late_a, late_sa, late_b, late_sb, (head_a,))
-    heads = head_end(head_a, over_y(other_a), head_b, over_x(other_b), (late[0],))
-    latent_grad = latent_back(back, dres, latent_in, gain_attn, w_query, w_key, w_value, (heads,))
-    heads = in_group(heads, Z_LINES)
+    two_own, two_far, two_send = combine(at, two, (y_own,))
+    two_got = over_z(two_send, 1)
+
+    turned = turn(four, (two_own,))
+    back = in_group(turned, PLANES).reshape(16, 3 * HEAD_DIM, rows)
+    one_own, one_send = cross(one_own, one_far, one_got, (turned,))
+    head_mine, head_theirs = head_product(at, line, four, (one_own,))
+    head_own, head_far, head_send = head_split(at, head_mine, swap(head_theirs), ())
+    head_got = over_z(head_send, 1)
+    latent_grad = latent_back(back, dres, latent_in, gain_attn, w_query, w_key, w_value, (head_own,))
+    two_own, two_send = cross(two_own, two_far, two_got, (latent_grad,))
+    head_own, head_send = cross(head_own, head_far, head_got, (two_own,))
+    heads = head_end(head_own, over_z(head_send, 3), ())
+    heads = in_group(heads, PLANES)
     place = dp * 16 + ctx
-    down_sum = unpack_down(sum_z(down), ff // 32, width, (latent_grad,))
-    wide = split * rows
-    mine0, theirs0 = unpack(at, sum_z(early), own, wide, 0, (down_sum,))
-    query_sum, key_sum, value_sum, dots = head_rows(place.reshape(1).astype(jnp.int32), heads, w_query, w_key, w_value)
-    mine1, theirs1, out_sum = unpack(at, sum_z(late), own, ff // 2 - wide, width, (mine0, dots))
-    gate_sum, up_sum, ffn_dots = finish(at, place, (mine0, mine1), (swap(theirs0), swap(theirs1)), w_gate, w_up)
-
-    def own_gain(v):
-        return lax.dynamic_slice_in_dim(v, place * own, own, 0)
-
-    gain_attn_sum = dots[:, 0] / own_gain(gain_attn)
-    gain_ffn_sum = ffn_dots[:, 0] / own_gain(gain_ffn)
+    where = jnp.stack([place, dp]).astype(jnp.int32)
+    query_sum, key_sum, value_sum, gain_attn_sum = head_rows(where, heads, gain_attn, w_query, w_key, w_value)
+    down_sum, mine, theirs, out_sum = unpack(at, (one_own, over_z(one_send, 3), two_own, over_z(two_send, 3)), own, ff // 2, ff // 32, width, (gain_attn_sum,))
+    gate_sum, up_sum, gain_ffn_sum = finish(where, mine, swap(theirs), gain_ffn, w_gate, w_up)
     return (
         latents,
         latent_grad,

time: 279 us -> 254 us (0.910)
  starting transfers between devices: 70.5 us -> 54.9 us
  local copies, waits for them, and re-layouts: 37.8 us -> 27 us
  waiting for transfers between devices: 82.1 us -> 89.7 us
    unnamed x194 -> x141, local copies, waits for them, and re-layouts: 37.8 us -> 24.7 us
    ppermute x12 -> x6, starting transfers between devices: 15.7 us -> 6.76 us  [over_z(): return lax.ppermute(v, 'ctx', [(i, i ^ 4 * k) for i in range(16)])]
    all_to_all x3, waiting for transfers between devices: 0.01 us -> 8.92 us  [in_group(): return lax.all_to_all(v, 'ctx', 0, 0, tiled=True, axis_index_groups=groups)]
    ppermute x9 -> x7, waiting for transfers between devices: 3.09 us -> 11.5 us  [over_y(): return lax.ppermute(v, 'ctx', Y_PAIRS)]
    all_to_all x3, waiting for transfers between devices: 12 us -> 6.66 us  [to_ctx(): return lax.all_to_all(v, 'ctx', 0, 0, tiled=True)]
    ppermute x9 -> x7, starting transfers between devices: 11 us -> 8.05 us  [over_y(): return lax.ppermute(v, 'ctx', Y_PAIRS)]
    pallas_call x26 -> x23, Pallas kernels: 72.6 us -> 70.3 us  [call(): pl.pallas_call(body, in_specs=[SMEM] * smem + [VMEM] * (held - smem - far...]
    ppermute x12 -> x6, waiting for transfers between devices: 27.8 us -> 25.6 us  [over_z(): return lax.ppermute(v, 'ctx', [(i, i ^ 4 * k) for i in range(16)])]
  transfers between devices with their start and end apart: 45 -> 34, of which waited for: 18 -> 17; matrix products, arithmetic and copies ran while one was open for 2% -> 2% of each run, Pallas kernels for 21% -> 22%
where the time goes in v3:
time: 254 us; the launch traced here: 251 us
  waiting for transfers between devices  89.7 us (35%)
  Pallas kernels  75.6 us (30%)
  starting transfers between devices  54.9 us (22%)
  local copies, waits for them, and re-layouts  27 us (11%)
  other arithmetic  2.93 us (1%)
    pallas_call x23, Pallas kernels, call(): pl.pallas_call(body, in_specs=[SMEM] * smem + [VMEM] * (held - smem - far...  70.3 us
    ppermute x7, waiting for transfers between devices, over_x(): return lax.ppermute(v, 'ctx', X_PAIRS)  34 us
    ppermute x6, waiting for transfers between devices, over_z(): return lax.ppermute(v, 'ctx', [(i, i ^ 4 * k) for i in range(16)])  25.6 us
    unnamed x141, local copies, waits for them, and re-layouts  24.7 us
    all_to_all x3, starting transfers between devices, to_ctx(): return lax.all_to_all(v, 'ctx', 0, 0, tiled=True)  20.1 us
    all_to_all x3, starting transfers between devices, in_group(): return lax.all_to_all(v, 'ctx', 0, 0, tiled=True, axis_index_groups=groups)  12.8 us
    ppermute x7, waiting for transfers between devices, over_y(): return lax.ppermute(v, 'ctx', Y_PAIRS)  11.5 us
    all_to_all x3, waiting for transfers between devices, in_group(): return lax.all_to_all(v, 'ctx', 0, 0, tiled=True, axis_index_groups=groups)  8.92 us
  transfers between devices with their start and end apart: 34, of which 17 were waited for; matrix products, arithmetic and copies ran while one was open for 2% of the time, Pallas kernels for 22%

profile of v3, /device:TPU:10, one launch (start us, length us, event | category | flops | bytes accessed | tf_op | source)
XLA Modules:
  0.0 251.3 jit_solution(12950813240881562668)
XLA Ops:
  2.3 4.3 %norm_qkv.1 = (bf16[128,1024]{1,0:T(8,128)(2,1)S(1)}, bf16[16,192,128]{2,1,0:T(8,128)(2,1)}) custom-call(bf16[128,1024]{1,0:T(8,128)(2,1)S(1)} %copy-done.12, f32[1,1024]{1,0:T(1,128)S(1)} %bitcast.22, bf16[1024,1024]{1,0:T(8,128)(2,1)} %wq_ref.1, bf16[1024,1024]{1,0:T(8,128)(2,1)} %wk_ref.1, bf16[1024,1024]{1,0:T(8,128)(2,1)} %wv_ref.1), custom_call_target="tpu_custom_call" | custom-call | flops 1000000 | bytes 100000 | tf_op jit(solution)/shard_map/norm_qkv/pallas_call | solution.py:169
  6.7 7.2 %all-to-all-start = ((bf16[16,192,128]{2,1,0:T(8,128)(2,1)}), bf16[16,192,128]{2,1,0:T(8,128)(2,1)S(1)}, u32[]{:S(2)}, u32[]{:S(2)}) async-start(bf16[16,192,128]{2,1,0:T(8,128)(2,1)} %get-tuple-element.74), calls=%async_computation | async-start | bytes 1572864 | tf_op jit(solution)/shard_map/all_to_all | solution.py:1037
  16.5 1.5 collective-permute-start.2
  18.2 16.6 %collective-permute-done.1.refs_5_ = bf16[256,512]{1,0:T(8,128)(2,1)S(1)} collective-permute-done((bf16[256,512]{1,0:T(8,128)(2,1)S(1)}, bf16[256,512]{1,0:T(8,128)(2,1)S(1)}, u32[]{:S(2)}, u32[]{:S(2)}) %collective-permute-start.1) | collective-permute-done | bytes 262176 | tf_op jit(solution)/shard_map/ppermute | solution.py:1017
  34.8 9.6 %attn_fwd.1 = (bf16[16,64,128]{2,1,0:T(8,128)(2,1)}, f32[16,64,128]{2,1,0:T(8,128)S(1)}, f32[8,1,256]{2,1,0:T(1,128)S(1)}, f32[8,1,256]{2,1,0:T(1,128)S(1)}) custom-call(s32[16]{0:T(128)S(1)} %select_reduce_fusion.refs_0_, s32[8]{0:T(128)S(1)} %and_select_fusion.refs_1_, s32[4]{0:T(128)S(1)} %bitcast.27, s32[1]{0:T(128)} %constant.70.clone.1.refs_3_, ...), custom_call_target="tpu_custom_call" | custom-call | flops 1000000 | bytes 100000 | tf_op jit(solution)/shard_map/attn_fwd/pallas_call | solution.py:169
  45.2 6.6 %all-to-all-start.1 = ((bf16[16,64,128]{2,1,0:T(8,128)(2,1)}), bf16[16,64,128]{2,1,0:T(8,128)(2,1)S(1)}, u32[]{:S(2)}, u32[]{:S(2)}) async-start(bf16[16,64,128]{2,1,0:T(8,128)(2,1)} %get-tuple-element.75), calls=%async_computation.1 | async-start | bytes 524288 | tf_op jit(solution)/shard_map/all_to_all | solution.py:1037
  52.8 1.5 collective-permute-start.5
  54.4 6.7 %all-to-all-done.1 = bf16[16,64,128]{2,1,0:T(8,128)(2,1)S(1)} async-done(((bf16[16,64,128]{2,1,0:T(8,128)(2,1)}), bf16[16,64,128]{2,1,0:T(8,128)(2,1)S(1)}, u32[]{:S(2)}, u32[]{:S(2)}) %all-to-all-start.1) | async-done | bytes 262176 | tf_op jit(solution)/shard_map/all_to_all | solution.py:1037
  61.1 2.7 %out_norm.1 = (f32[128,1024]{1,0:T(8,128)S(1)}, bf16[128,1024]{1,0:T(8,128)(2,1)S(1)}, bf16[512,128]{1,0:T(8,128)(2,1)S(1)}) custom-call(s32[4]{0:T(128)S(1)} %pad_add_fusion.refs_0_, bf16[1024,128]{1,0:T(8,128)(2,1)S(1)} %bitcast.19, bf16[128,1024]{1,0:T(8,128)(2,1)S(1)} %copy-done.13, f32[1,1024]{1,0:T(1,128)S(1)} %bitcast.24, bf16[1024,1024]{1,0:T(8,128)(2,1)} %refs_5_.4), custom_call_target="tpu_custom_call" | custom-call | flops 1000000 | bytes 100000 | tf_op jit(solution)/shard_map/out_norm/pallas_call | solution.py:169
  63.9 5.4 %collective-permute-done.5.refs_8_.refs_2_ = bf16[256,1024]{1,0:T(8,128)(2,1)S(1)} collective-permute-done((bf16[256,1024]{1,0:T(8,128)(2,1)S(1)}, bf16[256,1024]{1,0:T(8,128)(2,1)S(1)}, u32[]{:S(2)}, u32[]{:S(2)}) %collective-permute-start.5) | collective-permute-done | bytes 524320 | tf_op jit(solution)/shard_map/ppermute | solution.py:1021
  69.3 9.1 %ffn.1 = (bf16[256,1408]{1,0:T(8,128)(2,1)S(1)}, f32[128,1024]{1,0:T(8,128)S(1)}, bf16[128,1024]{1,0:T(8,128)(2,1)S(1)}, bf16[3584,128]{1,0:T(8,128)(2,1)}, bf16...) custom-call(s32[4]{0:T(128)S(1)} %pad_add_fusion.refs_0_, ...), custom_call_target="tpu_custom_call" | custom-call | flops 1000000 | bytes 100000 | tf_op jit(solution)/shard_map/ffn/pallas_call | solution.py:169
  81.7 1.5 collective-permute-done.8.refs_1_
  83.2 2.3 ffn_back.1
  87.1 6.3 %all-to-all-start.2 = ((bf16[16,64,128]{2,1,0:T(8,128)(2,1)}), bf16[16,64,128]{2,1,0:T(8,128)(2,1)}, u32[]{:S(2)}, u32[]{:S(2)}) async-start(bf16[16,64,128]{2,1,0:T(8,128)(2,1)} %bitcast.21), calls=%async_computation.2 | async-start | bytes 524288 | tf_op jit(solution)/shard_map/all_to_all | solution.py:1037
  99.6 6.1 %collective-permute-done.6.refs_2_.refs_1_ = bf16[3584,128]{1,0:T(8,128)(2,1)S(1)} collective-permute-done((bf16[3584,128]{1,0:T(8,128)(2,1)}, bf16[3584,128]{1,0:T(8,128)(2,1)S(1)}, u32[]{:S(2)}, u32[]{:S(2)}) %collective-permute-start.6) | collective-permute-done | bytes 917536 | tf_op jit(solution)/shard_map/ppermute | solution.py:1017
  107.7 2.9 %first_product.2 = (bf16[4,640,128]{2,1,0:T(8,128)(2,1)S(1)}, bf16[4,640,128]{2,1,0:T(8,128)(2,1)}) custom-call(bf16[2560,128]{1,0:T(8,128)(2,1)S(1)} %copy-done.5, bf16[3584,128]{1,0:T(8,128)(2,1)} %get-tuple-element.81.refs_1_, bf16[3584,128]{1,0:T(8,128)(2,1)S(1)} %collective-permute-done.6.refs_2_.refs_1_, bf16[128,1024]{1,0:T(8,128)(2,1)S(1)} %copy-done, ...), custom_call_target="tpu_custom_call" | custom-call | flops 1000000 | bytes 100000 | tf_op jit(solution)/shard_map/first_product/pallas_call | solution.py:169
  110.6 3.1 %first_product.3 = (bf16[4,640,128]{2,1,0:T(8,128)(2,1)S(1)}, bf16[4,640,128]{2,1,0:T(8,128)(2,1)}) custom-call(bf16[2560,128]{1,0:T(8,128)(2,1)S(1)} %copy-done.2, bf16[3584,128]{1,0:T(8,128)(2,1)} %get-tuple-element.90.refs_1_, bf16[3584,128]{1,0:T(8,128)(2,1)S(1)} %collective-permute-done.11.refs_2_.refs_1_, bf16[128,1024]{1,0:T(8,128)(2,1)S(1)} %copy-done, ...), custom_call_target="tpu_custom_call" | custom-call | flops 1000000 | bytes 100000 | tf_op jit(solution)/shard_map/first_product/pallas_call | solution.py:169
  116.1 1.1 copy-done.8
  118.2 10.9 %attn_bwd.1.refs_6_ = bf16[16,192,128]{2,1,0:T(8,128)(2,1)} custom-call(s32[16]{0:T(128)S(1)} %select_reduce_fusion.refs_0_, s32[8]{0:T(128)S(1)} %and_select_fusion.refs_1_, s32[4]{0:T(128)S(1)} %bitcast.28, s32[1]{0:T(128)} %constant.70.clone.1.refs_3_, bf16[16,192,128]{2,1,0:T(8,128)(2,1)S(1)} %all-to-all-done.refs_4_, ...), custom_call_target="tpu_custom_call" | custom-call | flops 1000000 | bytes 100000 | tf_op jit(solution)/shard_map/attn_bwd/pallas_call | solution.py:169
  129.2 4.9 %all-to-all-start.3 = ((bf16[16,192,128]{2,1,0:T(8,128)(2,1)}), bf16[16,192,128]{2,1,0:T(8,128)(2,1)S(1)}, u32[]{:S(2)}, u32[]{:S(2)}) async-start(bf16[16,192,128]{2,1,0:T(8,128)(2,1)} %attn_bwd.1.refs_6_), calls=%async_computation.3 | async-start | bytes 1572864 | tf_op jit(solution)/shard_map/all_to_all | solution.py:1033
  134.0 1.2 collective-permute-start.13
  136.3 1.2 collective-permute-start.14
  137.5 4.8 %collective-permute-done.16.refs_5_ = bf16[1024,128]{1,0:T(8,128)(2,1)S(1)} collective-permute-done((bf16[1024,128]{1,0:T(8,128)(2,1)}, bf16[1024,128]{1,0:T(8,128)(2,1)S(1)}, u32[]{:S(2)}, u32[]{:S(2)}) %collective-permute-start.16) | collective-permute-done | bytes 262176 | tf_op jit(solution)/shard_map/ppermute | solution.py:1017
  144.5 1.7 second_product.2
  146.2 1.4 collective-permute-done.13.refs_3_
  147.7 3.2 %collective-permute-done.14.refs_5_ = bf16[1024,128]{1,0:T(8,128)(2,1)S(1)} collective-permute-done((bf16[1024,128]{1,0:T(8,128)(2,1)S(1)}, bf16[1024,128]{1,0:T(8,128)(2,1)S(1)}, u32[]{:S(2)}, u32[]{:S(2)}) %collective-permute-start.14) | collective-permute-done | bytes 262176 | tf_op jit(solution)/shard_map/ppermute | solution.py:1021
  152.7 2.4 combine.2
  155.4 1.7 collective-permute-start.19
  158.0 3.3 %ffn_out.1 = (f32[128,1024]{1,0:T(8,128)S(1)}, bf16[128,1024]{1,0:T(8,128)(2,1)S(1)}) custom-call(s32[4]{0:T(128)S(1)} %pad_add_fusion.refs_0_, bf16[256,1408]{1,0:T(8,128)(2,1)S(1)} %copy-done.35, bf16[2816,1024]{1,0:T(8,128)(2,1)} %refs_2_.6, bf16[1280,128]{1,0:T(8,128)(2,1)S(1)} %get-tuple-element.104.refs_3_.refs_0_), custom_call_target="tpu_custom_call" | custom-call | flops 1000000 | bytes 100000 | tf_op jit(solution)/shard_map/ffn_out/pallas_call | solution.py:169
  162.0 6.5 %collective-permute-done.19.refs_4_ = bf16[4,576,128]{2,1,0:T(8,128)(2,1)S(1)} collective-permute-done((bf16[4,576,128]{2,1,0:T(8,128)(2,1)S(1)}, bf16[4,576,128]{2,1,0:T(8,128)(2,1)S(1)}, u32[]{:S(2)}, u32[]{:S(2)}) %collective-permute-start.19) | collective-permute-done | bytes 589856 | tf_op jit(solution)/shard_map/ppermute | solution.py:1017
  168.6 1.5 collective-permute-done.18.refs_2_
  174.0 2.9 %head_product.1 = (f32[512,768]{1,0:T(8,128)S(1)}, bf16[512,768]{1,0:T(8,128)(2,1)}) custom-call(s32[4]{0:T(128)S(1)} %pad_add_fusion.refs_0_, bf16[256,1024]{1,0:T(8,128)(2,1)S(1)} %copy-done.22, bf16[256,1024]{1,0:T(8,128)(2,1)S(1)} %copy-done.16, bf16[4,4,192,128]{3,2,1,0:T(8,128)(2,1)S(1)} %bitcast.17, ...), custom_call_target="tpu_custom_call" | custom-call | flops 1000000 | bytes 100000 | tf_op jit(solution)/shard_map/head_product/pallas_call | solution.py:169
  177.0 3.8 %all-to-all-start.4 = ((bf16[4,4,192,128]{3,2,1,0:T(8,128)(2,1)}), bf16[4,4,192,128]{3,2,1,0:T(8,128)(2,1)S(1)}, u32[]{:S(2)}, u32[]{:S(2)}) async-start(bf16[4,4,192,128]{3,2,1,0:T(8,128)(2,1)} %turn.1.refs_3_), calls=%async_computation.4 | async-start | bytes 1572864 | tf_op jit(solution)/shard_map/all_to_all | solution.py:1033
  180.7 1.5 collective-permute-start.23
  182.2 2.0 head_split.1
  185.4 6.4 %all-to-all-done.4 = bf16[4,4,192,128]{3,2,1,0:T(8,128)(2,1)S(1)} async-done(((bf16[4,4,192,128]{3,2,1,0:T(8,128)(2,1)}), bf16[4,4,192,128]{3,2,1,0:T(8,128)(2,1)S(1)}, u32[]{:S(2)}, u32[]{:S(2)}) %all-to-all-start.4) | async-done | bytes 786464 | tf_op jit(solution)/shard_map/all_to_all | solution.py:1033
  192.9 5.7 %latent_back.1.refs_3_ = bf16[128,1024]{1,0:T(8,128)(2,1)} custom-call(bf16[16,192,128]{2,1,0:T(8,128)(2,1)S(1)} %bitcast.18, f32[128,1024]{1,0:T(8,128)S(1)} %copy-done.39, bf16[128,1024]{1,0:T(8,128)(2,1)S(1)} %copy-done.14, f32[1,1024]{1,0:T(1,128)S(1)} %bitcast.23, bf16[1024,1024]{1,0:T(8,128)(2,1)} %wq_ref.1, bf16[1024,1024]{1,0:T(8,128)(2,1)} %wk_ref.1, ...), custom_call_target="tpu_custom_call" | custom-call | flops 1000000 | bytes 100000 | tf_op jit(solution)/shard_map/latent_back/pallas_call | solution.py:169
  199.7 1.2 cross.4
  200.9 4.0 %collective-permute-done.22.refs_2_ = bf16[256,768]{1,0:T(8,128)(2,1)S(1)} collective-permute-done((bf16[256,768]{1,0:T(8,128)(2,1)}, bf16[256,768]{1,0:T(8,128)(2,1)S(1)}, u32[]{:S(2)}, u32[]{:S(2)}) %collective-permute-start.22) | collective-permute-done | bytes 393248 | tf_op jit(solution)/shard_map/ppermute | solution.py:1025
  205.9 2.4 collective-permute-start.24
  208.4 1.9 collective-permute-start.26
  210.4 21.3 %collective-permute-done.24.refs_1_ = bf16[128,768]{1,0:T(8,128)(2,1)S(1)} collective-permute-done((bf16[128,768]{1,0:T(8,128)(2,1)S(1)}, bf16[128,768]{1,0:T(8,128)(2,1)S(1)}, u32[]{:S(2)}, u32[]{:S(2)}) %collective-permute-start.24) | collective-permute-done | bytes 196640 | tf_op jit(solution)/shard_map/ppermute | solution.py:1025
  232.4 4.2 %all-to-all-start.5 = ((bf16[4,32,768]{2,1,0:T(8,128)(2,1)}), bf16[4,32,768]{2,1,0:T(8,128)(2,1)}, u32[]{:S(2)}, u32[]{:S(2)}) async-start(bf16[4,32,768]{2,1,0:T(8,128)(2,1)} %head_end.1), calls=%async_computation.5 | async-start | bytes 393216 | tf_op jit(solution)/shard_map/all_to_all | solution.py:1033
  238.5 2.5 all-to-all-done.5.in_ref
  241.0 2.5 %head_rows.1 = (f32[32,1024]{1,0:T(8,128)}, f32[32,1024]{1,0:T(8,128)}, f32[32,1024]{1,0:T(8,128)}, f32[1,32]{1,0:T(1,128)}) custom-call(s32[2]{0:T(128)} %pad_add_fusion.1.at_ref, bf16[4,32,768]{2,1,0:T(8,128)(2,1)} %all-to-all-done.5.in_ref, f32[32,32]{1,0:T(8,128)} %reshape.90.gain_ref, bf16[1024,1024]{1,0:T(8,128)(2,1)} %wq_ref.1, ...), custom_call_target="tpu_custom_call" | custom-call | flops 1000000 | bytes 100000 | tf_op jit(solution)/shard_map/head_rows/pallas_call | solution.py:993
  244.5 1.5 unpack.1
  245.9 1.9 add_convert_fusion
  248.5 2.8 %finish.1 = (f32[32,2816]{1,0:T(8,128)}, f32[32,2816]{1,0:T(8,128)}, f32[1,32]{1,0:T(1,128)}) custom-call(s32[2]{0:T(128)} %pad_add_fusion.1.at_ref, f32[2,32,1408]{2,1,0:T(8,128)} %copy-done.44, bf16[2,32,1408]{2,1,0:T(8,128)(2,1)} %copy-done.67, f32[32,32]{1,0:T(8,128)} %reshape.92.gain_ref, bf16[1024,2816]{1,0:T(8,128)(2,1)} %wg_ref.1, ...), custom_call_target="tpu_custom_call" | custom-call | flops 1000000 | bytes 100000 | tf_op jit(solution)/shard_map/finish/pallas_call | solution.py:850
  (201 shorter events, 42.2 us)
Async XLA Ops:
  6.7 28.1 %all-to-all-start = ((bf16[16,192,128]{2,1,0:T(8,128)(2,1)}), bf16[16,192,128]{2,1,0:T(8,128)(2,1)S(1)}, u32[]{:S(2)}, u32[]{:S(2)}) async-start(bf16[16,192,128]{2,1,0:T(8,128)(2,1)} %get-tuple-element.74), calls=%async_computation | async-start | bytes 1572864 | tf_op jit(solution)/shard_map/all_to_all | solution.py:1037
  13.9 1.6 collective-permute-start
  13.9 37.9 %collective-permute-start.4 = (bf16[128,1024]{1,0:T(8,128)(2,1)S(1)}, bf16[128,1024]{1,0:T(8,128)(2,1)}, u32[]{:S(2)}, u32[]{:S(2)}) collective-permute-start(bf16[128,1024]{1,0:T(8,128)(2,1)S(1)} %get-tuple-element.78), channel_id=1, source_target_pairs={{0,1},{1,0},{2,3},{3,2},{4,5},{5,4},{6,7},{7,6},{8,9},{9,8},{10,11... | collective-permute-start | bytes 786440 | tf_op jit(solution)/shard_map/ppermute | solution.py:1017
  15.5 45.6 %copy-start.13 = (bf16[128,1024]{1,0:T(8,128)(2,1)S(1)}, bf16[128,1024]{1,0:T(8,128)(2,1)}, u32[]{:S(2)}) copy-start(bf16[128,1024]{1,0:T(8,128)(2,1)} %refs_2_.7) | copy-start | bytes 786436
  15.5 45.6 %copy-start.56 = (f32[1024]{0:T(1024)S(1)}, f32[1024]{0:T(1024)}, u32[]{:S(2)}) copy-start(f32[1024]{0:T(1024)} %param.19) | copy-start | bytes 12292
  15.5 19.2 %collective-permute-start.1 = (bf16[256,512]{1,0:T(8,128)(2,1)S(1)}, bf16[256,512]{1,0:T(8,128)(2,1)S(1)}, u32[]{:S(2)}, u32[]{:S(2)}) collective-permute-start(bf16[256,512]{1,0:T(8,128)(2,1)S(1)} %pad_maximum_fusion), channel_id=1, source_target_pairs={{0,1},{1,0},{2,3},{3,2},{4,5},{5,4},{6,7},{7,6},{8,9},{9,8},{10,11... | collective-permute-start | bytes 786440 | tf_op jit(solution)/shard_map/ppermute | solution.py:1017
  16.5 18.3 %collective-permute-start.2 = (bf16[256,512]{1,0:T(8,128)(2,1)S(1)}, bf16[256,512]{1,0:T(8,128)(2,1)S(1)}, u32[]{:S(2)}, u32[]{:S(2)}) collective-permute-start(bf16[256,512]{1,0:T(8,128)(2,1)S(1)} %pad_maximum_fusion.1), channel_id=1, source_target_pairs={{0,2},{1,3},{2,0},{3,1},{4,6},{5,7},{6,4},{7,5},{8,10},{9,11},{10,... | collective-permute-start | bytes 786440 | tf_op jit(solution)/shard_map/ppermute | solution.py:1021
  34.8 17.0 %copy-start.25 = (bf16[256,512]{1,0:T(8,128)(2,1)}, bf16[256,512]{1,0:T(8,128)(2,1)S(1)}, u32[]{:S(2)}) copy-start(bf16[256,512]{1,0:T(8,128)(2,1)S(1)} %collective-permute-done.1.refs_5_) | copy-start | bytes 786436
  34.8 17.0 %copy-start.27 = (bf16[256,512]{1,0:T(8,128)(2,1)}, bf16[256,512]{1,0:T(8,128)(2,1)S(1)}, u32[]{:S(2)}) copy-start(bf16[256,512]{1,0:T(8,128)(2,1)S(1)} %collective-permute-done.2.refs_6_.refs_5_) | copy-start | bytes 786436
  45.2 15.9 %all-to-all-start.1 = ((bf16[16,64,128]{2,1,0:T(8,128)(2,1)}), bf16[16,64,128]{2,1,0:T(8,128)(2,1)S(1)}, u32[]{:S(2)}, u32[]{:S(2)}) async-start(bf16[16,64,128]{2,1,0:T(8,128)(2,1)} %get-tuple-element.75), calls=%async_computation.1 | async-start | bytes 524288 | tf_op jit(solution)/shard_map/all_to_all | solution.py:1037
  52.8 25.6 %copy-start.21 = (bf16[256,1024]{1,0:T(8,128)(2,1)}, bf16[256,1024]{1,0:T(8,128)(2,1)S(1)}, u32[]{:S(2)}) copy-start(bf16[256,1024]{1,0:T(8,128)(2,1)S(1)} %constant_dynamic-update-slice_fusion.refs_1_) | copy-start | bytes 1572868
  52.8 16.4 %collective-permute-start.5 = (bf16[256,1024]{1,0:T(8,128)(2,1)S(1)}, bf16[256,1024]{1,0:T(8,128)(2,1)S(1)}, u32[]{:S(2)}, u32[]{:S(2)}) collective-permute-start(bf16[256,1024]{1,0:T(8,128)(2,1)S(1)} %constant_dynamic-update-slice_fusion.refs_1_), channel_id=1, source_target_pairs={{0,2},{1,3},{2,0},{3,1},{4,6},{5,7},{6,4},{7,5},{8,10},{9,11},{10,... | collective-permute-start | bytes 1572872 | tf_op jit(solution)/shard_map/ppermute | solution.py:1021
  63.8 19.4 %copy-start.17 = (f32[128,1024]{1,0:T(8,128)}, f32[128,1024]{1,0:T(8,128)S(1)}, u32[]{:S(2)}) copy-start(f32[128,1024]{1,0:T(8,128)S(1)} %get-tuple-element.76.refs_2_) | copy-start | bytes 1572868
  63.8 5.5 %collective-permute-start.3 = (bf16[128,1024]{1,0:T(8,128)(2,1)S(1)}, bf16[128,1024]{1,0:T(8,128)(2,1)S(1)}, u32[]{:S(2)}, u32[]{:S(2)}) collective-permute-start(bf16[128,1024]{1,0:T(8,128)(2,1)S(1)} %get-tuple-element.77.refs_1_), channel_id=1, source_target_pairs={{0,16},{16,0},{1,17},{17,1},{2,18},{18,2},{3,19},{19,3},{4,20},{20... | collective-permute-start | bytes 786440 | tf_op jit(solution)/shard_map/ppermute | solution.py:1013
  80.1 25.6 %collective-permute-start.6 = (bf16[3584,128]{1,0:T(8,128)(2,1)}, bf16[3584,128]{1,0:T(8,128)(2,1)S(1)}, u32[]{:S(2)}, u32[]{:S(2)}) collective-permute-start(bf16[3584,128]{1,0:T(8,128)(2,1)} %get-tuple-element.81.refs_1_), channel_id=1, source_target_pairs={{0,1},{1,0},{2,3},{3,2},{4,5},{5,4},{6,7},{7,6},{8,9},{9,8},{10,11... | collective-permute-start | bytes 2752520 | tf_op jit(solution)/shard_map/ppermute | solution.py:1017
  80.8 29.7 %collective-permute-start.11 = (bf16[3584,128]{1,0:T(8,128)(2,1)}, bf16[3584,128]{1,0:T(8,128)(2,1)S(1)}, u32[]{:S(2)}, u32[]{:S(2)}) collective-permute-start(bf16[3584,128]{1,0:T(8,128)(2,1)} %get-tuple-element.90.refs_1_), channel_id=1, source_target_pairs={{0,2},{1,3},{2,0},{3,1},{4,6},{5,7},{6,4},{7,5},{8,10},{9,11},{10,... | collective-permute-start | bytes 2752520 | tf_op jit(solution)/shard_map/ppermute | solution.py:1021
  81.7 1.5 collective-permute-start.8
  87.1 29.0 %all-to-all-start.2 = ((bf16[16,64,128]{2,1,0:T(8,128)(2,1)}), bf16[16,64,128]{2,1,0:T(8,128)(2,1)}, u32[]{:S(2)}, u32[]{:S(2)}) async-start(bf16[16,64,128]{2,1,0:T(8,128)(2,1)} %bitcast.21), calls=%async_computation.2 | async-start | bytes 524288 | tf_op jit(solution)/shard_map/all_to_all | solution.py:1037
  93.5 1.9 collective-permute-start.9
  93.5 1.9 collective-permute-start.7
  94.0 16.6 %copy-start.2 = (bf16[2560,128]{1,0:T(8,128)(2,1)S(1)}, bf16[2560,128]{1,0:T(8,128)(2,1)}, u32[]{:S(2)}) copy-start(bf16[2560,128]{1,0:T(8,128)(2,1)} %copy-done.1) | copy-start | bytes 1966084
  94.0 16.6 %copy-start.28 = (bf16[256,512]{1,0:T(8,128)(2,1)S(1)}, bf16[256,512]{1,0:T(8,128)(2,1)}, u32[]{:S(2)}) copy-start(bf16[256,512]{1,0:T(8,128)(2,1)} %copy-done.27) | copy-start | bytes 786436
  94.0 42.3 %collective-permute-start.15 = (bf16[1792,128]{1,0:T(8,128)(2,1)}, bf16[1792,128]{1,0:T(8,128)(2,1)}, u32[]{:S(2)}, u32[]{:S(2)}) collective-permute-start(bf16[1792,128]{1,0:T(8,128)(2,1)} %copy-done.42), channel_id=1, source_target_pairs={{0,1},{1,0},{2,3},{3,2},{4,5},{5,4},{6,7},{7,6},{8,9},{9,8},{10,11... | collective-permute-start | bytes 1376264 | tf_op jit(solution)/shard_map/ppermute | solution.py:1017
  114.5 38.1 %collective-permute-start.12 = (bf16[4,640,128]{2,1,0:T(8,128)(2,1)}, bf16[4,640,128]{2,1,0:T(8,128)(2,1)}, u32[]{:S(2)}, u32[]{:S(2)}) collective-permute-start(bf16[4,640,128]{2,1,0:T(8,128)(2,1)} %get-tuple-element.92), channel_id=1, source_target_pairs={{0,1},{1,0},{2,3},{3,2},{4,5},{5,4},{6,7},{7,6},{8,9},{9,8},{10,11... | collective-permute-start | bytes 1966088 | tf_op jit(solution)/shard_map/ppermute | solution.py:1017
  115.2 37.4 %collective-permute-start.10 = (bf16[4,640,128]{2,1,0:T(8,128)(2,1)}, bf16[4,640,128]{2,1,0:T(8,128)(2,1)}, u32[]{:S(2)}, u32[]{:S(2)}) collective-permute-start(bf16[4,640,128]{2,1,0:T(8,128)(2,1)} %get-tuple-element.88), channel_id=1, source_target_pairs={{0,2},{1,3},{2,0},{3,1},{4,6},{5,7},{6,4},{7,5},{8,10},{9,11},{10,... | collective-permute-start | bytes 1966088 | tf_op jit(solution)/shard_map/ppermute | solution.py:1021
  118.2 18.1 %copy-start.64 = (bf16[1024,128]{1,0:T(8,128)(2,1)S(1)}, bf16[1024,128]{1,0:T(8,128)(2,1)}, u32[]{:S(2)}) copy-start(bf16[1024,128]{1,0:T(8,128)(2,1)} %copy-done.63) | copy-start | bytes 786436
  118.2 24.1 %copy-start.30 = (bf16[1024,128]{1,0:T(8,128)(2,1)S(1)}, bf16[1024,128]{1,0:T(8,128)(2,1)}, u32[]{:S(2)}) copy-start(bf16[1024,128]{1,0:T(8,128)(2,1)} %copy-done.29) | copy-start | bytes 786436
  129.2 21.7 %copy-start.48 = (bf16[1024,128]{1,0:T(8,128)(2,1)S(1)}, bf16[1024,128]{1,0:T(8,128)(2,1)}, u32[]{:S(2)}) copy-start(bf16[1024,128]{1,0:T(8,128)(2,1)} %copy-done.47) | copy-start | bytes 786436
  129.2 43.2 %all-to-all-start.3 = ((bf16[16,192,128]{2,1,0:T(8,128)(2,1)}), bf16[16,192,128]{2,1,0:T(8,128)(2,1)S(1)}, u32[]{:S(2)}, u32[]{:S(2)}) async-start(bf16[16,192,128]{2,1,0:T(8,128)(2,1)} %attn_bwd.1.refs_6_), calls=%async_computation.3 | async-start | bytes 1572864 | tf_op jit(solution)/shard_map/all_to_all | solution.py:1033
  134.0 16.9 %copy-start.3 = (bf16[2560,128]{1,0:T(8,128)(2,1)S(1)}, bf16[2560,128]{1,0:T(8,128)(2,1)}, u32[]{:S(2)}) copy-start(bf16[2560,128]{1,0:T(8,128)(2,1)} %copy-done.1) | copy-start | bytes 1966084
  134.0 13.7 %collective-permute-start.13 = (bf16[1792,128]{1,0:T(8,128)(2,1)}, bf16[1792,128]{1,0:T(8,128)(2,1)S(1)}, u32[]{:S(2)}, u32[]{:S(2)}) collective-permute-start(bf16[1792,128]{1,0:T(8,128)(2,1)} %copy-done.40), channel_id=1, source_target_pairs={{0,2},{1,3},{2,0},{3,1},{4,6},{5,7},{6,4},{7,5},{8,10},{9,11},{10,... | collective-permute-start | bytes 1376264 | tf_op jit(solution)/shard_map/ppermute | solution.py:1021
  135.2 7.1 %collective-permute-start.16 = (bf16[1024,128]{1,0:T(8,128)(2,1)}, bf16[1024,128]{1,0:T(8,128)(2,1)S(1)}, u32[]{:S(2)}, u32[]{:S(2)}) collective-permute-start(bf16[1024,128]{1,0:T(8,128)(2,1)} %copy-done.65), channel_id=1, source_target_pairs={{0,1},{1,0},{2,3},{3,2},{4,5},{5,4},{6,7},{7,6},{8,9},{9,8},{10,11... | collective-permute-start | bytes 786440 | tf_op jit(solution)/shard_map/ppermute | solution.py:1017
  136.3 14.6 %collective-permute-start.14 = (bf16[1024,128]{1,0:T(8,128)(2,1)S(1)}, bf16[1024,128]{1,0:T(8,128)(2,1)S(1)}, u32[]{:S(2)}, u32[]{:S(2)}) collective-permute-start(bf16[1024,128]{1,0:T(8,128)(2,1)S(1)} %copy-done.64), channel_id=1, source_target_pairs={{0,2},{1,3},{2,0},{3,1},{4,6},{5,7},{6,4},{7,5},{8,10},{9,11},{10,... | collective-permute-start | bytes 786440 | tf_op jit(solution)/shard_map/ppermute | solution.py:1021
  155.1 18.3 %collective-permute-start.20 = (bf16[2560,128]{1,0:T(8,128)(2,1)}, bf16[2560,128]{1,0:T(8,128)(2,1)S(1)}, u32[]{:S(2)}, u32[]{:S(2)}) collective-permute-start(bf16[2560,128]{1,0:T(8,128)(2,1)} %get-tuple-element.112), channel_id=1, source_target_pairs={{0,4},{1,5},{2,6},{3,7},{4,0},{5,1},{6,2},{7,3},{8,12},{9,13},{10,... | collective-permute-start | bytes 1966088 | tf_op jit(solution)/shard_map/ppermute | solution.py:1025
  155.4 13.2 %collective-permute-start.19 = (bf16[4,576,128]{2,1,0:T(8,128)(2,1)S(1)}, bf16[4,576,128]{2,1,0:T(8,128)(2,1)S(1)}, u32[]{:S(2)}, u32[]{:S(2)}) collective-permute-start(bf16[4,576,128]{2,1,0:T(8,128)(2,1)S(1)} %get-tuple-element.108), channel_id=1, source_target_pairs={{0,1},{1,0},{2,3},{3,2},{4,5},{5,4},{6,7},{7,6},{8,9},{9,8},{10,11... | collective-permute-start | bytes 1769480 | tf_op jit(solution)/shard_map/ppermute | solution.py:1017
  157.1 12.9 %collective-permute-start.18 = (bf16[4,576,128]{2,1,0:T(8,128)(2,1)S(1)}, bf16[4,576,128]{2,1,0:T(8,128)(2,1)S(1)}, u32[]{:S(2)}, u32[]{:S(2)}) collective-permute-start(bf16[4,576,128]{2,1,0:T(8,128)(2,1)S(1)} %get-tuple-element.107), channel_id=1, source_target_pairs={{0,2},{1,3},{2,0},{3,1},{4,6},{5,7},{6,4},{7,5},{8,10},{9,11},{10,... | collective-permute-start | bytes 1769480 | tf_op jit(solution)/shard_map/ppermute | solution.py:1021
  176.9 5.3 %collective-permute-start.21 = (bf16[512,768]{1,0:T(8,128)(2,1)}, bf16[512,768]{1,0:T(8,128)(2,1)}, u32[]{:S(2)}, u32[]{:S(2)}) collective-permute-start(bf16[512,768]{1,0:T(8,128)(2,1)} %get-tuple-element.115), channel_id=1, source_target_pairs={{0,16},{16,0},{1,17},{17,1},{2,18},{18,2},{3,19},{19,3},{4,20},{20... | collective-permute-start | bytes 2359304 | tf_op jit(solution)/shard_map/ppermute | solution.py:1013
  177.0 14.9 %all-to-all-start.4 = ((bf16[4,4,192,128]{3,2,1,0:T(8,128)(2,1)}), bf16[4,4,192,128]{3,2,1,0:T(8,128)(2,1)S(1)}, u32[]{:S(2)}, u32[]{:S(2)}) async-start(bf16[4,4,192,128]{3,2,1,0:T(8,128)(2,1)} %turn.1.refs_3_), calls=%async_computation.4 | async-start | bytes 1572864 | tf_op jit(solution)/shard_map/all_to_all | solution.py:1033
  180.7 18.0 %collective-permute-start.23 = (bf16[2304,128]{1,0:T(8,128)(2,1)}, bf16[2304,128]{1,0:T(8,128)(2,1)}, u32[]{:S(2)}, u32[]{:S(2)}) collective-permute-start(bf16[2304,128]{1,0:T(8,128)(2,1)} %copy-done.58), channel_id=1, source_target_pairs={{0,4},{1,5},{2,6},{3,7},{4,0},{5,1},{6,2},{7,3},{8,12},{9,13},{10,... | collective-permute-start | bytes 1769480 | tf_op jit(solution)/shard_map/ppermute | solution.py:1025
  184.9 20.0 %collective-permute-start.22 = (bf16[256,768]{1,0:T(8,128)(2,1)}, bf16[256,768]{1,0:T(8,128)(2,1)S(1)}, u32[]{:S(2)}, u32[]{:S(2)}) collective-permute-start(bf16[256,768]{1,0:T(8,128)(2,1)} %get-tuple-element.118), channel_id=1, source_target_pairs={{0,4},{1,5},{2,6},{3,7},{4,0},{5,1},{6,2},{7,3},{8,12},{9,13},{10,... | collective-permute-start | bytes 1179656 | tf_op jit(solution)/shard_map/ppermute | solution.py:1025
  192.9 15.4 %copy-start.60 = (bf16[1280,128]{1,0:T(8,128)(2,1)S(1)}, bf16[1280,128]{1,0:T(8,128)(2,1)}, u32[]{:S(2)}) copy-start(bf16[1280,128]{1,0:T(8,128)(2,1)} %copy-done.59) | copy-start | bytes 983044
  192.9 17.4 %copy-start.62 = (bf16[128,1024]{1,0:T(8,128)(2,1)S(1)}, bf16[128,1024]{1,0:T(8,128)(2,1)}, u32[]{:S(2)}) copy-start(bf16[128,1024]{1,0:T(8,128)(2,1)} %copy-done.61) | copy-start | bytes 786436
  205.9 25.8 %collective-permute-start.24 = (bf16[128,768]{1,0:T(8,128)(2,1)S(1)}, bf16[128,768]{1,0:T(8,128)(2,1)S(1)}, u32[]{:S(2)}, u32[]{:S(2)}) collective-permute-start(bf16[128,768]{1,0:T(8,128)(2,1)S(1)} %get-tuple-element.123), channel_id=1, source_target_pairs={{0,12},{1,13},{2,14},{3,15},{4,8},{5,9},{6,10},{7,11},{8,4},{9,5},... | collective-permute-start | bytes 589832 | tf_op jit(solution)/shard_map/ppermute | solution.py:1025
  208.3 35.2 %collective-permute-start.25 = (bf16[1280,128]{1,0:T(8,128)(2,1)S(1)}, bf16[1280,128]{1,0:T(8,128)(2,1)S(1)}, u32[]{:S(2)}, u32[]{:S(2)}) collective-permute-start(bf16[1280,128]{1,0:T(8,128)(2,1)S(1)} %copy-done.60), channel_id=1, source_target_pairs={{0,12},{1,13},{2,14},{3,15},{4,8},{5,9},{6,10},{7,11},{8,4},{9,5},... | collective-permute-start | bytes 983048 | tf_op jit(solution)/shard_map/ppermute | solution.py:1025
  208.4 35.4 %collective-permute-start.26 = (bf16[1152,128]{1,0:T(8,128)(2,1)S(1)}, bf16[1152,128]{1,0:T(8,128)(2,1)S(1)}, u32[]{:S(2)}, u32[]{:S(2)}) collective-permute-start(bf16[1152,128]{1,0:T(8,128)(2,1)S(1)} %get-tuple-element.129), channel_id=1, source_target_pairs={{0,12},{1,13},{2,14},{3,15},{4,8},{5,9},{6,10},{7,11},{8,4},{9,5},... | collective-permute-start | bytes 884744 | tf_op jit(solution)/shard_map/ppermute | solution.py:1025
  210.4 35.5 %collective-permute-start.17 = (bf16[128,1024]{1,0:T(8,128)(2,1)S(1)}, bf16[128,1024]{1,0:T(8,128)(2,1)}, u32[]{:S(2)}, u32[]{:S(2)}) collective-permute-start(bf16[128,1024]{1,0:T(8,128)(2,1)S(1)} %copy-done.62), channel_id=1, source_target_pairs={{0,16},{16,0},{1,17},{17,1},{2,18},{18,2},{3,19},{19,3},{4,20},{20... | collective-permute-start | bytes 786440 | tf_op jit(solution)/shard_map/ppermute | solution.py:1013
  232.4 8.6 %all-to-all-start.5 = ((bf16[4,32,768]{2,1,0:T(8,128)(2,1)}), bf16[4,32,768]{2,1,0:T(8,128)(2,1)}, u32[]{:S(2)}, u32[]{:S(2)}) async-start(bf16[4,32,768]{2,1,0:T(8,128)(2,1)} %head_end.1), calls=%async_computation.5 | async-start | bytes 393216 | tf_op jit(solution)/shard_map/all_to_all | solution.py:1033
  245.9 1.9 collective-permute-start.27
  (56 other events, 229.8 us)

commit v4 on v3

--- a/solution.py
+++ b/solution.py
@@ -170,7 +170,7 @@
         body,
         in_specs=[SMEM] * smem + [VMEM] * (held - smem - far) + [HBM] * far + [ANY] * len(after),
         out_specs=[VMEM] * len(outs),
-        out_shape=[jax.ShapeDtypeStruct(*o) for o in outs],
+        out_shape=[pltpu.HBM(*o[:2]) if len(o) > 2 else jax.ShapeDtypeStruct(*o) for o in outs],
         scratch_shapes=list(scratch),
         cost_estimate=COST,
         compiler_params=pltpu.CompilerParams(vmem_limit_bytes=vmem * 2**20),
@@ -451,12 +451,13 @@
     n_ref[...] = (resid * inv * gain_ref[...]).astype(BF16)
 
 
-def out_norm(at, ab, x, gain, w):
+def out_norm(at, ab, x, gain, w, after):
     rows, width = x.shape
     return call(
         out_norm_kernel,
         "out_norm",
         (at, ab, x, gain.reshape(1, width), w),
+        after,
         smem=1,
         outs=[((rows, width), F32), ((rows, width), BF16), ((width // 2, rows), BF16)],
         scratch=[pltpu.VMEM(w.shape, BF16), pltpu.SemaphoreType.DMA],
@@ -564,7 +565,8 @@
         after,
         smem=1,
         outs=[((2 * rows, share), BF16), ((rows, width), F32), ((rows, width), BF16)]
-        + [((n, rows), BF16) for n in sizes],
+        + [((n, rows), BF16) for n in sizes[:4]]
+        + [((n, rows), BF16, HBM) for n in sizes[4:]],
         scratch=[
             pltpu.VMEM((2 * rows, width), BF16),
             pltpu.VMEM((2 * rows, width), BF16),
@@ -787,60 +789,85 @@
     sum_ref[...] = total
 
 
-def unpack_kernel(at_ref, a0, a1, b0, b1, down_ref, mine_ref, theirs_ref, out_ref, a_ref, b_ref):
-    add_lines((a0, a1), a_ref)
-    add_lines((b0, b1), b_ref)
-    rows = a0.shape[1]
-    _, own, wide = mine_ref.shape
+def shares(ref, at, own, dp, mine_ref, theirs_ref, part, t):
+    rows = ref.shape[1]
+    lanes = slice(t * rows, (t + 1) * rows)
+    mine_ref[part, :, lanes] = ref[pl.ds(pl.multiple_of(at + dp * own, own), own), :]
+    theirs_ref[part, :, lanes] = ref[pl.ds(pl.multiple_of(at + (1 - dp) * own, own), own), :].astype(BF16)
+
+
+def unpack_one_kernel(at_ref, i0, i1, down_ref, mine_ref, theirs_ref, sum_ref):
+    add_lines((i0, i1), sum_ref)
+    rows = i0.shape[1]
+    own = mine_ref.shape[1]
     chunk, width = down_ref.shape
     padded = -(-chunk // 16) * 16
     count = width // 2 // rows
-    dp = at_ref[0]
     for part in range(2):
-        base = part * (a0.shape[0] // 2)
+        base = part * (i0.shape[0] // 2)
         for j in range(count):
             lanes = slice((part * count + j) * rows, (part * count + j + 1) * rows)
-            down_ref[:, lanes] = a_ref[base + j * padded : base + j * padded + chunk, :]
-        for t in range(wide // rows):
-            ref, at = a_ref, base + count * padded + t * 2 * own
-            if t >= EARLY:
-                ref, at = b_ref, part * (b0.shape[0] // 2) + (t - EARLY) * 2 * own
-            lanes = slice(t * rows, (t + 1) * rows)
-            mine_ref[part, :, lanes] = ref[pl.ds(pl.multiple_of(at + dp * own, own), own), :]
-            theirs_ref[part, :, lanes] = ref[pl.ds(pl.multiple_of(at + (1 - dp) * own, own), own), :].astype(BF16)
-        base = part * (b0.shape[0] // 2) + (wide // rows - EARLY) * 2 * own
+            down_ref[:, lanes] = sum_ref[base + j * padded : base + j * padded + chunk, :]
+        for t in range(EARLY):
+            shares(sum_ref, base + count * padded + t * 2 * own, own, at_ref[0], mine_ref, theirs_ref, part, t)
+
+
+def unpack_one(at, v, own, chunk, width, after):
+    wide = EARLY * v[0].shape[1]
+    outs = [((chunk, width), F32), ((2, own, wide), F32), ((2, own, wide), BF16)]
+    scratch = [pltpu.VMEM(v[0].shape, F32)]
+    return call(unpack_one_kernel, "unpack_one", (at, *v), after, smem=1, outs=outs, scratch=scratch)
+
+
+def unpack_two_kernel(at_ref, i0, i1, mine_ref, theirs_ref, out_ref, sum_ref):
+    add_lines((i0, i1), sum_ref)
+    rows = i0.shape[1]
+    own, width = out_ref.shape
+    tiles = mine_ref.shape[2] // rows
+    count = width // 2 // rows
+    for part in range(2):
+        base = part * (i0.shape[0] // 2)
+        for t in range(tiles):
+            shares(sum_ref, base + t * 2 * own, own, at_ref[0], mine_ref, theirs_ref, part, t)
+        base += tiles * 2 * own
         for j in range(count):
             lanes = slice((part * count + j) * rows, (part * count + j + 1) * rows)
-            out_ref[:, lanes] = b_ref[base + j * own : base + (j + 1) * own, :]
-
-
-def unpack(at, v, own, wide, chunk, width, after):
-    outs = [((chunk, width), F32), ((2, own, wide), F32), ((2, own, wide), BF16), ((own, width), F32)]
-    scratch = [pltpu.VMEM(v[0].shape, F32), pltpu.VMEM(v[2].shape, F32)]
-    return call(unpack_kernel, "unpack", (at, *v), after, smem=1, outs=outs, scratch=scratch)
-
-
-def finish_kernel(at_ref, mine, theirs, gain_ref, wg_ref, wu_ref, gate_ref, up_ref, dots_ref):
+            out_ref[:, lanes] = sum_ref[base + j * own : base + (j + 1) * own, :]
+
+
+def unpack_two(at, v, own, wide, width, after):
+    wide -= EARLY * v[0].shape[1]
+    outs = [((2, own, wide), F32), ((2, own, wide), BF16), ((own, width), F32)]
+    scratch = [pltpu.VMEM(v[0].shape, F32)]
+    return call(unpack_two_kernel, "unpack_two", (at, *v), after, smem=1, outs=outs, scratch=scratch)
+
+
+def finish_kernel(at_ref, m0, m1, o0, o1, gain_ref, wg_ref, wu_ref, gate_ref, up_ref, dots_ref):
     dp = at_ref[1]
     share = gate_ref.shape[1] // 2
+    early = m0.shape[2]
     for part, ref in enumerate((gate_ref, up_ref)):
+
+        def put(at, a, b):
+            ref[:, at : at + early] = a[part].astype(F32)
+            ref[:, at + early : at + share] = b[part].astype(F32)
 
         @pl.when(dp == 0)
         def _():
-            ref[:, :share] = mine[part]
-            ref[:, share:] = theirs[part].astype(F32)
+            put(0, m0, m1)
+            put(share, o0, o1)
 
         @pl.when(dp == 1)
         def _():
-            ref[:, :share] = theirs[part].astype(F32)
-            ref[:, share:] = mine[part]
+            put(0, o0, o1)
+            put(share, m0, m1)
 
     total = gate_ref[...] * wg_ref[...].astype(F32) + up_ref[...] * wu_ref[...].astype(F32)
     dots_ref[...] = by_gain(jnp.sum(total, axis=1, keepdims=True), gain_ref, at_ref[0])
 
 
 def finish(where, mine, theirs, gain, wg, wu):
-    own, ff = mine.shape[1], wg.shape[1]
+    own, ff = mine[0].shape[1], wg.shape[1]
     count = wg.shape[0] // own
 
     def whole(*shape):
@@ -852,13 +879,13 @@
         grid_spec=pltpu.PrefetchScalarGridSpec(
             num_scalar_prefetch=1,
             grid=(1,),
-            in_specs=[whole(*mine.shape), whole(*theirs.shape), whole(count, own), weight, weight],
+            in_specs=[whole(*v.shape) for v in (*mine, *theirs)] + [whole(count, own), weight, weight],
             out_specs=[whole(own, ff), whole(own, ff), whole(1, own)],
         ),
         out_shape=[jax.ShapeDtypeStruct((own, ff), F32)] * 2 + [jax.ShapeDtypeStruct((1, own), F32)],
         cost_estimate=COST,
         name="finish",
-    )(where, mine, theirs, gain.reshape(count, own), in_hbm(wg), in_hbm(wu))
+    )(where, *mine, *theirs, gain.reshape(count, own), in_hbm(wg), in_hbm(wu))
     return gate, up, dots.reshape(own)
 
 
@@ -1070,12 +1097,12 @@
     line = (line, over_y(line))
     out, full, top, inv = attn_fwd(1, scalars, qkv, (dy_x, dy_y))
     attn_t = to_ctx(out).reshape(width, rows)
-    resid, normed_two, attn_send = out_norm(at, attn_t, latent_in, gain_ffn, w_out)
+    resid, normed_two, attn_send = out_norm(at, attn_t, latent_in, gain_ffn, w_out, (line[1],))
     normed_mate = swap(normed_two)
     attn_mate = swap(attn_send)
 
     hid, d_own, d_mate, send_x, send_y, tiles_x, tiles_y, kept_x, kept_y = ffn(
-        at, normed_two, normed_mate, cotangent, dy_mate, w_gate, w_up, w_down, (line[1],)
+        at, normed_two, normed_mate, cotangent, dy_mate, w_gate, w_up, w_down, ()
     )
     d_got = swap(d_mate)
     got_x, got_y = over_x(send_x), over_y(send_y)
@@ -1089,7 +1116,9 @@
     one_a, other_a = first_product(0, kept_x, send_x, got_x, dy_a, (out_x[0],))
     one_b, other_b = first_product(1, kept_y, send_y, got_y, dy_b, (one_a,))
     one = (one_a, over_y(other_a), one_b, over_x(other_b))
-    grad_qkv = attn_bwd(1, lambda slot: slot, scalars, qkv, grad_attn, full, top, inv, (one_b,))
+    grad_qkv = attn_bwd(
+        1, lambda slot: slot, scalars, qkv, grad_attn, full, top, inv, (one_b, tiles_x[1], tiles_y[1], out_x[1], out_y[1])
+    )
     four = in_group(grad_qkv, Z_LINES).reshape(4, 4, 3 * HEAD_DIM, rows)
     two_a, other_a = second_product(width, kept_x, got_x, tiles_x, out_x, (grad_qkv,))
     two_b, other_b = second_product(width, kept_y, got_y, tiles_y, out_y, (two_a,))
@@ -1107,16 +1136,22 @@
     head_mine, head_theirs = head_product(at, line, four, (one_own,))
     head_own, head_far, head_send = head_split(at, head_mine, swap(head_theirs), ())
     head_got = over_z(head_send, 1)
-    latent_grad = latent_back(back, dres, latent_in, gain_attn, w_query, w_key, w_value, (head_own,))
-    two_own, two_send = cross(two_own, two_far, two_got, (latent_grad,))
-    head_own, head_send = cross(head_own, head_far, head_got, (two_own,))
+    down_sum, mine0, theirs0 = unpack_one(
+        at, (one_own, over_z(one_send, 3)), own, ff // 32, width, (head_own,)
+    )
+    two_own, two_send = cross(two_own, two_far, two_got, (down_sum,))
+    latent_grad = latent_back(back, dres, latent_in, gain_attn, w_query, w_key, w_value, (two_own,))
+    head_own, head_send = cross(head_own, head_far, head_got, (latent_grad,))
     heads = head_end(head_own, over_z(head_send, 3), ())
     heads = in_group(heads, PLANES)
     place = dp * 16 + ctx
     where = jnp.stack([place, dp]).astype(jnp.int32)
-    query_sum, key_sum, value_sum, gain_attn_sum = head_rows(where, heads, gain_attn, w_query, w_key, w_value)
-    down_sum, mine, theirs, out_sum = unpack(at, (one_own, over_z(one_send, 3), two_own, over_z(two_send, 3)), own, ff // 2, ff // 32, width, (gain_attn_sum,))
-    gate_sum, up_sum, gain_ffn_sum = finish(where, mine, swap(theirs), gain_ffn, w_gate, w_up)
+    mine1, theirs1, out_sum = unpack_two(at, (two_own, over_z(two_send, 3)), own, ff // 2, width, (head_own,))
+    theirs = (swap(theirs0), swap(theirs1))
+    query_sum, key_sum, value_sum, gain_attn_sum = head_rows(
+        where, order(heads, (out_sum,)), gain_attn, w_query, w_key, w_value
+    )
+    gate_sum, up_sum, gain_ffn_sum = finish(where, (mine0, mine1), theirs, gain_ffn, w_gate, w_up)
     return (
         latents,
         latent_grad,

time: 254 us -> 234 us (0.921)
  waiting for transfers between devices: 89.7 us -> 59.9 us
  starting transfers between devices: 54.9 us -> 63.1 us
  Pallas kernels: 75.6 us -> 81.3 us
    ppermute x7, waiting for transfers between devices: 34 us -> 21.7 us  [over_x(): return lax.ppermute(v, 'ctx', X_PAIRS)]
    ppermute x6, waiting for transfers between devices: 25.6 us -> 13.3 us  [over_z(): return lax.ppermute(v, 'ctx', [(i, i ^ 4 * k) for i in range(16)])]
    all_to_all x3, waiting for transfers between devices: 8.92 us -> 0.01 us  [in_group(): return lax.all_to_all(v, 'ctx', 0, 0, tiled=True, axis_index_groups=groups)]
    ppermute x6, starting transfers between devices: 6.76 us -> 14.1 us  [over_z(): return lax.ppermute(v, 'ctx', [(i, i ^ 4 * k) for i in range(16)])]
    pallas_call x23 -> x24, Pallas kernels: 70.3 us -> 75.9 us  [call(): pl.pallas_call(body, in_specs=[SMEM] * smem + [VMEM] * (held - smem - far...]
  transfers between devices with their start and end apart: 34 -> 35, of which waited for: 17 -> 13; matrix products, arithmetic and copies ran while one was open for 2% -> 2% of each run, Pallas kernels for 22% -> 25%
where the time goes in v4:
time: 234 us; the launch traced here: 233 us
  Pallas kernels  81.3 us (35%)
  starting transfers between devices  63.1 us (27%)
  waiting for transfers between devices  59.9 us (26%)
  local copies, waits for them, and re-layouts  25 us (11%)
  other arithmetic  2.85 us (1%)
    pallas_call x24, Pallas kernels, call(): pl.pallas_call(body, in_specs=[SMEM] * smem + [VMEM] * (held - smem - far...  75.9 us
    unnamed x141, local copies, waits for them, and re-layouts  23.6 us
    ppermute x7, waiting for transfers between devices, over_x(): return lax.ppermute(v, 'ctx', X_PAIRS)  21.7 us
    all_to_all x3, starting transfers between devices, to_ctx(): return lax.all_to_all(v, 'ctx', 0, 0, tiled=True)  19.3 us
    ppermute x6, starting transfers between devices, over_z(): return lax.ppermute(v, 'ctx', [(i, i ^ 4 * k) for i in range(16)])  14.1 us
    ppermute x7, waiting for transfers between devices, over_y(): return lax.ppermute(v, 'ctx', Y_PAIRS)  13.9 us
    ppermute x6, waiting for transfers between devices, over_z(): return lax.ppermute(v, 'ctx', [(i, i ^ 4 * k) for i in range(16)])  13.3 us
    all_to_all x3, starting transfers between devices, in_group(): return lax.all_to_all(v, 'ctx', 0, 0, tiled=True, axis_index_groups=groups)  13 us
  transfers between devices with their start and end apart: 35, of which 13 were waited for; matrix products, arithmetic and copies ran while one was open for 2% of the time, Pallas kernels for 25%

profile of v4, /device:TPU:10, one launch (start us, length us, event | category | flops | bytes accessed | tf_op | source)
XLA Modules:
  0.0 233.4 jit_solution(14971559443032559817)
XLA Ops:
  2.3 4.4 %norm_qkv.1 = (bf16[128,1024]{1,0:T(8,128)(2,1)S(1)}, bf16[16,192,128]{2,1,0:T(8,128)(2,1)}) custom-call(bf16[128,1024]{1,0:T(8,128)(2,1)S(1)} %copy-done.10, f32[1,1024]{1,0:T(1,128)S(1)} %bitcast.22, bf16[1024,1024]{1,0:T(8,128)(2,1)} %wq_ref.1, bf16[1024,1024]{1,0:T(8,128)(2,1)} %wk_ref.1, bf16[1024,1024]{1,0:T(8,128)(2,1)} %wv_ref.1), custom_call_target="tpu_custom_call" | custom-call | flops 1000000 | bytes 100000 | tf_op jit(solution)/shard_map/norm_qkv/pallas_call | solution.py:169
  6.7 7.2 %all-to-all-start = ((bf16[16,192,128]{2,1,0:T(8,128)(2,1)}), bf16[16,192,128]{2,1,0:T(8,128)(2,1)S(1)}, u32[]{:S(2)}, u32[]{:S(2)}) async-start(bf16[16,192,128]{2,1,0:T(8,128)(2,1)} %get-tuple-element.76), calls=%async_computation | async-start | bytes 1572864 | tf_op jit(solution)/shard_map/all_to_all | solution.py:1064
  16.5 1.5 collective-permute-start.2
  18.1 8.2 %collective-permute-done.3 = bf16[128,1024]{1,0:T(8,128)(2,1)S(1)} collective-permute-done((bf16[128,1024]{1,0:T(8,128)(2,1)S(1)}, bf16[128,1024]{1,0:T(8,128)(2,1)S(1)}, u32[]{:S(2)}, u32[]{:S(2)}) %collective-permute-start.3) | collective-permute-done | bytes 262176 | tf_op jit(solution)/shard_map/ppermute | solution.py:1044
  26.3 2.4 %collective-permute-start.4 = (bf16[256,1024]{1,0:T(8,128)(2,1)S(1)}, bf16[256,1024]{1,0:T(8,128)(2,1)S(1)}, u32[]{:S(2)}, u32[]{:S(2)}) collective-permute-start(bf16[256,1024]{1,0:T(8,128)(2,1)S(1)} %constant_dynamic-update-slice_fusion.refs_1_), channel_id=1, source_target_pairs={{0,2},{1,3},{2,0},{3,1},{4,6},{5,7},{6,4},{7,5},{8,10},{9,11},{10,... | collective-permute-start | bytes 1572872 | tf_op jit(solution)/shard_map/ppermute | solution.py:1048
  28.8 5.9 %collective-permute-done.1.refs_5_ = bf16[256,512]{1,0:T(8,128)(2,1)S(1)} collective-permute-done((bf16[256,512]{1,0:T(8,128)(2,1)S(1)}, bf16[256,512]{1,0:T(8,128)(2,1)S(1)}, u32[]{:S(2)}, u32[]{:S(2)}) %collective-permute-start.1) | collective-permute-done | bytes 262176 | tf_op jit(solution)/shard_map/ppermute | solution.py:1044
  34.8 8.9 %attn_fwd.1 = (bf16[16,64,128]{2,1,0:T(8,128)(2,1)S(1)}, f32[16,64,128]{2,1,0:T(8,128)S(1)}, f32[8,1,256]{2,1,0:T(1,128)S(1)}, f32[8,1,256]{2,1,0:T(1,128)S(1)}) custom-call(s32[16]{0:T(128)S(1)} %select_reduce_fusion.refs_0_, s32[8]{0:T(128)S(1)} %and_select_fusion.refs_1_, s32[4]{0:T(128)S(1)} %bitcast.27, s32[1]{0:T(128)} %constant.70.clone.1.refs_3_, ...), custom_call_target="tpu_custom_call" | custom-call | flops 1000000 | bytes 100000 | tf_op jit(solution)/shard_map/attn_fwd/pallas_call | solution.py:169
  45.9 6.6 %all-to-all-start.1 = ((bf16[16,64,128]{2,1,0:T(8,128)(2,1)}), bf16[16,64,128]{2,1,0:T(8,128)(2,1)S(1)}, u32[]{:S(2)}, u32[]{:S(2)}) async-start(bf16[16,64,128]{2,1,0:T(8,128)(2,1)} %copy-done.46), calls=%async_computation.1 | async-start | bytes 524288 | tf_op jit(solution)/shard_map/all_to_all | solution.py:1064
  52.5 8.8 %all-to-all-done.1 = bf16[16,64,128]{2,1,0:T(8,128)(2,1)S(1)} async-done(((bf16[16,64,128]{2,1,0:T(8,128)(2,1)}), bf16[16,64,128]{2,1,0:T(8,128)(2,1)S(1)}, u32[]{:S(2)}, u32[]{:S(2)}) %all-to-all-start.1) | async-done | bytes 262176 | tf_op jit(solution)/shard_map/all_to_all | solution.py:1064
  61.3 2.8 %out_norm.1 = (f32[128,1024]{1,0:T(8,128)S(1)}, bf16[128,1024]{1,0:T(8,128)(2,1)S(1)}, bf16[512,128]{1,0:T(8,128)(2,1)}) custom-call(s32[4]{0:T(128)S(1)} %pad_add_fusion.refs_0_, bf16[1024,128]{1,0:T(8,128)(2,1)S(1)} %bitcast.19, bf16[128,1024]{1,0:T(8,128)(2,1)S(1)} %copy-done.11, f32[1,1024]{1,0:T(1,128)S(1)} %bitcast.24, bf16[1024,1024]{1,0:T(8,128)(2,1)} %refs_5_.4, ...), custom_call_target="tpu_custom_call" | custom-call | flops 1000000 | bytes 100000 | tf_op jit(solution)/shard_map/out_norm/pallas_call | solution.py:169
  64.2 1.5 collective-permute-done.5.refs_2_
  65.8 9.6 %ffn.1 = (bf16[256,1408]{1,0:T(8,128)(2,1)S(1)}, f32[128,1024]{1,0:T(8,128)S(1)}, bf16[128,1024]{1,0:T(8,128)(2,1)S(1)}, bf16[3584,128]{1,0:T(8,128)(2,1)}, bf16...) custom-call(s32[4]{0:T(128)S(1)} %pad_add_fusion.refs_0_, ...), custom_call_target="tpu_custom_call" | custom-call | flops 1000000 | bytes 100000 | tf_op jit(solution)/shard_map/ffn/pallas_call | solution.py:169
  75.4 1.5 collective-permute-start.6
  79.4 2.4 %ffn_back.1 = (f32[128,1024]{1,0:T(8,128)S(1)}, bf16[128,1024]{1,0:T(8,128)(2,1)}, bf16[1024,128]{1,0:T(8,128)(2,1)S(1)}) custom-call(f32[128,1024]{1,0:T(8,128)S(1)} %get-tuple-element.85.refs_0_, bf16[128,1024]{1,0:T(8,128)(2,1)S(1)} %collective-permute-done.8.refs_1_, f32[128,1024]{1,0:T(8,128)S(1)} %get-tuple-element.79.refs_2_, f32[1,1024]{1,0:T(1,128)S(1)} %bitcast.25, ...), custom_call_target="tpu_custom_call" | custom-call | flops 1000000 | bytes 100000 | tf_op jit(solution)/shard_map/ffn_back/pallas_call | solution.py:169
  83.4 5.5 %all-to-all-start.2 = ((bf16[16,64,128]{2,1,0:T(8,128)(2,1)}), bf16[16,64,128]{2,1,0:T(8,128)(2,1)}, u32[]{:S(2)}, u32[]{:S(2)}) async-start(bf16[16,64,128]{2,1,0:T(8,128)(2,1)} %bitcast.21), calls=%async_computation.2 | async-start | bytes 524288 | tf_op jit(solution)/shard_map/all_to_all | solution.py:1064
  89.5 2.3 out_product.1
  92.6 1.5 collective-permute-start.14
  94.0 6.9 %collective-permute-done.6.refs_2_.refs_1_ = bf16[3584,128]{1,0:T(8,128)(2,1)S(1)} collective-permute-done((bf16[3584,128]{1,0:T(8,128)(2,1)}, bf16[3584,128]{1,0:T(8,128)(2,1)S(1)}, u32[]{:S(2)}, u32[]{:S(2)}) %collective-permute-start.6) | collective-permute-done | bytes 917536 | tf_op jit(solution)/shard_map/ppermute | solution.py:1044
  100.9 1.5 collective-permute-start.16
  104.4 2.9 %first_product.2 = (bf16[4,640,128]{2,1,0:T(8,128)(2,1)S(1)}, bf16[4,640,128]{2,1,0:T(8,128)(2,1)}) custom-call(bf16[2560,128]{1,0:T(8,128)(2,1)S(1)} %copy-done.3, bf16[3584,128]{1,0:T(8,128)(2,1)} %get-tuple-element.83.refs_1_, bf16[3584,128]{1,0:T(8,128)(2,1)S(1)} %collective-permute-done.6.refs_2_.refs_1_, bf16[128,1024]{1,0:T(8,128)(2,1)S(1)} %copy-done, ...), custom_call_target="tpu_custom_call" | custom-call | flops 1000000 | bytes 100000 | tf_op jit(solution)/shard_map/first_product/pallas_call | solution.py:169
  108.2 2.9 %first_product.3 = (bf16[4,640,128]{2,1,0:T(8,128)(2,1)S(1)}, bf16[4,640,128]{2,1,0:T(8,128)(2,1)}) custom-call(bf16[2560,128]{1,0:T(8,128)(2,1)S(1)} %copy-done.1, bf16[3584,128]{1,0:T(8,128)(2,1)} %get-tuple-element.92.refs_1_, bf16[3584,128]{1,0:T(8,128)(2,1)S(1)} %collective-permute-done.11.refs_2_.refs_1_, bf16[128,1024]{1,0:T(8,128)(2,1)S(1)} %copy-done, ...), custom_call_target="tpu_custom_call" | custom-call | flops 1000000 | bytes 100000 | tf_op jit(solution)/shard_map/first_product/pallas_call | solution.py:169
  114.1 4.5 %collective-permute-done.14.refs_13_.refs_5_ = bf16[1024,128]{1,0:T(8,128)(2,1)S(1)} collective-permute-done((bf16[1024,128]{1,0:T(8,128)(2,1)}, bf16[1024,128]{1,0:T(8,128)(2,1)S(1)}, u32[]{:S(2)}, u32[]{:S(2)}) %collective-permute-start.14) | collective-permute-done | bytes 262176 | tf_op jit(solution)/shard_map/ppermute | solution.py:1048
  121.8 10.9 %attn_bwd.1.refs_6_ = bf16[16,192,128]{2,1,0:T(8,128)(2,1)} custom-call(s32[16]{0:T(128)S(1)} %copy-done.62, s32[8]{0:T(128)S(1)} %copy-done.60, s32[4]{0:T(128)S(1)} %bitcast.28, s32[1]{0:T(128)} %constant.70.clone.1.refs_3_, bf16[16,192,128]{2,1,0:T(8,128)(2,1)S(1)} %all-to-all-done.refs_4_, bf16[16,64,128]{2,1,0:T(8,128)(2,1)} %all-to-all-done.2.refs_5_, ...), custom_call_target="tpu_custom_call" | custom-call | flops 1000000 | bytes 100000 | tf_op jit(solution)/shard_map/attn_bwd/pallas_call | solution.py:169
  132.6 4.6 %all-to-all-start.3 = ((bf16[16,192,128]{2,1,0:T(8,128)(2,1)}), bf16[16,192,128]{2,1,0:T(8,128)(2,1)S(1)}, u32[]{:S(2)}, u32[]{:S(2)}) async-start(bf16[16,192,128]{2,1,0:T(8,128)(2,1)} %attn_bwd.1.refs_6_), calls=%async_computation.3 | async-start | bytes 1572864 | tf_op jit(solution)/shard_map/all_to_all | solution.py:1060
  140.3 1.8 second_product.2
  142.1 2.0 second_product.3
  144.1 2.5 %combine.2 = (bf16[1280,128]{1,0:T(8,128)(2,1)S(1)}, bf16[1280,128]{1,0:T(8,128)(2,1)S(1)}, bf16[2560,128]{1,0:T(8,128)(2,1)}) custom-call(s32[4]{0:T(128)S(1)} %pad_add_fusion.refs_0_, bf16[4,640,128]{2,1,0:T(8,128)(2,1)S(1)} %copy-done.6, bf16[4,640,128]{2,1,0:T(8,128)(2,1)} %collective-permute-done.10.refs_2_, bf16[4,640,128]{2,1,0:T(8,128)(2,1)S(1)} %copy-done.9, ...), custom_call_target="tpu_custom_call" | custom-call | flops 1000000 | bytes 100000 | tf_op jit(solution)/shard_map/combine/pallas_call | solution.py:169
  148.2 4.0 %ffn_out.1 = (f32[128,1024]{1,0:T(8,128)S(1)}, bf16[128,1024]{1,0:T(8,128)(2,1)}) custom-call(s32[4]{0:T(128)S(1)} %pad_add_fusion.refs_0_, bf16[256,1408]{1,0:T(8,128)(2,1)S(1)} %copy-done.34, bf16[2816,1024]{1,0:T(8,128)(2,1)} %refs_2_.6, bf16[1280,128]{1,0:T(8,128)(2,1)S(1)} %get-tuple-element.106.refs_3_.refs_0_), custom_call_target="tpu_custom_call" | custom-call | flops 1000000 | bytes 100000 | tf_op jit(solution)/shard_map/ffn_out/pallas_call | solution.py:169
  152.2 8.6 %collective-permute-done.18.refs_2_ = bf16[4,576,128]{2,1,0:T(8,128)(2,1)S(1)} collective-permute-done((bf16[4,576,128]{2,1,0:T(8,128)(2,1)S(1)}, bf16[4,576,128]{2,1,0:T(8,128)(2,1)S(1)}, u32[]{:S(2)}, u32[]{:S(2)}) %collective-permute-start.18) | collective-permute-done | bytes 589856 | tf_op jit(solution)/shard_map/ppermute | solution.py:1048
  161.5 1.6 combine.3
  165.4 2.9 %head_product.1 = (f32[512,768]{1,0:T(8,128)S(1)}, bf16[512,768]{1,0:T(8,128)(2,1)}) custom-call(s32[4]{0:T(128)S(1)} %pad_add_fusion.refs_0_, bf16[256,1024]{1,0:T(8,128)(2,1)S(1)} %copy-done.23, bf16[256,1024]{1,0:T(8,128)(2,1)S(1)} %copy-done.16, bf16[4,4,192,128]{3,2,1,0:T(8,128)(2,1)S(1)} %bitcast.17, ...), custom_call_target="tpu_custom_call" | custom-call | flops 1000000 | bytes 100000 | tf_op jit(solution)/shard_map/head_product/pallas_call | solution.py:169
  168.3 1.8 collective-permute-start.20
  170.0 4.0 %all-to-all-start.4 = ((bf16[4,4,192,128]{3,2,1,0:T(8,128)(2,1)}), bf16[4,4,192,128]{3,2,1,0:T(8,128)(2,1)S(1)}, u32[]{:S(2)}, u32[]{:S(2)}) async-start(bf16[4,4,192,128]{3,2,1,0:T(8,128)(2,1)} %turn.1.refs_3_), calls=%async_computation.4 | async-start | bytes 1572864 | tf_op jit(solution)/shard_map/all_to_all | solution.py:1060
  174.1 2.0 collective-permute-start.22
  176.1 2.0 head_split.1
  178.2 1.8 collective-permute-start.24
  180.0 4.1 %collective-permute-done.22.refs_2_ = bf16[1280,128]{1,0:T(8,128)(2,1)S(1)} collective-permute-done((bf16[1280,128]{1,0:T(8,128)(2,1)}, bf16[1280,128]{1,0:T(8,128)(2,1)S(1)}, u32[]{:S(2)}, u32[]{:S(2)}) %collective-permute-start.22) | collective-permute-done | bytes 327712 | tf_op jit(solution)/shard_map/ppermute | solution.py:1052
  184.1 1.4 unpack_one.1
  189.7 1.8 cross.4
  191.5 8.4 %collective-permute-start.26 = (bf16[1152,128]{1,0:T(8,128)(2,1)}, bf16[1152,128]{1,0:T(8,128)(2,1)S(1)}, u32[]{:S(2)}, u32[]{:S(2)}) collective-permute-start(bf16[1152,128]{1,0:T(8,128)(2,1)} %get-tuple-element.128), channel_id=1, source_target_pairs={{0,12},{1,13},{2,14},{3,15},{4,8},{5,9},{6,10},{7,11},{8,4},{9,5},... | collective-permute-start | bytes 884744 | tf_op jit(solution)/shard_map/ppermute | solution.py:1052
  199.9 5.6 %latent_back.1.refs_3_ = bf16[128,1024]{1,0:T(8,128)(2,1)} custom-call(bf16[16,192,128]{2,1,0:T(8,128)(2,1)S(1)} %bitcast.18, f32[128,1024]{1,0:T(8,128)S(1)} %copy-done.38, bf16[128,1024]{1,0:T(8,128)(2,1)S(1)} %copy-done.12, f32[1,1024]{1,0:T(1,128)S(1)} %bitcast.23, bf16[1024,1024]{1,0:T(8,128)(2,1)} %wq_ref.1, bf16[1024,1024]{1,0:T(8,128)(2,1)} %wk_ref.1, ...), custom_call_target="tpu_custom_call" | custom-call | flops 1000000 | bytes 100000 | tf_op jit(solution)/shard_map/latent_back/pallas_call | solution.py:169
  209.2 3.7 %collective-permute-done.26.refs_2_ = bf16[1152,128]{1,0:T(8,128)(2,1)S(1)} collective-permute-done((bf16[1152,128]{1,0:T(8,128)(2,1)}, bf16[1152,128]{1,0:T(8,128)(2,1)S(1)}, u32[]{:S(2)}, u32[]{:S(2)}) %collective-permute-start.26) | collective-permute-done | bytes 294944 | tf_op jit(solution)/shard_map/ppermute | solution.py:1052
  212.9 1.3 unpack_two.1
  214.2 5.6 %collective-permute-done.25.refs_1_ = bf16[128,768]{1,0:T(8,128)(2,1)S(1)} collective-permute-done((bf16[128,768]{1,0:T(8,128)(2,1)S(1)}, bf16[128,768]{1,0:T(8,128)(2,1)S(1)}, u32[]{:S(2)}, u32[]{:S(2)}) %collective-permute-start.25) | collective-permute-done | bytes 196640 | tf_op jit(solution)/shard_map/ppermute | solution.py:1052
  220.4 4.4 %all-to-all-start.5 = ((bf16[4,32,768]{2,1,0:T(8,128)(2,1)}), bf16[4,32,768]{2,1,0:T(8,128)(2,1)S(1)}, u32[]{:S(2)}, u32[]{:S(2)}) async-start(bf16[4,32,768]{2,1,0:T(8,128)(2,1)} %head_end.1), calls=%async_computation.5 | async-start | bytes 393216 | tf_op jit(solution)/shard_map/all_to_all | solution.py:1060
  224.8 1.7 add_convert_fusion
  227.2 2.9 %finish.1 = (f32[32,2816]{1,0:T(8,128)}, f32[32,2816]{1,0:T(8,128)}, f32[1,32]{1,0:T(1,128)}) custom-call(s32[2]{0:T(128)} %pad_add_fusion.1.at_ref, f32[2,32,512]{2,1,0:T(8,128)} %copy-done.51, f32[2,32,896]{2,1,0:T(8,128)} %copy-done.48, bf16[2,32,512]{2,1,0:T(8,128)(2,1)} %copy-done.67, bf16[2,32,896]{2,1,0:T(8,128)(2,1)} %copy-done.66, ...), custom_call_target="tpu_custom_call" | custom-call | flops 1000000 | bytes 100000 | tf_op jit(solution)/shard_map/finish/pallas_call | solution.py:877
  230.8 2.5 %head_rows.1 = (f32[32,1024]{1,0:T(8,128)}, f32[32,1024]{1,0:T(8,128)}, f32[32,1024]{1,0:T(8,128)}, f32[1,32]{1,0:T(1,128)}) custom-call(s32[2]{0:T(128)} %pad_add_fusion.1.at_ref, bf16[4,32,768]{2,1,0:T(8,128)(2,1)} %order.1.in_ref, f32[32,32]{1,0:T(8,128)} %reshape.90.gain_ref, bf16[1024,1024]{1,0:T(8,128)(2,1)} %wq_ref.1, bf16[1024,1024]{1,0:T(8,128)(2,1)} %wk_ref.1, ...), custom_call_target="tpu_custom_call" | custom-call | flops 1000000 | bytes 100000 | tf_op jit(solution)/shard_map/head_rows/pallas_call | solution.py:1020
  (205 shorter events, 38.5 us)
Async XLA Ops:
  6.7 22.1 %copy-start.69 = (s32[1,16]{1,0:T(1,128)S(1)}, s32[1,16]{1,0:T(1,128)}, u32[]{:S(2)}) copy-start(s32[1,16]{1,0:T(1,128)} %param.25) | copy-start | bytes 196
  6.7 28.1 %all-to-all-start = ((bf16[16,192,128]{2,1,0:T(8,128)(2,1)}), bf16[16,192,128]{2,1,0:T(8,128)(2,1)S(1)}, u32[]{:S(2)}, u32[]{:S(2)}) async-start(bf16[16,192,128]{2,1,0:T(8,128)(2,1)} %get-tuple-element.76), calls=%async_computation | async-start | bytes 1572864 | tf_op jit(solution)/shard_map/all_to_all | solution.py:1064
  13.9 1.6 collective-permute-start
  13.9 12.3 %collective-permute-start.3 = (bf16[128,1024]{1,0:T(8,128)(2,1)S(1)}, bf16[128,1024]{1,0:T(8,128)(2,1)S(1)}, u32[]{:S(2)}, u32[]{:S(2)}) collective-permute-start(bf16[128,1024]{1,0:T(8,128)(2,1)S(1)} %get-tuple-element.78), channel_id=1, source_target_pairs={{0,1},{1,0},{2,3},{3,2},{4,5},{5,4},{6,7},{7,6},{8,9},{9,8},{10,11... | collective-permute-start | bytes 786440 | tf_op jit(solution)/shard_map/ppermute | solution.py:1044
  14.8 29.0 %copy-start.57 = (s32[4,1]{0,1:T(1,128)}, s32[4,1]{0,1:T(1,128)S(1)}, u32[]{:S(2)}) copy-start(s32[4,1]{0,1:T(1,128)S(1)} %reduce-window.8) | copy-start | bytes 52
  14.9 28.9 %copy-start.59 = (s32[8]{0:T(128)}, s32[8]{0:T(128)S(1)}, u32[]{:S(2)}) copy-start(s32[8]{0:T(128)S(1)} %and_select_fusion.refs_1_) | copy-start | bytes 100
  15.5 45.8 %copy-start.11 = (bf16[128,1024]{1,0:T(8,128)(2,1)S(1)}, bf16[128,1024]{1,0:T(8,128)(2,1)}, u32[]{:S(2)}) copy-start(bf16[128,1024]{1,0:T(8,128)(2,1)} %refs_2_.7) | copy-start | bytes 786436
  15.5 45.8 %copy-start.54 = (f32[1024]{0:T(1024)S(1)}, f32[1024]{0:T(1024)}, u32[]{:S(2)}) copy-start(f32[1024]{0:T(1024)} %param.19) | copy-start | bytes 12292
  15.5 19.2 %collective-permute-start.1 = (bf16[256,512]{1,0:T(8,128)(2,1)S(1)}, bf16[256,512]{1,0:T(8,128)(2,1)S(1)}, u32[]{:S(2)}, u32[]{:S(2)}) collective-permute-start(bf16[256,512]{1,0:T(8,128)(2,1)S(1)} %pad_maximum_fusion), channel_id=1, source_target_pairs={{0,1},{1,0},{2,3},{3,2},{4,5},{5,4},{6,7},{7,6},{8,9},{9,8},{10,11... | collective-permute-start | bytes 786440 | tf_op jit(solution)/shard_map/ppermute | solution.py:1044
  16.5 18.2 %collective-permute-start.2 = (bf16[256,512]{1,0:T(8,128)(2,1)S(1)}, bf16[256,512]{1,0:T(8,128)(2,1)S(1)}, u32[]{:S(2)}, u32[]{:S(2)}) collective-permute-start(bf16[256,512]{1,0:T(8,128)(2,1)S(1)} %pad_maximum_fusion.1), channel_id=1, source_target_pairs={{0,2},{1,3},{2,0},{3,1},{4,6},{5,7},{6,4},{7,5},{8,10},{9,11},{10,... | collective-permute-start | bytes 786440 | tf_op jit(solution)/shard_map/ppermute | solution.py:1048
  26.3 37.8 %copy-start.22 = (bf16[256,1024]{1,0:T(8,128)(2,1)}, bf16[256,1024]{1,0:T(8,128)(2,1)S(1)}, u32[]{:S(2)}) copy-start(bf16[256,1024]{1,0:T(8,128)(2,1)S(1)} %constant_dynamic-update-slice_fusion.refs_1_) | copy-start | bytes 1572868
  26.3 26.2 %collective-permute-start.4 = (bf16[256,1024]{1,0:T(8,128)(2,1)S(1)}, bf16[256,1024]{1,0:T(8,128)(2,1)S(1)}, u32[]{:S(2)}, u32[]{:S(2)}) collective-permute-start(bf16[256,1024]{1,0:T(8,128)(2,1)S(1)} %constant_dynamic-update-slice_fusion.refs_1_), channel_id=1, source_target_pairs={{0,2},{1,3},{2,0},{3,1},{4,6},{5,7},{6,4},{7,5},{8,10},{9,11},{10,... | collective-permute-start | bytes 1572872 | tf_op jit(solution)/shard_map/ppermute | solution.py:1048
  34.8 29.3 %copy-start.26 = (bf16[256,512]{1,0:T(8,128)(2,1)}, bf16[256,512]{1,0:T(8,128)(2,1)S(1)}, u32[]{:S(2)}) copy-start(bf16[256,512]{1,0:T(8,128)(2,1)S(1)} %collective-permute-done.1.refs_5_) | copy-start | bytes 786436
  34.8 29.4 %copy-start.28 = (bf16[256,512]{1,0:T(8,128)(2,1)}, bf16[256,512]{1,0:T(8,128)(2,1)S(1)}, u32[]{:S(2)}) copy-start(bf16[256,512]{1,0:T(8,128)(2,1)S(1)} %collective-permute-done.2.refs_6_.refs_5_) | copy-start | bytes 786436
  45.9 15.5 %all-to-all-start.1 = ((bf16[16,64,128]{2,1,0:T(8,128)(2,1)}), bf16[16,64,128]{2,1,0:T(8,128)(2,1)S(1)}, u32[]{:S(2)}, u32[]{:S(2)}) async-start(bf16[16,64,128]{2,1,0:T(8,128)(2,1)} %copy-done.46), calls=%async_computation.1 | async-start | bytes 524288 | tf_op jit(solution)/shard_map/all_to_all | solution.py:1064
  52.5 22.9 %copy-start.15 = (bf16[256,1024]{1,0:T(8,128)(2,1)}, bf16[256,1024]{1,0:T(8,128)(2,1)S(1)}, u32[]{:S(2)}) copy-start(bf16[256,1024]{1,0:T(8,128)(2,1)S(1)} %collective-permute-done.4.refs_5_.refs_2_) | copy-start | bytes 1572868
  64.2 1.6 collective-permute-start.5
  75.4 25.6 %collective-permute-start.6 = (bf16[3584,128]{1,0:T(8,128)(2,1)}, bf16[3584,128]{1,0:T(8,128)(2,1)S(1)}, u32[]{:S(2)}, u32[]{:S(2)}) collective-permute-start(bf16[3584,128]{1,0:T(8,128)(2,1)} %get-tuple-element.83.refs_1_), channel_id=1, source_target_pairs={{0,1},{1,0},{2,3},{3,2},{4,5},{5,4},{6,7},{7,6},{8,9},{9,8},{10,11... | collective-permute-start | bytes 2752520 | tf_op jit(solution)/shard_map/ppermute | solution.py:1044
  76.9 30.5 %collective-permute-start.11 = (bf16[3584,128]{1,0:T(8,128)(2,1)}, bf16[3584,128]{1,0:T(8,128)(2,1)S(1)}, u32[]{:S(2)}, u32[]{:S(2)}) collective-permute-start(bf16[3584,128]{1,0:T(8,128)(2,1)} %get-tuple-element.92.refs_1_), channel_id=1, source_target_pairs={{0,2},{1,3},{2,0},{3,1},{4,6},{5,7},{6,4},{7,5},{8,10},{9,11},{10,... | collective-permute-start | bytes 2752520 | tf_op jit(solution)/shard_map/ppermute | solution.py:1048
  77.6 1.8 collective-permute-start.8
  77.6 11.2 %collective-permute-start.7 = (bf16[512,128]{1,0:T(8,128)(2,1)}, bf16[512,128]{1,0:T(8,128)(2,1)S(1)}, u32[]{:S(2)}, u32[]{:S(2)}) collective-permute-start(bf16[512,128]{1,0:T(8,128)(2,1)} %get-tuple-element.84), channel_id=1, source_target_pairs={{0,16},{16,0},{1,17},{17,1},{2,18},{18,2},{3,19},{19,3},{4,20},{20... | collective-permute-start | bytes 393224 | tf_op jit(solution)/shard_map/ppermute | solution.py:1040
  78.2 34.6 %collective-permute-start.13 = (bf16[1792,128]{1,0:T(8,128)(2,1)}, bf16[1792,128]{1,0:T(8,128)(2,1)}, u32[]{:S(2)}, u32[]{:S(2)}) collective-permute-start(bf16[1792,128]{1,0:T(8,128)(2,1)} %get-tuple-element.95.refs_2_), channel_id=1, source_target_pairs={{0,2},{1,3},{2,0},{3,1},{4,6},{5,7},{6,4},{7,5},{8,10},{9,11},{10,... | collective-permute-start | bytes 1376264 | tf_op jit(solution)/shard_map/ppermute | solution.py:1048
  82.7 6.9 %collective-permute-start.9 = (bf16[128,1024]{1,0:T(8,128)(2,1)}, bf16[128,1024]{1,0:T(8,128)(2,1)}, u32[]{:S(2)}, u32[]{:S(2)}) collective-permute-start(bf16[128,1024]{1,0:T(8,128)(2,1)} %get-tuple-element.87.refs_3_), channel_id=1, source_target_pairs={{0,16},{16,0},{1,17},{17,1},{2,18},{18,2},{3,19},{19,3},{4,20},{20... | collective-permute-start | bytes 786440 | tf_op jit(solution)/shard_map/ppermute | solution.py:1040
  83.4 30.7 %all-to-all-start.2 = ((bf16[16,64,128]{2,1,0:T(8,128)(2,1)}), bf16[16,64,128]{2,1,0:T(8,128)(2,1)}, u32[]{:S(2)}, u32[]{:S(2)}) async-start(bf16[16,64,128]{2,1,0:T(8,128)(2,1)} %bitcast.21), calls=%async_computation.2 | async-start | bytes 524288 | tf_op jit(solution)/shard_map/all_to_all | solution.py:1064
  88.9 19.4 %copy-start.1 = (bf16[2560,128]{1,0:T(8,128)(2,1)S(1)}, bf16[2560,128]{1,0:T(8,128)(2,1)}, u32[]{:S(2)}) copy-start(bf16[2560,128]{1,0:T(8,128)(2,1)} %get-tuple-element.91.refs_0_) | copy-start | bytes 1966084
  88.9 24.4 %collective-permute-start.15 = (bf16[1792,128]{1,0:T(8,128)(2,1)}, bf16[1792,128]{1,0:T(8,128)(2,1)S(1)}, u32[]{:S(2)}, u32[]{:S(2)}) collective-permute-start(bf16[1792,128]{1,0:T(8,128)(2,1)} %copy-done.39), channel_id=1, source_target_pairs={{0,1},{1,0},{2,3},{3,2},{4,5},{5,4},{6,7},{7,6},{8,9},{9,8},{10,11... | collective-permute-start | bytes 1376264 | tf_op jit(solution)/shard_map/ppermute | solution.py:1044
  92.6 26.0 %collective-permute-start.14 = (bf16[1024,128]{1,0:T(8,128)(2,1)}, bf16[1024,128]{1,0:T(8,128)(2,1)S(1)}, u32[]{:S(2)}, u32[]{:S(2)}) collective-permute-start(bf16[1024,128]{1,0:T(8,128)(2,1)} %get-tuple-element.97), channel_id=1, source_target_pairs={{0,2},{1,3},{2,0},{3,1},{4,6},{5,7},{6,4},{7,5},{8,10},{9,11},{10,... | collective-permute-start | bytes 786440 | tf_op jit(solution)/shard_map/ppermute | solution.py:1048
  100.9 17.7 %collective-permute-start.16 = (bf16[1024,128]{1,0:T(8,128)(2,1)}, bf16[1024,128]{1,0:T(8,128)(2,1)}, u32[]{:S(2)}, u32[]{:S(2)}) collective-permute-start(bf16[1024,128]{1,0:T(8,128)(2,1)} %get-tuple-element.99), channel_id=1, source_target_pairs={{0,1},{1,0},{2,3},{3,2},{4,5},{5,4},{6,7},{7,6},{8,9},{9,8},{10,11... | collective-permute-start | bytes 786440 | tf_op jit(solution)/shard_map/ppermute | solution.py:1044
  107.4 36.7 %collective-permute-start.10 = (bf16[4,640,128]{2,1,0:T(8,128)(2,1)}, bf16[4,640,128]{2,1,0:T(8,128)(2,1)}, u32[]{:S(2)}, u32[]{:S(2)}) collective-permute-start(bf16[4,640,128]{2,1,0:T(8,128)(2,1)} %get-tuple-element.90), channel_id=1, source_target_pairs={{0,2},{1,3},{2,0},{3,1},{4,6},{5,7},{6,4},{7,5},{8,10},{9,11},{10,... | collective-permute-start | bytes 1966088 | tf_op jit(solution)/shard_map/ppermute | solution.py:1048
  112.7 31.4 %collective-permute-start.12 = (bf16[4,640,128]{2,1,0:T(8,128)(2,1)}, bf16[4,640,128]{2,1,0:T(8,128)(2,1)}, u32[]{:S(2)}, u32[]{:S(2)}) collective-permute-start(bf16[4,640,128]{2,1,0:T(8,128)(2,1)} %get-tuple-element.94), channel_id=1, source_target_pairs={{0,1},{1,0},{2,3},{3,2},{4,5},{5,4},{6,7},{7,6},{8,9},{9,8},{10,11... | collective-permute-start | bytes 1966088 | tf_op jit(solution)/shard_map/ppermute | solution.py:1044
  132.6 31.2 %all-to-all-start.3 = ((bf16[16,192,128]{2,1,0:T(8,128)(2,1)}), bf16[16,192,128]{2,1,0:T(8,128)(2,1)S(1)}, u32[]{:S(2)}, u32[]{:S(2)}) async-start(bf16[16,192,128]{2,1,0:T(8,128)(2,1)} %attn_bwd.1.refs_6_), calls=%async_computation.3 | async-start | bytes 1572864 | tf_op jit(solution)/shard_map/all_to_all | solution.py:1060
  146.6 18.1 %collective-permute-start.21 = (bf16[2560,128]{1,0:T(8,128)(2,1)}, bf16[2560,128]{1,0:T(8,128)(2,1)S(1)}, u32[]{:S(2)}, u32[]{:S(2)}) collective-permute-start(bf16[2560,128]{1,0:T(8,128)(2,1)} %get-tuple-element.116), channel_id=1, source_target_pairs={{0,4},{1,5},{2,6},{3,7},{4,0},{5,1},{6,2},{7,3},{8,12},{9,13},{10,... | collective-permute-start | bytes 1966088 | tf_op jit(solution)/shard_map/ppermute | solution.py:1052
  146.7 14.2 %collective-permute-start.18 = (bf16[4,576,128]{2,1,0:T(8,128)(2,1)S(1)}, bf16[4,576,128]{2,1,0:T(8,128)(2,1)S(1)}, u32[]{:S(2)}, u32[]{:S(2)}) collective-permute-start(bf16[4,576,128]{2,1,0:T(8,128)(2,1)S(1)} %get-tuple-element.109), channel_id=1, source_target_pairs={{0,2},{1,3},{2,0},{3,1},{4,6},{5,7},{6,4},{7,5},{8,10},{9,11},{10,... | collective-permute-start | bytes 1769480 | tf_op jit(solution)/shard_map/ppermute | solution.py:1048
  147.6 13.9 %collective-permute-start.19 = (bf16[4,576,128]{2,1,0:T(8,128)(2,1)S(1)}, bf16[4,576,128]{2,1,0:T(8,128)(2,1)S(1)}, u32[]{:S(2)}, u32[]{:S(2)}) collective-permute-start(bf16[4,576,128]{2,1,0:T(8,128)(2,1)S(1)} %get-tuple-element.110), channel_id=1, source_target_pairs={{0,1},{1,0},{2,3},{3,2},{4,5},{5,4},{6,7},{7,6},{8,9},{9,8},{10,11... | collective-permute-start | bytes 1769480 | tf_op jit(solution)/shard_map/ppermute | solution.py:1044
  168.3 7.8 %collective-permute-start.23 = (bf16[512,768]{1,0:T(8,128)(2,1)}, bf16[512,768]{1,0:T(8,128)(2,1)}, u32[]{:S(2)}, u32[]{:S(2)}) collective-permute-start(bf16[512,768]{1,0:T(8,128)(2,1)} %get-tuple-element.120), channel_id=1, source_target_pairs={{0,16},{16,0},{1,17},{17,1},{2,18},{18,2},{3,19},{19,3},{4,20},{20... | collective-permute-start | bytes 2359304 | tf_op jit(solution)/shard_map/ppermute | solution.py:1040
  168.3 17.8 %collective-permute-start.20 = (bf16[2304,128]{1,0:T(8,128)(2,1)}, bf16[2304,128]{1,0:T(8,128)(2,1)}, u32[]{:S(2)}, u32[]{:S(2)}) collective-permute-start(bf16[2304,128]{1,0:T(8,128)(2,1)} %get-tuple-element.114), channel_id=1, source_target_pairs={{0,4},{1,5},{2,6},{3,7},{4,0},{5,1},{6,2},{7,3},{8,12},{9,13},{10,... | collective-permute-start | bytes 1769480 | tf_op jit(solution)/shard_map/ppermute | solution.py:1052
  170.0 29.8 %all-to-all-start.4 = ((bf16[4,4,192,128]{3,2,1,0:T(8,128)(2,1)}), bf16[4,4,192,128]{3,2,1,0:T(8,128)(2,1)S(1)}, u32[]{:S(2)}, u32[]{:S(2)}) async-start(bf16[4,4,192,128]{3,2,1,0:T(8,128)(2,1)} %turn.1.refs_3_), calls=%async_computation.4 | async-start | bytes 1572864 | tf_op jit(solution)/shard_map/all_to_all | solution.py:1060
  174.1 10.0 %collective-permute-start.22 = (bf16[1280,128]{1,0:T(8,128)(2,1)}, bf16[1280,128]{1,0:T(8,128)(2,1)S(1)}, u32[]{:S(2)}, u32[]{:S(2)}) collective-permute-start(bf16[1280,128]{1,0:T(8,128)(2,1)} %copy-done.63), channel_id=1, source_target_pairs={{0,12},{1,13},{2,14},{3,15},{4,8},{5,9},{6,10},{7,11},{8,4},{9,5},... | collective-permute-start | bytes 983048 | tf_op jit(solution)/shard_map/ppermute | solution.py:1052
  176.1 23.8 %copy-start.12 = (bf16[128,1024]{1,0:T(8,128)(2,1)S(1)}, bf16[128,1024]{1,0:T(8,128)(2,1)}, u32[]{:S(2)}) copy-start(bf16[128,1024]{1,0:T(8,128)(2,1)} %refs_2_.7) | copy-start | bytes 786436
  176.1 23.8 %copy-start.53 = (f32[1024]{0:T(1024)S(1)}, f32[1024]{0:T(1024)}, u32[]{:S(2)}) copy-start(f32[1024]{0:T(1024)} %param.14) | copy-start | bytes 12292
  178.2 21.7 %copy-start.38 = (f32[128,1024]{1,0:T(8,128)S(1)}, f32[128,1024]{1,0:T(8,128)}, u32[]{:S(2)}) copy-start(f32[128,1024]{1,0:T(8,128)} %copy-done.37) | copy-start | bytes 1572868
  178.2 27.4 %collective-permute-start.24 = (bf16[256,768]{1,0:T(8,128)(2,1)}, bf16[256,768]{1,0:T(8,128)(2,1)S(1)}, u32[]{:S(2)}, u32[]{:S(2)}) collective-permute-start(bf16[256,768]{1,0:T(8,128)(2,1)} %get-tuple-element.125), channel_id=1, source_target_pairs={{0,4},{1,5},{2,6},{3,7},{4,0},{5,1},{6,2},{7,3},{8,12},{9,13},{10,... | collective-permute-start | bytes 1179656 | tf_op jit(solution)/shard_map/ppermute | solution.py:1052
  191.5 21.4 %collective-permute-start.26 = (bf16[1152,128]{1,0:T(8,128)(2,1)}, bf16[1152,128]{1,0:T(8,128)(2,1)S(1)}, u32[]{:S(2)}, u32[]{:S(2)}) collective-permute-start(bf16[1152,128]{1,0:T(8,128)(2,1)} %get-tuple-element.128), channel_id=1, source_target_pairs={{0,12},{1,13},{2,14},{3,15},{4,8},{5,9},{6,10},{7,11},{8,4},{9,5},... | collective-permute-start | bytes 884744 | tf_op jit(solution)/shard_map/ppermute | solution.py:1052
  199.9 24.9 %collective-permute-start.17 = (bf16[128,1024]{1,0:T(8,128)(2,1)}, bf16[128,1024]{1,0:T(8,128)(2,1)}, u32[]{:S(2)}, u32[]{:S(2)}) collective-permute-start(bf16[128,1024]{1,0:T(8,128)(2,1)} %get-tuple-element.108), channel_id=1, source_target_pairs={{0,16},{16,0},{1,17},{17,1},{2,18},{18,2},{3,19},{19,3},{4,20},{20... | collective-permute-start | bytes 786440 | tf_op jit(solution)/shard_map/ppermute | solution.py:1040
  206.7 13.0 %collective-permute-start.25 = (bf16[128,768]{1,0:T(8,128)(2,1)S(1)}, bf16[128,768]{1,0:T(8,128)(2,1)S(1)}, u32[]{:S(2)}, u32[]{:S(2)}) collective-permute-start(bf16[128,768]{1,0:T(8,128)(2,1)S(1)} %get-tuple-element.127), channel_id=1, source_target_pairs={{0,12},{1,13},{2,14},{3,15},{4,8},{5,9},{6,10},{7,11},{8,4},{9,5},... | collective-permute-start | bytes 589832 | tf_op jit(solution)/shard_map/ppermute | solution.py:1052
  208.7 17.9 %collective-permute-start.27 = (bf16[2,32,512]{2,1,0:T(8,128)(2,1)}, bf16[2,32,512]{2,1,0:T(8,128)(2,1)S(1)}, u32[]{:S(2)}, u32[]{:S(2)}) collective-permute-start(bf16[2,32,512]{2,1,0:T(8,128)(2,1)} %copy-done.64), channel_id=1, source_target_pairs={{0,16},{16,0},{1,17},{17,1},{2,18},{18,2},{3,19},{19,3},{4,20},{20... | collective-permute-start | bytes 196616 | tf_op jit(solution)/shard_map/ppermute | solution.py:1040
  214.2 12.4 %collective-permute-start.28 = (bf16[2,32,896]{2,1,0:T(8,128)(2,1)S(1)}, bf16[2,32,896]{2,1,0:T(8,128)(2,1)S(1)}, u32[]{:S(2)}, u32[]{:S(2)}) collective-permute-start(bf16[2,32,896]{2,1,0:T(8,128)(2,1)S(1)} %get-tuple-element.137), channel_id=1, source_target_pairs={{0,16},{16,0},{1,17},{17,1},{2,18},{18,2},{3,19},{19,3},{4,20},{20... | collective-permute-start | bytes 344072 | tf_op jit(solution)/shard_map/ppermute | solution.py:1040
  220.4 9.7 %all-to-all-start.5 = ((bf16[4,32,768]{2,1,0:T(8,128)(2,1)}), bf16[4,32,768]{2,1,0:T(8,128)(2,1)S(1)}, u32[]{:S(2)}, u32[]{:S(2)}) async-start(bf16[4,32,768]{2,1,0:T(8,128)(2,1)} %head_end.1), calls=%async_computation.5 | async-start | bytes 393216 | tf_op jit(solution)/shard_map/all_to_all | solution.py:1060
  (57 other events, 273.5 us)

commit v5 on v4

--- a/solution.py
+++ b/solution.py
@@ -32,8 +32,13 @@
 def block_mask(ends_ref, i, j, blk):
     pos = lax.broadcasted_iota(jnp.int32, (1, blk), 1) + i * blk
     start = query_starts(ends_ref, pos) - j * blk
-    key = lax.broadcasted_iota(jnp.int32, (blk, blk), 0)
+    key = lax.broadcasted_iota(jnp.int32, (2 * blk, blk), 0)
     return (key <= pos - j * blk) & (key >= start)
+
+
+def four_slots(slot_ref, j, count):
+    n = jnp.minimum(j + 1, count - 1)
+    return slot_ref[2 * j], slot_ref[2 * j + 1], slot_ref[2 * n], slot_ref[2 * n + 1]
 
 
 def attn_fwd_kernel(rep, slot_ref, low_ref, ends_ref, part_ref, qkv_ref, out_ref, full_ref, top_ref, inv_ref, key_ref):
@@ -55,11 +60,14 @@
         s0, s1 = slot_ref[2 * i], slot_ref[2 * i + 1]
         q = jnp.concatenate([qkv_ref[s0, :hd, :], qkv_ref[s1, :hd, :]], axis=1)
 
-        def key_block(j, state):
+        low = low_ref[i]
+
+        def key_block(n, state):
             top, mass, acc = state
-            k0, k1 = slot_ref[2 * j], slot_ref[2 * j + 1]
-            k = jnp.concatenate([key_ref[k0], key_ref[k1]], axis=0)
-            v = jnp.concatenate([qkv_ref[k0, 2 * hd :, :], qkv_ref[k1, 2 * hd :, :]], axis=1)
+            j = low + 2 * n
+            keys = four_slots(slot_ref, j, count)
+            k = jnp.concatenate([key_ref[t] for t in keys], axis=0)
+            v = jnp.concatenate([qkv_ref[t, 2 * hd :, :] for t in keys], axis=1)
             s = dot(k, q, ((1,), (0,))) * (SCALE * LOG2E)
             s = jnp.where(block_mask(ends_ref, i, j, blk), s, NEG_FILL)
             new_top = jnp.maximum(top, jnp.max(s, axis=0, keepdims=True))
@@ -74,14 +82,14 @@
             jnp.zeros((1, blk), F32),
             jnp.zeros((hd, blk), F32),
         )
-        top, mass, acc = lax.fori_loop(low_ref[i], i + 1, key_block, init)
+        top, mass, acc = lax.fori_loop(0, (i + 2 - low) // 2, key_block, init)
         inv = 1.0 / mass
         acc = acc * inv
         full_ref[s0] = acc[:, :rows]
         full_ref[s1] = acc[:, rows:]
-        low = acc.astype(BF16)
-        out_ref[s0] = low[:, :rows]
-        out_ref[s1] = low[:, rows:]
+        rounded = acc.astype(BF16)
+        out_ref[s0] = rounded[:, :rows]
+        out_ref[s1] = rounded[:, rows:]
         top_ref[i] = top
         inv_ref[i] = inv
         return c
@@ -120,20 +128,29 @@
         delta = jnp.sum(da.astype(F32) * full, axis=0, keepdims=True)
         top, inv = top_ref[i], inv_ref[i]
 
-        def key_block(j, dq):
-            k0, k1 = slot_ref[2 * j], slot_ref[2 * j + 1]
-            k = jnp.concatenate([key_ref[k0], key_ref[k1]], axis=0)
-            v = jnp.concatenate([value_ref[k0], value_ref[k1]], axis=0)
+        low = low_ref[i]
+
+        def key_block(n, dq):
+            j = low + 2 * n
+            after = jnp.minimum(j + 1, count - 1)
+            keys = four_slots(slot_ref, j, count)
+            k = jnp.concatenate([key_ref[t] for t in keys], axis=0)
+            v = jnp.concatenate([value_ref[t] for t in keys], axis=0)
             s = dot(k, q, ((1,), (0,))) * (SCALE * LOG2E)
             s = jnp.where(block_mask(ends_ref, i, j, blk), s, NEG_FILL)
             p = jnp.exp2(s - top) * inv
             dp = dot(v, da, ((1,), (0,)))
             ds = (p * (dp - delta)).astype(BF16)
-            dk_ref[j] += dot(q, ds, ((1,), (1,)))
-            dv_ref[j] += dot(da, p.astype(BF16), ((1,), (1,)))
-            return dq + dot(pair(qkv_ref, k0, k1, hd, 2 * hd), ds, ((1,), (0,)))
-
-        dq = lax.fori_loop(low_ref[i], i + 1, key_block, jnp.zeros((hd, blk), F32))
+            dk = dot(q, ds, ((1,), (1,)))
+            dv = dot(da, p.astype(BF16), ((1,), (1,)))
+            dk_ref[j] += dk[:, :blk]
+            dk_ref[after] += dk[:, blk:]
+            dv_ref[j] += dv[:, :blk]
+            dv_ref[after] += dv[:, blk:]
+            k_t = jnp.concatenate([qkv_ref[t, hd : 2 * hd, :] for t in keys], axis=1)
+            return dq + dot(k_t, ds, ((1,), (0,)))
+
+        dq = lax.fori_loop(0, (i + 2 - low) // 2, key_block, jnp.zeros((hd, blk), F32))
         dq = (dq * SCALE).astype(BF16)
         out_ref[place(s0), :hd, :] = dq[:, :rows]
         out_ref[place(s1), :hd, :] = dq[:, rows:]
@@ -158,24 +175,34 @@
     return pltpu.with_memory_space_constraint(v, pltpu.HBM)
 
 
+class Chain:
+    last = ()
+
+
 def call(kernel, name, args, after=(), smem=0, outs=(), scratch=(), vmem=24, far=0):
     held = len(args)
-
-    def body(*refs):
-        return kernel(*refs[:held], *refs[held + len(after) :])
-
+    after = (*after, *Chain.last)
+    skip = held + len(after)
     if far:
         args = (*args[: held - far], *(in_hbm(v) for v in args[held - far :]))
-    return pl.pallas_call(
+
+    def body(*refs):
+        refs[skip][...] = jnp.zeros((8, 128), F32)
+        kernel(*refs[:held], *refs[skip + 1 :])
+
+    token, *result = pl.pallas_call(
         body,
         in_specs=[SMEM] * smem + [VMEM] * (held - smem - far) + [HBM] * far + [ANY] * len(after),
-        out_specs=[VMEM] * len(outs),
-        out_shape=[pltpu.HBM(*o[:2]) if len(o) > 2 else jax.ShapeDtypeStruct(*o) for o in outs],
+        out_specs=[VMEM] * (1 + len(outs)),
+        out_shape=[jax.ShapeDtypeStruct((8, 128), F32)]
+        + [pltpu.HBM(*o[:2]) if len(o) > 2 else jax.ShapeDtypeStruct(*o) for o in outs],
         scratch_shapes=list(scratch),
         cost_estimate=COST,
         compiler_params=pltpu.CompilerParams(vmem_limit_bytes=vmem * 2**20),
         name=name,
     )(*args, *after)
+    Chain.last = (token,)
+    return result
 
 
 def order(v, after):
@@ -283,6 +310,7 @@
     seq_lengths,
     span_order,
 ):
+    Chain.last = ()
     n_dp, n_ctx = moves.n_dp, moves.n_ctx
     rows, width = latent_in.shape
     ff = w_gate.shape[1]
@@ -426,7 +454,7 @@
     return call(
         norm_qkv_kernel,
         "norm_qkv",
-        (x, gain.reshape(1, width), wq, wk, wv),
+        (in_hbm(x), gain.reshape(1, width), wq, wk, wv),
         outs=[
             ((rows, width), BF16),
             ((HEADS, 3 * HEAD_DIM, rows), BF16),
@@ -474,7 +502,7 @@
     share = g_w.shape[1]
     high = kx_ref.shape[0]
     first = pl.multiple_of(at_ref[0] * share, 128)
-    parts = ((0, 768), (768, share))
+    parts = ((0, 256), (256, 768), (768, share))
     loads = []
     for n, (lo, hi) in enumerate(parts):
         cols = pl.ds(pl.multiple_of(first + lo, 128), hi - lo)
@@ -577,7 +605,7 @@
             pltpu.VMEM((width, share), BF16),
             pltpu.VMEM((width, share), BF16),
             pltpu.VMEM((share, width), BF16),
-            pltpu.SemaphoreType.DMA((2, 3)),
+            pltpu.SemaphoreType.DMA((3, 3)),
         ],
         vmem=40,
         far=3,
@@ -1079,6 +1107,7 @@
     seq_lengths,
     span_order,
 ):
+    Chain.last = ()
     rows, width = latent_in.shape
     ff = w_gate.shape[1]
     half, own = width // 2, width // 32
@@ -1089,18 +1118,19 @@
     dy_mate = swap(cotangent)
     dy_x = over_x(jnp.concatenate([cotangent[:, :half], dy_mate[:, :half]], axis=0))
     dy_y = over_y(jnp.concatenate([cotangent[:, half:], dy_mate[:, half:]], axis=0))
+    dy_a, dy_b = (cotangent, dy_mate, dy_x), (cotangent, dy_mate, dy_y)
+    place = dp * 16 + ctx
+    where = jnp.stack([place, dp]).astype(jnp.int32)
 
     normed, qkv = norm_qkv(latent_in, gain_attn, w_query, w_key, w_value)
     qkv = to_ctx(qkv)
-
     line = jnp.concatenate([normed, over_x(normed)], axis=0)
     line = (line, over_y(line))
-    out, full, top, inv = attn_fwd(1, scalars, qkv, (dy_x, dy_y))
+    out, full, top, inv = attn_fwd(1, scalars, qkv, ())
     attn_t = to_ctx(out).reshape(width, rows)
-    resid, normed_two, attn_send = out_norm(at, attn_t, latent_in, gain_ffn, w_out, (line[1],))
+    resid, normed_two, attn_send = out_norm(at, attn_t, latent_in, gain_ffn, w_out, (line[1], dy_x, dy_y))
     normed_mate = swap(normed_two)
     attn_mate = swap(attn_send)
-
     hid, d_own, d_mate, send_x, send_y, tiles_x, tiles_y, kept_x, kept_y = ffn(
         at, normed_two, normed_mate, cotangent, dy_mate, w_gate, w_up, w_down, ()
     )
@@ -1111,47 +1141,41 @@
     grad_attn = to_ctx(grad_attn.reshape(HEADS, HEAD_DIM, rows))
     out_x, out_sx, out_y, out_sy = out_product(at, attn_t, attn_mate, dres_low, swap(dres_low), ())
     out_x, out_y = (out_x, over_x(out_sx)), (out_y, over_y(out_sy))
-
-    dy_a, dy_b = (cotangent, dy_mate, dy_x), (cotangent, dy_mate, dy_y)
-    one_a, other_a = first_product(0, kept_x, send_x, got_x, dy_a, (out_x[0],))
-    one_b, other_b = first_product(1, kept_y, send_y, got_y, dy_b, (one_a,))
-    one = (one_a, over_y(other_a), one_b, over_x(other_b))
-    grad_qkv = attn_bwd(
-        1, lambda slot: slot, scalars, qkv, grad_attn, full, top, inv, (one_b, tiles_x[1], tiles_y[1], out_x[1], out_y[1])
-    )
+    one_a, other_a = first_product(0, kept_x, send_x, got_x, dy_a, ())
+    sent_a = over_y(other_a)
+    one_b, other_b = first_product(1, kept_y, send_y, got_y, dy_b, ())
+    sent_b = over_x(other_b)
+    grad_qkv = attn_bwd(1, lambda slot: slot, scalars, qkv, grad_attn, full, top, inv, (tiles_x[1], tiles_y[1], out_x[1], out_y[1]))
     four = in_group(grad_qkv, Z_LINES).reshape(4, 4, 3 * HEAD_DIM, rows)
-    two_a, other_a = second_product(width, kept_x, got_x, tiles_x, out_x, (grad_qkv,))
-    two_b, other_b = second_product(width, kept_y, got_y, tiles_y, out_y, (two_a,))
-    two = (two_a, over_y(other_a), two_b, over_x(other_b))
-    one_own, one_far, one_send = combine(at, one, (two_b,))
+    two_a, other_a = second_product(width, kept_x, got_x, tiles_x, out_x, ())
+    sent_two_a = over_y(other_a)
+    two_b, other_b = second_product(width, kept_y, got_y, tiles_y, out_y, ())
+    sent_two_b = over_x(other_b)
+    one_own, one_far, one_send = combine(at, (one_a, sent_a, one_b, sent_b), ())
     one_got = over_z(one_send, 1)
-    y_own, y_mate = ffn_out(at, hid, w_down, (one_own,))
+    y_own, y_mate = ffn_out(at, hid, w_down, ())
     latents = (resid + y_own + swap(y_mate).astype(F32)).astype(BF16)
-    two_own, two_far, two_send = combine(at, two, (y_own,))
+    two_own, two_far, two_send = combine(at, (two_a, sent_two_a, two_b, sent_two_b), ())
     two_got = over_z(two_send, 1)
-
-    turned = turn(four, (two_own,))
-    back = in_group(turned, PLANES).reshape(16, 3 * HEAD_DIM, rows)
-    one_own, one_send = cross(one_own, one_far, one_got, (turned,))
-    head_mine, head_theirs = head_product(at, line, four, (one_own,))
-    head_own, head_far, head_send = head_split(at, head_mine, swap(head_theirs), ())
+    back = in_group(turn(four, ()), PLANES).reshape(16, 3 * HEAD_DIM, rows)
+    one_own, one_send = cross(one_own, one_far, one_got, ())
+    one_got = over_z(one_send, 3)
+    head_mine, head_theirs = head_product(at, line, four, ())
+    head_theirs = swap(head_theirs)
+    head_own, head_far, head_send = head_split(at, head_mine, head_theirs, ())
     head_got = over_z(head_send, 1)
-    down_sum, mine0, theirs0 = unpack_one(
-        at, (one_own, over_z(one_send, 3)), own, ff // 32, width, (head_own,)
-    )
-    two_own, two_send = cross(two_own, two_far, two_got, (down_sum,))
-    latent_grad = latent_back(back, dres, latent_in, gain_attn, w_query, w_key, w_value, (two_own,))
-    head_own, head_send = cross(head_own, head_far, head_got, (latent_grad,))
-    heads = head_end(head_own, over_z(head_send, 3), ())
-    heads = in_group(heads, PLANES)
-    place = dp * 16 + ctx
-    where = jnp.stack([place, dp]).astype(jnp.int32)
-    mine1, theirs1, out_sum = unpack_two(at, (two_own, over_z(two_send, 3)), own, ff // 2, width, (head_own,))
-    theirs = (swap(theirs0), swap(theirs1))
-    query_sum, key_sum, value_sum, gain_attn_sum = head_rows(
-        where, order(heads, (out_sum,)), gain_attn, w_query, w_key, w_value
-    )
-    gate_sum, up_sum, gain_ffn_sum = finish(where, (mine0, mine1), theirs, gain_ffn, w_gate, w_up)
+    down_sum, mine0, theirs0 = unpack_one(at, (one_own, one_got), own, ff // 32, width, ())
+    theirs0 = swap(theirs0)
+    two_own, two_send = cross(two_own, two_far, two_got, ())
+    two_got = over_z(two_send, 3)
+    latent_grad = latent_back(back, dres, latent_in, gain_attn, w_query, w_key, w_value, ())
+    head_own, head_send = cross(head_own, head_far, head_got, ())
+    head_got = over_z(head_send, 3)
+    mine1, theirs1, out_sum = unpack_two(at, (two_own, two_got), own, ff // 2, width, ())
+    theirs1 = swap(theirs1)
+    heads = in_group(head_end(head_own, head_got, ()), PLANES)
+    query_sum, key_sum, value_sum, gain_attn_sum = head_rows(where, heads, gain_attn, w_query, w_key, w_value)
+    gate_sum, up_sum, gain_ffn_sum = finish(where, (mine0, mine1), (theirs0, theirs1), gain_ffn, w_gate, w_up)
     return (
         latents,
         latent_grad,

time: 234 us -> 231 us (0.987)
  waiting for transfers between devices: 59.9 us -> 45.5 us
  starting transfers between devices: 63.1 us -> 68.2 us
  local copies, waits for them, and re-layouts: 25 us -> 28.5 us
    ppermute x6, starting transfers between devices: 14.1 us -> 19.9 us  [over_z(): return lax.ppermute(v, 'ctx', [(i, i ^ 4 * k) for i in range(16)])]
    ppermute x6, waiting for transfers between devices: 13.3 us -> 9.05 us  [over_z(): return lax.ppermute(v, 'ctx', [(i, i ^ 4 * k) for i in range(16)])]
    all_to_all x3, waiting for transfers between devices: 8.82 us -> 4.92 us  [to_ctx(): return lax.all_to_all(v, 'ctx', 0, 0, tiled=True)]
    ppermute x7, waiting for transfers between devices: 13.9 us -> 10.8 us  [over_y(): return lax.ppermute(v, 'ctx', Y_PAIRS)]
    unnamed x141 -> x151, local copies, waits for them, and re-layouts: 23.6 us -> 26.4 us
    ppermute x7, waiting for transfers between devices: 21.7 us -> 18.9 us  [over_x(): return lax.ppermute(v, 'ctx', X_PAIRS)]
  transfers between devices with their start and end apart: 35 -> 35, of which waited for: 13 -> 12; matrix products, arithmetic and copies ran while one was open for 2% -> 3% of each run, Pallas kernels for 25% -> 25%
where the time goes in v5:
time: 231 us; the launch traced here: 229 us
  Pallas kernels  80.5 us (35%)
  starting transfers between devices  68.2 us (30%)
  waiting for transfers between devices  45.5 us (20%)
  local copies, waits for them, and re-layouts  28.5 us (12%)
  other arithmetic  5.15 us (2%)
    pallas_call x24, Pallas kernels, call(): pl.pallas_call(body, in_specs=[SMEM] * smem + [VMEM] * (held - smem - far...  75.1 us
    unnamed x151, local copies, waits for them, and re-layouts  26.4 us
    ppermute x6, starting transfers between devices, over_z(): return lax.ppermute(v, 'ctx', [(i, i ^ 4 * k) for i in range(16)])  19.9 us
    all_to_all x3, starting transfers between devices, to_ctx(): return lax.all_to_all(v, 'ctx', 0, 0, tiled=True)  19 us
    ppermute x7, waiting for transfers between devices, over_x(): return lax.ppermute(v, 'ctx', X_PAIRS)  18.9 us
    all_to_all x3, starting transfers between devices, in_group(): return lax.all_to_all(v, 'ctx', 0, 0, tiled=True, axis_index_groups=groups)  13 us
    ppermute x7, waiting for transfers between devices, over_y(): return lax.ppermute(v, 'ctx', Y_PAIRS)  10.8 us
    ppermute x7, starting transfers between devices, over_y(): return lax.ppermute(v, 'ctx', Y_PAIRS)  9.25 us
  transfers between devices with their start and end apart: 35, of which 12 were waited for; matrix products, arithmetic and copies ran while one was open for 3% of the time, Pallas kernels for 25%

profile of v5, /device:TPU:10, one launch (start us, length us, event | category | flops | bytes accessed | tf_op | source)
XLA Modules:
  0.0 229.1 jit_solution(8151059879052039578)
XLA Ops:
  1.3 5.3 %norm_qkv.1 = (f32[8,128]{1,0:T(8,128)S(1)}, bf16[128,1024]{1,0:T(8,128)(2,1)S(1)}, bf16[16,192,128]{2,1,0:T(8,128)(2,1)}) custom-call(bf16[128,1024]{1,0:T(8,128)(2,1)} %refs_2_.7, f32[1,1024]{1,0:T(1,128)S(1)} %bitcast.22, bf16[1024,1024]{1,0:T(8,128)(2,1)} %wq_ref.1, bf16[1024,1024]{1,0:T(8,128)(2,1)} %wk_ref.1, bf16[1024,1024]{1,0:T(8,128)(2,1)} %wv_ref.1), custom_call_target="tpu_custom_call" | custom-call | flops 1000000 | bytes 100000 | tf_op jit(solution)/shard_map/norm_qkv/pallas_call | solution.py:193
  6.6 7.2 %all-to-all-start = ((bf16[16,192,128]{2,1,0:T(8,128)(2,1)}), bf16[16,192,128]{2,1,0:T(8,128)(2,1)S(1)}, u32[]{:S(2)}, u32[]{:S(2)}) async-start(bf16[16,192,128]{2,1,0:T(8,128)(2,1)} %get-tuple-element.103), calls=%async_computation | async-start | bytes 1572864 | tf_op jit(solution)/shard_map/all_to_all | solution.py:1092
  14.9 10.5 %collective-permute-done = bf16[128,1024]{1,0:T(8,128)(2,1)S(1)} collective-permute-done((bf16[128,1024]{1,0:T(8,128)(2,1)S(1)}, bf16[128,1024]{1,0:T(8,128)(2,1)S(1)}, u32[]{:S(2)}, u32[]{:S(2)}) %collective-permute-start) | collective-permute-done | bytes 262176 | tf_op jit(solution)/shard_map/ppermute | solution.py:1072
  25.5 2.0 collective-permute-start.1
  28.1 4.9 %all-to-all-done.refs_4_ = bf16[16,192,128]{2,1,0:T(8,128)(2,1)S(1)} async-done(((bf16[16,192,128]{2,1,0:T(8,128)(2,1)}), bf16[16,192,128]{2,1,0:T(8,128)(2,1)S(1)}, u32[]{:S(2)}, u32[]{:S(2)}) %all-to-all-start) | async-done | bytes 786464 | tf_op jit(solution)/shard_map/all_to_all | solution.py:1092
  33.0 9.5 %attn_fwd.1 = (f32[8,128]{1,0:T(8,128)S(1)}, bf16[16,64,128]{2,1,0:T(8,128)(2,1)}, f32[16,64,128]{2,1,0:T(8,128)S(1)}, f32[8,1,256]{2,1,0:T(1,128)S(1)}, f32[8,1,256]{2,1,0:T(1,128)S(1)}) custom-call(s32[16]{0:T(128)S(1)} %select_reduce_fusion.refs_0_, s32[8]{0:T(128)S(1)} %and_select_fusion.refs_1_, s32[4]{0:T(128)S(1)} %bitcast.27, ...), custom_call_target="tpu_custom_call" | custom-call | flops 1000000 | bytes 100000 | tf_op jit(solution)/shard_map/attn_fwd/pallas_call | solution.py:193
  43.9 5.6 %all-to-all-start.1 = ((bf16[16,64,128]{2,1,0:T(8,128)(2,1)}), bf16[16,64,128]{2,1,0:T(8,128)(2,1)S(1)}, u32[]{:S(2)}, u32[]{:S(2)}) async-start(bf16[16,64,128]{2,1,0:T(8,128)(2,1)} %get-tuple-element.105), calls=%async_computation.1 | async-start | bytes 524288 | tf_op jit(solution)/shard_map/all_to_all | solution.py:1092
  50.8 1.6 pad_maximum_fusion.1
  52.4 1.5 collective-permute-start.4
  54.0 4.3 %collective-permute-done.3.refs_6_.refs_5_ = bf16[256,512]{1,0:T(8,128)(2,1)S(1)} collective-permute-done((bf16[256,512]{1,0:T(8,128)(2,1)}, bf16[256,512]{1,0:T(8,128)(2,1)S(1)}, u32[]{:S(2)}, u32[]{:S(2)}) %collective-permute-start.3) | collective-permute-done | bytes 262176 | tf_op jit(solution)/shard_map/ppermute | solution.py:1072
  58.3 1.4 collective-permute-done.4.refs_7_.refs_5_
  59.7 2.8 %out_norm.1 = (f32[8,128]{1,0:T(8,128)S(1)}, f32[128,1024]{1,0:T(8,128)S(1)}, bf16[128,1024]{1,0:T(8,128)(2,1)S(1)}, bf16[512,128]{1,0:T(8,128)(2,1)}) custom-call(s32[4]{0:T(128)S(1)} %pad_add_fusion.refs_0_, bf16[1024,128]{1,0:T(8,128)(2,1)S(1)} %bitcast.19, bf16[128,1024]{1,0:T(8,128)(2,1)S(1)} %copy-done.5, f32[1,1024]{1,0:T(1,128)S(1)} %bitcast.24, ...), custom_call_target="tpu_custom_call" | custom-call | flops 1000000 | bytes 100000 | tf_op jit(solution)/shard_map/out_norm/pallas_call | solution.py:193
  62.6 1.5 collective-permute-done.5.refs_2_
  64.1 9.2 %ffn.1 = (f32[8,128]{1,0:T(8,128)S(1)}, bf16[256,1408]{1,0:T(8,128)(2,1)S(1)}, f32[128,1024]{1,0:T(8,128)S(1)}, bf16[128,1024]{1,0:T(8,128)(2,1)S(1)}, bf16[3584...) custom-call(s32[4]{0:T(128)S(1)} %pad_add_fusion.refs_0_, ...), custom_call_target="tpu_custom_call" | custom-call | flops 1000000 | bytes 100000 | tf_op jit(solution)/shard_map/ffn/pallas_call | solution.py:193
  73.4 1.4 collective-permute-start.6
  77.5 2.4 %ffn_back.1 = (f32[8,128]{1,0:T(8,128)S(1)}, f32[128,1024]{1,0:T(8,128)S(1)}, bf16[128,1024]{1,0:T(8,128)(2,1)}, bf16[1024,128]{1,0:T(8,128)(2,1)S(1)}) custom-call(f32[128,1024]{1,0:T(8,128)S(1)} %get-tuple-element.115.refs_0_, bf16[128,1024]{1,0:T(8,128)(2,1)S(1)} %collective-permute-done.8.refs_1_, f32[128,1024]{1,0:T(8,128)S(1)} %get-tuple-element.108.refs_2_, ...), custom_call_target="tpu_custom_call" | custom-call | flops 1000000 | bytes 100000 | tf_op jit(solution)/shard_map/ffn_back/pallas_call | solution.py:193
  82.0 6.3 %all-to-all-start.2 = ((bf16[16,64,128]{2,1,0:T(8,128)(2,1)}), bf16[16,64,128]{2,1,0:T(8,128)(2,1)}, u32[]{:S(2)}, u32[]{:S(2)}) async-start(bf16[16,64,128]{2,1,0:T(8,128)(2,1)} %bitcast.21), calls=%async_computation.2 | async-start | bytes 524288 | tf_op jit(solution)/shard_map/all_to_all | solution.py:1092
  90.6 2.4 %out_product.1 = (f32[8,128]{1,0:T(8,128)S(1)}, bf16[1024,128]{1,0:T(8,128)(2,1)S(1)}, bf16[1024,128]{1,0:T(8,128)(2,1)}, bf16[1024,128]{1,0:T(8,128)(2,1)S(1)}, bf16[1024,128]{1,0:T(8,128)(2,1)}) custom-call(s32[4]{0:T(128)S(1)} %pad_add_fusion.refs_0_, bf16[1024,128]{1,0:T(8,128)(2,1)S(1)} %bitcast.20, ...), custom_call_target="tpu_custom_call" | custom-call | flops 1000000 | bytes 100000 | tf_op jit(solution)/shard_map/out_product/pallas_call | solution.py:193
  94.4 1.5 collective-permute-start.14
  95.9 3.1 %collective-permute-done.6.refs_2_.refs_1_ = bf16[3584,128]{1,0:T(8,128)(2,1)S(1)} collective-permute-done((bf16[3584,128]{1,0:T(8,128)(2,1)}, bf16[3584,128]{1,0:T(8,128)(2,1)S(1)}, u32[]{:S(2)}, u32[]{:S(2)}) %collective-permute-start.6) | collective-permute-done | bytes 917536 | tf_op jit(solution)/shard_map/ppermute | solution.py:1072
  102.3 2.9 %first_product.2 = (f32[8,128]{1,0:T(8,128)S(1)}, bf16[4,640,128]{2,1,0:T(8,128)(2,1)S(1)}, bf16[4,640,128]{2,1,0:T(8,128)(2,1)}) custom-call(bf16[2560,128]{1,0:T(8,128)(2,1)S(1)} %copy-done.3, bf16[3584,128]{1,0:T(8,128)(2,1)} %get-tuple-element.113.refs_1_, bf16[3584,128]{1,0:T(8,128)(2,1)S(1)} %collective-permute-done.6.refs_2_.refs_1_, ...), custom_call_target="tpu_custom_call" | custom-call | flops 1000000 | bytes 100000 | tf_op jit(solution)/shard_map/first_product/pallas_call | solution.py:193
  107.1 2.9 %first_product.3 = (f32[8,128]{1,0:T(8,128)S(1)}, bf16[4,640,128]{2,1,0:T(8,128)(2,1)S(1)}, bf16[4,640,128]{2,1,0:T(8,128)(2,1)}) custom-call(bf16[2560,128]{1,0:T(8,128)(2,1)S(1)} %copy-done.1, bf16[3584,128]{1,0:T(8,128)(2,1)} %get-tuple-element.124.refs_1_, bf16[3584,128]{1,0:T(8,128)(2,1)S(1)} %collective-permute-done.11.refs_2_.refs_1_, ...), custom_call_target="tpu_custom_call" | custom-call | flops 1000000 | bytes 100000 | tf_op jit(solution)/shard_map/first_product/pallas_call | solution.py:193
  112.3 4.2 %collective-permute-done.14.refs_12_.refs_5_ = bf16[1024,128]{1,0:T(8,128)(2,1)} collective-permute-done((bf16[1024,128]{1,0:T(8,128)(2,1)}, bf16[1024,128]{1,0:T(8,128)(2,1)}, u32[]{:S(2)}, u32[]{:S(2)}) %collective-permute-start.14) | collective-permute-done | bytes 262176 | tf_op jit(solution)/shard_map/ppermute | solution.py:1076
  118.6 10.1 %attn_bwd.1 = (f32[8,128]{1,0:T(8,128)S(1)}, bf16[16,192,128]{2,1,0:T(8,128)(2,1)S(1)}) custom-call(s32[16]{0:T(128)S(1)} %copy-done.68, s32[8]{0:T(128)S(1)} %copy-done.66, s32[4]{0:T(128)S(1)} %bitcast.28, s32[1]{0:T(128)} %constant.70.clone.1.refs_3_, bf16[16,192,128]{2,1,0:T(8,128)(2,1)S(1)} %all-to-all-done.refs_4_, ...), custom_call_target="tpu_custom_call" | custom-call | flops 1000000 | bytes 100000 | tf_op jit(solution)/shard_map/attn_bwd/pallas_call | solution.py:193
  129.7 4.8 %all-to-all-start.3 = ((bf16[16,192,128]{2,1,0:T(8,128)(2,1)}), bf16[16,192,128]{2,1,0:T(8,128)(2,1)S(1)}, u32[]{:S(2)}, u32[]{:S(2)}) async-start(bf16[16,192,128]{2,1,0:T(8,128)(2,1)} %copy-done.21), calls=%async_computation.3 | async-start | bytes 1572864 | tf_op jit(solution)/shard_map/all_to_all | solution.py:1088
  137.6 1.7 second_product.2
  139.4 2.1 second_product.3
  141.5 2.3 %combine.2 = (f32[8,128]{1,0:T(8,128)S(1)}, bf16[1280,128]{1,0:T(8,128)(2,1)S(1)}, bf16[1280,128]{1,0:T(8,128)(2,1)S(1)}, bf16[2560,128]{1,0:T(8,128)(2,1)}) custom-call(s32[4]{0:T(128)S(1)} %pad_add_fusion.refs_0_, bf16[4,640,128]{2,1,0:T(8,128)(2,1)S(1)} %copy-done.26, bf16[4,640,128]{2,1,0:T(8,128)(2,1)} %collective-permute-done.10.refs_2_, ...), custom_call_target="tpu_custom_call" | custom-call | flops 1000000 | bytes 100000 | tf_op jit(solution)/shard_map/combine/pallas_call | solution.py:193
  145.7 4.0 %ffn_out.1 = (f32[8,128]{1,0:T(8,128)S(1)}, f32[128,1024]{1,0:T(8,128)S(1)}, bf16[128,1024]{1,0:T(8,128)(2,1)}) custom-call(s32[4]{0:T(128)S(1)} %pad_add_fusion.refs_0_, bf16[256,1408]{1,0:T(8,128)(2,1)S(1)} %copy-done.24, bf16[2816,1024]{1,0:T(8,128)(2,1)} %refs_2_.6, f32[8,128]{1,0:T(8,128)S(1)} %get-tuple-element.142.refs_3_), custom_call_target="tpu_custom_call" | custom-call | flops 1000000 | bytes 100000 | tf_op jit(solution)/shard_map/ffn_out/pallas_call | solution.py:193
  150.5 5.2 %collective-permute-done.18.refs_2_ = bf16[4,576,128]{2,1,0:T(8,128)(2,1)S(1)} collective-permute-done((bf16[4,576,128]{2,1,0:T(8,128)(2,1)S(1)}, bf16[4,576,128]{2,1,0:T(8,128)(2,1)S(1)}, u32[]{:S(2)}, u32[]{:S(2)}) %collective-permute-start.18) | collective-permute-done | bytes 589856 | tf_op jit(solution)/shard_map/ppermute | solution.py:1076
  156.8 1.5 combine.3
  164.7 2.8 %head_product.1 = (f32[8,128]{1,0:T(8,128)S(1)}, f32[512,768]{1,0:T(8,128)S(1)}, bf16[512,768]{1,0:T(8,128)(2,1)}) custom-call(s32[4]{0:T(128)S(1)} %pad_add_fusion.refs_0_, bf16[256,1024]{1,0:T(8,128)(2,1)S(1)} %copy-done.16, bf16[256,1024]{1,0:T(8,128)(2,1)S(1)} %copy-done.11, bf16[4,4,192,128]{3,2,1,0:T(8,128)(2,1)S(1)} %bitcast.17, ...), custom_call_target="tpu_custom_call" | custom-call | flops 1000000 | bytes 100000 | tf_op jit(solution)/shard_map/head_product/pallas_call | solution.py:193
  167.6 1.9 collective-permute-start.20
  169.5 4.3 %all-to-all-start.4 = ((bf16[4,4,192,128]{3,2,1,0:T(8,128)(2,1)}), bf16[4,4,192,128]{3,2,1,0:T(8,128)(2,1)S(1)}, u32[]{:S(2)}, u32[]{:S(2)}) async-start(bf16[4,4,192,128]{3,2,1,0:T(8,128)(2,1)} %copy-done.22), calls=%async_computation.4 | async-start | bytes 1572864 | tf_op jit(solution)/shard_map/all_to_all | solution.py:1088
  173.8 1.7 collective-permute-start.22
  175.6 1.4 head_split.1
  177.6 1.6 collective-permute-start.24
  179.3 4.3 %collective-permute-done.22.refs_2_ = bf16[1280,128]{1,0:T(8,128)(2,1)S(1)} collective-permute-done((bf16[1280,128]{1,0:T(8,128)(2,1)}, bf16[1280,128]{1,0:T(8,128)(2,1)S(1)}, u32[]{:S(2)}, u32[]{:S(2)}) %collective-permute-start.22) | collective-permute-done | bytes 327712 | tf_op jit(solution)/shard_map/ppermute | solution.py:1080
  183.6 1.4 unpack_one.1
  186.3 8.6 %collective-permute-start.26 = (bf16[1152,128]{1,0:T(8,128)(2,1)S(1)}, bf16[1152,128]{1,0:T(8,128)(2,1)S(1)}, u32[]{:S(2)}, u32[]{:S(2)}) collective-permute-start(bf16[1152,128]{1,0:T(8,128)(2,1)S(1)} %get-tuple-element.178), channel_id=1, source_target_pairs={{0,12},{1,13},{2,14},{3,15},{4,8},{5,9},{6,10},{7,11},{8,4},{9,5},... | collective-permute-start | bytes 884744 | tf_op jit(solution)/shard_map/ppermute | solution.py:1080
  195.0 5.6 %latent_back.1 = (f32[8,128]{1,0:T(8,128)S(1)}, bf16[128,1024]{1,0:T(8,128)(2,1)}) custom-call(bf16[16,192,128]{2,1,0:T(8,128)(2,1)S(1)} %bitcast.18, f32[128,1024]{1,0:T(8,128)S(1)} %copy-done.30, bf16[128,1024]{1,0:T(8,128)(2,1)S(1)} %copy-done.5, f32[1,1024]{1,0:T(1,128)S(1)} %bitcast.23, bf16[1024,1024]{1,0:T(8,128)(2,1)} %wq_ref.1, ...), custom_call_target="tpu_custom_call" | custom-call | flops 1000000 | bytes 100000 | tf_op jit(solution)/shard_map/latent_back/pallas_call | solution.py:193
  200.8 6.0 %collective-permute-start.25 = (bf16[128,768]{1,0:T(8,128)(2,1)S(1)}, bf16[128,768]{1,0:T(8,128)(2,1)S(1)}, u32[]{:S(2)}, u32[]{:S(2)}) collective-permute-start(bf16[128,768]{1,0:T(8,128)(2,1)S(1)} %get-tuple-element.176), channel_id=1, source_target_pairs={{0,12},{1,13},{2,14},{3,15},{4,8},{5,9},{6,10},{7,11},{8,4},{9,5},... | collective-permute-start | bytes 589832 | tf_op jit(solution)/shard_map/ppermute | solution.py:1080
  208.7 1.3 unpack_two.1
  211.2 4.7 %collective-permute-done.25.refs_1_ = bf16[128,768]{1,0:T(8,128)(2,1)S(1)} collective-permute-done((bf16[128,768]{1,0:T(8,128)(2,1)S(1)}, bf16[128,768]{1,0:T(8,128)(2,1)S(1)}, u32[]{:S(2)}, u32[]{:S(2)}) %collective-permute-start.25) | collective-permute-done | bytes 196640 | tf_op jit(solution)/shard_map/ppermute | solution.py:1080
  216.6 3.9 %all-to-all-start.5 = ((bf16[4,32,768]{2,1,0:T(8,128)(2,1)}), bf16[4,32,768]{2,1,0:T(8,128)(2,1)S(1)}, u32[]{:S(2)}, u32[]{:S(2)}) async-start(bf16[4,32,768]{2,1,0:T(8,128)(2,1)} %get-tuple-element.181), calls=%async_computation.5 | async-start | bytes 393216 | tf_op jit(solution)/shard_map/all_to_all | solution.py:1088
  220.6 1.7 add_convert_fusion
  223.0 2.9 %finish.1 = (f32[32,2816]{1,0:T(8,128)}, f32[32,2816]{1,0:T(8,128)}, f32[1,32]{1,0:T(1,128)}) custom-call(s32[2]{0:T(128)} %pad_add_fusion.1.at_ref, f32[2,32,512]{2,1,0:T(8,128)} %copy-done.55, f32[2,32,896]{2,1,0:T(8,128)} %copy-done.50, bf16[2,32,512]{2,1,0:T(8,128)(2,1)} %copy-done.72, bf16[2,32,896]{2,1,0:T(8,128)(2,1)} %copy-done.71, ...), custom_call_target="tpu_custom_call" | custom-call | flops 1000000 | bytes 100000 | tf_op jit(solution)/shard_map/finish/pallas_call | solution.py:905
  226.5 2.5 %head_rows.1 = (f32[32,1024]{1,0:T(8,128)}, f32[32,1024]{1,0:T(8,128)}, f32[32,1024]{1,0:T(8,128)}, f32[1,32]{1,0:T(1,128)}) custom-call(s32[2]{0:T(128)} %pad_add_fusion.1.at_ref, bf16[4,32,768]{2,1,0:T(8,128)(2,1)} %copy-done.70, f32[32,32]{1,0:T(8,128)} %reshape.90.gain_ref, bf16[1024,1024]{1,0:T(8,128)(2,1)} %wq_ref.1, bf16[1024,1024]{1,0:T(8,128)(2,1)} %wk_ref.1, ...), custom_call_target="tpu_custom_call" | custom-call | flops 1000000 | bytes 100000 | tf_op jit(solution)/shard_map/head_rows/pallas_call | solution.py:1048
  (214 shorter events, 44.8 us)
Async XLA Ops:
  6.6 26.4 %all-to-all-start = ((bf16[16,192,128]{2,1,0:T(8,128)(2,1)}), bf16[16,192,128]{2,1,0:T(8,128)(2,1)S(1)}, u32[]{:S(2)}, u32[]{:S(2)}) async-start(bf16[16,192,128]{2,1,0:T(8,128)(2,1)} %get-tuple-element.103), calls=%async_computation | async-start | bytes 1572864 | tf_op jit(solution)/shard_map/all_to_all | solution.py:1092
  13.8 11.6 %collective-permute-start = (bf16[128,1024]{1,0:T(8,128)(2,1)S(1)}, bf16[128,1024]{1,0:T(8,128)(2,1)S(1)}, u32[]{:S(2)}, u32[]{:S(2)}) collective-permute-start(bf16[128,1024]{1,0:T(8,128)(2,1)S(1)} %get-tuple-element.106), channel_id=1, source_target_pairs={{0,1},{1,0},{2,3},{3,2},{4,5},{5,4},{6,7},{7,6},{8,9},{9,8},{10,11... | collective-permute-start | bytes 786440 | tf_op jit(solution)/shard_map/ppermute | solution.py:1072
  14.4 13.0 %collective-permute-start.2 = (bf16[128,1024]{1,0:T(8,128)(2,1)S(1)}, bf16[128,1024]{1,0:T(8,128)(2,1)S(1)}, u32[]{:S(2)}, u32[]{:S(2)}) collective-permute-start(bf16[128,1024]{1,0:T(8,128)(2,1)S(1)} %copy-done), channel_id=1, source_target_pairs={{0,16},{16,0},{1,17},{17,1},{2,18},{18,2},{3,19},{19,3},{4,20},{20... | collective-permute-start | bytes 786440 | tf_op jit(solution)/shard_map/ppermute | solution.py:1068
  14.6 37.8 %copy-start.63 = (s32[4,1]{0,1:T(1,128)}, s32[4,1]{0,1:T(1,128)S(1)}, u32[]{:S(2)}) copy-start(s32[4,1]{0,1:T(1,128)S(1)} %reduce-window.8) | copy-start | bytes 52
  14.7 45.0 %copy-start.5 = (bf16[128,1024]{1,0:T(8,128)(2,1)S(1)}, bf16[128,1024]{1,0:T(8,128)(2,1)}, u32[]{:S(2)}) copy-start(bf16[128,1024]{1,0:T(8,128)(2,1)} %refs_2_.7) | copy-start | bytes 786436
  14.7 45.0 %copy-start.58 = (f32[1024]{0:T(1024)S(1)}, f32[1024]{0:T(1024)}, u32[]{:S(2)}) copy-start(f32[1024]{0:T(1024)} %param.19) | copy-start | bytes 12292
  14.7 47.8 %copy-start.65 = (s32[8]{0:T(128)}, s32[8]{0:T(128)S(1)}, u32[]{:S(2)}) copy-start(s32[8]{0:T(128)S(1)} %and_select_fusion.refs_1_) | copy-start | bytes 100
  14.9 47.6 %copy-start.67 = (s32[16]{0:T(128)}, s32[16]{0:T(128)S(1)}, u32[]{:S(2)}) copy-start(s32[16]{0:T(128)S(1)} %select_reduce_fusion.refs_0_) | copy-start | bytes 196
  25.5 37.1 %copy-start.15 = (bf16[256,1024]{1,0:T(8,128)(2,1)}, bf16[256,1024]{1,0:T(8,128)(2,1)S(1)}, u32[]{:S(2)}) copy-start(bf16[256,1024]{1,0:T(8,128)(2,1)S(1)} %constant_dynamic-update-slice_fusion.refs_1_) | copy-start | bytes 1572868
  25.5 34.2 %collective-permute-start.1 = (bf16[256,1024]{1,0:T(8,128)(2,1)S(1)}, bf16[256,1024]{1,0:T(8,128)(2,1)S(1)}, u32[]{:S(2)}, u32[]{:S(2)}) collective-permute-start(bf16[256,1024]{1,0:T(8,128)(2,1)S(1)} %constant_dynamic-update-slice_fusion.refs_1_), channel_id=1, source_target_pairs={{0,2},{1,3},{2,0},{3,1},{4,6},{5,7},{6,4},{7,5},{8,10},{9,11},{10,... | collective-permute-start | bytes 1572872 | tf_op jit(solution)/shard_map/ppermute | solution.py:1076
  43.9 15.7 %all-to-all-start.1 = ((bf16[16,64,128]{2,1,0:T(8,128)(2,1)}), bf16[16,64,128]{2,1,0:T(8,128)(2,1)S(1)}, u32[]{:S(2)}, u32[]{:S(2)}) async-start(bf16[16,64,128]{2,1,0:T(8,128)(2,1)} %get-tuple-element.105), calls=%async_computation.1 | async-start | bytes 524288 | tf_op jit(solution)/shard_map/all_to_all | solution.py:1092
  50.2 8.0 %collective-permute-start.3 = (bf16[256,512]{1,0:T(8,128)(2,1)}, bf16[256,512]{1,0:T(8,128)(2,1)S(1)}, u32[]{:S(2)}, u32[]{:S(2)}) collective-permute-start(bf16[256,512]{1,0:T(8,128)(2,1)} %pad_maximum_fusion), channel_id=1, source_target_pairs={{0,1},{1,0},{2,3},{3,2},{4,5},{5,4},{6,7},{7,6},{8,9},{9,8},{10,11... | collective-permute-start | bytes 786440 | tf_op jit(solution)/shard_map/ppermute | solution.py:1072
  52.4 7.2 %collective-permute-start.4 = (bf16[256,512]{1,0:T(8,128)(2,1)}, bf16[256,512]{1,0:T(8,128)(2,1)S(1)}, u32[]{:S(2)}, u32[]{:S(2)}) collective-permute-start(bf16[256,512]{1,0:T(8,128)(2,1)} %pad_maximum_fusion.1), channel_id=1, source_target_pairs={{0,2},{1,3},{2,0},{3,1},{4,6},{5,7},{6,4},{7,5},{8,10},{9,11},{10,... | collective-permute-start | bytes 786440 | tf_op jit(solution)/shard_map/ppermute | solution.py:1076
  62.5 1.6 collective-permute-start.5
  73.4 25.6 %collective-permute-start.6 = (bf16[3584,128]{1,0:T(8,128)(2,1)}, bf16[3584,128]{1,0:T(8,128)(2,1)S(1)}, u32[]{:S(2)}, u32[]{:S(2)}) collective-permute-start(bf16[3584,128]{1,0:T(8,128)(2,1)} %get-tuple-element.113.refs_1_), channel_id=1, source_target_pairs={{0,1},{1,0},{2,3},{3,2},{4,5},{5,4},{6,7},{7,6},{8,9},{9,8},{10,11... | collective-permute-start | bytes 2752520 | tf_op jit(solution)/shard_map/ppermute | solution.py:1072
  74.7 31.3 %collective-permute-start.11 = (bf16[3584,128]{1,0:T(8,128)(2,1)}, bf16[3584,128]{1,0:T(8,128)(2,1)S(1)}, u32[]{:S(2)}, u32[]{:S(2)}) collective-permute-start(bf16[3584,128]{1,0:T(8,128)(2,1)} %get-tuple-element.124.refs_1_), channel_id=1, source_target_pairs={{0,2},{1,3},{2,0},{3,1},{4,6},{5,7},{6,4},{7,5},{8,10},{9,11},{10,... | collective-permute-start | bytes 2752520 | tf_op jit(solution)/shard_map/ppermute | solution.py:1076
  75.7 1.7 collective-permute-start.8
  75.7 12.5 %collective-permute-start.7 = (bf16[512,128]{1,0:T(8,128)(2,1)}, bf16[512,128]{1,0:T(8,128)(2,1)S(1)}, u32[]{:S(2)}, u32[]{:S(2)}) collective-permute-start(bf16[512,128]{1,0:T(8,128)(2,1)} %get-tuple-element.114), channel_id=1, source_target_pairs={{0,16},{16,0},{1,17},{17,1},{2,18},{18,2},{3,19},{19,3},{4,20},{20... | collective-permute-start | bytes 393224 | tf_op jit(solution)/shard_map/ppermute | solution.py:1068
  76.3 34.6 %collective-permute-start.13 = (bf16[1792,128]{1,0:T(8,128)(2,1)}, bf16[1792,128]{1,0:T(8,128)(2,1)}, u32[]{:S(2)}, u32[]{:S(2)}) collective-permute-start(bf16[1792,128]{1,0:T(8,128)(2,1)} %get-tuple-element.128.refs_2_), channel_id=1, source_target_pairs={{0,2},{1,3},{2,0},{3,1},{4,6},{5,7},{6,4},{7,5},{8,10},{9,11},{10,... | collective-permute-start | bytes 1376264 | tf_op jit(solution)/shard_map/ppermute | solution.py:1076
  81.3 7.6 %collective-permute-start.9 = (bf16[128,1024]{1,0:T(8,128)(2,1)}, bf16[128,1024]{1,0:T(8,128)(2,1)}, u32[]{:S(2)}, u32[]{:S(2)}) collective-permute-start(bf16[128,1024]{1,0:T(8,128)(2,1)} %get-tuple-element.118.refs_3_), channel_id=1, source_target_pairs={{0,16},{16,0},{1,17},{17,1},{2,18},{18,2},{3,19},{19,3},{4,20},{20... | collective-permute-start | bytes 786440 | tf_op jit(solution)/shard_map/ppermute | solution.py:1068
  82.0 30.3 %all-to-all-start.2 = ((bf16[16,64,128]{2,1,0:T(8,128)(2,1)}), bf16[16,64,128]{2,1,0:T(8,128)(2,1)}, u32[]{:S(2)}, u32[]{:S(2)}) async-start(bf16[16,64,128]{2,1,0:T(8,128)(2,1)} %bitcast.21), calls=%async_computation.2 | async-start | bytes 524288 | tf_op jit(solution)/shard_map/all_to_all | solution.py:1092
  88.3 23.2 %collective-permute-start.15 = (bf16[1792,128]{1,0:T(8,128)(2,1)}, bf16[1792,128]{1,0:T(8,128)(2,1)S(1)}, u32[]{:S(2)}, u32[]{:S(2)}) collective-permute-start(bf16[1792,128]{1,0:T(8,128)(2,1)} %copy-done.35), channel_id=1, source_target_pairs={{0,1},{1,0},{2,3},{3,2},{4,5},{5,4},{6,7},{7,6},{8,9},{9,8},{10,11... | collective-permute-start | bytes 1376264 | tf_op jit(solution)/shard_map/ppermute | solution.py:1072
  90.6 16.5 %copy-start.1 = (bf16[2560,128]{1,0:T(8,128)(2,1)S(1)}, bf16[2560,128]{1,0:T(8,128)(2,1)}, u32[]{:S(2)}) copy-start(bf16[2560,128]{1,0:T(8,128)(2,1)} %get-tuple-element.123.refs_0_) | copy-start | bytes 1966084
  90.6 16.5 %copy-start.18 = (bf16[256,512]{1,0:T(8,128)(2,1)S(1)}, bf16[256,512]{1,0:T(8,128)(2,1)}, u32[]{:S(2)}) copy-start(bf16[256,512]{1,0:T(8,128)(2,1)} %copy-done.17) | copy-start | bytes 786436
  94.4 22.1 %collective-permute-start.14 = (bf16[1024,128]{1,0:T(8,128)(2,1)}, bf16[1024,128]{1,0:T(8,128)(2,1)}, u32[]{:S(2)}, u32[]{:S(2)}) collective-permute-start(bf16[1024,128]{1,0:T(8,128)(2,1)} %get-tuple-element.130), channel_id=1, source_target_pairs={{0,2},{1,3},{2,0},{3,1},{4,6},{5,7},{6,4},{7,5},{8,10},{9,11},{10,... | collective-permute-start | bytes 786440 | tf_op jit(solution)/shard_map/ppermute | solution.py:1076
  99.0 17.6 %collective-permute-start.16 = (bf16[1024,128]{1,0:T(8,128)(2,1)}, bf16[1024,128]{1,0:T(8,128)(2,1)}, u32[]{:S(2)}, u32[]{:S(2)}) collective-permute-start(bf16[1024,128]{1,0:T(8,128)(2,1)} %get-tuple-element.133), channel_id=1, source_target_pairs={{0,1},{1,0},{2,3},{3,2},{4,5},{5,4},{6,7},{7,6},{8,9},{9,8},{10,11... | collective-permute-start | bytes 786440 | tf_op jit(solution)/shard_map/ppermute | solution.py:1072
  106.0 35.5 %collective-permute-start.10 = (bf16[4,640,128]{2,1,0:T(8,128)(2,1)}, bf16[4,640,128]{2,1,0:T(8,128)(2,1)}, u32[]{:S(2)}, u32[]{:S(2)}) collective-permute-start(bf16[4,640,128]{2,1,0:T(8,128)(2,1)} %get-tuple-element.122), channel_id=1, source_target_pairs={{0,2},{1,3},{2,0},{3,1},{4,6},{5,7},{6,4},{7,5},{8,10},{9,11},{10,... | collective-permute-start | bytes 1966088 | tf_op jit(solution)/shard_map/ppermute | solution.py:1076
  110.8 30.7 %collective-permute-start.12 = (bf16[4,640,128]{2,1,0:T(8,128)(2,1)}, bf16[4,640,128]{2,1,0:T(8,128)(2,1)}, u32[]{:S(2)}, u32[]{:S(2)}) collective-permute-start(bf16[4,640,128]{2,1,0:T(8,128)(2,1)} %get-tuple-element.127), channel_id=1, source_target_pairs={{0,1},{1,0},{2,3},{3,2},{4,5},{5,4},{6,7},{7,6},{8,9},{9,8},{10,11... | collective-permute-start | bytes 1966088 | tf_op jit(solution)/shard_map/ppermute | solution.py:1072
  118.6 15.8 %copy-start.14 = (bf16[1792,128]{1,0:T(8,128)(2,1)S(1)}, bf16[1792,128]{1,0:T(8,128)(2,1)}, u32[]{:S(2)}) copy-start(bf16[1792,128]{1,0:T(8,128)(2,1)} %copy-done.12) | copy-start | bytes 1376260
  129.7 29.3 %all-to-all-start.3 = ((bf16[16,192,128]{2,1,0:T(8,128)(2,1)}), bf16[16,192,128]{2,1,0:T(8,128)(2,1)S(1)}, u32[]{:S(2)}, u32[]{:S(2)}) async-start(bf16[16,192,128]{2,1,0:T(8,128)(2,1)} %copy-done.21), calls=%async_computation.3 | async-start | bytes 1572864 | tf_op jit(solution)/shard_map/all_to_all | solution.py:1088
  143.8 16.2 %collective-permute-start.21 = (bf16[2560,128]{1,0:T(8,128)(2,1)}, bf16[2560,128]{1,0:T(8,128)(2,1)}, u32[]{:S(2)}, u32[]{:S(2)}) collective-permute-start(bf16[2560,128]{1,0:T(8,128)(2,1)} %get-tuple-element.159), channel_id=1, source_target_pairs={{0,4},{1,5},{2,6},{3,7},{4,0},{5,1},{6,2},{7,3},{8,12},{9,13},{10,... | collective-permute-start | bytes 1966088 | tf_op jit(solution)/shard_map/ppermute | solution.py:1080
  143.8 11.9 %collective-permute-start.18 = (bf16[4,576,128]{2,1,0:T(8,128)(2,1)S(1)}, bf16[4,576,128]{2,1,0:T(8,128)(2,1)S(1)}, u32[]{:S(2)}, u32[]{:S(2)}) collective-permute-start(bf16[4,576,128]{2,1,0:T(8,128)(2,1)S(1)} %get-tuple-element.147), channel_id=1, source_target_pairs={{0,2},{1,3},{2,0},{3,1},{4,6},{5,7},{6,4},{7,5},{8,10},{9,11},{10,... | collective-permute-start | bytes 1769480 | tf_op jit(solution)/shard_map/ppermute | solution.py:1076
  145.1 11.7 %collective-permute-start.19 = (bf16[4,576,128]{2,1,0:T(8,128)(2,1)S(1)}, bf16[4,576,128]{2,1,0:T(8,128)(2,1)S(1)}, u32[]{:S(2)}, u32[]{:S(2)}) collective-permute-start(bf16[4,576,128]{2,1,0:T(8,128)(2,1)S(1)} %get-tuple-element.149), channel_id=1, source_target_pairs={{0,1},{1,0},{2,3},{3,2},{4,5},{5,4},{6,7},{7,6},{8,9},{9,8},{10,11... | collective-permute-start | bytes 1769480 | tf_op jit(solution)/shard_map/ppermute | solution.py:1072
  167.6 8.0 %collective-permute-start.23 = (bf16[512,768]{1,0:T(8,128)(2,1)}, bf16[512,768]{1,0:T(8,128)(2,1)S(1)}, u32[]{:S(2)}, u32[]{:S(2)}) collective-permute-start(bf16[512,768]{1,0:T(8,128)(2,1)} %get-tuple-element.165), channel_id=1, source_target_pairs={{0,16},{16,0},{1,17},{17,1},{2,18},{18,2},{3,19},{19,3},{4,20},{20... | collective-permute-start | bytes 2359304 | tf_op jit(solution)/shard_map/ppermute | solution.py:1068
  167.6 17.4 %collective-permute-start.20 = (bf16[2304,128]{1,0:T(8,128)(2,1)}, bf16[2304,128]{1,0:T(8,128)(2,1)}, u32[]{:S(2)}, u32[]{:S(2)}) collective-permute-start(bf16[2304,128]{1,0:T(8,128)(2,1)} %get-tuple-element.156), channel_id=1, source_target_pairs={{0,4},{1,5},{2,6},{3,7},{4,0},{5,1},{6,2},{7,3},{8,12},{9,13},{10,... | collective-permute-start | bytes 1769480 | tf_op jit(solution)/shard_map/ppermute | solution.py:1080
  169.5 25.4 %all-to-all-start.4 = ((bf16[4,4,192,128]{3,2,1,0:T(8,128)(2,1)}), bf16[4,4,192,128]{3,2,1,0:T(8,128)(2,1)S(1)}, u32[]{:S(2)}, u32[]{:S(2)}) async-start(bf16[4,4,192,128]{3,2,1,0:T(8,128)(2,1)} %copy-done.22), calls=%async_computation.4 | async-start | bytes 1572864 | tf_op jit(solution)/shard_map/all_to_all | solution.py:1088
  173.8 9.8 %collective-permute-start.22 = (bf16[1280,128]{1,0:T(8,128)(2,1)}, bf16[1280,128]{1,0:T(8,128)(2,1)S(1)}, u32[]{:S(2)}, u32[]{:S(2)}) collective-permute-start(bf16[1280,128]{1,0:T(8,128)(2,1)} %copy-done.69), channel_id=1, source_target_pairs={{0,12},{1,13},{2,14},{3,15},{4,8},{5,9},{6,10},{7,11},{8,4},{9,5},... | collective-permute-start | bytes 983048 | tf_op jit(solution)/shard_map/ppermute | solution.py:1080
  175.6 19.4 %copy-start.57 = (f32[1024]{0:T(1024)S(1)}, f32[1024]{0:T(1024)}, u32[]{:S(2)}) copy-start(f32[1024]{0:T(1024)} %param.14) | copy-start | bytes 12292
  177.6 17.3 %copy-start.30 = (f32[128,1024]{1,0:T(8,128)S(1)}, f32[128,1024]{1,0:T(8,128)}, u32[]{:S(2)}) copy-start(f32[128,1024]{1,0:T(8,128)} %copy-done.29) | copy-start | bytes 1572868
  177.6 23.0 %collective-permute-start.24 = (bf16[256,768]{1,0:T(8,128)(2,1)}, bf16[256,768]{1,0:T(8,128)(2,1)S(1)}, u32[]{:S(2)}, u32[]{:S(2)}) collective-permute-start(bf16[256,768]{1,0:T(8,128)(2,1)} %get-tuple-element.173), channel_id=1, source_target_pairs={{0,4},{1,5},{2,6},{3,7},{4,0},{5,1},{6,2},{7,3},{8,12},{9,13},{10,... | collective-permute-start | bytes 1179656 | tf_op jit(solution)/shard_map/ppermute | solution.py:1080
  186.3 22.4 %collective-permute-start.26 = (bf16[1152,128]{1,0:T(8,128)(2,1)S(1)}, bf16[1152,128]{1,0:T(8,128)(2,1)S(1)}, u32[]{:S(2)}, u32[]{:S(2)}) collective-permute-start(bf16[1152,128]{1,0:T(8,128)(2,1)S(1)} %get-tuple-element.178), channel_id=1, source_target_pairs={{0,12},{1,13},{2,14},{3,15},{4,8},{5,9},{6,10},{7,11},{8,4},{9,5},... | collective-permute-start | bytes 884744 | tf_op jit(solution)/shard_map/ppermute | solution.py:1080
  194.9 25.6 %collective-permute-start.17 = (bf16[128,1024]{1,0:T(8,128)(2,1)}, bf16[128,1024]{1,0:T(8,128)(2,1)}, u32[]{:S(2)}, u32[]{:S(2)}) collective-permute-start(bf16[128,1024]{1,0:T(8,128)(2,1)} %get-tuple-element.144), channel_id=1, source_target_pairs={{0,16},{16,0},{1,17},{17,1},{2,18},{18,2},{3,19},{19,3},{4,20},{20... | collective-permute-start | bytes 786440 | tf_op jit(solution)/shard_map/ppermute | solution.py:1068
  200.6 19.9 %copy-start.9 = (f32[128,1024]{1,0:T(8,128)S(1)}, f32[128,1024]{1,0:T(8,128)}, u32[]{:S(2)}) copy-start(f32[128,1024]{1,0:T(8,128)} %copy-done.8) | copy-start | bytes 1572868
  200.6 19.9 %copy-start.32 = (f32[128,1024]{1,0:T(8,128)S(1)}, f32[128,1024]{1,0:T(8,128)}, u32[]{:S(2)}) copy-start(f32[128,1024]{1,0:T(8,128)} %copy-done.31) | copy-start | bytes 1572868
  200.8 15.1 %collective-permute-start.25 = (bf16[128,768]{1,0:T(8,128)(2,1)S(1)}, bf16[128,768]{1,0:T(8,128)(2,1)S(1)}, u32[]{:S(2)}, u32[]{:S(2)}) collective-permute-start(bf16[128,768]{1,0:T(8,128)(2,1)S(1)} %get-tuple-element.176), channel_id=1, source_target_pairs={{0,12},{1,13},{2,14},{3,15},{4,8},{5,9},{6,10},{7,11},{8,4},{9,5},... | collective-permute-start | bytes 589832 | tf_op jit(solution)/shard_map/ppermute | solution.py:1080
  208.7 13.6 %collective-permute-start.27 = (bf16[2,32,512]{2,1,0:T(8,128)(2,1)S(1)}, bf16[2,32,512]{2,1,0:T(8,128)(2,1)S(1)}, u32[]{:S(2)}, u32[]{:S(2)}) collective-permute-start(bf16[2,32,512]{2,1,0:T(8,128)(2,1)S(1)} %get-tuple-element.189), channel_id=1, source_target_pairs={{0,16},{16,0},{1,17},{17,1},{2,18},{18,2},{3,19},{19,3},{4,20},{20... | collective-permute-start | bytes 196616 | tf_op jit(solution)/shard_map/ppermute | solution.py:1068
  210.7 11.6 %collective-permute-start.28 = (bf16[2,32,896]{2,1,0:T(8,128)(2,1)S(1)}, bf16[2,32,896]{2,1,0:T(8,128)(2,1)S(1)}, u32[]{:S(2)}, u32[]{:S(2)}) collective-permute-start(bf16[2,32,896]{2,1,0:T(8,128)(2,1)S(1)} %get-tuple-element.190), channel_id=1, source_target_pairs={{0,16},{16,0},{1,17},{17,1},{2,18},{18,2},{3,19},{19,3},{4,20},{20... | collective-permute-start | bytes 344072 | tf_op jit(solution)/shard_map/ppermute | solution.py:1068
  216.6 9.2 %all-to-all-start.5 = ((bf16[4,32,768]{2,1,0:T(8,128)(2,1)}), bf16[4,32,768]{2,1,0:T(8,128)(2,1)S(1)}, u32[]{:S(2)}, u32[]{:S(2)}) async-start(bf16[4,32,768]{2,1,0:T(8,128)(2,1)} %get-tuple-element.181), calls=%async_computation.5 | async-start | bytes 393216 | tf_op jit(solution)/shard_map/all_to_all | solution.py:1088
  (62 other events, 281.1 us)

commit v6 on v5

--- a/solution.py
+++ b/solution.py
@@ -1157,9 +1157,9 @@
     latents = (resid + y_own + swap(y_mate).astype(F32)).astype(BF16)
     two_own, two_far, two_send = combine(at, (two_a, sent_two_a, two_b, sent_two_b), ())
     two_got = over_z(two_send, 1)
-    back = in_group(turn(four, ()), PLANES).reshape(16, 3 * HEAD_DIM, rows)
     one_own, one_send = cross(one_own, one_far, one_got, ())
     one_got = over_z(one_send, 3)
+    back = in_group(turn(four, ()), PLANES).reshape(16, 3 * HEAD_DIM, rows)
     head_mine, head_theirs = head_product(at, line, four, ())
     head_theirs = swap(head_theirs)
     head_own, head_far, head_send = head_split(at, head_mine, head_theirs, ())

time: 231 us -> 229 us (level)
  waiting for transfers between devices: 45.5 us -> 54.2 us
  starting transfers between devices: 68.2 us -> 62.3 us
  Pallas kernels: 80.5 us -> 77.6 us
    ppermute x6, waiting for transfers between devices: 9.05 us -> 16.7 us  [over_z(): return lax.ppermute(v, 'ctx', [(i, i ^ 4 * k) for i in range(16)])]
    ppermute x6, starting transfers between devices: 19.9 us -> 13.8 us  [over_z(): return lax.ppermute(v, 'ctx', [(i, i ^ 4 * k) for i in range(16)])]
    pallas_call x24, Pallas kernels: 75.1 us -> 72.2 us  [call(): pl.pallas_call(body, in_specs=[SMEM] * smem + [VMEM] * (held - smem - far...]
    unnamed x151 -> x147, local copies, waits for them, and re-layouts: 26.4 us -> 24.6 us
  transfers between devices with their start and end apart: 35 -> 35, of which waited for: 12 -> 13; matrix products, arithmetic and copies ran while one was open for 3% -> 3% of each run, Pallas kernels for 25% -> 24%
where the time goes in v6:
time: 229 us; the launch traced here: 227 us
  Pallas kernels  77.6 us (34%)
  starting transfers between devices  62.3 us (27%)
  waiting for transfers between devices  54.2 us (24%)
  local copies, waits for them, and re-layouts  26.7 us (12%)
  other arithmetic  5.22 us (2%)
    pallas_call x24, Pallas kernels, call(): pl.pallas_call(body, in_specs=[SMEM] * smem + [VMEM] * (held - smem - far...  72.2 us
    unnamed x147, local copies, waits for them, and re-layouts  24.6 us
    ppermute x7, waiting for transfers between devices, over_x(): return lax.ppermute(v, 'ctx', X_PAIRS)  19.9 us
    all_to_all x3, starting transfers between devices, to_ctx(): return lax.all_to_all(v, 'ctx', 0, 0, tiled=True)  18.8 us
    ppermute x6, waiting for transfers between devices, over_z(): return lax.ppermute(v, 'ctx', [(i, i ^ 4 * k) for i in range(16)])  16.7 us
    ppermute x6, starting transfers between devices, over_z(): return lax.ppermute(v, 'ctx', [(i, i ^ 4 * k) for i in range(16)])  13.8 us
    all_to_all x3, starting transfers between devices, in_group(): return lax.all_to_all(v, 'ctx', 0, 0, tiled=True, axis_index_groups=groups)  13.2 us
    ppermute x7, waiting for transfers between devices, over_y(): return lax.ppermute(v, 'ctx', Y_PAIRS)  11 us
  transfers between devices with their start and end apart: 35, of which 13 were waited for; matrix products, arithmetic and copies ran while one was open for 3% of the time, Pallas kernels for 24%

profile of v6, /device:TPU:10, one launch (start us, length us, event | category | flops | bytes accessed | tf_op | source)
XLA Modules:
  0.0 227.3 jit_solution(6816375133249350213)
XLA Ops:
  1.3 5.3 %norm_qkv.1 = (f32[8,128]{1,0:T(8,128)S(1)}, bf16[128,1024]{1,0:T(8,128)(2,1)S(1)}, bf16[16,192,128]{2,1,0:T(8,128)(2,1)}) custom-call(bf16[128,1024]{1,0:T(8,128)(2,1)} %refs_2_.7, f32[1,1024]{1,0:T(1,128)S(1)} %bitcast.22, bf16[1024,1024]{1,0:T(8,128)(2,1)} %wq_ref.1, bf16[1024,1024]{1,0:T(8,128)(2,1)} %wk_ref.1, bf16[1024,1024]{1,0:T(8,128)(2,1)} %wv_ref.1), custom_call_target="tpu_custom_call" | custom-call | flops 1000000 | bytes 100000 | tf_op jit(solution)/shard_map/norm_qkv/pallas_call | solution.py:193
  6.6 7.2 %all-to-all-start = ((bf16[16,192,128]{2,1,0:T(8,128)(2,1)}), bf16[16,192,128]{2,1,0:T(8,128)(2,1)S(1)}, u32[]{:S(2)}, u32[]{:S(2)}) async-start(bf16[16,192,128]{2,1,0:T(8,128)(2,1)} %get-tuple-element.103), calls=%async_computation | async-start | bytes 1572864 | tf_op jit(solution)/shard_map/all_to_all | solution.py:1092
  14.9 10.5 %collective-permute-done = bf16[128,1024]{1,0:T(8,128)(2,1)S(1)} collective-permute-done((bf16[128,1024]{1,0:T(8,128)(2,1)S(1)}, bf16[128,1024]{1,0:T(8,128)(2,1)S(1)}, u32[]{:S(2)}, u32[]{:S(2)}) %collective-permute-start) | collective-permute-done | bytes 262176 | tf_op jit(solution)/shard_map/ppermute | solution.py:1072
  25.5 2.0 collective-permute-start.1
  28.1 4.9 %all-to-all-done.refs_4_ = bf16[16,192,128]{2,1,0:T(8,128)(2,1)S(1)} async-done(((bf16[16,192,128]{2,1,0:T(8,128)(2,1)}), bf16[16,192,128]{2,1,0:T(8,128)(2,1)S(1)}, u32[]{:S(2)}, u32[]{:S(2)}) %all-to-all-start) | async-done | bytes 786464 | tf_op jit(solution)/shard_map/all_to_all | solution.py:1092
  33.0 9.0 %attn_fwd.1 = (f32[8,128]{1,0:T(8,128)S(1)}, bf16[16,64,128]{2,1,0:T(8,128)(2,1)}, f32[16,64,128]{2,1,0:T(8,128)S(1)}, f32[8,1,256]{2,1,0:T(1,128)S(1)}, f32[8,1,256]{2,1,0:T(1,128)S(1)}) custom-call(s32[16]{0:T(128)S(1)} %select_reduce_fusion.refs_0_, s32[8]{0:T(128)S(1)} %and_select_fusion.refs_1_, s32[4]{0:T(128)S(1)} %bitcast.27, ...), custom_call_target="tpu_custom_call" | custom-call | flops 1000000 | bytes 100000 | tf_op jit(solution)/shard_map/attn_fwd/pallas_call | solution.py:193
  43.4 5.6 %all-to-all-start.1 = ((bf16[16,64,128]{2,1,0:T(8,128)(2,1)}), bf16[16,64,128]{2,1,0:T(8,128)(2,1)S(1)}, u32[]{:S(2)}, u32[]{:S(2)}) async-start(bf16[16,64,128]{2,1,0:T(8,128)(2,1)} %get-tuple-element.105), calls=%async_computation.1 | async-start | bytes 524288 | tf_op jit(solution)/shard_map/all_to_all | solution.py:1092
  50.3 1.6 pad_maximum_fusion.1
  51.9 1.5 collective-permute-start.4
  53.4 4.9 %collective-permute-done.3.refs_6_.refs_5_ = bf16[256,512]{1,0:T(8,128)(2,1)S(1)} collective-permute-done((bf16[256,512]{1,0:T(8,128)(2,1)}, bf16[256,512]{1,0:T(8,128)(2,1)S(1)}, u32[]{:S(2)}, u32[]{:S(2)}) %collective-permute-start.3) | collective-permute-done | bytes 262176 | tf_op jit(solution)/shard_map/ppermute | solution.py:1072
  59.6 2.8 %out_norm.1 = (f32[8,128]{1,0:T(8,128)S(1)}, f32[128,1024]{1,0:T(8,128)S(1)}, bf16[128,1024]{1,0:T(8,128)(2,1)S(1)}, bf16[512,128]{1,0:T(8,128)(2,1)}) custom-call(s32[4]{0:T(128)S(1)} %pad_add_fusion.refs_0_, bf16[1024,128]{1,0:T(8,128)(2,1)S(1)} %bitcast.19, bf16[128,1024]{1,0:T(8,128)(2,1)S(1)} %copy-done.5, f32[1,1024]{1,0:T(1,128)S(1)} %bitcast.24, ...), custom_call_target="tpu_custom_call" | custom-call | flops 1000000 | bytes 100000 | tf_op jit(solution)/shard_map/out_norm/pallas_call | solution.py:193
  62.5 1.5 collective-permute-done.5.refs_2_
  64.0 9.2 %ffn.1 = (f32[8,128]{1,0:T(8,128)S(1)}, bf16[256,1408]{1,0:T(8,128)(2,1)S(1)}, f32[128,1024]{1,0:T(8,128)S(1)}, bf16[128,1024]{1,0:T(8,128)(2,1)S(1)}, bf16[3584...) custom-call(s32[4]{0:T(128)S(1)} %pad_add_fusion.refs_0_, ...), custom_call_target="tpu_custom_call" | custom-call | flops 1000000 | bytes 100000 | tf_op jit(solution)/shard_map/ffn/pallas_call | solution.py:193
  73.3 1.5 collective-permute-start.6
  77.1 2.4 %ffn_back.1 = (f32[8,128]{1,0:T(8,128)S(1)}, f32[128,1024]{1,0:T(8,128)S(1)}, bf16[128,1024]{1,0:T(8,128)(2,1)}, bf16[1024,128]{1,0:T(8,128)(2,1)S(1)}) custom-call(f32[128,1024]{1,0:T(8,128)S(1)} %get-tuple-element.115.refs_0_, bf16[128,1024]{1,0:T(8,128)(2,1)S(1)} %collective-permute-done.8.refs_1_, f32[128,1024]{1,0:T(8,128)S(1)} %get-tuple-element.108.refs_2_, ...), custom_call_target="tpu_custom_call" | custom-call | flops 1000000 | bytes 100000 | tf_op jit(solution)/shard_map/ffn_back/pallas_call | solution.py:193
  81.7 6.0 %all-to-all-start.2 = ((bf16[16,64,128]{2,1,0:T(8,128)(2,1)}), bf16[16,64,128]{2,1,0:T(8,128)(2,1)}, u32[]{:S(2)}, u32[]{:S(2)}) async-start(bf16[16,64,128]{2,1,0:T(8,128)(2,1)} %bitcast.21), calls=%async_computation.2 | async-start | bytes 524288 | tf_op jit(solution)/shard_map/all_to_all | solution.py:1092
  90.0 2.4 %out_product.1 = (f32[8,128]{1,0:T(8,128)S(1)}, bf16[1024,128]{1,0:T(8,128)(2,1)S(1)}, bf16[1024,128]{1,0:T(8,128)(2,1)}, bf16[1024,128]{1,0:T(8,128)(2,1)S(1)}, bf16[1024,128]{1,0:T(8,128)(2,1)}) custom-call(s32[4]{0:T(128)S(1)} %pad_add_fusion.refs_0_, bf16[1024,128]{1,0:T(8,128)(2,1)S(1)} %bitcast.20, ...), custom_call_target="tpu_custom_call" | custom-call | flops 1000000 | bytes 100000 | tf_op jit(solution)/shard_map/out_product/pallas_call | solution.py:193
  93.8 1.5 collective-permute-start.14
  95.3 3.6 %collective-permute-done.6.refs_2_.refs_1_ = bf16[3584,128]{1,0:T(8,128)(2,1)S(1)} collective-permute-done((bf16[3584,128]{1,0:T(8,128)(2,1)}, bf16[3584,128]{1,0:T(8,128)(2,1)S(1)}, u32[]{:S(2)}, u32[]{:S(2)}) %collective-permute-start.6) | collective-permute-done | bytes 917536 | tf_op jit(solution)/shard_map/ppermute | solution.py:1072
  98.9 1.4 collective-permute-start.16
  102.3 2.9 %first_product.2 = (f32[8,128]{1,0:T(8,128)S(1)}, bf16[4,640,128]{2,1,0:T(8,128)(2,1)S(1)}, bf16[4,640,128]{2,1,0:T(8,128)(2,1)}) custom-call(bf16[2560,128]{1,0:T(8,128)(2,1)S(1)} %copy-done.3, bf16[3584,128]{1,0:T(8,128)(2,1)} %get-tuple-element.113.refs_1_, bf16[3584,128]{1,0:T(8,128)(2,1)S(1)} %collective-permute-done.6.refs_2_.refs_1_, ...), custom_call_target="tpu_custom_call" | custom-call | flops 1000000 | bytes 100000 | tf_op jit(solution)/shard_map/first_product/pallas_call | solution.py:193
  107.0 2.9 %first_product.3 = (f32[8,128]{1,0:T(8,128)S(1)}, bf16[4,640,128]{2,1,0:T(8,128)(2,1)S(1)}, bf16[4,640,128]{2,1,0:T(8,128)(2,1)}) custom-call(bf16[2560,128]{1,0:T(8,128)(2,1)S(1)} %copy-done.1, bf16[3584,128]{1,0:T(8,128)(2,1)} %get-tuple-element.124.refs_1_, bf16[3584,128]{1,0:T(8,128)(2,1)S(1)} %collective-permute-done.11.refs_2_.refs_1_, ...), custom_call_target="tpu_custom_call" | custom-call | flops 1000000 | bytes 100000 | tf_op jit(solution)/shard_map/first_product/pallas_call | solution.py:193
  112.3 4.3 %collective-permute-done.14.refs_12_.refs_5_ = bf16[1024,128]{1,0:T(8,128)(2,1)} collective-permute-done((bf16[1024,128]{1,0:T(8,128)(2,1)}, bf16[1024,128]{1,0:T(8,128)(2,1)}, u32[]{:S(2)}, u32[]{:S(2)}) %collective-permute-start.14) | collective-permute-done | bytes 262176 | tf_op jit(solution)/shard_map/ppermute | solution.py:1076
  118.7 9.5 %attn_bwd.1 = (f32[8,128]{1,0:T(8,128)S(1)}, bf16[16,192,128]{2,1,0:T(8,128)(2,1)S(1)}) custom-call(s32[16]{0:T(128)S(1)} %copy-done.66, s32[8]{0:T(128)S(1)} %copy-done.64, s32[4]{0:T(128)S(1)} %bitcast.28, s32[1]{0:T(128)} %constant.70.clone.1.refs_3_, bf16[16,192,128]{2,1,0:T(8,128)(2,1)S(1)} %all-to-all-done.refs_4_, ...), custom_call_target="tpu_custom_call" | custom-call | flops 1000000 | bytes 100000 | tf_op jit(solution)/shard_map/attn_bwd/pallas_call | solution.py:193
  129.2 4.5 %all-to-all-start.3 = ((bf16[16,192,128]{2,1,0:T(8,128)(2,1)}), bf16[16,192,128]{2,1,0:T(8,128)(2,1)S(1)}, u32[]{:S(2)}, u32[]{:S(2)}) async-start(bf16[16,192,128]{2,1,0:T(8,128)(2,1)} %copy-done.21), calls=%async_computation.3 | async-start | bytes 1572864 | tf_op jit(solution)/shard_map/all_to_all | solution.py:1088
  136.8 1.7 second_product.2
  138.6 2.1 second_product.3
  140.7 1.6 combine.2
  144.6 4.0 %ffn_out.1 = (f32[8,128]{1,0:T(8,128)S(1)}, f32[128,1024]{1,0:T(8,128)S(1)}, bf16[128,1024]{1,0:T(8,128)(2,1)}) custom-call(s32[4]{0:T(128)S(1)} %pad_add_fusion.refs_0_, bf16[256,1408]{1,0:T(8,128)(2,1)S(1)} %copy-done.24, bf16[2816,1024]{1,0:T(8,128)(2,1)} %refs_2_.6, f32[8,128]{1,0:T(8,128)S(1)} %get-tuple-element.142.refs_3_), custom_call_target="tpu_custom_call" | custom-call | flops 1000000 | bytes 100000 | tf_op jit(solution)/shard_map/ffn_out/pallas_call | solution.py:193
  149.4 5.5 %collective-permute-done.19.refs_2_ = bf16[4,576,128]{2,1,0:T(8,128)(2,1)S(1)} collective-permute-done((bf16[4,576,128]{2,1,0:T(8,128)(2,1)S(1)}, bf16[4,576,128]{2,1,0:T(8,128)(2,1)S(1)}, u32[]{:S(2)}, u32[]{:S(2)}) %collective-permute-start.19) | collective-permute-done | bytes 589856 | tf_op jit(solution)/shard_map/ppermute | solution.py:1076
  156.0 1.5 combine.3
  157.5 1.5 collective-permute-done.18.refs_2_
  162.5 2.8 %head_product.1 = (f32[8,128]{1,0:T(8,128)S(1)}, f32[512,768]{1,0:T(8,128)S(1)}, bf16[512,768]{1,0:T(8,128)(2,1)}) custom-call(s32[4]{0:T(128)S(1)} %pad_add_fusion.refs_0_, bf16[256,1024]{1,0:T(8,128)(2,1)S(1)} %copy-done.16, bf16[256,1024]{1,0:T(8,128)(2,1)S(1)} %copy-done.11, bf16[4,4,192,128]{3,2,1,0:T(8,128)(2,1)S(1)} %bitcast.17, ...), custom_call_target="tpu_custom_call" | custom-call | flops 1000000 | bytes 100000 | tf_op jit(solution)/shard_map/head_product/pallas_call | solution.py:193
  165.4 2.2 collective-permute-start.21
  167.6 4.4 %all-to-all-start.4 = ((bf16[4,4,192,128]{3,2,1,0:T(8,128)(2,1)}), bf16[4,4,192,128]{3,2,1,0:T(8,128)(2,1)S(1)}, u32[]{:S(2)}, u32[]{:S(2)}) async-start(bf16[4,4,192,128]{3,2,1,0:T(8,128)(2,1)} %copy-done.22), calls=%async_computation.4 | async-start | bytes 1572864 | tf_op jit(solution)/shard_map/all_to_all | solution.py:1088
  172.0 1.9 collective-permute-start.22
  173.9 1.4 head_split.1
  175.9 1.5 collective-permute-start.24
  177.5 10.9 %collective-permute-done.22.refs_2_ = bf16[1280,128]{1,0:T(8,128)(2,1)S(1)} collective-permute-done((bf16[1280,128]{1,0:T(8,128)(2,1)}, bf16[1280,128]{1,0:T(8,128)(2,1)S(1)}, u32[]{:S(2)}, u32[]{:S(2)}) %collective-permute-start.22) | collective-permute-done | bytes 327712 | tf_op jit(solution)/shard_map/ppermute | solution.py:1080
  188.4 1.4 unpack_one.1
  191.1 2.6 %collective-permute-start.26 = (bf16[1152,128]{1,0:T(8,128)(2,1)S(1)}, bf16[1152,128]{1,0:T(8,128)(2,1)S(1)}, u32[]{:S(2)}, u32[]{:S(2)}) collective-permute-start(bf16[1152,128]{1,0:T(8,128)(2,1)S(1)} %get-tuple-element.178), channel_id=1, source_target_pairs={{0,12},{1,13},{2,14},{3,15},{4,8},{5,9},{6,10},{7,11},{8,4},{9,5},... | collective-permute-start | bytes 884744 | tf_op jit(solution)/shard_map/ppermute | solution.py:1080
  193.7 5.6 %latent_back.1 = (f32[8,128]{1,0:T(8,128)S(1)}, bf16[128,1024]{1,0:T(8,128)(2,1)}) custom-call(bf16[16,192,128]{2,1,0:T(8,128)(2,1)S(1)} %bitcast.18, f32[128,1024]{1,0:T(8,128)S(1)} %copy-done.30, bf16[128,1024]{1,0:T(8,128)(2,1)S(1)} %copy-done.5, f32[1,1024]{1,0:T(1,128)S(1)} %bitcast.23, bf16[1024,1024]{1,0:T(8,128)(2,1)} %wq_ref.1, ...), custom_call_target="tpu_custom_call" | custom-call | flops 1000000 | bytes 100000 | tf_op jit(solution)/shard_map/latent_back/pallas_call | solution.py:193
  199.5 5.5 %collective-permute-start.25 = (bf16[128,768]{1,0:T(8,128)(2,1)S(1)}, bf16[128,768]{1,0:T(8,128)(2,1)S(1)}, u32[]{:S(2)}, u32[]{:S(2)}) collective-permute-start(bf16[128,768]{1,0:T(8,128)(2,1)S(1)} %get-tuple-element.176), channel_id=1, source_target_pairs={{0,12},{1,13},{2,14},{3,15},{4,8},{5,9},{6,10},{7,11},{8,4},{9,5},... | collective-permute-start | bytes 589832 | tf_op jit(solution)/shard_map/ppermute | solution.py:1080
  209.5 4.2 %collective-permute-done.25.refs_1_ = bf16[128,768]{1,0:T(8,128)(2,1)S(1)} collective-permute-done((bf16[128,768]{1,0:T(8,128)(2,1)S(1)}, bf16[128,768]{1,0:T(8,128)(2,1)S(1)}, u32[]{:S(2)}, u32[]{:S(2)}) %collective-permute-start.25) | collective-permute-done | bytes 196640 | tf_op jit(solution)/shard_map/ppermute | solution.py:1080
  214.5 4.3 %all-to-all-start.5 = ((bf16[4,32,768]{2,1,0:T(8,128)(2,1)}), bf16[4,32,768]{2,1,0:T(8,128)(2,1)S(1)}, u32[]{:S(2)}, u32[]{:S(2)}) async-start(bf16[4,32,768]{2,1,0:T(8,128)(2,1)} %get-tuple-element.181), calls=%async_computation.5 | async-start | bytes 393216 | tf_op jit(solution)/shard_map/all_to_all | solution.py:1088
  218.8 1.7 add_convert_fusion
  221.2 2.9 %finish.1 = (f32[32,2816]{1,0:T(8,128)}, f32[32,2816]{1,0:T(8,128)}, f32[1,32]{1,0:T(1,128)}) custom-call(s32[2]{0:T(128)} %pad_add_fusion.1.at_ref, f32[2,32,512]{2,1,0:T(8,128)} %copy-done.53, f32[2,32,896]{2,1,0:T(8,128)} %copy-done.48, bf16[2,32,512]{2,1,0:T(8,128)(2,1)} %copy-done.70, bf16[2,32,896]{2,1,0:T(8,128)(2,1)} %copy-done.69, ...), custom_call_target="tpu_custom_call" | custom-call | flops 1000000 | bytes 100000 | tf_op jit(solution)/shard_map/finish/pallas_call | solution.py:905
  224.8 2.5 %head_rows.1 = (f32[32,1024]{1,0:T(8,128)}, f32[32,1024]{1,0:T(8,128)}, f32[32,1024]{1,0:T(8,128)}, f32[1,32]{1,0:T(1,128)}) custom-call(s32[2]{0:T(128)} %pad_add_fusion.1.at_ref, bf16[4,32,768]{2,1,0:T(8,128)(2,1)} %copy-done.68, f32[32,32]{1,0:T(8,128)} %reshape.90.gain_ref, bf16[1024,1024]{1,0:T(8,128)(2,1)} %wq_ref.1, bf16[1024,1024]{1,0:T(8,128)(2,1)} %wk_ref.1, ...), custom_call_target="tpu_custom_call" | custom-call | flops 1000000 | bytes 100000 | tf_op jit(solution)/shard_map/head_rows/pallas_call | solution.py:1048
  (210 shorter events, 43.3 us)
Async XLA Ops:
  6.6 26.4 %all-to-all-start = ((bf16[16,192,128]{2,1,0:T(8,128)(2,1)}), bf16[16,192,128]{2,1,0:T(8,128)(2,1)S(1)}, u32[]{:S(2)}, u32[]{:S(2)}) async-start(bf16[16,192,128]{2,1,0:T(8,128)(2,1)} %get-tuple-element.103), calls=%async_computation | async-start | bytes 1572864 | tf_op jit(solution)/shard_map/all_to_all | solution.py:1092
  13.9 11.6 %collective-permute-start = (bf16[128,1024]{1,0:T(8,128)(2,1)S(1)}, bf16[128,1024]{1,0:T(8,128)(2,1)S(1)}, u32[]{:S(2)}, u32[]{:S(2)}) collective-permute-start(bf16[128,1024]{1,0:T(8,128)(2,1)S(1)} %get-tuple-element.106), channel_id=1, source_target_pairs={{0,1},{1,0},{2,3},{3,2},{4,5},{5,4},{6,7},{7,6},{8,9},{9,8},{10,11... | collective-permute-start | bytes 786440 | tf_op jit(solution)/shard_map/ppermute | solution.py:1072
  14.4 13.0 %collective-permute-start.2 = (bf16[128,1024]{1,0:T(8,128)(2,1)S(1)}, bf16[128,1024]{1,0:T(8,128)(2,1)S(1)}, u32[]{:S(2)}, u32[]{:S(2)}) collective-permute-start(bf16[128,1024]{1,0:T(8,128)(2,1)S(1)} %copy-done), channel_id=1, source_target_pairs={{0,16},{16,0},{1,17},{17,1},{2,18},{18,2},{3,19},{19,3},{4,20},{20... | collective-permute-start | bytes 786440 | tf_op jit(solution)/shard_map/ppermute | solution.py:1068
  14.6 37.3 %copy-start.61 = (s32[4,1]{0,1:T(1,128)}, s32[4,1]{0,1:T(1,128)S(1)}, u32[]{:S(2)}) copy-start(s32[4,1]{0,1:T(1,128)S(1)} %reduce-window.8) | copy-start | bytes 52
  14.7 44.8 %copy-start.5 = (bf16[128,1024]{1,0:T(8,128)(2,1)S(1)}, bf16[128,1024]{1,0:T(8,128)(2,1)}, u32[]{:S(2)}) copy-start(bf16[128,1024]{1,0:T(8,128)(2,1)} %refs_2_.7) | copy-start | bytes 786436
  14.7 44.8 %copy-start.56 = (f32[1024]{0:T(1024)S(1)}, f32[1024]{0:T(1024)}, u32[]{:S(2)}) copy-start(f32[1024]{0:T(1024)} %param.19) | copy-start | bytes 12292
  14.8 47.6 %copy-start.63 = (s32[8]{0:T(128)}, s32[8]{0:T(128)S(1)}, u32[]{:S(2)}) copy-start(s32[8]{0:T(128)S(1)} %and_select_fusion.refs_1_) | copy-start | bytes 100
  14.9 47.5 %copy-start.65 = (s32[16]{0:T(128)}, s32[16]{0:T(128)S(1)}, u32[]{:S(2)}) copy-start(s32[16]{0:T(128)S(1)} %select_reduce_fusion.refs_0_) | copy-start | bytes 196
  25.5 36.9 %copy-start.15 = (bf16[256,1024]{1,0:T(8,128)(2,1)}, bf16[256,1024]{1,0:T(8,128)(2,1)S(1)}, u32[]{:S(2)}) copy-start(bf16[256,1024]{1,0:T(8,128)(2,1)S(1)} %constant_dynamic-update-slice_fusion.refs_1_) | copy-start | bytes 1572868
  25.5 34.0 %collective-permute-start.1 = (bf16[256,1024]{1,0:T(8,128)(2,1)S(1)}, bf16[256,1024]{1,0:T(8,128)(2,1)S(1)}, u32[]{:S(2)}, u32[]{:S(2)}) collective-permute-start(bf16[256,1024]{1,0:T(8,128)(2,1)S(1)} %constant_dynamic-update-slice_fusion.refs_1_), channel_id=1, source_target_pairs={{0,2},{1,3},{2,0},{3,1},{4,6},{5,7},{6,4},{7,5},{8,10},{9,11},{10,... | collective-permute-start | bytes 1572872 | tf_op jit(solution)/shard_map/ppermute | solution.py:1076
  43.4 16.1 %all-to-all-start.1 = ((bf16[16,64,128]{2,1,0:T(8,128)(2,1)}), bf16[16,64,128]{2,1,0:T(8,128)(2,1)S(1)}, u32[]{:S(2)}, u32[]{:S(2)}) async-start(bf16[16,64,128]{2,1,0:T(8,128)(2,1)} %get-tuple-element.105), calls=%async_computation.1 | async-start | bytes 524288 | tf_op jit(solution)/shard_map/all_to_all | solution.py:1092
  49.7 8.6 %collective-permute-start.3 = (bf16[256,512]{1,0:T(8,128)(2,1)}, bf16[256,512]{1,0:T(8,128)(2,1)S(1)}, u32[]{:S(2)}, u32[]{:S(2)}) collective-permute-start(bf16[256,512]{1,0:T(8,128)(2,1)} %pad_maximum_fusion), channel_id=1, source_target_pairs={{0,1},{1,0},{2,3},{3,2},{4,5},{5,4},{6,7},{7,6},{8,9},{9,8},{10,11... | collective-permute-start | bytes 786440 | tf_op jit(solution)/shard_map/ppermute | solution.py:1072
  51.9 7.6 %collective-permute-start.4 = (bf16[256,512]{1,0:T(8,128)(2,1)}, bf16[256,512]{1,0:T(8,128)(2,1)S(1)}, u32[]{:S(2)}, u32[]{:S(2)}) collective-permute-start(bf16[256,512]{1,0:T(8,128)(2,1)} %pad_maximum_fusion.1), channel_id=1, source_target_pairs={{0,2},{1,3},{2,0},{3,1},{4,6},{5,7},{6,4},{7,5},{8,10},{9,11},{10,... | collective-permute-start | bytes 786440 | tf_op jit(solution)/shard_map/ppermute | solution.py:1076
  62.4 1.6 collective-permute-start.5
  73.3 25.6 %collective-permute-start.6 = (bf16[3584,128]{1,0:T(8,128)(2,1)}, bf16[3584,128]{1,0:T(8,128)(2,1)S(1)}, u32[]{:S(2)}, u32[]{:S(2)}) collective-permute-start(bf16[3584,128]{1,0:T(8,128)(2,1)} %get-tuple-element.113.refs_1_), channel_id=1, source_target_pairs={{0,1},{1,0},{2,3},{3,2},{4,5},{5,4},{6,7},{7,6},{8,9},{9,8},{10,11... | collective-permute-start | bytes 2752520 | tf_op jit(solution)/shard_map/ppermute | solution.py:1072
  74.8 31.3 %collective-permute-start.11 = (bf16[3584,128]{1,0:T(8,128)(2,1)}, bf16[3584,128]{1,0:T(8,128)(2,1)S(1)}, u32[]{:S(2)}, u32[]{:S(2)}) collective-permute-start(bf16[3584,128]{1,0:T(8,128)(2,1)} %get-tuple-element.124.refs_1_), channel_id=1, source_target_pairs={{0,2},{1,3},{2,0},{3,1},{4,6},{5,7},{6,4},{7,5},{8,10},{9,11},{10,... | collective-permute-start | bytes 2752520 | tf_op jit(solution)/shard_map/ppermute | solution.py:1076
  75.6 1.5 collective-permute-start.8
  75.6 35.1 %collective-permute-start.13 = (bf16[1792,128]{1,0:T(8,128)(2,1)}, bf16[1792,128]{1,0:T(8,128)(2,1)}, u32[]{:S(2)}, u32[]{:S(2)}) collective-permute-start(bf16[1792,128]{1,0:T(8,128)(2,1)} %get-tuple-element.128.refs_2_), channel_id=1, source_target_pairs={{0,2},{1,3},{2,0},{3,1},{4,6},{5,7},{6,4},{7,5},{8,10},{9,11},{10,... | collective-permute-start | bytes 1376264 | tf_op jit(solution)/shard_map/ppermute | solution.py:1076
  76.8 10.9 %collective-permute-start.7 = (bf16[512,128]{1,0:T(8,128)(2,1)}, bf16[512,128]{1,0:T(8,128)(2,1)S(1)}, u32[]{:S(2)}, u32[]{:S(2)}) collective-permute-start(bf16[512,128]{1,0:T(8,128)(2,1)} %get-tuple-element.114), channel_id=1, source_target_pairs={{0,16},{16,0},{1,17},{17,1},{2,18},{18,2},{3,19},{19,3},{4,20},{20... | collective-permute-start | bytes 393224 | tf_op jit(solution)/shard_map/ppermute | solution.py:1068
  81.0 7.4 %collective-permute-start.9 = (bf16[128,1024]{1,0:T(8,128)(2,1)}, bf16[128,1024]{1,0:T(8,128)(2,1)}, u32[]{:S(2)}, u32[]{:S(2)}) collective-permute-start(bf16[128,1024]{1,0:T(8,128)(2,1)} %get-tuple-element.118.refs_3_), channel_id=1, source_target_pairs={{0,16},{16,0},{1,17},{17,1},{2,18},{18,2},{3,19},{19,3},{4,20},{20... | collective-permute-start | bytes 786440 | tf_op jit(solution)/shard_map/ppermute | solution.py:1068
  81.7 30.6 %all-to-all-start.2 = ((bf16[16,64,128]{2,1,0:T(8,128)(2,1)}), bf16[16,64,128]{2,1,0:T(8,128)(2,1)}, u32[]{:S(2)}, u32[]{:S(2)}) async-start(bf16[16,64,128]{2,1,0:T(8,128)(2,1)} %bitcast.21), calls=%async_computation.2 | async-start | bytes 524288 | tf_op jit(solution)/shard_map/all_to_all | solution.py:1092
  87.8 23.8 %collective-permute-start.15 = (bf16[1792,128]{1,0:T(8,128)(2,1)}, bf16[1792,128]{1,0:T(8,128)(2,1)S(1)}, u32[]{:S(2)}, u32[]{:S(2)}) collective-permute-start(bf16[1792,128]{1,0:T(8,128)(2,1)} %copy-done.35), channel_id=1, source_target_pairs={{0,1},{1,0},{2,3},{3,2},{4,5},{5,4},{6,7},{7,6},{8,9},{9,8},{10,11... | collective-permute-start | bytes 1376264 | tf_op jit(solution)/shard_map/ppermute | solution.py:1072
  90.0 16.9 %copy-start.18 = (bf16[256,512]{1,0:T(8,128)(2,1)S(1)}, bf16[256,512]{1,0:T(8,128)(2,1)}, u32[]{:S(2)}) copy-start(bf16[256,512]{1,0:T(8,128)(2,1)} %copy-done.17) | copy-start | bytes 786436
  93.8 22.7 %collective-permute-start.14 = (bf16[1024,128]{1,0:T(8,128)(2,1)}, bf16[1024,128]{1,0:T(8,128)(2,1)}, u32[]{:S(2)}, u32[]{:S(2)}) collective-permute-start(bf16[1024,128]{1,0:T(8,128)(2,1)} %get-tuple-element.130), channel_id=1, source_target_pairs={{0,2},{1,3},{2,0},{3,1},{4,6},{5,7},{6,4},{7,5},{8,10},{9,11},{10,... | collective-permute-start | bytes 786440 | tf_op jit(solution)/shard_map/ppermute | solution.py:1076
  98.9 17.7 %collective-permute-start.16 = (bf16[1024,128]{1,0:T(8,128)(2,1)}, bf16[1024,128]{1,0:T(8,128)(2,1)}, u32[]{:S(2)}, u32[]{:S(2)}) collective-permute-start(bf16[1024,128]{1,0:T(8,128)(2,1)} %get-tuple-element.133), channel_id=1, source_target_pairs={{0,1},{1,0},{2,3},{3,2},{4,5},{5,4},{6,7},{7,6},{8,9},{9,8},{10,11... | collective-permute-start | bytes 786440 | tf_op jit(solution)/shard_map/ppermute | solution.py:1072
  106.1 34.6 %collective-permute-start.10 = (bf16[4,640,128]{2,1,0:T(8,128)(2,1)}, bf16[4,640,128]{2,1,0:T(8,128)(2,1)}, u32[]{:S(2)}, u32[]{:S(2)}) collective-permute-start(bf16[4,640,128]{2,1,0:T(8,128)(2,1)} %get-tuple-element.122), channel_id=1, source_target_pairs={{0,2},{1,3},{2,0},{3,1},{4,6},{5,7},{6,4},{7,5},{8,10},{9,11},{10,... | collective-permute-start | bytes 1966088 | tf_op jit(solution)/shard_map/ppermute | solution.py:1076
  110.7 30.0 %collective-permute-start.12 = (bf16[4,640,128]{2,1,0:T(8,128)(2,1)}, bf16[4,640,128]{2,1,0:T(8,128)(2,1)}, u32[]{:S(2)}, u32[]{:S(2)}) collective-permute-start(bf16[4,640,128]{2,1,0:T(8,128)(2,1)} %get-tuple-element.127), channel_id=1, source_target_pairs={{0,1},{1,0},{2,3},{3,2},{4,5},{5,4},{6,7},{7,6},{8,9},{9,8},{10,11... | collective-permute-start | bytes 1966088 | tf_op jit(solution)/shard_map/ppermute | solution.py:1072
  129.2 30.7 %all-to-all-start.3 = ((bf16[16,192,128]{2,1,0:T(8,128)(2,1)}), bf16[16,192,128]{2,1,0:T(8,128)(2,1)S(1)}, u32[]{:S(2)}, u32[]{:S(2)}) async-start(bf16[16,192,128]{2,1,0:T(8,128)(2,1)} %copy-done.21), calls=%async_computation.3 | async-start | bytes 1572864 | tf_op jit(solution)/shard_map/all_to_all | solution.py:1088
  142.3 16.7 %collective-permute-start.18 = (bf16[2560,128]{1,0:T(8,128)(2,1)S(1)}, bf16[2560,128]{1,0:T(8,128)(2,1)S(1)}, u32[]{:S(2)}, u32[]{:S(2)}) collective-permute-start(bf16[2560,128]{1,0:T(8,128)(2,1)S(1)} %get-tuple-element.148), channel_id=1, source_target_pairs={{0,4},{1,5},{2,6},{3,7},{4,0},{5,1},{6,2},{7,3},{8,12},{9,13},{10,... | collective-permute-start | bytes 1966088 | tf_op jit(solution)/shard_map/ppermute | solution.py:1080
  142.4 12.6 %collective-permute-start.19 = (bf16[4,576,128]{2,1,0:T(8,128)(2,1)S(1)}, bf16[4,576,128]{2,1,0:T(8,128)(2,1)S(1)}, u32[]{:S(2)}, u32[]{:S(2)}) collective-permute-start(bf16[4,576,128]{2,1,0:T(8,128)(2,1)S(1)} %get-tuple-element.150), channel_id=1, source_target_pairs={{0,2},{1,3},{2,0},{3,1},{4,6},{5,7},{6,4},{7,5},{8,10},{9,11},{10,... | collective-permute-start | bytes 1769480 | tf_op jit(solution)/shard_map/ppermute | solution.py:1076
  143.7 12.3 %collective-permute-start.20 = (bf16[4,576,128]{2,1,0:T(8,128)(2,1)S(1)}, bf16[4,576,128]{2,1,0:T(8,128)(2,1)S(1)}, u32[]{:S(2)}, u32[]{:S(2)}) collective-permute-start(bf16[4,576,128]{2,1,0:T(8,128)(2,1)S(1)} %get-tuple-element.152), channel_id=1, source_target_pairs={{0,1},{1,0},{2,3},{3,2},{4,5},{5,4},{6,7},{7,6},{8,9},{9,8},{10,11... | collective-permute-start | bytes 1769480 | tf_op jit(solution)/shard_map/ppermute | solution.py:1072
  165.4 8.5 %collective-permute-start.23 = (bf16[512,768]{1,0:T(8,128)(2,1)}, bf16[512,768]{1,0:T(8,128)(2,1)S(1)}, u32[]{:S(2)}, u32[]{:S(2)}) collective-permute-start(bf16[512,768]{1,0:T(8,128)(2,1)} %get-tuple-element.165), channel_id=1, source_target_pairs={{0,16},{16,0},{1,17},{17,1},{2,18},{18,2},{3,19},{19,3},{4,20},{20... | collective-permute-start | bytes 2359304 | tf_op jit(solution)/shard_map/ppermute | solution.py:1068
  165.4 24.4 %collective-permute-start.21 = (bf16[2304,128]{1,0:T(8,128)(2,1)}, bf16[2304,128]{1,0:T(8,128)(2,1)}, u32[]{:S(2)}, u32[]{:S(2)}) collective-permute-start(bf16[2304,128]{1,0:T(8,128)(2,1)} %get-tuple-element.160), channel_id=1, source_target_pairs={{0,4},{1,5},{2,6},{3,7},{4,0},{5,1},{6,2},{7,3},{8,12},{9,13},{10,... | collective-permute-start | bytes 1769480 | tf_op jit(solution)/shard_map/ppermute | solution.py:1080
  167.6 26.1 %all-to-all-start.4 = ((bf16[4,4,192,128]{3,2,1,0:T(8,128)(2,1)}), bf16[4,4,192,128]{3,2,1,0:T(8,128)(2,1)S(1)}, u32[]{:S(2)}, u32[]{:S(2)}) async-start(bf16[4,4,192,128]{3,2,1,0:T(8,128)(2,1)} %copy-done.22), calls=%async_computation.4 | async-start | bytes 1572864 | tf_op jit(solution)/shard_map/all_to_all | solution.py:1088
  172.0 17.8 %copy-start.40 = (bf16[1152,128]{1,0:T(8,128)(2,1)S(1)}, bf16[1152,128]{1,0:T(8,128)(2,1)}, u32[]{:S(2)}) copy-start(bf16[1152,128]{1,0:T(8,128)(2,1)} %copy-done.39) | copy-start | bytes 884740
  172.0 17.8 %copy-start.42 = (bf16[1152,128]{1,0:T(8,128)(2,1)S(1)}, bf16[1152,128]{1,0:T(8,128)(2,1)}, u32[]{:S(2)}) copy-start(bf16[1152,128]{1,0:T(8,128)(2,1)} %copy-done.41) | copy-start | bytes 884740
  172.0 16.4 %collective-permute-start.22 = (bf16[1280,128]{1,0:T(8,128)(2,1)}, bf16[1280,128]{1,0:T(8,128)(2,1)S(1)}, u32[]{:S(2)}, u32[]{:S(2)}) collective-permute-start(bf16[1280,128]{1,0:T(8,128)(2,1)} %copy-done.67), channel_id=1, source_target_pairs={{0,12},{1,13},{2,14},{3,15},{4,8},{5,9},{6,10},{7,11},{8,4},{9,5},... | collective-permute-start | bytes 983048 | tf_op jit(solution)/shard_map/ppermute | solution.py:1080
  173.9 19.8 %copy-start.55 = (f32[1024]{0:T(1024)S(1)}, f32[1024]{0:T(1024)}, u32[]{:S(2)}) copy-start(f32[1024]{0:T(1024)} %param.14) | copy-start | bytes 12292
  175.9 17.7 %copy-start.30 = (f32[128,1024]{1,0:T(8,128)S(1)}, f32[128,1024]{1,0:T(8,128)}, u32[]{:S(2)}) copy-start(f32[128,1024]{1,0:T(8,128)} %copy-done.29) | copy-start | bytes 1572868
  175.9 23.4 %collective-permute-start.24 = (bf16[256,768]{1,0:T(8,128)(2,1)}, bf16[256,768]{1,0:T(8,128)(2,1)S(1)}, u32[]{:S(2)}, u32[]{:S(2)}) collective-permute-start(bf16[256,768]{1,0:T(8,128)(2,1)} %get-tuple-element.173), channel_id=1, source_target_pairs={{0,4},{1,5},{2,6},{3,7},{4,0},{5,1},{6,2},{7,3},{8,12},{9,13},{10,... | collective-permute-start | bytes 1179656 | tf_op jit(solution)/shard_map/ppermute | solution.py:1080
  191.1 16.0 %collective-permute-start.26 = (bf16[1152,128]{1,0:T(8,128)(2,1)S(1)}, bf16[1152,128]{1,0:T(8,128)(2,1)S(1)}, u32[]{:S(2)}, u32[]{:S(2)}) collective-permute-start(bf16[1152,128]{1,0:T(8,128)(2,1)S(1)} %get-tuple-element.178), channel_id=1, source_target_pairs={{0,12},{1,13},{2,14},{3,15},{4,8},{5,9},{6,10},{7,11},{8,4},{9,5},... | collective-permute-start | bytes 884744 | tf_op jit(solution)/shard_map/ppermute | solution.py:1080
  193.6 25.1 %collective-permute-start.17 = (bf16[128,1024]{1,0:T(8,128)(2,1)}, bf16[128,1024]{1,0:T(8,128)(2,1)}, u32[]{:S(2)}, u32[]{:S(2)}) collective-permute-start(bf16[128,1024]{1,0:T(8,128)(2,1)} %get-tuple-element.144), channel_id=1, source_target_pairs={{0,16},{16,0},{1,17},{17,1},{2,18},{18,2},{3,19},{19,3},{4,20},{20... | collective-permute-start | bytes 786440 | tf_op jit(solution)/shard_map/ppermute | solution.py:1068
  199.3 19.4 %copy-start.9 = (f32[128,1024]{1,0:T(8,128)S(1)}, f32[128,1024]{1,0:T(8,128)}, u32[]{:S(2)}) copy-start(f32[128,1024]{1,0:T(8,128)} %copy-done.8) | copy-start | bytes 1572868
  199.4 19.4 %copy-start.32 = (f32[128,1024]{1,0:T(8,128)S(1)}, f32[128,1024]{1,0:T(8,128)}, u32[]{:S(2)}) copy-start(f32[128,1024]{1,0:T(8,128)} %copy-done.31) | copy-start | bytes 1572868
  199.5 14.2 %collective-permute-start.25 = (bf16[128,768]{1,0:T(8,128)(2,1)S(1)}, bf16[128,768]{1,0:T(8,128)(2,1)S(1)}, u32[]{:S(2)}, u32[]{:S(2)}) collective-permute-start(bf16[128,768]{1,0:T(8,128)(2,1)S(1)} %get-tuple-element.176), channel_id=1, source_target_pairs={{0,12},{1,13},{2,14},{3,15},{4,8},{5,9},{6,10},{7,11},{8,4},{9,5},... | collective-permute-start | bytes 589832 | tf_op jit(solution)/shard_map/ppermute | solution.py:1080
  207.0 13.5 %collective-permute-start.27 = (bf16[2,32,512]{2,1,0:T(8,128)(2,1)S(1)}, bf16[2,32,512]{2,1,0:T(8,128)(2,1)S(1)}, u32[]{:S(2)}, u32[]{:S(2)}) collective-permute-start(bf16[2,32,512]{2,1,0:T(8,128)(2,1)S(1)} %get-tuple-element.189), channel_id=1, source_target_pairs={{0,16},{16,0},{1,17},{17,1},{2,18},{18,2},{3,19},{19,3},{4,20},{20... | collective-permute-start | bytes 196616 | tf_op jit(solution)/shard_map/ppermute | solution.py:1068
  209.0 11.6 %collective-permute-start.28 = (bf16[2,32,896]{2,1,0:T(8,128)(2,1)S(1)}, bf16[2,32,896]{2,1,0:T(8,128)(2,1)S(1)}, u32[]{:S(2)}, u32[]{:S(2)}) collective-permute-start(bf16[2,32,896]{2,1,0:T(8,128)(2,1)S(1)} %get-tuple-element.190), channel_id=1, source_target_pairs={{0,16},{16,0},{1,17},{17,1},{2,18},{18,2},{3,19},{19,3},{4,20},{20... | collective-permute-start | bytes 344072 | tf_op jit(solution)/shard_map/ppermute | solution.py:1068
  214.5 9.6 %all-to-all-start.5 = ((bf16[4,32,768]{2,1,0:T(8,128)(2,1)}), bf16[4,32,768]{2,1,0:T(8,128)(2,1)S(1)}, u32[]{:S(2)}, u32[]{:S(2)}) async-start(bf16[4,32,768]{2,1,0:T(8,128)(2,1)} %get-tuple-element.181), calls=%async_computation.5 | async-start | bytes 393216 | tf_op jit(solution)/shard_map/all_to_all | solution.py:1088
  (60 other events, 291.8 us)
